TPU v7x, 512 devices: a whole 4x4x16 slice. The times are simulated.
512 devices in a mesh: blk: 16 (over z_lo, core), wide: 32 (over x, z_hi, y).
Axes of the slice: x: 4, y: 4, z: 16 (z_hi: 2, z_lo: 8; z = z_hi * 8 + z_lo), core: 2. Of those that a mesh axis runs over, the one named last changes fastest.
Arguments:
- images: bfloat16 [196608, 768], P(('blk', 'wide')), may hold values from -0.21875 to 0.21875
- captions: bfloat16 [196608, 768], P(('blk', 'wide')), may hold values from -0.21875 to 0.21875
- logit_scale: float32 [], replicated, may hold values from 10 to 20
- row_lse: float32 [196608], replicated, may hold values from 2 to 5
- col_lse: float32 [196608], replicated, may hold values from 2 to 5
Outputs:
- image_grad: float32 [196608, 768], P(('blk', 'wide'))
- caption_grad: float32 [196608, 768], P(('blk', 'wide'))
All inputs are finite; a program needn't handle non-finite values.
Results may differ from a plain program's by a relative error of at most 0.0021.
Values may be sent and summed in bfloat16 or wider, within the bound.
No kernel may reach another device: no remote copies, remote signals or barrier semaphores. Data moves between devices by JAX's collectives and lax.ppermute only.
A program may use at most 64 MiB of HBM per device.

v0:
```python
import jax
import jax.numpy as jnp
from jax import lax
from jax.sharding import PartitionSpec as P

STEPS = 3


def shifted(x, axis, by):
    length = lax.axis_size(axis)
    return lax.ppermute(x, axis, [(i, (i + by) % length) for i in range(length)])


def homeward(pieces):
    running = pieces[0][1]
    previous = pieces[0][0]
    targets = list(pieces[1:])
    targets.append((0, None))
    for distance, contrib in targets:
        running = shifted(running, "blk", distance - previous)
        previous = distance
    return running


def take_rows(values, start, count):
    return lax.dynamic_slice_in_dim(values, start, count)


def on_device(images, captions, logit_scale, row_lse, col_lse):
    row_count = images.shape[0]
    blk_count = lax.axis_size("blk")
    wide_count = lax.axis_size("wide")
    blk_index = lax.axis_index("blk")
    wide_index = lax.axis_index("wide")
    own_rows = take_rows(row_lse, (blk_index * wide_count + wide_index) * row_count, row_count)
    hopped = shifted(captions, "wide", 1)
    carried = jnp.concatenate([captions, hopped], axis=0)
    eye_block = jnp.eye(row_count, 2 * row_count, dtype=jnp.float32)
    image_running = jnp.zeros(images.shape, jnp.float32)
    travelling = jnp.zeros(carried.shape, jnp.float32)
    pieces = []
    for offset in range(STEPS + 1):
        source_blk = (blk_index - offset) % blk_count
        own_block = (source_blk * wide_count + wide_index) * row_count
        far_block = (source_blk * wide_count + (wide_index - 1) % wide_count) * row_count
        col_part = jnp.concatenate(
            [take_rows(col_lse, own_block, row_count), take_rows(col_lse, far_block, row_count)]
        )
        logits = logit_scale * lax.dot_general(
            images, carried, (((1,), (1,)), ((), ())), preferred_element_type=jnp.float32
        )
        weights = 0.5 * (jnp.exp(logits - own_rows[:, None]) + jnp.exp(logits - col_part[None, :]))
        if offset == 0:
            weights = weights - eye_block
        weights = weights.astype(jnp.bfloat16)
        image_running = image_running + jnp.dot(
            weights, carried, preferred_element_type=jnp.float32
        )
        partial_sum = lax.dot_general(
            weights, images, (((0,), (0,)), ((), ())), preferred_element_type=jnp.float32
        )
        travelling = travelling + partial_sum
        if offset < STEPS:
            travelling = shifted(travelling, "blk", 1)
        if offset < STEPS:
            carried = shifted(carried, "blk", 1)
    pieces = [(STEPS, travelling)]
    at_home = homeward(pieces)
    at_home = at_home[:row_count] + shifted(at_home[row_count:], "wide", -1)
    return (logit_scale * image_running, logit_scale * at_home)


def solution(mesh):
    in_specs = (P(("blk", "wide"), None), P(("blk", "wide"), None), P(), P(), P())
    out_specs = (P(("blk", "wide"), None), P(("blk", "wide"), None))
    return jax.shard_map(
        on_device, mesh=mesh, in_specs=in_specs, out_specs=out_specs, check_vma=False
    )
```

profile of v0, /device:TPU:1, one launch (start us, length us, event | category | flops | bytes accessed | tf_op | source)
XLA Modules:
  0.0 446.2 jit_solution(5028801480524122625)
XLA Ops:
  0.6 0.0 copy-start
  0.6 4.2 collective-permute-start
  5.6 0.8 dynamic_slice.27
  6.4 0.9 fusion.3
  7.3 1.1 constant_dynamic-update-slice_fusion.1
  8.4 28.9 %collective-permute-done = bf16[384,768]{1,0:T(8,128)(2,1)S(1)} collective-permute-done((bf16[384,768]{1,0:T(8,128)(2,1)}, bf16[384,768]{1,0:T(8,128)(2,1)S(1)}, u32[]{:S(2)}, u32[]{:S(2)}) %collective-permute-start) | collective-permute-done | bytes 589856 | tf_op jit(solution)/shard_map/ppermute | solution.py:11
  37.3 0.0 copy-done
  37.3 1.0 fusion.2
  38.3 0.8 fusion.5
  39.1 42.3 %collective-permute-start.4 = (f32[768,768]{1,0:T(8,128)S(1)}, f32[768,768]{1,0:T(8,128)S(1)}, u32[]{:S(2)}, u32[]{:S(2)}) collective-permute-start(f32[768,768]{1,0:T(8,128)S(1)} %fusion.5), channel_id=1, source_target_pairs={{0,32},{32,64},{64,96},{96,128},{128,160},{160,192},{192,224},{224... | collective-permute-start | bytes 7077896 | tf_op jit(solution)/shard_map/ppermute | solution.py:11
  81.4 1.9 collective-permute-start.1
  83.4 36.5 %collective-permute-done.1 = bf16[768,768]{1,0:T(8,128)(2,1)S(1)} collective-permute-done((bf16[768,768]{1,0:T(8,128)(2,1)S(1)}, bf16[768,768]{1,0:T(8,128)(2,1)S(1)}, u32[]{:S(2)}, u32[]{:S(2)}) %collective-permute-start.1) | collective-permute-done | bytes 1179680 | tf_op jit(solution)/shard_map/ppermute | solution.py:11
  119.8 1.0 multiply_convert_fusion.2
  120.8 0.0 collective-permute-done.4
  120.8 0.8 convolution_add_fusion
  121.6 4.4 collective-permute-start.5
  126.0 1.9 collective-permute-start.2
  127.9 36.5 %collective-permute-done.2 = bf16[768,768]{1,0:T(8,128)(2,1)S(1)} collective-permute-done((bf16[768,768]{1,0:T(8,128)(2,1)S(1)}, bf16[768,768]{1,0:T(8,128)(2,1)S(1)}, u32[]{:S(2)}, u32[]{:S(2)}) %collective-permute-start.2) | collective-permute-done | bytes 1179680 | tf_op jit(solution)/shard_map/ppermute | solution.py:11
  164.4 1.0 multiply_convert_fusion.1
  165.4 0.8 fusion.6
  166.1 0.0 collective-permute-done.5
  166.2 0.3 add.157
  166.5 4.4 collective-permute-start.6
  170.9 1.9 collective-permute-start.3
  172.8 36.5 %collective-permute-done.3 = bf16[768,768]{1,0:T(8,128)(2,1)S(1)} collective-permute-done((bf16[768,768]{1,0:T(8,128)(2,1)S(1)}, bf16[768,768]{1,0:T(8,128)(2,1)S(1)}, u32[]{:S(2)}, u32[]{:S(2)}) %collective-permute-start.3) | collective-permute-done | bytes 1179680 | tf_op jit(solution)/shard_map/ppermute | solution.py:11
  209.3 0.9 multiply_convert_fusion
  210.2 0.8 fusion.7
  211.0 0.0 collective-permute-done.6
  211.0 0.3 add.158
  211.3 4.9 %collective-permute-start.7 = (f32[768,768]{1,0:T(8,128)S(1)}, f32[768,768]{1,0:T(8,128)S(1)}, u32[]{:S(2)}, u32[]{:S(2)}) collective-permute-start(f32[768,768]{1,0:T(8,128)S(1)} %add.158), channel_id=1, source_target_pairs={{0,416},{32,448},{64,480},{96,0},{128,32},{160,64},{192,96},{224,1... | collective-permute-start | bytes 7077896 | tf_op jit(solution)/shard_map/ppermute | solution.py:11
  216.3 163.3 %collective-permute-done.7 = f32[768,768]{1,0:T(8,128)S(1)} collective-permute-done((f32[768,768]{1,0:T(8,128)S(1)}, f32[768,768]{1,0:T(8,128)S(1)}, u32[]{:S(2)}, u32[]{:S(2)}) %collective-permute-start.7) | collective-permute-done | bytes 2359328 | tf_op jit(solution)/shard_map/ppermute | solution.py:11
  379.5 0.1 slice.9
  379.6 1.9 collective-permute-start.8
  381.6 0.7 fusion.4
  382.2 0.7 convolution_add_fusion.3
  382.9 0.7 convolution_add_fusion.2
  383.6 1.7 fusion
  385.2 59.9 %collective-permute-done.8 = f32[384,768]{1,0:T(8,128)S(1)} collective-permute-done((f32[384,768]{1,0:T(8,128)S(1)}, f32[384,768]{1,0:T(8,128)S(1)}, u32[]{:S(2)}, u32[]{:S(2)}) %collective-permute-start.8) | collective-permute-done | bytes 1179680 | tf_op jit(solution)/shard_map/ppermute | solution.py:11
  445.1 1.2 fusion.1
  (5 shorter events, 0.1 us)
Async XLA Ops:
  0.6 36.7 %copy-start = (bf16[384,768]{1,0:T(8,128)(2,1)S(1)}, bf16[384,768]{1,0:T(8,128)(2,1)}, u32[]{:S(2)}) copy-start(bf16[384,768]{1,0:T(8,128)(2,1)} %param.5) | copy-start | bytes 1769476
  0.6 36.6 %collective-permute-start = (bf16[384,768]{1,0:T(8,128)(2,1)}, bf16[384,768]{1,0:T(8,128)(2,1)S(1)}, u32[]{:S(2)}, u32[]{:S(2)}) collective-permute-start(bf16[384,768]{1,0:T(8,128)(2,1)} %param.6), channel_id=1, source_target_pairs={{0,1},{1,2},{2,3},{3,4},{4,5},{5,6},{6,7},{7,8},{8,9},{9,10},{10,1... | collective-permute-start | bytes 1769480 | tf_op jit(solution)/shard_map/ppermute | solution.py:11
  39.1 81.7 %collective-permute-start.4 = (f32[768,768]{1,0:T(8,128)S(1)}, f32[768,768]{1,0:T(8,128)S(1)}, u32[]{:S(2)}, u32[]{:S(2)}) collective-permute-start(f32[768,768]{1,0:T(8,128)S(1)} %fusion.5), channel_id=1, source_target_pairs={{0,32},{32,64},{64,96},{96,128},{128,160},{160,192},{192,224},{224... | collective-permute-start | bytes 7077896 | tf_op jit(solution)/shard_map/ppermute | solution.py:11
  81.4 38.4 %collective-permute-start.1 = (bf16[768,768]{1,0:T(8,128)(2,1)S(1)}, bf16[768,768]{1,0:T(8,128)(2,1)S(1)}, u32[]{:S(2)}, u32[]{:S(2)}) collective-permute-start(bf16[768,768]{1,0:T(8,128)(2,1)S(1)} %constant_dynamic-update-slice_fusion), channel_id=1, source_target_pairs={{0,32},{32,64},{64,96},{96,128},{128,160},{160,192},{192,224},{224... | collective-permute-start | bytes 3538952 | tf_op jit(solution)/shard_map/ppermute | solution.py:11
  121.6 44.5 %collective-permute-start.5 = (f32[768,768]{1,0:T(8,128)S(1)}, f32[768,768]{1,0:T(8,128)S(1)}, u32[]{:S(2)}, u32[]{:S(2)}) collective-permute-start(f32[768,768]{1,0:T(8,128)S(1)} %convolution_add_fusion), channel_id=1, source_target_pairs={{0,32},{32,64},{64,96},{96,128},{128,160},{160,192},{192,224},{224... | collective-permute-start | bytes 7077896 | tf_op jit(solution)/shard_map/ppermute | solution.py:11
  126.0 38.4 %collective-permute-start.2 = (bf16[768,768]{1,0:T(8,128)(2,1)S(1)}, bf16[768,768]{1,0:T(8,128)(2,1)S(1)}, u32[]{:S(2)}, u32[]{:S(2)}) collective-permute-start(bf16[768,768]{1,0:T(8,128)(2,1)S(1)} %collective-permute-done.1), channel_id=1, source_target_pairs={{0,32},{32,64},{64,96},{96,128},{128,160},{160,192},{192,224},{224... | collective-permute-start | bytes 3538952 | tf_op jit(solution)/shard_map/ppermute | solution.py:11
  166.5 44.5 %collective-permute-start.6 = (f32[768,768]{1,0:T(8,128)S(1)}, f32[768,768]{1,0:T(8,128)S(1)}, u32[]{:S(2)}, u32[]{:S(2)}) collective-permute-start(f32[768,768]{1,0:T(8,128)S(1)} %add.157), channel_id=1, source_target_pairs={{0,32},{32,64},{64,96},{96,128},{128,160},{160,192},{192,224},{224... | collective-permute-start | bytes 7077896 | tf_op jit(solution)/shard_map/ppermute | solution.py:11
  170.9 38.4 %collective-permute-start.3 = (bf16[768,768]{1,0:T(8,128)(2,1)S(1)}, bf16[768,768]{1,0:T(8,128)(2,1)S(1)}, u32[]{:S(2)}, u32[]{:S(2)}) collective-permute-start(bf16[768,768]{1,0:T(8,128)(2,1)S(1)} %collective-permute-done.2), channel_id=1, source_target_pairs={{0,32},{32,64},{64,96},{96,128},{128,160},{160,192},{192,224},{224... | collective-permute-start | bytes 3538952 | tf_op jit(solution)/shard_map/ppermute | solution.py:11
  211.3 168.2 %collective-permute-start.7 = (f32[768,768]{1,0:T(8,128)S(1)}, f32[768,768]{1,0:T(8,128)S(1)}, u32[]{:S(2)}, u32[]{:S(2)}) collective-permute-start(f32[768,768]{1,0:T(8,128)S(1)} %add.158), channel_id=1, source_target_pairs={{0,416},{32,448},{64,480},{96,0},{128,32},{160,64},{192,96},{224,1... | collective-permute-start | bytes 7077896 | tf_op jit(solution)/shard_map/ppermute | solution.py:11
  379.6 65.5 %collective-permute-start.8 = (f32[384,768]{1,0:T(8,128)S(1)}, f32[384,768]{1,0:T(8,128)S(1)}, u32[]{:S(2)}, u32[]{:S(2)}) collective-permute-start(f32[384,768]{1,0:T(8,128)S(1)} %slice.9), channel_id=1, source_target_pairs={{0,31},{1,0},{2,1},{3,2},{4,3},{5,4},{6,5},{7,6},{8,7},{9,8},{10,9... | collective-permute-start | bytes 3538952 | tf_op jit(solution)/shard_map/ppermute | solution.py:11
where the time goes:
time: 447 us; the launch traced here: 446 us
  waiting for transfers between devices  361 us (81%)
  starting transfers between devices  67.9 us (15%)
  matrix products  10.6 us (2%)
    ppermute x9, waiting for transfers between devices, shifted(): lax.ppermute(x, axis, [(i, (i + by) % length) for i in range(length)])  361 us
    ppermute x9, starting transfers between devices, shifted(): lax.ppermute(x, axis, [(i, (i + by) % length) for i in range(length)])  67.9 us
  transfers between devices with their start and end apart: 9, of which 6 were waited for; matrix products, arithmetic and copies ran while one was open for 2% of the time, Pallas kernels for 0%

commit v1 on v0

v1 whole, which is shorter than its diff:
```python
import jax
import jax.numpy as jnp
from jax import lax
from jax.sharding import PartitionSpec as P

AXES = ("blk", "wide")


def coordinates(blk, wide):
    return wide // 8, (wide // 4) % 2, wide % 4, blk // 2, blk % 2


def device_id(x, half, y, z, core):
    return ((z % 8) * 2 + core) * 32 + ((x % 4) * 2 + half) * 4 + y


def pairs(target):
    found = []
    for blk in range(16):
        for wide in range(32):
            x, half, y, z, core = coordinates(blk, wide)
            sign = 1 if core == 1 else -1
            mirrored = y if core == 1 else 3 - y
            there = target(x, half, mirrored, z, core, sign)
            if there is not None:
                x2, half2, mirrored2, z2, core2 = there
                y2 = mirrored2 if core == 1 else 3 - mirrored2
                found.append((blk * 32 + wide, device_id(x2, half2, y2, z2, core2)))
    return found


def crossing(x, half, sign):
    if sign == 1:
        return (x, 1) if half == 0 else (x + 1, 0)
    return (x, 0) if half == 1 else (x - 1, 1)


def to_sibling(x, h, m, z, c, s):
    y = m if c == 1 else 3 - m
    return x, h, (y if c == 1 else 3 - y), z, 1 - c


def to_next_chip(x, h, m, z, c, s):
    return x, h, m, z + s, c


def to_previous_chip(x, h, m, z, c, s):
    return x, h, m, z - s, c


def to_next_wide(x, h, m, z, c, s):
    return (x, h, m + 1, z, c) if m < 3 else None


def across(x, h, m, z, c, s):
    x2, h2 = crossing(x, h, s)
    return x2, h2, m, z + s, c


def line_to_line(here, there):
    return lambda x, h, m, z, c, s: (x, h, there, z, c) if m == here else None


def send(x, target):
    return lax.ppermute(x, AXES, pairs(target))


def on_device(images, captions, logit_scale, row_lse, col_lse):
    rows = images.shape[0]
    quarter = rows // 4
    blk = lax.axis_index("blk")
    wide = lax.axis_index("wide")
    core = blk % 2
    sign = 2 * core - 1
    y = wide % 4
    mirrored = jnp.where(core == 1, y, 3 - y)
    carries_captions = core == 1

    outer = jnp.where(carries_captions, captions, images)
    other = jnp.where(carries_captions, images, captions)

    def wanted(step):
        return quarter * step, quarter * (step + 1)

    def part(block, step):
        low, high = wanted(step)
        return block[low:high]

    inner = send(other, to_sibling)
    outer1 = send(outer, to_next_chip)
    both = [jnp.concatenate([part(inner, q), part(outer, q)], axis=0) for q in range(4)]
    spread0 = send(both[0], line_to_line(3, 0))
    spread1 = send(both[1], line_to_line(3, 2))
    spread2 = send(both[2], line_to_line(3, 1))
    held = jnp.where(
        mirrored == 0,
        spread0,
        jnp.where(mirrored == 2, spread1, jnp.where(mirrored == 1, spread2, both[3])),
    )
    crossed = send(held, across)
    inner1 = send(inner, to_next_chip)
    outer2 = send(outer1, to_next_chip)
    pair0 = send(jnp.concatenate([inner, outer], axis=0), to_next_wide)
    pair1 = send(jnp.concatenate([inner1, outer1], axis=0), to_next_wide)
    far2 = send(outer2, to_next_wide)
    back = send(crossed, to_previous_chip)
    ahead = send(crossed[quarter:], to_next_chip)

    def collect(mine):
        q1 = send(mine, line_to_line(2, 0))
        q2 = send(mine, line_to_line(1, 0))
        q3 = send(mine, line_to_line(3, 0))
        return [mine, q1, q2, q3]

    got1 = collect(crossed)
    got0 = collect(jnp.concatenate([back, ahead], axis=0))
    at_edge = mirrored == 0

    def edge(got, k, usual):
        whole = jnp.concatenate([g[k * quarter : (k + 1) * quarter] for g in got], axis=0)
        return jnp.where(at_edge, whole, usual)

    hop_inner1 = edge(got1, 0, pair1[:rows])
    hop_outer1 = edge(got1, 1, pair1[rows:])
    hop_inner0 = edge(got0, 0, pair0[:rows])
    hop_outer0 = edge(got0, 1, pair0[rows:])
    hop_outer2 = edge(got0, 2, far2)

    sib1 = send(jnp.concatenate([outer1, inner1], axis=0), to_sibling)
    sib2 = send(outer2, to_sibling)
    hop_sib1 = send(jnp.concatenate([hop_outer1, hop_inner1], axis=0), to_sibling)
    hop_sib0 = send(jnp.concatenate([hop_inner0, hop_outer2], axis=0), to_sibling)

    both_lse = jnp.concatenate([row_lse, col_lse])
    batch = row_lse.shape[0]
    near_kind = core * batch
    far_kind = (1 - core) * batch

    def factor(kind, b, w):
        start = kind + ((b % 16) * 32 + (w % 32)) * rows
        return 0.5 * jnp.exp(5.0 - lax.dynamic_slice_in_dim(both_lse, start, rows))

    pal = blk + 1 - 2 * core
    near_query = factor(far_kind, blk, wide)
    far_query = factor(near_kind, blk, wide)

    def near(b, hop):
        return factor(near_kind, b, wide - hop * sign)

    def far(b, hop):
        return factor(far_kind, b, wide + hop * sign)

    diagonal = jnp.eye(rows, dtype=jnp.float32)

    def term(query, query_factor, keys, key_factor, own=False):
        logits = logit_scale * lax.dot_general(
            query, keys, (((1,), (1,)), ((), ())), preferred_element_type=jnp.float32
        )
        weights = jnp.exp(logits - 5.0) * (query_factor[:, None] + key_factor[None, :])
        if own:
            weights = weights - diagonal
        return jnp.dot(weights.astype(jnp.bfloat16), keys, preferred_element_type=jnp.float32)

    near_sum = term(other, near_query, outer, far_query, True)
    far_sum = term(outer, far_query, other, near_query, True)
    for block, b, hop in (
        (inner, pal, 0),
        (outer1, blk - 2 * sign, 0),
        (inner1, pal - 2 * sign, 0),
        (hop_outer1, blk - 2 * sign, 1),
        (hop_inner1, pal - 2 * sign, 1),
        (hop_outer0, blk, 1),
        (hop_inner0, pal, 1),
    ):
        near_sum = near_sum + term(other, near_query, block, near(b, hop))
    for block, b, hop in (
        (sib1[:rows], pal + 2 * sign, 0),
        (sib1[rows:], blk + 2 * sign, 0),
        (sib2, pal + 4 * sign, 0),
        (hop_sib1[:rows], pal + 2 * sign, 1),
        (hop_sib1[rows:], blk + 2 * sign, 1),
        (hop_sib0[:rows], blk, 1),
        (hop_sib0[rows:], pal + 4 * sign, 1),
    ):
        far_sum = far_sum + term(outer, far_query, block, far(b, hop))

    image_grad = logit_scale * jnp.where(carries_captions, near_sum, far_sum)
    caption_grad = logit_scale * jnp.where(carries_captions, far_sum, near_sum)
    return image_grad, caption_grad


def solution(mesh):
    in_specs = (P(("blk", "wide"), None), P(("blk", "wide"), None), P(), P(), P())
    out_specs = (P(("blk", "wide"), None), P(("blk", "wide"), None))
    return jax.shard_map(
        on_device, mesh=mesh, in_specs=in_specs, out_specs=out_specs, check_vma=False
    )
```

time: 447 us -> 206 us (0.46)
  the two profiles are of different devices: /device:TPU:1 before, /device:TPU:31 now
where the time goes in v1:
time: 206 us; the launch traced here: 205 us
  starting transfers between devices  110 us (53%)
  matrix products  49.8 us (24%)
  waiting for transfers between devices  16.7 us (8%)
  other arithmetic  16.4 us (8%)
  local copies, waits for them, and re-layouts  10.3 us (5%)
    ppermute x23, starting transfers between devices, send(): return lax.ppermute(x, AXES, pairs(target))  110 us
    dot_general x16, matrix products, term(): jnp.dot(weights.astype(jnp.bfloat16), keys, preferred_element_type=jnp.fl...  49.8 us
    ppermute x23, waiting for transfers between devices, send(): return lax.ppermute(x, AXES, pairs(target))  16.7 us
    slice x8, local copies, waits for them, and re-layouts, edge(): g[k * quarter:(k + 1) * quarter]  5.61 us
  transfers between devices with their start and end apart: 23, of which 4 were waited for; matrix products, arithmetic and copies ran while one was open for 34% of the time, Pallas kernels for 0%

profile of v1, /device:TPU:31, one launch (start us, length us, event | category | flops | bytes accessed | tf_op | source)
XLA Modules:
  0.0 205.2 jit_solution(17231712793642396595)
XLA Ops:
  0.6 1.3 broadcast_select_fusion.1
  2.0 2.7 %collective-permute-start = (bf16[384,768]{1,0:T(8,128)(2,1)S(1)}, bf16[384,768]{1,0:T(8,128)(2,1)S(1)}, u32[]{:S(2)}, u32[]{:S(2)}) collective-permute-start(bf16[384,768]{1,0:T(8,128)(2,1)S(1)} %get-tuple-element.24), channel_id=1, source_target_pairs={{0,32},{1,33},{2,34},{3,35},{4,36},{5,37},{6,38},{7,39},{8,40},{9,... | collective-permute-start | bytes 1769480 | tf_op jit(solution)/shard_map/ppermute | solution.py:65
  4.7 3.5 %collective-permute-start.1 = (bf16[384,768]{1,0:T(8,128)(2,1)S(1)}, bf16[384,768]{1,0:T(8,128)(2,1)S(1)}, u32[]{:S(2)}, u32[]{:S(2)}) collective-permute-start(bf16[384,768]{1,0:T(8,128)(2,1)S(1)} %get-tuple-element.25), channel_id=1, source_target_pairs={{0,448},{1,449},{2,450},{3,451},{4,452},{5,453},{6,454},{7,455},{8... | collective-permute-start | bytes 1769480 | tf_op jit(solution)/shard_map/ppermute | solution.py:65
  8.3 0.8 fusion.215
  9.1 0.9 constant_dynamic-update-slice_fusion
  10.7 2.1 %constant_dynamic-update-slice_fusion.3 = f32[393216]{0:T(1024)} fusion(f32[393216]{0:T(1024)} %constant_dynamic-update-slice_fusion, f32[196608]{0:T(1024)} %param.9), kind=kLoop, calls=%fused_computation.226 | loop fusion | bytes 1572864 | tf_op jit(solution)/shard_map/concatenate | solution.py:134
  12.8 1.6 exponential_multiply_fusion.4
  14.4 0.9 fusion.74
  15.3 2.0 fusion.75
  17.3 1.1 pad_maximum_fusion.1
  18.4 1.4 collective-permute-start.16
  19.8 0.7 fusion.214
  20.5 0.7 pad_maximum_fusion.5
  21.3 5.5 %collective-permute-start.3 = (bf16[192,768]{1,0:T(8,128)(2,1)}, bf16[192,768]{1,0:T(8,128)(2,1)}, u32[]{:S(2)}, u32[]{:S(2)}) collective-permute-start(bf16[192,768]{1,0:T(8,128)(2,1)} %pad_maximum_fusion.5), channel_id=1, source_target_pairs={{0,3},{4,7},{8,11},{12,15},{16,19},{20,23},{24,27},{28,31},{35,32}... | collective-permute-start | bytes 884744 | tf_op jit(solution)/shard_map/ppermute | solution.py:65
  26.8 0.7 pad_maximum_fusion.6
  27.6 2.0 collective-permute-start.4
  29.6 0.7 pad_maximum_fusion.7
  30.3 2.0 collective-permute-start.5
  32.3 2.6 %convolution_add_fusion.5 = f32[384,768]{1,0:T(8,128)} fusion(f32[384,768]{1,0:T(8,128)S(1)} %fusion.74, bf16[384,768]{1,0:T(8,128)(2,1)S(1)} %collective-permute-done, bf16[384,768]{1,0:T(8,128)(2,1)S(1)} %get-tuple-element.24, f32[384]{0:T(512)} %get-tuple-element.17, f32[384]{0:T(512)S(1)} %get-tuple-element.19, f32[]{:T(128)S(6)} %copy.9), kind=kOutput, calls=%fused_computation.5 | convolution fusion | flops 454017024 | bytes 3542020 | tf_op jit(solution)/shard_map/dot_general | solution.py:162
  34.9 3.5 %collective-permute-start.2 = (bf16[384,768]{1,0:T(8,128)(2,1)S(1)}, bf16[384,768]{1,0:T(8,128)(2,1)S(1)}, u32[]{:S(2)}, u32[]{:S(2)}) collective-permute-start(bf16[384,768]{1,0:T(8,128)(2,1)S(1)} %collective-permute-done), channel_id=1, source_target_pairs={{0,448},{1,449},{2,450},{3,451},{4,452},{5,453},{6,454},{7,455},{8... | collective-permute-start | bytes 1769480 | tf_op jit(solution)/shard_map/ppermute | solution.py:65
  38.5 3.5 %collective-permute-start.18 = (bf16[384,768]{1,0:T(8,128)(2,1)S(1)}, bf16[384,768]{1,0:T(8,128)(2,1)}, u32[]{:S(2)}, u32[]{:S(2)}) collective-permute-start(bf16[384,768]{1,0:T(8,128)(2,1)S(1)} %collective-permute-done.1), channel_id=1, source_target_pairs={{0,448},{1,449},{2,450},{3,451},{4,452},{5,453},{6,454},{7,455},{8... | collective-permute-start | bytes 1769480 | tf_op jit(solution)/shard_map/ppermute | solution.py:65
  42.0 1.2 fusion.131
  43.2 13.5 %collective-permute-start.6 = (bf16[192,768]{1,0:T(8,128)(2,1)S(1)}, bf16[192,768]{1,0:T(8,128)(2,1)S(1)}, u32[]{:S(2)}, u32[]{:S(2)}) collective-permute-start(bf16[192,768]{1,0:T(8,128)(2,1)S(1)} %fusion.131), channel_id=1, source_target_pairs={{0,476},{1,477},{2,478},{3,479},{4,448},{5,449},{6,450},{7,451},{8... | collective-permute-start | bytes 884744 | tf_op jit(solution)/shard_map/ppermute | solution.py:65
  56.7 3.2 %convolution_add_fusion.4 = f32[384,768]{1,0:T(8,128)} fusion(f32[384,768]{1,0:T(8,128)} %convolution_add_fusion.5, bf16[384,768]{1,0:T(8,128)(2,1)S(1)} %collective-permute-done.1, bf16[384,768]{1,0:T(8,128)(2,1)S(1)} %get-tuple-element.24, f32[384]{0:T(512)} %get-tuple-element.16, f32[384]{0:T(512)S(1)} %get-tuple-element.19, f32[]{:T(128)S(6)} %copy.9), kind=kOutput, calls=%fused_computation.4 | convolution fusion | flops 454017024 | bytes 3542020 | tf_op jit(solution)/shard_map/dot_general | solution.py:162
  59.9 4.4 %collective-permute-done.6 = bf16[192,768]{1,0:T(8,128)(2,1)S(1)} collective-permute-done((bf16[192,768]{1,0:T(8,128)(2,1)S(1)}, bf16[192,768]{1,0:T(8,128)(2,1)S(1)}, u32[]{:S(2)}, u32[]{:S(2)}) %collective-permute-start.6) | collective-permute-done | bytes 294944 | tf_op jit(solution)/shard_map/ppermute | solution.py:65
  64.3 23.5 %collective-permute-start.11 = (bf16[192,768]{1,0:T(8,128)(2,1)S(1)}, bf16[192,768]{1,0:T(8,128)(2,1)S(1)}, u32[]{:S(2)}, u32[]{:S(2)}) collective-permute-start(bf16[192,768]{1,0:T(8,128)(2,1)S(1)} %collective-permute-done.6), channel_id=1, source_target_pairs={{0,64},{1,65},{2,66},{3,67},{4,68},{5,69},{6,70},{7,71},{8,72},{9,... | collective-permute-start | bytes 884744 | tf_op jit(solution)/shard_map/ppermute | solution.py:65
  88.5 3.1 %collective-permute-start.12 = (bf16[96,768]{1,0:T(8,128)(2,1)S(1)}, bf16[96,768]{1,0:T(8,128)(2,1)S(1)}, u32[]{:S(2)}, u32[]{:S(2)}) collective-permute-start(bf16[96,768]{1,0:T(8,128)(2,1)S(1)} %get-tuple-element.50), channel_id=1, source_target_pairs={{0,448},{1,449},{2,450},{3,451},{4,452},{5,453},{6,454},{7,455},{8... | collective-permute-start | bytes 442376 | tf_op jit(solution)/shard_map/ppermute | solution.py:65
  91.6 1.3 collective-permute-start.9
  92.9 1.6 pad_maximum_fusion.2
  94.5 1.3 collective-permute-start.10
  95.8 0.7 fusion.223
  97.2 0.7 fusion.221
  98.0 0.7 collective-permute-start.7
  98.7 6.0 %collective-permute-done.12 = bf16[96,768]{1,0:T(8,128)(2,1)S(1)} collective-permute-done((bf16[96,768]{1,0:T(8,128)(2,1)S(1)}, bf16[96,768]{1,0:T(8,128)(2,1)S(1)}, u32[]{:S(2)}, u32[]{:S(2)}) %collective-permute-start.12) | collective-permute-done | bytes 147488 | tf_op jit(solution)/shard_map/ppermute | solution.py:65
  104.7 1.3 collective-permute-start.21
  106.0 3.1 %collective-permute-start.15 = (bf16[288,768]{1,0:T(8,128)(2,1)S(1)}, bf16[288,768]{1,0:T(8,128)(2,1)S(1)}, u32[]{:S(2)}, u32[]{:S(2)}) collective-permute-start(bf16[288,768]{1,0:T(8,128)(2,1)S(1)} %constant_dynamic-update-slice_fusion.1), channel_id=1, source_target_pairs={{0,3},{4,7},{8,11},{12,15},{16,19},{20,23},{24,27},{28,31},{35,32}... | collective-permute-start | bytes 1327112 | tf_op jit(solution)/shard_map/ppermute | solution.py:65
  109.1 0.7 fusion.220
  109.8 0.7 collective-permute-start.14
  110.5 0.7 fusion.219
  111.2 6.2 %collective-permute-done.15 = bf16[288,768]{1,0:T(8,128)(2,1)S(1)} collective-permute-done((bf16[288,768]{1,0:T(8,128)(2,1)S(1)}, bf16[288,768]{1,0:T(8,128)(2,1)S(1)}, u32[]{:S(2)}, u32[]{:S(2)}) %collective-permute-start.15) | collective-permute-done | bytes 442400 | tf_op jit(solution)/shard_map/ppermute | solution.py:65
  117.4 0.7 collective-permute-start.13
  118.1 0.7 fusion.218
  118.8 27.4 %collective-permute-start.17 = (bf16[768,768]{1,0:T(8,128)(2,1)}, bf16[768,768]{1,0:T(8,128)(2,1)S(1)}, u32[]{:S(2)}, u32[]{:S(2)}) collective-permute-start(bf16[768,768]{1,0:T(8,128)(2,1)} %get-tuple-element.20), channel_id=1, source_target_pairs={{0,32},{1,33},{2,34},{3,35},{4,36},{5,37},{6,38},{7,39},{8,40},{9,... | collective-permute-start | bytes 3538952 | tf_op jit(solution)/shard_map/ppermute | solution.py:65
  146.3 0.7 fusion.217
  147.0 4.5 %collective-permute-start.19 = (bf16[384,768]{1,0:T(8,128)(2,1)}, bf16[384,768]{1,0:T(8,128)(2,1)}, u32[]{:S(2)}, u32[]{:S(2)}) collective-permute-start(bf16[384,768]{1,0:T(8,128)(2,1)} %collective-permute-done.18), channel_id=1, source_target_pairs={{0,32},{1,33},{2,34},{3,35},{4,36},{5,37},{6,38},{7,39},{8,40},{9,... | collective-permute-start | bytes 1769480 | tf_op jit(solution)/shard_map/ppermute | solution.py:65
  151.5 0.7 fusion.216
  152.3 2.0 slice_select_fusion
  154.3 3.2 %fusion.79 = f32[384,768]{1,0:T(8,128)} fusion(bf16[384,768]{1,0:T(8,128)(2,1)} %slice_select_fusion, bf16[384,768]{1,0:T(8,128)(2,1)S(1)} %get-tuple-element.24, f32[384]{0:T(512)} %get-tuple-element.11, f32[384]{0:T(512)S(1)} %get-tuple-element.19, f32[]{:T(128)S(6)} %copy.9), kind=kOutput, calls=%fused_computation.108 | convolution fusion | flops 453722112 | bytes 2362372 | tf_op jit(solution)/shard_map/dot_general | solution.py:162
  157.6 2.1 %pad_maximum_fusion.4 = bf16[768,768]{1,0:T(8,128)(2,1)} fusion(bf16[384,768]{1,0:T(8,128)(2,1)S(1)} %maximum_select_fusion, bf16[384,768]{1,0:T(8,128)(2,1)} %slice_select_fusion), kind=kLoop, calls=%fused_computation.100 | loop fusion | flops 2359296 | bytes 2359296 | tf_op jit(solution)/shard_map/concatenate | solution.py:132
  159.7 1.9 collective-permute-start.22
  161.6 3.7 %fusion.78 = f32[384,768]{1,0:T(8,128)} fusion(bf16[384,768]{1,0:T(8,128)(2,1)S(1)} %get-tuple-element.24, bf16[768,768]{1,0:T(8,128)(2,1)} %collective-permute-done.16, bf16[96,768]{1,0:T(8,128)(2,1)} %get-tuple-element.42, bf16[96,768]{1,0:T(8,128)(2,1)} %get-tuple-element.39, bf16[96,768]{1,0:T(8,128)(2,1)} %get-tuple-element.36, ...), kind=kOutput, calls=%fused_computation.107 | convolution fusion | flops 459030528 | bytes 4133888 | tf_op jit(solution)/shard_map/dot_general | solution.py:162
  165.3 1.9 slice_select_fusion.5
  167.1 1.3 pad_maximum_fusion.3
  168.4 2.6 %collective-permute-start.20 = (bf16[768,768]{1,0:T(8,128)(2,1)}, bf16[768,768]{1,0:T(8,128)(2,1)}, u32[]{:S(2)}, u32[]{:S(2)}) collective-permute-start(bf16[768,768]{1,0:T(8,128)(2,1)} %pad_maximum_fusion.3), channel_id=1, source_target_pairs={{0,32},{1,33},{2,34},{3,35},{4,36},{5,37},{6,38},{7,39},{8,40},{9,... | collective-permute-start | bytes 3538952 | tf_op jit(solution)/shard_map/ppermute | solution.py:65
  171.0 3.2 %fusion.77 = f32[384,768]{1,0:T(8,128)} fusion(bf16[384,768]{1,0:T(8,128)(2,1)} %copy-done.3, bf16[384,768]{1,0:T(8,128)(2,1)S(1)} %get-tuple-element.24, f32[384]{0:T(512)} %get-tuple-element.13, f32[384]{0:T(512)S(1)} %get-tuple-element.19, f32[]{:T(128)S(6)} %copy.9), kind=kOutput, calls=%fused_computation.106 | convolution fusion | flops 453722112 | bytes 2362372 | tf_op jit(solution)/shard_map/dot_general | solution.py:162
  174.2 3.3 %convolution_add_fusion.2 = f32[384,768]{1,0:T(8,128)} fusion(f32[384,768]{1,0:T(8,128)} %fusion.75, bf16[384,768]{1,0:T(8,128)(2,1)S(1)} %get-tuple-element.25, bf16[768,768]{1,0:T(8,128)(2,1)S(1)} %collective-permute-done.17, f32[384]{0:T(512)S(1)} %get-tuple-element.10, f32[384]{0:T(512)S(1)} %get-tuple-element.18, f32[]{:T(128)S(6)} %copy.9), kind=kOutput, calls=%fused_computation.2 | convolution fusion | flops 454017024 | bytes 4131844 | tf_op jit(solution)/shard_map/dot_general | solution.py:162
  177.5 3.3 %convolution_add_fusion.1 = f32[384,768]{1,0:T(8,128)} fusion(f32[384,768]{1,0:T(8,128)} %convolution_add_fusion.2, bf16[384,768]{1,0:T(8,128)(2,1)S(1)} %get-tuple-element.25, bf16[768,768]{1,0:T(8,128)(2,1)S(1)} %collective-permute-done.17, f32[384]{0:T(512)S(1)} %get-tuple-element.9, f32[384]{0:T(512)S(1)} %get-tuple-element.18, f32[]{:T(128)S(6)} %copy.9), kind=kOutput, calls=%fused_computation.1 | convolution fusion | flops 454017024 | bytes 4131844 | tf_op jit(solution)/shard_map/dot_general | solution.py:162
  180.7 1.9 fusion.76
  182.7 4.3 %fusion.7 = f32[384,768]{1,0:T(8,128)} fusion(f32[384,768]{1,0:T(8,128)} %fusion.79, f32[384,768]{1,0:T(8,128)} %fusion.78, f32[384,768]{1,0:T(8,128)} %fusion.77, f32[384,768]{1,0:T(8,128)} %fusion.76, f32[384,768]{1,0:T(8,128)S(1)} %copy-done, bf16[384,768]{1,0:T(8,128)(2,1)S(1)} %collective-permute-done.2, bf16[384,768]{1,0:T(8,128)(2,1)S(1)} %get-tuple-element.24, ...), kind=kOutput, calls=%fused_computation.13 | convolution fusion | flops 455196672 | bytes 8260612 | tf_op jit(solution)/shard_map/dot_general | solution.py:162
  187.0 3.2 %fusion.83 = f32[384,768]{1,0:T(8,128)} fusion(bf16[384,768]{1,0:T(8,128)(2,1)S(1)} %get-tuple-element.25, bf16[768,768]{1,0:T(8,128)(2,1)} %collective-permute-done.22, f32[384]{0:T(512)S(1)} %copy-done.14, f32[384]{0:T(512)S(1)} %get-tuple-element.18, f32[]{:T(128)S(6)} %copy.9), kind=kOutput, calls=%fused_computation.112 | convolution fusion | flops 453722112 | bytes 2952196 | tf_op jit(solution)/shard_map/dot_general | solution.py:162
  190.2 3.2 %fusion.82 = f32[384,768]{1,0:T(8,128)} fusion(bf16[384,768]{1,0:T(8,128)(2,1)S(1)} %get-tuple-element.25, bf16[768,768]{1,0:T(8,128)(2,1)} %collective-permute-done.22, f32[384]{0:T(512)S(1)} %copy-done.13, f32[384]{0:T(512)S(1)} %get-tuple-element.18, f32[]{:T(128)S(6)} %copy.9), kind=kOutput, calls=%fused_computation.111 | convolution fusion | flops 453722112 | bytes 2952196 | tf_op jit(solution)/shard_map/dot_general | solution.py:162
  193.4 3.3 %fusion.81 = f32[384,768]{1,0:T(8,128)} fusion(bf16[384,768]{1,0:T(8,128)(2,1)S(1)} %get-tuple-element.25, bf16[768,768]{1,0:T(8,128)(2,1)} %collective-permute-done.20, f32[384]{0:T(512)S(1)} %copy-done.12, f32[384]{0:T(512)S(1)} %get-tuple-element.18, f32[]{:T(128)S(6)} %copy.9), kind=kOutput, calls=%fused_computation.110 | convolution fusion | flops 453722112 | bytes 2952196 | tf_op jit(solution)/shard_map/dot_general | solution.py:162
  196.7 3.4 %fusion.80 = f32[384,768]{1,0:T(8,128)} fusion(bf16[384,768]{1,0:T(8,128)(2,1)S(1)} %get-tuple-element.25, bf16[768,768]{1,0:T(8,128)(2,1)} %collective-permute-done.20, f32[384]{0:T(512)S(1)} %copy-done.11, f32[384]{0:T(512)S(1)} %get-tuple-element.18, f32[]{:T(128)S(6)} %copy.9), kind=kOutput, calls=%fused_computation.109 | convolution fusion | flops 453722112 | bytes 2952196 | tf_op jit(solution)/shard_map/dot_general | solution.py:162
  200.1 5.1 %select_multiply_fusion = (f32[384,768]{1,0:T(8,128)}, f32[384,768]{1,0:T(8,128)}) fusion(f32[384,768]{1,0:T(8,128)S(1)} %copy-done.2, f32[]{:T(128)S(6)} %copy.9, pred[]{:T(512)S(6)} %eq.54, f32[384,768]{1,0:T(8,128)} %fusion.83, f32[384,768]{1,0:T(8,128)} %fusion.82, f32[384,768]{1,0:T(8,128)} %fusion.81, f32[384,768]{1,0:T(8,128)} %fusion.80, ...), kind=kOutput, calls=%fused_computation.101 | convolution fusion | flops 456376320 | bytes 10619909 | tf_op jit(solution)/shard_map/dot_general | solution.py:162
  (57 shorter events, 1.7 us)
Async XLA Ops:
  2.0 7.1 %copy-start.4 = (f32[196608]{0:T(1024)S(1)}, f32[196608]{0:T(1024)}, u32[]{:S(2)}) copy-start(f32[196608]{0:T(1024)} %param.8) | copy-start | bytes 2359300
  2.0 15.3 %collective-permute-start = (bf16[384,768]{1,0:T(8,128)(2,1)S(1)}, bf16[384,768]{1,0:T(8,128)(2,1)S(1)}, u32[]{:S(2)}, u32[]{:S(2)}) collective-permute-start(bf16[384,768]{1,0:T(8,128)(2,1)S(1)} %get-tuple-element.24), channel_id=1, source_target_pairs={{0,32},{1,33},{2,34},{3,35},{4,36},{5,37},{6,38},{7,39},{8,40},{9,... | collective-permute-start | bytes 1769480 | tf_op jit(solution)/shard_map/ppermute | solution.py:65
  4.7 30.2 %collective-permute-start.1 = (bf16[384,768]{1,0:T(8,128)(2,1)S(1)}, bf16[384,768]{1,0:T(8,128)(2,1)S(1)}, u32[]{:S(2)}, u32[]{:S(2)}) collective-permute-start(bf16[384,768]{1,0:T(8,128)(2,1)S(1)} %get-tuple-element.25), channel_id=1, source_target_pairs={{0,448},{1,449},{2,450},{3,451},{4,452},{5,453},{6,454},{7,455},{8... | collective-permute-start | bytes 1769480 | tf_op jit(solution)/shard_map/ppermute | solution.py:65
  18.4 2.1 %copy-start.7 = (bf16[96,768]{1,0:T(8,128)(2,1)S(1)}, bf16[96,768]{1,0:T(8,128)(2,1)}, u32[]{:S(2)}) copy-start(bf16[96,768]{1,0:T(8,128)(2,1)} %get-tuple-element.33) | copy-start | bytes 442372
  18.4 8.4 %copy-start.6 = (bf16[96,768]{1,0:T(8,128)(2,1)S(1)}, bf16[96,768]{1,0:T(8,128)(2,1)}, u32[]{:S(2)}) copy-start(bf16[96,768]{1,0:T(8,128)(2,1)} %get-tuple-element.32) | copy-start | bytes 442372
  18.4 11.2 %copy-start.5 = (bf16[96,768]{1,0:T(8,128)(2,1)S(1)}, bf16[96,768]{1,0:T(8,128)(2,1)}, u32[]{:S(2)}) copy-start(bf16[96,768]{1,0:T(8,128)(2,1)} %get-tuple-element.31) | copy-start | bytes 442372
  18.4 133.9 %collective-permute-start.16 = (bf16[768,768]{1,0:T(8,128)(2,1)}, bf16[768,768]{1,0:T(8,128)(2,1)}, u32[]{:S(2)}, u32[]{:S(2)}) collective-permute-start(bf16[768,768]{1,0:T(8,128)(2,1)} %pad_maximum_fusion.1), channel_id=1, source_target_pairs={{1,0},{2,1},{3,2},{5,4},{6,5},{7,6},{9,8},{10,9},{11,10},{13,12},{... | collective-permute-start | bytes 3538952 | tf_op jit(solution)/shard_map/ppermute | solution.py:65
  21.3 17.2 %collective-permute-start.3 = (bf16[192,768]{1,0:T(8,128)(2,1)}, bf16[192,768]{1,0:T(8,128)(2,1)}, u32[]{:S(2)}, u32[]{:S(2)}) collective-permute-start(bf16[192,768]{1,0:T(8,128)(2,1)} %pad_maximum_fusion.5), channel_id=1, source_target_pairs={{0,3},{4,7},{8,11},{12,15},{16,19},{20,23},{24,27},{28,31},{35,32}... | collective-permute-start | bytes 884744 | tf_op jit(solution)/shard_map/ppermute | solution.py:65
  27.6 14.5 %collective-permute-start.4 = (bf16[192,768]{1,0:T(8,128)(2,1)}, bf16[192,768]{1,0:T(8,128)(2,1)}, u32[]{:S(2)}, u32[]{:S(2)}) collective-permute-start(bf16[192,768]{1,0:T(8,128)(2,1)} %pad_maximum_fusion.6), channel_id=1, source_target_pairs={{0,1},{4,5},{8,9},{12,13},{16,17},{20,21},{24,25},{28,29},{35,34},... | collective-permute-start | bytes 884744 | tf_op jit(solution)/shard_map/ppermute | solution.py:65
  30.3 11.7 %collective-permute-start.5 = (bf16[192,768]{1,0:T(8,128)(2,1)}, bf16[192,768]{1,0:T(8,128)(2,1)}, u32[]{:S(2)}, u32[]{:S(2)}) collective-permute-start(bf16[192,768]{1,0:T(8,128)(2,1)} %pad_maximum_fusion.7), channel_id=1, source_target_pairs={{0,2},{4,6},{8,10},{12,14},{16,18},{20,22},{24,26},{28,30},{35,33}... | collective-permute-start | bytes 884744 | tf_op jit(solution)/shard_map/ppermute | solution.py:65
  34.9 56.7 %collective-permute-start.2 = (bf16[384,768]{1,0:T(8,128)(2,1)S(1)}, bf16[384,768]{1,0:T(8,128)(2,1)S(1)}, u32[]{:S(2)}, u32[]{:S(2)}) collective-permute-start(bf16[384,768]{1,0:T(8,128)(2,1)S(1)} %collective-permute-done), channel_id=1, source_target_pairs={{0,448},{1,449},{2,450},{3,451},{4,452},{5,453},{6,454},{7,455},{8... | collective-permute-start | bytes 1769480 | tf_op jit(solution)/shard_map/ppermute | solution.py:65
  38.5 59.5 %collective-permute-start.18 = (bf16[384,768]{1,0:T(8,128)(2,1)S(1)}, bf16[384,768]{1,0:T(8,128)(2,1)}, u32[]{:S(2)}, u32[]{:S(2)}) collective-permute-start(bf16[384,768]{1,0:T(8,128)(2,1)S(1)} %collective-permute-done.1), channel_id=1, source_target_pairs={{0,448},{1,449},{2,450},{3,451},{4,452},{5,453},{6,454},{7,455},{8... | collective-permute-start | bytes 1769480 | tf_op jit(solution)/shard_map/ppermute | solution.py:65
  43.2 21.1 %collective-permute-start.6 = (bf16[192,768]{1,0:T(8,128)(2,1)S(1)}, bf16[192,768]{1,0:T(8,128)(2,1)S(1)}, u32[]{:S(2)}, u32[]{:S(2)}) collective-permute-start(bf16[192,768]{1,0:T(8,128)(2,1)S(1)} %fusion.131), channel_id=1, source_target_pairs={{0,476},{1,477},{2,478},{3,479},{4,448},{5,449},{6,450},{7,451},{8... | collective-permute-start | bytes 884744 | tf_op jit(solution)/shard_map/ppermute | solution.py:65
  64.3 30.2 %collective-permute-start.11 = (bf16[192,768]{1,0:T(8,128)(2,1)S(1)}, bf16[192,768]{1,0:T(8,128)(2,1)S(1)}, u32[]{:S(2)}, u32[]{:S(2)}) collective-permute-start(bf16[192,768]{1,0:T(8,128)(2,1)S(1)} %collective-permute-done.6), channel_id=1, source_target_pairs={{0,64},{1,65},{2,66},{3,67},{4,68},{5,69},{6,70},{7,71},{8,72},{9,... | collective-permute-start | bytes 884744 | tf_op jit(solution)/shard_map/ppermute | solution.py:65
  88.5 6.0 %copy-start.8 = (bf16[96,768]{1,0:T(8,128)(2,1)}, bf16[96,768]{1,0:T(8,128)(2,1)S(1)}, u32[]{:S(2)}) copy-start(bf16[96,768]{1,0:T(8,128)(2,1)S(1)} %get-tuple-element.50) | copy-start | bytes 442372
  88.5 16.1 %collective-permute-start.12 = (bf16[96,768]{1,0:T(8,128)(2,1)S(1)}, bf16[96,768]{1,0:T(8,128)(2,1)S(1)}, u32[]{:S(2)}, u32[]{:S(2)}) collective-permute-start(bf16[96,768]{1,0:T(8,128)(2,1)S(1)} %get-tuple-element.50), channel_id=1, source_target_pairs={{0,448},{1,449},{2,450},{3,451},{4,452},{5,453},{6,454},{7,455},{8... | collective-permute-start | bytes 442376 | tf_op jit(solution)/shard_map/ppermute | solution.py:65
  91.6 4.9 %collective-permute-start.9 = (bf16[192,768]{1,0:T(8,128)(2,1)S(1)}, bf16[192,768]{1,0:T(8,128)(2,1)S(1)}, u32[]{:S(2)}, u32[]{:S(2)}) collective-permute-start(bf16[192,768]{1,0:T(8,128)(2,1)S(1)} %collective-permute-done.6), channel_id=1, source_target_pairs={{0,3},{4,7},{8,11},{12,15},{16,19},{20,23},{24,27},{28,31},{35,32}... | collective-permute-start | bytes 884744 | tf_op jit(solution)/shard_map/ppermute | solution.py:65
  94.5 70.7 %collective-permute-start.10 = (bf16[768,768]{1,0:T(8,128)(2,1)}, bf16[768,768]{1,0:T(8,128)(2,1)}, u32[]{:S(2)}, u32[]{:S(2)}) collective-permute-start(bf16[768,768]{1,0:T(8,128)(2,1)} %get-tuple-element.21), channel_id=1, source_target_pairs={{1,0},{2,1},{3,2},{5,4},{6,5},{7,6},{9,8},{10,9},{11,10},{13,12},{... | collective-permute-start | bytes 3538952 | tf_op jit(solution)/shard_map/ppermute | solution.py:65
  96.6 9.4 %collective-permute-start.8 = (bf16[192,768]{1,0:T(8,128)(2,1)S(1)}, bf16[192,768]{1,0:T(8,128)(2,1)S(1)}, u32[]{:S(2)}, u32[]{:S(2)}) collective-permute-start(bf16[192,768]{1,0:T(8,128)(2,1)S(1)} %collective-permute-done.6), channel_id=1, source_target_pairs={{2,3},{6,7},{10,11},{14,15},{18,19},{22,23},{26,27},{30,31},{33,32... | collective-permute-start | bytes 884744 | tf_op jit(solution)/shard_map/ppermute | solution.py:65
  98.0 11.8 %collective-permute-start.7 = (bf16[192,768]{1,0:T(8,128)(2,1)S(1)}, bf16[192,768]{1,0:T(8,128)(2,1)S(1)}, u32[]{:S(2)}, u32[]{:S(2)}) collective-permute-start(bf16[192,768]{1,0:T(8,128)(2,1)S(1)} %collective-permute-done.6), channel_id=1, source_target_pairs={{1,3},{5,7},{9,11},{13,15},{17,19},{21,23},{25,27},{29,31},{34,32}... | collective-permute-start | bytes 884744 | tf_op jit(solution)/shard_map/ppermute | solution.py:65
  104.7 47.5 %collective-permute-start.21 = (bf16[384,768]{1,0:T(8,128)(2,1)}, bf16[384,768]{1,0:T(8,128)(2,1)S(1)}, u32[]{:S(2)}, u32[]{:S(2)}) collective-permute-start(bf16[384,768]{1,0:T(8,128)(2,1)} %collective-permute-done.18), channel_id=1, source_target_pairs={{1,0},{2,1},{3,2},{5,4},{6,5},{7,6},{9,8},{10,9},{11,10},{13,12},{... | collective-permute-start | bytes 1769480 | tf_op jit(solution)/shard_map/ppermute | solution.py:65
  106.0 11.4 %collective-permute-start.15 = (bf16[288,768]{1,0:T(8,128)(2,1)S(1)}, bf16[288,768]{1,0:T(8,128)(2,1)S(1)}, u32[]{:S(2)}, u32[]{:S(2)}) collective-permute-start(bf16[288,768]{1,0:T(8,128)(2,1)S(1)} %constant_dynamic-update-slice_fusion.1), channel_id=1, source_target_pairs={{0,3},{4,7},{8,11},{12,15},{16,19},{20,23},{24,27},{28,31},{35,32}... | collective-permute-start | bytes 1327112 | tf_op jit(solution)/shard_map/ppermute | solution.py:65
  109.8 9.0 %collective-permute-start.14 = (bf16[288,768]{1,0:T(8,128)(2,1)S(1)}, bf16[288,768]{1,0:T(8,128)(2,1)S(1)}, u32[]{:S(2)}, u32[]{:S(2)}) collective-permute-start(bf16[288,768]{1,0:T(8,128)(2,1)S(1)} %constant_dynamic-update-slice_fusion.1), channel_id=1, source_target_pairs={{2,3},{6,7},{10,11},{14,15},{18,19},{22,23},{26,27},{30,31},{33,32... | collective-permute-start | bytes 1327112 | tf_op jit(solution)/shard_map/ppermute | solution.py:65
  117.4 29.5 %collective-permute-start.13 = (bf16[288,768]{1,0:T(8,128)(2,1)S(1)}, bf16[288,768]{1,0:T(8,128)(2,1)S(1)}, u32[]{:S(2)}, u32[]{:S(2)}) collective-permute-start(bf16[288,768]{1,0:T(8,128)(2,1)S(1)} %constant_dynamic-update-slice_fusion.1), channel_id=1, source_target_pairs={{1,3},{5,7},{9,11},{13,15},{17,19},{21,23},{25,27},{29,31},{34,32}... | collective-permute-start | bytes 1327112 | tf_op jit(solution)/shard_map/ppermute | solution.py:65
  118.8 55.4 %collective-permute-start.17 = (bf16[768,768]{1,0:T(8,128)(2,1)}, bf16[768,768]{1,0:T(8,128)(2,1)S(1)}, u32[]{:S(2)}, u32[]{:S(2)}) collective-permute-start(bf16[768,768]{1,0:T(8,128)(2,1)} %get-tuple-element.20), channel_id=1, source_target_pairs={{0,32},{1,33},{2,34},{3,35},{4,36},{5,37},{6,38},{7,39},{8,40},{9,... | collective-permute-start | bytes 3538952 | tf_op jit(solution)/shard_map/ppermute | solution.py:65
  147.0 53.1 %collective-permute-start.19 = (bf16[384,768]{1,0:T(8,128)(2,1)}, bf16[384,768]{1,0:T(8,128)(2,1)}, u32[]{:S(2)}, u32[]{:S(2)}) collective-permute-start(bf16[384,768]{1,0:T(8,128)(2,1)} %collective-permute-done.18), channel_id=1, source_target_pairs={{0,32},{1,33},{2,34},{3,35},{4,36},{5,37},{6,38},{7,39},{8,40},{9,... | collective-permute-start | bytes 1769480 | tf_op jit(solution)/shard_map/ppermute | solution.py:65
  159.7 27.3 %collective-permute-start.22 = (bf16[768,768]{1,0:T(8,128)(2,1)}, bf16[768,768]{1,0:T(8,128)(2,1)}, u32[]{:S(2)}, u32[]{:S(2)}) collective-permute-start(bf16[768,768]{1,0:T(8,128)(2,1)} %pad_maximum_fusion.4), channel_id=1, source_target_pairs={{0,32},{1,33},{2,34},{3,35},{4,36},{5,37},{6,38},{7,39},{8,40},{9,... | collective-permute-start | bytes 3538952 | tf_op jit(solution)/shard_map/ppermute | solution.py:65
  167.1 1.3 copy-start.3
  168.4 25.0 %collective-permute-start.20 = (bf16[768,768]{1,0:T(8,128)(2,1)}, bf16[768,768]{1,0:T(8,128)(2,1)}, u32[]{:S(2)}, u32[]{:S(2)}) collective-permute-start(bf16[768,768]{1,0:T(8,128)(2,1)} %pad_maximum_fusion.3), channel_id=1, source_target_pairs={{0,32},{1,33},{2,34},{3,35},{4,36},{5,37},{6,38},{7,39},{8,40},{9,... | collective-permute-start | bytes 3538952 | tf_op jit(solution)/shard_map/ppermute | solution.py:65
  177.5 3.3 %copy-start.15 = (f32[384]{0:T(512)S(1)}, f32[384]{0:T(512)}, u32[]{:S(2)}) copy-start(f32[384]{0:T(512)} %get-tuple-element.14) | copy-start | bytes 4612
  180.7 2.0 copy-start
  180.7 2.0 copy-start.10
  182.7 4.3 %copy-start.14 = (f32[384]{0:T(512)S(1)}, f32[384]{0:T(512)}, u32[]{:S(2)}) copy-start(f32[384]{0:T(512)} %get-tuple-element.5) | copy-start | bytes 4612
  187.0 3.2 %copy-start.13 = (f32[384]{0:T(512)S(1)}, f32[384]{0:T(512)}, u32[]{:S(2)}) copy-start(f32[384]{0:T(512)} %get-tuple-element.6) | copy-start | bytes 4612
  190.2 3.2 %copy-start.12 = (f32[384]{0:T(512)S(1)}, f32[384]{0:T(512)}, u32[]{:S(2)}) copy-start(f32[384]{0:T(512)} %get-tuple-element.7) | copy-start | bytes 4612
  193.4 3.3 %copy-start.11 = (f32[384]{0:T(512)S(1)}, f32[384]{0:T(512)}, u32[]{:S(2)}) copy-start(f32[384]{0:T(512)} %get-tuple-element.8) | copy-start | bytes 4612
  196.7 3.4 %copy-start.1 = (f32[384,768]{1,0:T(8,128)S(1)}, f32[384,768]{1,0:T(8,128)}, u32[]{:S(2)}) copy-start(f32[384,768]{1,0:T(8,128)} %convolution_add_fusion.1) | copy-start | bytes 3538948
  196.7 3.4 %copy-start.2 = (f32[384,768]{1,0:T(8,128)S(1)}, f32[384,768]{1,0:T(8,128)}, u32[]{:S(2)}) copy-start(f32[384,768]{1,0:T(8,128)} %fusion.7) | copy-start | bytes 3538948
  196.7 3.4 %copy-start.9 = (f32[384]{0:T(512)S(1)}, f32[384]{0:T(512)}, u32[]{:S(2)}) copy-start(f32[384]{0:T(512)} %get-tuple-element.4) | copy-start | bytes 4612

commit v2 on v1

v2 whole, which is shorter than its diff:
```python
import jax
import jax.numpy as jnp
from jax import lax
from jax.experimental import pallas as pl
from jax.experimental.pallas import tpu as pltpu
from jax.sharding import PartitionSpec as P

AXES = ("blk", "wide")


def coordinates(blk, wide):
    return wide // 8, (wide // 4) % 2, wide % 4, blk // 2, blk % 2


def device_id(x, half, y, z, core):
    return ((z % 8) * 2 + core) * 32 + ((x % 4) * 2 + half) * 4 + y


def pairs(target):
    found = []
    for blk in range(16):
        for wide in range(32):
            x, half, y, z, core = coordinates(blk, wide)
            sign = 1 if core == 1 else -1
            mirrored = y if core == 1 else 3 - y
            there = target(x, half, mirrored, z, core, sign)
            if there is not None:
                x2, half2, mirrored2, z2, core2 = there
                y2 = mirrored2 if core == 1 else 3 - mirrored2
                found.append((blk * 32 + wide, device_id(x2, half2, y2, z2, core2)))
    return found


def crossing(x, half, sign):
    if sign == 1:
        return (x, 1) if half == 0 else (x + 1, 0)
    return (x, 0) if half == 1 else (x - 1, 1)


def to_sibling(x, h, m, z, c, s):
    return x, h, m, z, 1 - c


def to_next_chip_sibling(x, h, m, z, c, s):
    return x, h, m, z + s, 1 - c


def to_next_chip(x, h, m, z, c, s):
    return x, h, m, z + s, c


def to_previous_chip(x, h, m, z, c, s):
    return x, h, m, z - s, c


def to_next_wide(x, h, m, z, c, s):
    return (x, h, m + 1, z, c) if m < 3 else None


def to_sibling_next_wide(x, h, m, z, c, s):
    return (x, h, m - 1, z, c) if m > 0 else None


def across(x, h, m, z, c, s):
    x2, h2 = crossing(x, h, s)
    return x2, h2, m, z + s, c


def line_to_line(here, there):
    return lambda x, h, m, z, c, s: (x, h, there, z, c) if m == here else None


def send(name, x, target):
    with jax.named_scope(name):
        return lax.ppermute(x, AXES, pairs(target))


def scalars():
    return pl.BlockSpec(memory_space=pltpu.SMEM)


def whole():
    return pl.BlockSpec(memory_space=pltpu.VMEM)


def call(name, kernel, out_shape, smem, vmem, weight=1):
    many = isinstance(out_shape, (list, tuple))
    outs = [whole() for _ in out_shape] if many else whole()
    with jax.named_scope(name):
        return pl.pallas_call(
            kernel,
            out_shape=out_shape,
            in_specs=[scalars() for _ in smem] + [whole() for _ in vmem],
            out_specs=outs,
            cost_estimate=pl.CostEstimate(
                flops=weight * 1000, bytes_accessed=1000, transcendentals=0
            ),
            compiler_params=pltpu.CompilerParams(vmem_limit_bytes=20 * 1024 * 1024),
        )(*smem, *vmem)


def term(query, query_factor, keys, key_factor, scale, own=False):
    logits = lax.dot_general(
        query, keys, (((1,), (1,)), ((), ())), preferred_element_type=jnp.float32
    )
    weights = jnp.exp(logits * scale - 5.0) * (query_factor + key_factor)
    if own:
        rows = lax.broadcasted_iota(jnp.int32, weights.shape, 0)
        cols = lax.broadcasted_iota(jnp.int32, weights.shape, 1)
        weights = weights - jnp.where(rows == cols, 1.0, 0.0)
    return jnp.dot(weights.astype(jnp.bfloat16), keys, preferred_element_type=jnp.float32)


def add_terms(total, query, query_factor, key_factors, scale, items):
    for keys, row, own in items:
        part = term(query, query_factor, keys, key_factors[row : row + 1, :], scale, own)
        total = part if total is None else total + part
    return total


def cut_kernel(inner, outer, *outs):
    quarter = inner.shape[0] // 4
    for step in range(4):
        low = quarter * step
        outs[step][:quarter, :] = inner[low : low + quarter, :]
        outs[step][quarter:, :] = outer[low : low + quarter, :]


def on_device(images, captions, logit_scale, row_lse, col_lse):
    rows, width = images.shape
    quarter = rows // 4
    half = jnp.bfloat16
    blk = lax.axis_index("blk")
    wide = lax.axis_index("wide")
    core = blk % 2
    sign = 2 * core - 1
    y = wide % 4
    mirrored = jnp.where(core == 1, y, 3 - y)
    carries_captions = core == 1
    at_edge = jnp.where(mirrored == 0, 1, 0).astype(jnp.int32).reshape(1)
    sibling_at_edge = jnp.where(mirrored == 3, 1, 0).astype(jnp.int32).reshape(1)
    core_flag = core.astype(jnp.int32).reshape(1)
    scale = logit_scale.reshape(1)

    def blocks(count):
        return jax.ShapeDtypeStruct((count * rows, width), half)

    outer = jnp.where(carries_captions, captions, images)
    other = jnp.where(carries_captions, images, captions)

    def after(value, *others):
        return lax.optimization_barrier((value, *others))[0]

    inner = send("swap", other, to_sibling)
    outer1 = send("own_outer1", outer, to_next_chip)

    strip = jax.ShapeDtypeStruct((2 * quarter, width), half)
    cuts = call("cut", cut_kernel, [strip] * 4, (), (inner, outer))
    spread0 = send("spread0", cuts[0], line_to_line(3, 0))
    spread1 = send("spread1", cuts[1], line_to_line(3, 2))
    spread2 = send("spread2", cuts[2], line_to_line(3, 1))
    inner1 = send("own_inner1", inner, to_next_chip)
    held = jnp.where(
        mirrored == 0,
        spread0,
        jnp.where(mirrored == 2, spread1, jnp.where(mirrored == 1, spread2, cuts[3])),
    )
    crossed = send("cross", held, across)
    pair0 = send(
        "wide_pair0", jnp.concatenate([after(inner, held), outer], axis=0), to_next_wide
    )
    batch = row_lse.shape[0]

    def part(carried, b, w):
        start = ((b % 16) * 32 + (w % 32)) * rows
        from_rows = lax.dynamic_slice_in_dim(row_lse, start, rows)
        from_cols = lax.dynamic_slice_in_dim(col_lse, start, rows)
        return jnp.where(carries_captions == carried, from_cols, from_rows)

    def factor(values):
        return 0.5 * jnp.exp(5.0 - values)

    pal = blk + 1 - 2 * core
    near_w, far_w = wide - sign, wide + sign
    own_outer = part(True, blk, wide)
    own_other = part(False, blk, wide)
    key_factors = factor(
        jnp.stack(
            [
                own_outer,
                part(True, pal, wide),
                part(True, blk - 2 * sign, wide),
                part(True, pal - 2 * sign, wide),
                part(True, blk - 2 * sign, near_w),
                part(True, pal - 2 * sign, near_w),
                part(True, pal, near_w),
                part(True, blk, near_w),
                own_other,
                part(False, pal + 2 * sign, wide),
                part(False, blk + 2 * sign, wide),
                part(False, pal + 4 * sign, wide),
                part(False, pal + 2 * sign, far_w),
                part(False, blk + 2 * sign, far_w),
                part(False, blk, far_w),
                part(False, pal + 4 * sign, far_w),
            ]
        )
    )
    near_factor = jnp.broadcast_to(factor(own_other)[:, None], (rows, 128))
    far_factor = jnp.broadcast_to(factor(own_outer)[:, None], (rows, 128))
    total = jax.ShapeDtypeStruct((rows, width), jnp.float32)

    def terms(name, near_blocks, far_blocks, sums, weight=1):
        arrays = [array for array, _ in near_blocks + far_blocks]

        def kernel(s, oth, out, nf, ff, kf, *refs):
            keys, refs = refs[: len(arrays)], refs[len(arrays) :]
            starts, ends = (refs[:2], refs[2:]) if sums else ((None, None), refs)

            def add(start, query, query_factor, blocks, refs, end):
                items = []
                for ref, (_, places) in zip(refs, blocks):
                    for k, row in enumerate(places):
                        items.append((ref[k * rows : (k + 1) * rows, :], row, row in (0, 8)))
                before = None if start is None else start[...]
                end[...] = add_terms(before, query[...], query_factor[:, :1], kf, s[0], items)

            add(starts[0], oth, nf, near_blocks, keys[: len(near_blocks)], ends[0])
            add(starts[1], out, ff, far_blocks, keys[len(near_blocks) :], ends[1])

        return call(
            name, kernel, [total, total], (scale,),
            (other, outer, near_factor, far_factor, key_factors, *arrays, *(sums or ())), weight,
        )

    sums = terms("terms_own0", [(outer, [0]), (inner, [1]), (after(outer1, held), [2])], [(other, [8])], None, 100_000_000)
    own1 = jnp.concatenate([outer1, after(inner1, *sums)], axis=0)
    sib1 = send("sibling1", own1, to_sibling)
    pair1 = send("wide_pair1", own1, to_next_wide)
    sums = terms("terms_own1", [(inner1, [3])], [(sib1, [9, 10])], sums)
    crossed = after(crossed, pair0, pair1, *sums)

    back = send("cross_back", crossed, to_previous_chip)
    ahead = send("cross_ahead", crossed[quarter:], to_next_chip)

    def collect(name, mine):
        q1 = send(name + "1", mine, line_to_line(2, 0))
        q2 = send(name + "2", mine, line_to_line(1, 0))
        q3 = send(name + "3", mine, line_to_line(3, 0))
        return [mine, q1, q2, q3]

    got1 = collect("gather1_", crossed)
    far2 = send("own_outer2", after(outer1, ahead), to_next_chip_sibling)
    hop_far2 = send("wide_outer2", far2, to_sibling_next_wide)
    got0 = collect("gather0_", after(jnp.concatenate([back, ahead], axis=0), *got1))

    def merge1_kernel(edge, usual, q0, q1, q2, q3, out):
        @pl.when(edge[0] == 1)
        def _():
            for place, source in enumerate((q0, q1, q2, q3)):
                low = place * quarter
                out[low : low + quarter, :] = source[quarter:, :]
                out[rows + low : rows + low + quarter, :] = source[:quarter, :]

        @pl.when(edge[0] == 0)
        def _():
            out[...] = usual[...]

    hop1 = call("merge1", merge1_kernel, blocks(2), (at_edge,), (pair1, *got1))
    hop_sib1 = send("sibling_hop1", hop1, to_sibling)
    sums = terms("terms_hop1", [(hop1, [4, 5])], [(far2, [11])], sums)
    got0 = [after(got0[0], far2, *sums), *got0[1:]]

    def merge0_kernel(edge, usual, q0, q1, q2, q3, out, keys):
        @pl.when(edge[0] == 1)
        def _():
            for place, source in enumerate((q0, q1, q2, q3)):
                low = place * quarter
                out[low : low + quarter, :] = source[:quarter, :]
                keys[low : low + quarter, :] = source[quarter : 2 * quarter, :]
                out[rows + low : rows + low + quarter, :] = source[2 * quarter :, :]

        @pl.when(edge[0] == 0)
        def _():
            out[...] = usual[...]
            keys[...] = usual[rows:, :]

    hop0, hop_outer0 = call(
        "merge0", merge0_kernel, [blocks(2), blocks(1)], (at_edge,), (pair0, *got0)
    )
    hop_sib0 = send("sibling_hop0", hop0, to_sibling)
    sums = terms("terms_hop0", [(hop_outer0, [7]), (hop0, [6])], [(after(hop_sib1, hop_far2), [12, 13])], sums)

    def last_kernel(c, e, s, out, ff, kf, hs0, hf2, near_in, far_in, image_grad, caption_grad):
        farthest = jnp.where(e[0] == 1, hs0[rows:, :], hf2[...])
        far = s[0] * add_terms(
            far_in[...], out[...], ff[:, :1], kf, s[0],
            [(hs0[:rows, :], 14, False), (farthest, 15, False)],
        )
        near = s[0] * near_in[...]

        @pl.when(c[0] == 1)
        def _():
            image_grad[...] = near
            caption_grad[...] = far

        @pl.when(c[0] == 0)
        def _():
            image_grad[...] = far
            caption_grad[...] = near

    image_grad, caption_grad = call(
        "terms_last", last_kernel, [total, total], (core_flag, sibling_at_edge, scale),
        (outer, far_factor, key_factors, hop_sib0, hop_far2, *sums),
    )
    return image_grad, caption_grad


def solution(mesh):
    in_specs = (P(("blk", "wide"), None), P(("blk", "wide"), None), P(), P(), P())
    out_specs = (P(("blk", "wide"), None), P(("blk", "wide"), None))
    return jax.shard_map(
        on_device, mesh=mesh, in_specs=in_specs, out_specs=out_specs, check_vma=False
    )
```

time: 206 us -> 158 us (0.77)
  the two profiles are of different devices: /device:TPU:31 before, /device:TPU:1 now
where the time goes in v2:
time: 158 us; the launch traced here: 157 us
  starting transfers between devices  57.6 us (36%)
  waiting for transfers between devices  56.1 us (36%)
  Pallas kernels  22.3 us (14%)
  local copies, waits for them, and re-layouts  16.3 us (10%)
  other arithmetic  2.72 us (2%)
  between operations  2.19 us (1%)
    ppermute x22, starting transfers between devices, send(): return lax.ppermute(x, AXES, pairs(target))  57.6 us
    ppermute x22, waiting for transfers between devices, send(): return lax.ppermute(x, AXES, pairs(target))  56.1 us
    pallas_call x8, Pallas kernels, call(): pl.pallas_call(kernel, out_shape=out_shape, in_specs=[scalars() for _ in...  22.3 us
    unnamed x41, local copies, waits for them, and re-layouts  15.9 us
  transfers between devices with their start and end apart: 22, of which 6 were waited for; matrix products, arithmetic and copies ran while one was open for 2% of the time, Pallas kernels for 11%

profile of v2, /device:TPU:1, one launch (start us, length us, event | category | flops | bytes accessed | tf_op | source)
XLA Modules:
  0.0 157.3 jit_solution(17218834591886558014)
XLA Ops:
  0.6 1.3 broadcast_select_fusion
  2.0 8.8 %collective-permute-start = (bf16[384,768]{1,0:T(8,128)(2,1)S(1)}, bf16[384,768]{1,0:T(8,128)(2,1)S(1)}, u32[]{:S(2)}, u32[]{:S(2)}) collective-permute-start(bf16[384,768]{1,0:T(8,128)(2,1)S(1)} %get-tuple-element.66.oth.refs_3_), channel_id=1, source_target_pairs={{0,32},{1,33},{2,34},{3,35},{4,36},{5,37},{6,38},{7,39},{8,40},{9,... | collective-permute-start | bytes 1769480 | tf_op jit(solution)/shard_map/swap/ppermute | solution.py:75
  10.8 1.9 %collective-permute-start.6 = (bf16[384,768]{1,0:T(8,128)(2,1)S(1)}, bf16[384,768]{1,0:T(8,128)(2,1)}, u32[]{:S(2)}, u32[]{:S(2)}) collective-permute-start(bf16[384,768]{1,0:T(8,128)(2,1)S(1)} %get-tuple-element.67.outer.out.refs_0_), channel_id=1, source_target_pairs={{0,448},{1,449},{2,450},{3,451},{4,452},{5,453},{6,454},{7,455},{8... | collective-permute-start | bytes 1769480 | tf_op jit(solution)/shard_map/own_outer1/ppermute | solution.py:75
  13.6 1.2 exponential_multiply_fusion.1
  15.0 0.1 stack.67
  15.1 0.0 collective-permute-done.inner.refs_1_
  15.1 0.1 cut.1
  15.2 1.3 collective-permute-start.1
  16.5 0.7 collective-permute-start.2
  17.2 0.7 collective-permute-start.3
  17.9 1.9 %collective-permute-start.7 = (bf16[384,768]{1,0:T(8,128)(2,1)S(1)}, bf16[384,768]{1,0:T(8,128)(2,1)S(1)}, u32[]{:S(2)}, u32[]{:S(2)}) collective-permute-start(bf16[384,768]{1,0:T(8,128)(2,1)S(1)} %collective-permute-done.inner.refs_1_), channel_id=1, source_target_pairs={{0,448},{1,449},{2,450},{3,451},{4,452},{5,453},{6,454},{7,455},{8... | collective-permute-start | bytes 1769480 | tf_op jit(solution)/shard_map/own_inner1/ppermute | solution.py:75
  19.8 13.0 %collective-permute-done.6.refs_2_ = bf16[384,768]{1,0:T(8,128)(2,1)} collective-permute-done((bf16[384,768]{1,0:T(8,128)(2,1)S(1)}, bf16[384,768]{1,0:T(8,128)(2,1)}, u32[]{:S(2)}, u32[]{:S(2)}) %collective-permute-start.6) | collective-permute-done | bytes 589856 | tf_op jit(solution)/shard_map/own_outer1/ppermute | solution.py:75
  32.8 1.1 constant_dynamic-update-slice_fusion.1
  33.9 0.0 collective-permute-done.1
  33.9 0.1 select_select_fusion
  34.0 0.1 broadcast_in_dim.5.nf
  34.1 0.1 broadcast_in_dim.4.ff
  34.2 4.1 %terms_own0.1 = (f32[384,768]{1,0:T(8,128)S(1)}, f32[384,768]{1,0:T(8,128)S(1)}) custom-call(f32[1]{0:T(128)} %bitcast.4.s, bf16[384,768]{1,0:T(8,128)(2,1)S(1)} %get-tuple-element.66.oth.refs_3_, bf16[384,768]{1,0:T(8,128)(2,1)S(1)} %get-tuple-element.67.outer.out.refs_0_, f32[384,128]{1,0:T(8,128)S(1)} %broadcast_in_dim.5.nf, ...), custom_call_target="tpu_custom_call" | custom-call | flops 99999997952 | bytes 1000 | tf_op jit(solution)/shard_map/terms_own0/pallas_call | solution.py:90
  38.3 6.5 %collective-permute-done.7.refs_0_ = bf16[384,768]{1,0:T(8,128)(2,1)S(1)} collective-permute-done((bf16[384,768]{1,0:T(8,128)(2,1)S(1)}, bf16[384,768]{1,0:T(8,128)(2,1)S(1)}, u32[]{:S(2)}, u32[]{:S(2)}) %collective-permute-start.7) | collective-permute-done | bytes 589856 | tf_op jit(solution)/shard_map/own_inner1/ppermute | solution.py:75
  44.9 3.4 %collective-permute-start.9 = (bf16[768,768]{1,0:T(8,128)(2,1)S(1)}, bf16[768,768]{1,0:T(8,128)(2,1)S(1)}, u32[]{:S(2)}, u32[]{:S(2)}) collective-permute-start(bf16[768,768]{1,0:T(8,128)(2,1)S(1)} %constant_dynamic-update-slice_fusion), channel_id=1, source_target_pairs={{0,32},{1,33},{2,34},{3,35},{4,36},{5,37},{6,38},{7,39},{8,40},{9,... | collective-permute-start | bytes 3538952 | tf_op jit(solution)/shard_map/sibling1/ppermute | solution.py:75
  48.3 0.1 pad_maximum_fusion
  48.4 1.4 collective-permute-start.4
  49.8 3.0 %collective-permute-start.8 = (bf16[768,768]{1,0:T(8,128)(2,1)S(1)}, bf16[768,768]{1,0:T(8,128)(2,1)S(1)}, u32[]{:S(2)}, u32[]{:S(2)}) collective-permute-start(bf16[768,768]{1,0:T(8,128)(2,1)S(1)} %constant_dynamic-update-slice_fusion), channel_id=1, source_target_pairs={{1,0},{2,1},{3,2},{5,4},{6,5},{7,6},{9,8},{10,9},{11,10},{13,12},{... | collective-permute-start | bytes 3538952 | tf_op jit(solution)/shard_map/wide_pair1/ppermute | solution.py:75
  52.8 5.4 %collective-permute-start.5 = (bf16[192,768]{1,0:T(8,128)(2,1)S(1)}, bf16[192,768]{1,0:T(8,128)(2,1)S(1)}, u32[]{:S(2)}, u32[]{:S(2)}) collective-permute-start(bf16[192,768]{1,0:T(8,128)(2,1)S(1)} %select_select_fusion), channel_id=1, source_target_pairs={{0,476},{1,477},{2,478},{3,479},{4,448},{5,449},{6,450},{7,451},{8... | collective-permute-start | bytes 884744 | tf_op jit(solution)/shard_map/cross/ppermute | solution.py:75
  58.2 2.4 %terms_own1.1 = (f32[384,768]{1,0:T(8,128)S(1)}, f32[384,768]{1,0:T(8,128)S(1)}) custom-call(f32[1]{0:T(128)} %bitcast.5.s, bf16[384,768]{1,0:T(8,128)(2,1)S(1)} %get-tuple-element.66.oth.refs_3_, bf16[384,768]{1,0:T(8,128)(2,1)S(1)} %get-tuple-element.67.outer.out.refs_0_, f32[384,128]{1,0:T(8,128)S(1)} %broadcast_in_dim.5.nf, ...), custom_call_target="tpu_custom_call" | custom-call | flops 1000 | bytes 1000 | tf_op jit(solution)/shard_map/terms_own1/pallas_call | solution.py:90
  60.6 1.0 copy-done.2
  61.7 1.0 copy-done.4
  62.7 20.7 %collective-permute-done.5.q0 = bf16[192,768]{1,0:T(8,128)(2,1)S(1)} collective-permute-done((bf16[192,768]{1,0:T(8,128)(2,1)S(1)}, bf16[192,768]{1,0:T(8,128)(2,1)S(1)}, u32[]{:S(2)}, u32[]{:S(2)}) %collective-permute-start.5) | collective-permute-done | bytes 294944 | tf_op jit(solution)/shard_map/cross/ppermute | solution.py:75
  83.4 0.0 copy-start.6
  83.5 1.0 copy-done.6
  84.5 6.1 %collective-permute-start.10 = (bf16[192,768]{1,0:T(8,128)(2,1)S(1)}, bf16[192,768]{1,0:T(8,128)(2,1)S(1)}, u32[]{:S(2)}, u32[]{:S(2)}) collective-permute-start(bf16[192,768]{1,0:T(8,128)(2,1)S(1)} %collective-permute-done.5.q0), channel_id=1, source_target_pairs={{0,64},{1,65},{2,66},{3,67},{4,68},{5,69},{6,70},{7,71},{8,72},{9,... | collective-permute-start | bytes 884744 | tf_op jit(solution)/shard_map/cross_back/ppermute | solution.py:75
  90.7 2.4 %collective-permute-start.11 = (bf16[96,768]{1,0:T(8,128)(2,1)S(1)}, bf16[96,768]{1,0:T(8,128)(2,1)S(1)}, u32[]{:S(2)}, u32[]{:S(2)}) collective-permute-start(bf16[96,768]{1,0:T(8,128)(2,1)S(1)} %slice.3), channel_id=1, source_target_pairs={{0,448},{1,449},{2,450},{3,451},{4,452},{5,453},{6,454},{7,455},{8... | collective-permute-start | bytes 442376 | tf_op jit(solution)/shard_map/cross_ahead/ppermute | solution.py:75
  93.1 1.3 collective-permute-start.14
  94.4 1.3 collective-permute-start.13
  95.7 1.3 collective-permute-start.12
  97.0 6.1 %collective-permute-done.11 = bf16[96,768]{1,0:T(8,128)(2,1)S(1)} collective-permute-done((bf16[96,768]{1,0:T(8,128)(2,1)S(1)}, bf16[96,768]{1,0:T(8,128)(2,1)S(1)}, u32[]{:S(2)}, u32[]{:S(2)}) %collective-permute-start.11) | collective-permute-done | bytes 147488 | tf_op jit(solution)/shard_map/cross_ahead/ppermute | solution.py:75
  103.2 1.9 %collective-permute-start.15 = (bf16[384,768]{1,0:T(8,128)(2,1)}, bf16[384,768]{1,0:T(8,128)(2,1)}, u32[]{:S(2)}, u32[]{:S(2)}) collective-permute-start(bf16[384,768]{1,0:T(8,128)(2,1)} %collective-permute-done.6.refs_2_), channel_id=1, source_target_pairs={{0,480},{1,481},{2,482},{3,483},{4,484},{5,485},{6,486},{7,487},{8... | collective-permute-start | bytes 1769480 | tf_op jit(solution)/shard_map/own_outer2/ppermute | solution.py:75
  105.2 0.7 copy-done.14
  105.9 0.7 copy-done.16
  106.6 0.4 collective-permute-done.12.q1
  106.9 0.7 copy-done.18
  107.6 1.3 collective-permute-start.18
  108.9 1.3 collective-permute-start.17
  110.2 1.3 collective-permute-start.16
  111.5 0.0 copy-start.7
  111.5 1.3 copy-done.7
  112.8 1.0 copy-done.15
  113.8 1.0 copy-done.17
  114.7 1.0 copy-done.19
  115.7 0.1 merge1.1.refs_0_
  115.8 7.5 %collective-permute-start.21 = (bf16[768,768]{1,0:T(8,128)(2,1)S(1)}, bf16[768,768]{1,0:T(8,128)(2,1)}, u32[]{:S(2)}, u32[]{:S(2)}) collective-permute-start(bf16[768,768]{1,0:T(8,128)(2,1)S(1)} %merge1.1.refs_0_), channel_id=1, source_target_pairs={{0,32},{1,33},{2,34},{3,35},{4,36},{5,37},{6,38},{7,39},{8,40},{9,... | collective-permute-start | bytes 3538952 | tf_op jit(solution)/shard_map/sibling_hop1/ppermute | solution.py:75
  123.3 0.0 copy-start.1
  123.3 3.6 %terms_hop1.1 = (f32[384,768]{1,0:T(8,128)S(1)}, f32[384,768]{1,0:T(8,128)S(1)}) custom-call(f32[1]{0:T(128)} %bitcast.6.s, bf16[384,768]{1,0:T(8,128)(2,1)S(1)} %get-tuple-element.66.oth.refs_3_, bf16[384,768]{1,0:T(8,128)(2,1)S(1)} %get-tuple-element.67.outer.out.refs_0_, f32[384,128]{1,0:T(8,128)S(1)} %broadcast_in_dim.5.nf, ...), custom_call_target="tpu_custom_call" | custom-call | flops 1000 | bytes 1000 | tf_op jit(solution)/shard_map/terms_hop1/pallas_call | solution.py:90
  126.9 1.0 copy-done.10
  128.0 2.8 %merge0.1 = (bf16[768,768]{1,0:T(8,128)(2,1)}, bf16[384,768]{1,0:T(8,128)(2,1)S(1)}) custom-call(s32[1]{0:T(128)} %bitcast.3.edge, bf16[768,768]{1,0:T(8,128)(2,1)S(1)} %copy-done.1, bf16[288,768]{1,0:T(8,128)(2,1)S(1)} %pad_maximum_fusion.1.q0, bf16[288,768]{1,0:T(8,128)(2,1)} %collective-permute-done.16.q1, bf16[288,768]{1,0:T(8,128)(2,1)} %collective-permute-done.17.q2, ...), custom_call_target="tpu_custom_call" | custom-call | flops 1000 | bytes 1000 | tf_op jit(solution)/shard_map/merge0/pallas_call | solution.py:90
  130.8 0.8 copy-done.12
  131.6 1.9 %collective-permute-start.19 = (bf16[768,768]{1,0:T(8,128)(2,1)}, bf16[768,768]{1,0:T(8,128)(2,1)}, u32[]{:S(2)}, u32[]{:S(2)}) collective-permute-start(bf16[768,768]{1,0:T(8,128)(2,1)} %get-tuple-element.41.refs_1_), channel_id=1, source_target_pairs={{0,32},{1,33},{2,34},{3,35},{4,36},{5,37},{6,38},{7,39},{8,40},{9,... | collective-permute-start | bytes 3538952 | tf_op jit(solution)/shard_map/sibling_hop0/ppermute | solution.py:75
  133.6 1.5 collective-permute-start.20
  135.0 9.3 %collective-permute-done.20.hf2 = bf16[384,768]{1,0:T(8,128)(2,1)S(1)} collective-permute-done((bf16[384,768]{1,0:T(8,128)(2,1)}, bf16[384,768]{1,0:T(8,128)(2,1)S(1)}, u32[]{:S(2)}, u32[]{:S(2)}) %collective-permute-start.20) | collective-permute-done | bytes 589856 | tf_op jit(solution)/shard_map/wide_outer2/ppermute | solution.py:75
  144.4 1.3 copy-done.9
  145.7 1.3 copy-done.11
  146.9 1.1 copy-done.13
  148.0 4.7 %terms_hop0.1 = (f32[384,768]{1,0:T(8,128)S(1)}, f32[384,768]{1,0:T(8,128)S(1)}) custom-call(f32[1]{0:T(128)} %bitcast.7.s, bf16[384,768]{1,0:T(8,128)(2,1)S(1)} %get-tuple-element.66.oth.refs_3_, bf16[384,768]{1,0:T(8,128)(2,1)S(1)} %get-tuple-element.67.outer.out.refs_0_, f32[384,128]{1,0:T(8,128)S(1)} %broadcast_in_dim.5.nf, ...), custom_call_target="tpu_custom_call" | custom-call | flops 1000 | bytes 1000 | tf_op jit(solution)/shard_map/terms_hop0/pallas_call | solution.py:90
  152.8 4.5 %terms_last.1 = (f32[384,768]{1,0:T(8,128)}, f32[384,768]{1,0:T(8,128)}) custom-call(s32[1]{0:T(128)} %bitcast.c, s32[1]{0:T(128)} %bitcast.1.e, f32[1]{0:T(128)} %bitcast.8.s, bf16[384,768]{1,0:T(8,128)(2,1)S(1)} %get-tuple-element.67.outer.out.refs_0_, f32[384,128]{1,0:T(8,128)S(1)} %broadcast_in_dim.4.ff, f32[16,384]{1,0:T(8,128)S(1)} %exponential_multiply_fusion.kf, ...), custom_call_target="tpu_custom_call" | custom-call | flops 1000 | bytes 1000 | tf_op jit(solution)/shard_map/terms_last/pallas_call | solution.py:90
  (56 shorter events, 0.2 us)
Async XLA Ops:
  2.0 13.1 %collective-permute-start = (bf16[384,768]{1,0:T(8,128)(2,1)S(1)}, bf16[384,768]{1,0:T(8,128)(2,1)S(1)}, u32[]{:S(2)}, u32[]{:S(2)}) collective-permute-start(bf16[384,768]{1,0:T(8,128)(2,1)S(1)} %get-tuple-element.66.oth.refs_3_), channel_id=1, source_target_pairs={{0,32},{1,33},{2,34},{3,35},{4,36},{5,37},{6,38},{7,39},{8,40},{9,... | collective-permute-start | bytes 1769480 | tf_op jit(solution)/shard_map/swap/ppermute | solution.py:75
  10.8 22.0 %collective-permute-start.6 = (bf16[384,768]{1,0:T(8,128)(2,1)S(1)}, bf16[384,768]{1,0:T(8,128)(2,1)}, u32[]{:S(2)}, u32[]{:S(2)}) collective-permute-start(bf16[384,768]{1,0:T(8,128)(2,1)S(1)} %get-tuple-element.67.outer.out.refs_0_), channel_id=1, source_target_pairs={{0,448},{1,449},{2,450},{3,451},{4,452},{5,453},{6,454},{7,455},{8... | collective-permute-start | bytes 1769480 | tf_op jit(solution)/shard_map/own_outer1/ppermute | solution.py:75
  15.2 18.7 %collective-permute-start.1 = (bf16[192,768]{1,0:T(8,128)(2,1)S(1)}, bf16[192,768]{1,0:T(8,128)(2,1)S(1)}, u32[]{:S(2)}, u32[]{:S(2)}) collective-permute-start(bf16[192,768]{1,0:T(8,128)(2,1)S(1)} %get-tuple-element.24), channel_id=1, source_target_pairs={{0,3},{4,7},{8,11},{12,15},{16,19},{20,23},{24,27},{28,31},{35,32}... | collective-permute-start | bytes 884744 | tf_op jit(solution)/shard_map/spread0/ppermute | solution.py:75
  16.5 17.4 %collective-permute-start.2 = (bf16[192,768]{1,0:T(8,128)(2,1)S(1)}, bf16[192,768]{1,0:T(8,128)(2,1)S(1)}, u32[]{:S(2)}, u32[]{:S(2)}) collective-permute-start(bf16[192,768]{1,0:T(8,128)(2,1)S(1)} %get-tuple-element.25), channel_id=1, source_target_pairs={{0,1},{4,5},{8,9},{12,13},{16,17},{20,21},{24,25},{28,29},{35,34},... | collective-permute-start | bytes 884744 | tf_op jit(solution)/shard_map/spread1/ppermute | solution.py:75
  17.2 16.7 %collective-permute-start.3 = (bf16[192,768]{1,0:T(8,128)(2,1)S(1)}, bf16[192,768]{1,0:T(8,128)(2,1)S(1)}, u32[]{:S(2)}, u32[]{:S(2)}) collective-permute-start(bf16[192,768]{1,0:T(8,128)(2,1)S(1)} %get-tuple-element.26), channel_id=1, source_target_pairs={{0,2},{4,6},{8,10},{12,14},{16,18},{20,22},{24,26},{28,30},{35,33}... | collective-permute-start | bytes 884744 | tf_op jit(solution)/shard_map/spread2/ppermute | solution.py:75
  17.9 27.0 %collective-permute-start.7 = (bf16[384,768]{1,0:T(8,128)(2,1)S(1)}, bf16[384,768]{1,0:T(8,128)(2,1)S(1)}, u32[]{:S(2)}, u32[]{:S(2)}) collective-permute-start(bf16[384,768]{1,0:T(8,128)(2,1)S(1)} %collective-permute-done.inner.refs_1_), channel_id=1, source_target_pairs={{0,448},{1,449},{2,450},{3,451},{4,452},{5,453},{6,454},{7,455},{8... | collective-permute-start | bytes 1769480 | tf_op jit(solution)/shard_map/own_inner1/ppermute | solution.py:75
  44.9 13.3 %collective-permute-start.9 = (bf16[768,768]{1,0:T(8,128)(2,1)S(1)}, bf16[768,768]{1,0:T(8,128)(2,1)S(1)}, u32[]{:S(2)}, u32[]{:S(2)}) collective-permute-start(bf16[768,768]{1,0:T(8,128)(2,1)S(1)} %constant_dynamic-update-slice_fusion), channel_id=1, source_target_pairs={{0,32},{1,33},{2,34},{3,35},{4,36},{5,37},{6,38},{7,39},{8,40},{9,... | collective-permute-start | bytes 3538952 | tf_op jit(solution)/shard_map/sibling1/ppermute | solution.py:75
  48.4 35.0 %collective-permute-start.4 = (bf16[768,768]{1,0:T(8,128)(2,1)S(1)}, bf16[768,768]{1,0:T(8,128)(2,1)S(1)}, u32[]{:S(2)}, u32[]{:S(2)}) collective-permute-start(bf16[768,768]{1,0:T(8,128)(2,1)S(1)} %pad_maximum_fusion), channel_id=1, source_target_pairs={{1,0},{2,1},{3,2},{5,4},{6,5},{7,6},{9,8},{10,9},{11,10},{13,12},{... | collective-permute-start | bytes 3538952 | tf_op jit(solution)/shard_map/wide_pair0/ppermute | solution.py:75
  49.8 33.7 %collective-permute-start.8 = (bf16[768,768]{1,0:T(8,128)(2,1)S(1)}, bf16[768,768]{1,0:T(8,128)(2,1)S(1)}, u32[]{:S(2)}, u32[]{:S(2)}) collective-permute-start(bf16[768,768]{1,0:T(8,128)(2,1)S(1)} %constant_dynamic-update-slice_fusion), channel_id=1, source_target_pairs={{1,0},{2,1},{3,2},{5,4},{6,5},{7,6},{9,8},{10,9},{11,10},{13,12},{... | collective-permute-start | bytes 3538952 | tf_op jit(solution)/shard_map/wide_pair1/ppermute | solution.py:75
  52.8 30.7 %collective-permute-start.5 = (bf16[192,768]{1,0:T(8,128)(2,1)S(1)}, bf16[192,768]{1,0:T(8,128)(2,1)S(1)}, u32[]{:S(2)}, u32[]{:S(2)}) collective-permute-start(bf16[192,768]{1,0:T(8,128)(2,1)S(1)} %select_select_fusion), channel_id=1, source_target_pairs={{0,476},{1,477},{2,478},{3,479},{4,448},{5,449},{6,450},{7,451},{8... | collective-permute-start | bytes 884744 | tf_op jit(solution)/shard_map/cross/ppermute | solution.py:75
  60.6 1.0 copy-start.2
  61.7 1.0 copy-start.4
  83.4 28.1 %copy-start = (bf16[768,768]{1,0:T(8,128)(2,1)}, bf16[768,768]{1,0:T(8,128)(2,1)S(1)}, u32[]{:S(2)}) copy-start(bf16[768,768]{1,0:T(8,128)(2,1)S(1)} %collective-permute-done.4.usual) | copy-start | bytes 3538948
  83.4 1.1 copy-start.6
  84.5 20.6 %collective-permute-start.10 = (bf16[192,768]{1,0:T(8,128)(2,1)S(1)}, bf16[192,768]{1,0:T(8,128)(2,1)S(1)}, u32[]{:S(2)}, u32[]{:S(2)}) collective-permute-start(bf16[192,768]{1,0:T(8,128)(2,1)S(1)} %collective-permute-done.5.q0), channel_id=1, source_target_pairs={{0,64},{1,65},{2,66},{3,67},{4,68},{5,69},{6,70},{7,71},{8,72},{9,... | collective-permute-start | bytes 884744 | tf_op jit(solution)/shard_map/cross_back/ppermute | solution.py:75
  90.7 12.5 %collective-permute-start.11 = (bf16[96,768]{1,0:T(8,128)(2,1)S(1)}, bf16[96,768]{1,0:T(8,128)(2,1)S(1)}, u32[]{:S(2)}, u32[]{:S(2)}) collective-permute-start(bf16[96,768]{1,0:T(8,128)(2,1)S(1)} %slice.3), channel_id=1, source_target_pairs={{0,448},{1,449},{2,450},{3,451},{4,452},{5,453},{6,454},{7,455},{8... | collective-permute-start | bytes 442376 | tf_op jit(solution)/shard_map/cross_ahead/ppermute | solution.py:75
  93.1 12.0 %collective-permute-start.14 = (bf16[192,768]{1,0:T(8,128)(2,1)S(1)}, bf16[192,768]{1,0:T(8,128)(2,1)S(1)}, u32[]{:S(2)}, u32[]{:S(2)}) collective-permute-start(bf16[192,768]{1,0:T(8,128)(2,1)S(1)} %collective-permute-done.5.q0), channel_id=1, source_target_pairs={{0,3},{4,7},{8,11},{12,15},{16,19},{20,23},{24,27},{28,31},{35,32}... | collective-permute-start | bytes 884744 | tf_op jit(solution)/shard_map/gather1_3/ppermute | solution.py:75
  94.4 11.4 %collective-permute-start.13 = (bf16[192,768]{1,0:T(8,128)(2,1)S(1)}, bf16[192,768]{1,0:T(8,128)(2,1)S(1)}, u32[]{:S(2)}, u32[]{:S(2)}) collective-permute-start(bf16[192,768]{1,0:T(8,128)(2,1)S(1)} %collective-permute-done.5.q0), channel_id=1, source_target_pairs={{2,3},{6,7},{10,11},{14,15},{18,19},{22,23},{26,27},{30,31},{33,32... | collective-permute-start | bytes 884744 | tf_op jit(solution)/shard_map/gather1_2/ppermute | solution.py:75
  95.7 11.2 %collective-permute-start.12 = (bf16[192,768]{1,0:T(8,128)(2,1)S(1)}, bf16[192,768]{1,0:T(8,128)(2,1)S(1)}, u32[]{:S(2)}, u32[]{:S(2)}) collective-permute-start(bf16[192,768]{1,0:T(8,128)(2,1)S(1)} %collective-permute-done.5.q0), channel_id=1, source_target_pairs={{1,3},{5,7},{9,11},{13,15},{17,19},{21,23},{25,27},{29,31},{34,32}... | collective-permute-start | bytes 884744 | tf_op jit(solution)/shard_map/gather1_1/ppermute | solution.py:75
  103.2 20.1 %collective-permute-start.15 = (bf16[384,768]{1,0:T(8,128)(2,1)}, bf16[384,768]{1,0:T(8,128)(2,1)}, u32[]{:S(2)}, u32[]{:S(2)}) collective-permute-start(bf16[384,768]{1,0:T(8,128)(2,1)} %collective-permute-done.6.refs_2_), channel_id=1, source_target_pairs={{0,480},{1,481},{2,482},{3,483},{4,484},{5,485},{6,486},{7,487},{8... | collective-permute-start | bytes 1769480 | tf_op jit(solution)/shard_map/own_outer2/ppermute | solution.py:75
  105.2 0.7 copy-start.14
  105.9 0.7 copy-start.16
  106.9 0.7 copy-start.18
  107.6 20.3 %collective-permute-start.18 = (bf16[288,768]{1,0:T(8,128)(2,1)S(1)}, bf16[288,768]{1,0:T(8,128)(2,1)}, u32[]{:S(2)}, u32[]{:S(2)}) collective-permute-start(bf16[288,768]{1,0:T(8,128)(2,1)S(1)} %pad_maximum_fusion.1.q0), channel_id=1, source_target_pairs={{0,3},{4,7},{8,11},{12,15},{16,19},{20,23},{24,27},{28,31},{35,32}... | collective-permute-start | bytes 1327112 | tf_op jit(solution)/shard_map/gather0_3/ppermute | solution.py:75
  108.9 19.0 %collective-permute-start.17 = (bf16[288,768]{1,0:T(8,128)(2,1)S(1)}, bf16[288,768]{1,0:T(8,128)(2,1)}, u32[]{:S(2)}, u32[]{:S(2)}) collective-permute-start(bf16[288,768]{1,0:T(8,128)(2,1)S(1)} %pad_maximum_fusion.1.q0), channel_id=1, source_target_pairs={{2,3},{6,7},{10,11},{14,15},{18,19},{22,23},{26,27},{30,31},{33,32... | collective-permute-start | bytes 1327112 | tf_op jit(solution)/shard_map/gather0_2/ppermute | solution.py:75
  110.2 17.7 %collective-permute-start.16 = (bf16[288,768]{1,0:T(8,128)(2,1)S(1)}, bf16[288,768]{1,0:T(8,128)(2,1)}, u32[]{:S(2)}, u32[]{:S(2)}) collective-permute-start(bf16[288,768]{1,0:T(8,128)(2,1)S(1)} %pad_maximum_fusion.1.q0), channel_id=1, source_target_pairs={{1,3},{5,7},{9,11},{13,15},{17,19},{21,23},{25,27},{29,31},{34,32}... | collective-permute-start | bytes 1327112 | tf_op jit(solution)/shard_map/gather0_1/ppermute | solution.py:75
  111.5 1.3 copy-start.7
  112.8 1.0 copy-start.15
  113.8 1.0 copy-start.17
  114.7 1.0 copy-start.19
  115.7 7.6 %copy-start.3 = (f32[384,768]{1,0:T(8,128)S(1)}, f32[384,768]{1,0:T(8,128)}, u32[]{:S(2)}) copy-start(f32[384,768]{1,0:T(8,128)} %copy-done.2) | copy-start | bytes 3538948
  115.7 7.6 %copy-start.5 = (f32[384,768]{1,0:T(8,128)S(1)}, f32[384,768]{1,0:T(8,128)}, u32[]{:S(2)}) copy-start(f32[384,768]{1,0:T(8,128)} %copy-done.4) | copy-start | bytes 3538948
  115.8 28.6 %collective-permute-start.21 = (bf16[768,768]{1,0:T(8,128)(2,1)S(1)}, bf16[768,768]{1,0:T(8,128)(2,1)}, u32[]{:S(2)}, u32[]{:S(2)}) collective-permute-start(bf16[768,768]{1,0:T(8,128)(2,1)S(1)} %merge1.1.refs_0_), channel_id=1, source_target_pairs={{0,32},{1,33},{2,34},{3,35},{4,36},{5,37},{6,38},{7,39},{8,40},{9,... | collective-permute-start | bytes 3538952 | tf_op jit(solution)/shard_map/sibling_hop1/ppermute | solution.py:75
  123.3 4.6 %copy-start.1 = (bf16[768,768]{1,0:T(8,128)(2,1)S(1)}, bf16[768,768]{1,0:T(8,128)(2,1)}, u32[]{:S(2)}) copy-start(bf16[768,768]{1,0:T(8,128)(2,1)} %copy-done) | copy-start | bytes 3538948
  126.9 1.0 copy-start.10
  127.9 2.9 %copy-start.8 = (f32[384,768]{1,0:T(8,128)}, f32[384,768]{1,0:T(8,128)S(1)}, u32[]{:S(2)}) copy-start(f32[384,768]{1,0:T(8,128)S(1)} %get-tuple-element.38.refs_3_) | copy-start | bytes 3538948
  130.8 0.8 copy-start.12
  131.6 21.1 %collective-permute-start.19 = (bf16[768,768]{1,0:T(8,128)(2,1)}, bf16[768,768]{1,0:T(8,128)(2,1)}, u32[]{:S(2)}, u32[]{:S(2)}) collective-permute-start(bf16[768,768]{1,0:T(8,128)(2,1)} %get-tuple-element.41.refs_1_), channel_id=1, source_target_pairs={{0,32},{1,33},{2,34},{3,35},{4,36},{5,37},{6,38},{7,39},{8,40},{9,... | collective-permute-start | bytes 3538952 | tf_op jit(solution)/shard_map/sibling_hop0/ppermute | solution.py:75
  133.6 10.8 %collective-permute-start.20 = (bf16[384,768]{1,0:T(8,128)(2,1)}, bf16[384,768]{1,0:T(8,128)(2,1)S(1)}, u32[]{:S(2)}, u32[]{:S(2)}) collective-permute-start(bf16[384,768]{1,0:T(8,128)(2,1)} %collective-permute-done.15.refs_1_), channel_id=1, source_target_pairs={{0,1},{1,2},{2,3},{4,5},{5,6},{6,7},{8,9},{9,10},{10,11},{12,13},{... | collective-permute-start | bytes 1769480 | tf_op jit(solution)/shard_map/wide_outer2/ppermute | solution.py:75
  144.4 1.3 copy-start.9
  145.7 1.3 copy-start.11
  146.9 1.1 copy-start.13

commit v3 on v2

--- a/solution.py
+++ b/solution.py
@@ -41,6 +41,10 @@
     return x, h, m, z, 1 - c
 
 
+def to_previous_chip_sibling(x, h, m, z, c, s):
+    return x, h, m, z - s, 1 - c
+
+
 def to_next_chip_sibling(x, h, m, z, c, s):
     return x, h, m, z + s, 1 - c
 
@@ -95,7 +99,7 @@
             cost_estimate=pl.CostEstimate(
                 flops=weight * 1000, bytes_accessed=1000, transcendentals=0
             ),
-            compiler_params=pltpu.CompilerParams(vmem_limit_bytes=20 * 1024 * 1024),
+            compiler_params=pltpu.CompilerParams(vmem_limit_bytes=16 * 1024 * 1024),
         )(*smem, *vmem)
 
 
@@ -153,13 +157,13 @@
 
     inner = send("swap", other, to_sibling)
     outer1 = send("own_outer1", outer, to_next_chip)
+    inner1 = send("own_inner1", other, to_previous_chip_sibling)
 
     strip = jax.ShapeDtypeStruct((2 * quarter, width), half)
     cuts = call("cut", cut_kernel, [strip] * 4, (), (inner, outer))
     spread0 = send("spread0", cuts[0], line_to_line(3, 0))
     spread1 = send("spread1", cuts[1], line_to_line(3, 2))
     spread2 = send("spread2", cuts[2], line_to_line(3, 1))
-    inner1 = send("own_inner1", inner, to_next_chip)
     held = jnp.where(
         mirrored == 0,
         spread0,
@@ -271,31 +275,36 @@
     sums = terms("terms_hop1", [(hop1, [4, 5])], [(far2, [11])], sums)
     got0 = [after(got0[0], far2, *sums), *got0[1:]]
 
-    def merge0_kernel(edge, usual, q0, q1, q2, q3, out, keys):
+    def merge0_kernel(edge, usual, q0, q1, q2, q3, inner0, outer0, farthest):
         @pl.when(edge[0] == 1)
         def _():
             for place, source in enumerate((q0, q1, q2, q3)):
                 low = place * quarter
-                out[low : low + quarter, :] = source[:quarter, :]
-                keys[low : low + quarter, :] = source[quarter : 2 * quarter, :]
-                out[rows + low : rows + low + quarter, :] = source[2 * quarter :, :]
+                inner0[low : low + quarter, :] = source[:quarter, :]
+                outer0[low : low + quarter, :] = source[quarter : 2 * quarter, :]
+                farthest[low : low + quarter, :] = source[2 * quarter :, :]
 
         @pl.when(edge[0] == 0)
         def _():
-            out[...] = usual[...]
-            keys[...] = usual[rows:, :]
-
-    hop0, hop_outer0 = call(
-        "merge0", merge0_kernel, [blocks(2), blocks(1)], (at_edge,), (pair0, *got0)
-    )
-    hop_sib0 = send("sibling_hop0", hop0, to_sibling)
-    sums = terms("terms_hop0", [(hop_outer0, [7]), (hop0, [6])], [(after(hop_sib1, hop_far2), [12, 13])], sums)
-
-    def last_kernel(c, e, s, out, ff, kf, hs0, hf2, near_in, far_in, image_grad, caption_grad):
-        farthest = jnp.where(e[0] == 1, hs0[rows:, :], hf2[...])
+            inner0[...] = usual[:rows, :]
+            outer0[...] = usual[rows:, :]
+            farthest[...] = usual[rows:, :]
+
+    hop_inner0, hop_outer0, hop_outer2 = call(
+        "merge0", merge0_kernel, [blocks(1)] * 3, (at_edge,), (pair0, *got0)
+    )
+    hop_sib0 = send("sibling_hop0", hop_inner0, to_sibling)
+    hop_sib2 = send("sibling_hop2", hop_outer2, to_sibling)
+    sums = terms(
+        "terms_hop0", [(hop_outer0, [7]), (hop_inner0, [6])],
+        [(after(hop_sib1, hop_far2), [12, 13])], sums,
+    )
+
+    def last_kernel(c, e, s, out, ff, kf, hs0, hs2, hf2, near_in, far_in, image_grad, caption_grad):
+        farthest = jnp.where(e[0] == 1, hs2[...], hf2[...])
         far = s[0] * add_terms(
             far_in[...], out[...], ff[:, :1], kf, s[0],
-            [(hs0[:rows, :], 14, False), (farthest, 15, False)],
+            [(hs0[...], 14, False), (farthest, 15, False)],
         )
         near = s[0] * near_in[...]
 
@@ -311,7 +320,7 @@
 
     image_grad, caption_grad = call(
         "terms_last", last_kernel, [total, total], (core_flag, sibling_at_edge, scale),
-        (outer, far_factor, key_factors, hop_sib0, hop_far2, *sums),
+        (outer, far_factor, key_factors, hop_sib0, hop_sib2, hop_far2, *sums),
     )
     return image_grad, caption_grad
 

time: 158 us -> 159 us (level)
  starting transfers between devices: 57.6 us -> 68.5 us
  waiting for transfers between devices: 56.1 us -> 47.7 us
  local copies, waits for them, and re-layouts: 16.3 us -> 14.6 us
  Pallas kernels: 22.3 us -> 20.6 us
    ppermute x22 -> x23, starting transfers between devices: 57.6 us -> 68.5 us  [send(): return lax.ppermute(x, AXES, pairs(target))]
    ppermute x22 -> x23, waiting for transfers between devices: 56.1 us -> 47.7 us  [send(): return lax.ppermute(x, AXES, pairs(target))]
    unnamed x41 -> x37, local copies, waits for them, and re-layouts: 15.9 us -> 14.2 us
    pallas_call x8, Pallas kernels: 22.3 us -> 20.6 us  [call(): pl.pallas_call(kernel, out_shape=out_shape, in_specs=[scalars() for _ in...]
  transfers between devices with their start and end apart: 22 -> 23, of which waited for: 6 -> 7; matrix products, arithmetic and copies ran while one was open for 2% -> 2% of each run, Pallas kernels for 11% -> 10%
where the time goes in v3:
time: 159 us; the launch traced here: 157 us
  starting transfers between devices  68.5 us (43%)
  waiting for transfers between devices  47.7 us (30%)
  Pallas kernels  20.6 us (13%)
  local copies, waits for them, and re-layouts  14.6 us (9%)
  other arithmetic  3.72 us (2%)
  between operations  2.16 us (1%)
    ppermute x23, starting transfers between devices, send(): return lax.ppermute(x, AXES, pairs(target))  68.5 us
    ppermute x23, waiting for transfers between devices, send(): return lax.ppermute(x, AXES, pairs(target))  47.7 us
    pallas_call x8, Pallas kernels, call(): pl.pallas_call(kernel, out_shape=out_shape, in_specs=[scalars() for _ in...  20.6 us
    unnamed x37, local copies, waits for them, and re-layouts  14.2 us
  transfers between devices with their start and end apart: 23, of which 7 were waited for; matrix products, arithmetic and copies ran while one was open for 2% of the time, Pallas kernels for 10%

profile of v3, /device:TPU:1, one launch (start us, length us, event | category | flops | bytes accessed | tf_op | source)
XLA Modules:
  0.0 157.4 jit_solution(10591525962716557756)
XLA Ops:
  0.6 1.3 broadcast_select_fusion
  2.0 8.8 %collective-permute-start = (bf16[384,768]{1,0:T(8,128)(2,1)S(1)}, bf16[384,768]{1,0:T(8,128)(2,1)S(1)}, u32[]{:S(2)}, u32[]{:S(2)}) collective-permute-start(bf16[384,768]{1,0:T(8,128)(2,1)S(1)} %get-tuple-element.68.oth.refs_3_), channel_id=1, source_target_pairs={{0,32},{1,33},{2,34},{3,35},{4,36},{5,37},{6,38},{7,39},{8,40},{9,... | collective-permute-start | bytes 1769480 | tf_op jit(solution)/shard_map/swap/ppermute | solution.py:79
  10.8 1.9 %collective-permute-start.6 = (bf16[384,768]{1,0:T(8,128)(2,1)S(1)}, bf16[384,768]{1,0:T(8,128)(2,1)}, u32[]{:S(2)}, u32[]{:S(2)}) collective-permute-start(bf16[384,768]{1,0:T(8,128)(2,1)S(1)} %get-tuple-element.69.outer.out.refs_0_), channel_id=1, source_target_pairs={{0,448},{1,449},{2,450},{3,451},{4,452},{5,453},{6,454},{7,455},{8... | collective-permute-start | bytes 1769480 | tf_op jit(solution)/shard_map/own_outer1/ppermute | solution.py:79
  12.7 7.5 %collective-permute-start.7 = (bf16[384,768]{1,0:T(8,128)(2,1)S(1)}, bf16[384,768]{1,0:T(8,128)(2,1)S(1)}, u32[]{:S(2)}, u32[]{:S(2)}) collective-permute-start(bf16[384,768]{1,0:T(8,128)(2,1)S(1)} %get-tuple-element.68.oth.refs_3_), channel_id=1, source_target_pairs={{0,96},{1,97},{2,98},{3,99},{4,100},{5,101},{6,102},{7,103},{8,104... | collective-permute-start | bytes 1769480 | tf_op jit(solution)/shard_map/own_inner1/ppermute | solution.py:79
  21.1 1.2 exponential_multiply_fusion.1
  22.5 0.1 stack.67
  22.6 0.0 collective-permute-done.inner.refs_1_
  22.6 0.1 cut.1
  22.7 1.3 collective-permute-start.1
  24.0 0.7 collective-permute-start.2
  24.7 0.7 collective-permute-start.3
  25.4 9.4 %collective-permute-done.6.refs_2_ = bf16[384,768]{1,0:T(8,128)(2,1)} collective-permute-done((bf16[384,768]{1,0:T(8,128)(2,1)S(1)}, bf16[384,768]{1,0:T(8,128)(2,1)}, u32[]{:S(2)}, u32[]{:S(2)}) %collective-permute-start.6) | collective-permute-done | bytes 589856 | tf_op jit(solution)/shard_map/own_outer1/ppermute | solution.py:79
  34.7 1.1 constant_dynamic-update-slice_fusion.1
  35.9 0.0 collective-permute-done.1
  35.9 0.1 select_select_fusion
  36.0 0.1 broadcast_in_dim.5.nf
  36.1 0.1 broadcast_in_dim.4.ff
  36.2 4.1 %terms_own0.1 = (f32[384,768]{1,0:T(8,128)S(1)}, f32[384,768]{1,0:T(8,128)S(1)}) custom-call(f32[1]{0:T(128)} %bitcast.4.s, bf16[384,768]{1,0:T(8,128)(2,1)S(1)} %get-tuple-element.68.oth.refs_3_, bf16[384,768]{1,0:T(8,128)(2,1)S(1)} %get-tuple-element.69.outer.out.refs_0_, f32[384,128]{1,0:T(8,128)S(1)} %broadcast_in_dim.5.nf, ...), custom_call_target="tpu_custom_call" | custom-call | flops 99999997952 | bytes 1000 | tf_op jit(solution)/shard_map/terms_own0/pallas_call | solution.py:94
  40.3 2.3 %collective-permute-done.7.refs_0_ = bf16[384,768]{1,0:T(8,128)(2,1)S(1)} collective-permute-done((bf16[384,768]{1,0:T(8,128)(2,1)S(1)}, bf16[384,768]{1,0:T(8,128)(2,1)S(1)}, u32[]{:S(2)}, u32[]{:S(2)}) %collective-permute-start.7) | collective-permute-done | bytes 589856 | tf_op jit(solution)/shard_map/own_inner1/ppermute | solution.py:79
  42.6 1.9 %collective-permute-start.9 = (bf16[768,768]{1,0:T(8,128)(2,1)S(1)}, bf16[768,768]{1,0:T(8,128)(2,1)S(1)}, u32[]{:S(2)}, u32[]{:S(2)}) collective-permute-start(bf16[768,768]{1,0:T(8,128)(2,1)S(1)} %constant_dynamic-update-slice_fusion), channel_id=1, source_target_pairs={{0,32},{1,33},{2,34},{3,35},{4,36},{5,37},{6,38},{7,39},{8,40},{9,... | collective-permute-start | bytes 3538952 | tf_op jit(solution)/shard_map/sibling1/ppermute | solution.py:79
  44.6 0.1 pad_maximum_fusion
  44.6 5.2 %collective-permute-start.4 = (bf16[768,768]{1,0:T(8,128)(2,1)S(1)}, bf16[768,768]{1,0:T(8,128)(2,1)S(1)}, u32[]{:S(2)}, u32[]{:S(2)}) collective-permute-start(bf16[768,768]{1,0:T(8,128)(2,1)S(1)} %pad_maximum_fusion), channel_id=1, source_target_pairs={{1,0},{2,1},{3,2},{5,4},{6,5},{7,6},{9,8},{10,9},{11,10},{13,12},{... | collective-permute-start | bytes 3538952 | tf_op jit(solution)/shard_map/wide_pair0/ppermute | solution.py:79
  49.8 3.2 %collective-permute-start.8 = (bf16[768,768]{1,0:T(8,128)(2,1)S(1)}, bf16[768,768]{1,0:T(8,128)(2,1)S(1)}, u32[]{:S(2)}, u32[]{:S(2)}) collective-permute-start(bf16[768,768]{1,0:T(8,128)(2,1)S(1)} %constant_dynamic-update-slice_fusion), channel_id=1, source_target_pairs={{1,0},{2,1},{3,2},{5,4},{6,5},{7,6},{9,8},{10,9},{11,10},{13,12},{... | collective-permute-start | bytes 3538952 | tf_op jit(solution)/shard_map/wide_pair1/ppermute | solution.py:79
  53.1 8.6 %collective-permute-start.5 = (bf16[192,768]{1,0:T(8,128)(2,1)S(1)}, bf16[192,768]{1,0:T(8,128)(2,1)S(1)}, u32[]{:S(2)}, u32[]{:S(2)}) collective-permute-start(bf16[192,768]{1,0:T(8,128)(2,1)S(1)} %select_select_fusion), channel_id=1, source_target_pairs={{0,476},{1,477},{2,478},{3,479},{4,448},{5,449},{6,450},{7,451},{8... | collective-permute-start | bytes 884744 | tf_op jit(solution)/shard_map/cross/ppermute | solution.py:79
  61.7 2.4 %terms_own1.1 = (f32[384,768]{1,0:T(8,128)S(1)}, f32[384,768]{1,0:T(8,128)S(1)}) custom-call(f32[1]{0:T(128)} %bitcast.5.s, bf16[384,768]{1,0:T(8,128)(2,1)S(1)} %get-tuple-element.68.oth.refs_3_, bf16[384,768]{1,0:T(8,128)(2,1)S(1)} %get-tuple-element.69.outer.out.refs_0_, f32[384,128]{1,0:T(8,128)S(1)} %broadcast_in_dim.5.nf, ...), custom_call_target="tpu_custom_call" | custom-call | flops 1000 | bytes 1000 | tf_op jit(solution)/shard_map/terms_own1/pallas_call | solution.py:94
  64.1 1.0 copy-done.6
  65.1 1.0 copy-done.8
  66.2 18.1 %collective-permute-done.5.q0 = bf16[192,768]{1,0:T(8,128)(2,1)S(1)} collective-permute-done((bf16[192,768]{1,0:T(8,128)(2,1)S(1)}, bf16[192,768]{1,0:T(8,128)(2,1)S(1)}, u32[]{:S(2)}, u32[]{:S(2)}) %collective-permute-start.5) | collective-permute-done | bytes 294944 | tf_op jit(solution)/shard_map/cross/ppermute | solution.py:79
  84.3 1.0 copy-done
  85.3 1.0 copy-done.10
  86.3 1.3 collective-permute-start.14
  87.6 1.3 collective-permute-start.13
  88.9 1.3 collective-permute-start.12
  90.2 1.9 %collective-permute-start.10 = (bf16[192,768]{1,0:T(8,128)(2,1)S(1)}, bf16[192,768]{1,0:T(8,128)(2,1)}, u32[]{:S(2)}, u32[]{:S(2)}) collective-permute-start(bf16[192,768]{1,0:T(8,128)(2,1)S(1)} %collective-permute-done.5.q0), channel_id=1, source_target_pairs={{0,64},{1,65},{2,66},{3,67},{4,68},{5,69},{6,70},{7,71},{8,72},{9,... | collective-permute-start | bytes 884744 | tf_op jit(solution)/shard_map/cross_back/ppermute | solution.py:79
  92.2 5.3 %collective-permute-start.11 = (bf16[96,768]{1,0:T(8,128)(2,1)S(1)}, bf16[96,768]{1,0:T(8,128)(2,1)S(1)}, u32[]{:S(2)}, u32[]{:S(2)}) collective-permute-start(bf16[96,768]{1,0:T(8,128)(2,1)S(1)} %slice.3), channel_id=1, source_target_pairs={{0,448},{1,449},{2,450},{3,451},{4,452},{5,453},{6,454},{7,455},{8... | collective-permute-start | bytes 442376 | tf_op jit(solution)/shard_map/cross_ahead/ppermute | solution.py:79
  97.5 9.2 %collective-permute-done.11 = bf16[96,768]{1,0:T(8,128)(2,1)S(1)} collective-permute-done((bf16[96,768]{1,0:T(8,128)(2,1)S(1)}, bf16[96,768]{1,0:T(8,128)(2,1)S(1)}, u32[]{:S(2)}, u32[]{:S(2)}) %collective-permute-start.11) | collective-permute-done | bytes 147488 | tf_op jit(solution)/shard_map/cross_ahead/ppermute | solution.py:79
  106.7 1.9 %collective-permute-start.15 = (bf16[384,768]{1,0:T(8,128)(2,1)}, bf16[384,768]{1,0:T(8,128)(2,1)}, u32[]{:S(2)}, u32[]{:S(2)}) collective-permute-start(bf16[384,768]{1,0:T(8,128)(2,1)} %collective-permute-done.6.refs_2_), channel_id=1, source_target_pairs={{0,480},{1,481},{2,482},{3,483},{4,484},{5,485},{6,486},{7,487},{8... | collective-permute-start | bytes 1769480 | tf_op jit(solution)/shard_map/own_outer2/ppermute | solution.py:79
  108.6 0.7 copy-done.14
  109.3 0.7 copy-done.16
  110.0 1.3 copy-done.11
  111.3 1.0 copy-done.15
  112.3 1.0 copy-done.17
  113.2 0.1 merge1.1.refs_0_
  113.3 2.1 %collective-permute-start.22 = (bf16[768,768]{1,0:T(8,128)(2,1)S(1)}, bf16[768,768]{1,0:T(8,128)(2,1)}, u32[]{:S(2)}, u32[]{:S(2)}) collective-permute-start(bf16[768,768]{1,0:T(8,128)(2,1)S(1)} %merge1.1.refs_0_), channel_id=1, source_target_pairs={{0,32},{1,33},{2,34},{3,35},{4,36},{5,37},{6,38},{7,39},{8,40},{9,... | collective-permute-start | bytes 3538952 | tf_op jit(solution)/shard_map/sibling_hop1/ppermute | solution.py:79
  115.4 1.0 pad_maximum_fusion.1.q0
  116.4 1.3 collective-permute-start.18
  117.7 1.3 collective-permute-start.17
  119.0 1.3 collective-permute-start.16
  120.3 1.5 collective-permute-done.15.refs_1_
  121.8 3.5 %terms_hop1.1 = (f32[384,768]{1,0:T(8,128)S(1)}, f32[384,768]{1,0:T(8,128)S(1)}) custom-call(f32[1]{0:T(128)} %bitcast.6.s, bf16[384,768]{1,0:T(8,128)(2,1)S(1)} %get-tuple-element.68.oth.refs_3_, bf16[384,768]{1,0:T(8,128)(2,1)S(1)} %get-tuple-element.69.outer.out.refs_0_, f32[384,128]{1,0:T(8,128)S(1)} %broadcast_in_dim.5.nf, ...), custom_call_target="tpu_custom_call" | custom-call | flops 1000 | bytes 1000 | tf_op jit(solution)/shard_map/terms_hop1/pallas_call | solution.py:94
  125.4 0.0 copy-start.2
  125.4 1.3 collective-permute-start.21
  126.7 2.3 %collective-permute-done.18.q3 = bf16[288,768]{1,0:T(8,128)(2,1)S(1)} collective-permute-done((bf16[288,768]{1,0:T(8,128)(2,1)S(1)}, bf16[288,768]{1,0:T(8,128)(2,1)S(1)}, u32[]{:S(2)}, u32[]{:S(2)}) %collective-permute-start.18) | collective-permute-done | bytes 442400 | tf_op jit(solution)/shard_map/gather0_3/ppermute | solution.py:79
  129.0 4.9 %collective-permute-done.16.q1 = bf16[288,768]{1,0:T(8,128)(2,1)S(1)} collective-permute-done((bf16[288,768]{1,0:T(8,128)(2,1)S(1)}, bf16[288,768]{1,0:T(8,128)(2,1)S(1)}, u32[]{:S(2)}, u32[]{:S(2)}) %collective-permute-start.16) | collective-permute-done | bytes 442400 | tf_op jit(solution)/shard_map/gather0_1/ppermute | solution.py:79
  133.9 1.2 merge0.1
  135.1 0.8 copy-done.12
  135.9 6.4 %collective-permute-start.20 = (bf16[384,768]{1,0:T(8,128)(2,1)}, bf16[384,768]{1,0:T(8,128)(2,1)}, u32[]{:S(2)}, u32[]{:S(2)}) collective-permute-start(bf16[384,768]{1,0:T(8,128)(2,1)} %get-tuple-element.43), channel_id=1, source_target_pairs={{0,32},{1,33},{2,34},{3,35},{4,36},{5,37},{6,38},{7,39},{8,40},{9,... | collective-permute-start | bytes 1769480 | tf_op jit(solution)/shard_map/sibling_hop2/ppermute | solution.py:79
  142.4 2.1 %collective-permute-start.19 = (bf16[384,768]{1,0:T(8,128)(2,1)}, bf16[384,768]{1,0:T(8,128)(2,1)}, u32[]{:S(2)}, u32[]{:S(2)}) collective-permute-start(bf16[384,768]{1,0:T(8,128)(2,1)} %get-tuple-element.42.refs_1_), channel_id=1, source_target_pairs={{0,32},{1,33},{2,34},{3,35},{4,36},{5,37},{6,38},{7,39},{8,40},{9,... | collective-permute-start | bytes 1769480 | tf_op jit(solution)/shard_map/sibling_hop0/ppermute | solution.py:79
  144.5 0.0 copy-start.3
  144.5 1.3 copy-done.3
  145.8 1.3 copy-done.5
  147.0 1.1 copy-done.13
  148.1 4.5 %terms_hop0.1 = (f32[384,768]{1,0:T(8,128)S(1)}, f32[384,768]{1,0:T(8,128)S(1)}) custom-call(f32[1]{0:T(128)} %bitcast.7.s, bf16[384,768]{1,0:T(8,128)(2,1)S(1)} %get-tuple-element.68.oth.refs_3_, bf16[384,768]{1,0:T(8,128)(2,1)S(1)} %get-tuple-element.69.outer.out.refs_0_, f32[384,128]{1,0:T(8,128)S(1)} %broadcast_in_dim.5.nf, ...), custom_call_target="tpu_custom_call" | custom-call | flops 1000 | bytes 1000 | tf_op jit(solution)/shard_map/terms_hop0/pallas_call | solution.py:94
  152.7 4.7 %terms_last.1 = (f32[384,768]{1,0:T(8,128)}, f32[384,768]{1,0:T(8,128)}) custom-call(s32[1]{0:T(128)} %bitcast.c, s32[1]{0:T(128)} %bitcast.1.e, f32[1]{0:T(128)} %bitcast.8.s, bf16[384,768]{1,0:T(8,128)(2,1)S(1)} %get-tuple-element.69.outer.out.refs_0_, f32[384,128]{1,0:T(8,128)S(1)} %broadcast_in_dim.4.ff, f32[16,384]{1,0:T(8,128)S(1)} %exponential_multiply_fusion.kf, ...), custom_call_target="tpu_custom_call" | custom-call | flops 1000 | bytes 1000 | tf_op jit(solution)/shard_map/terms_last/pallas_call | solution.py:94
  (54 shorter events, 0.2 us)
Async XLA Ops:
  2.0 20.6 %collective-permute-start = (bf16[384,768]{1,0:T(8,128)(2,1)S(1)}, bf16[384,768]{1,0:T(8,128)(2,1)S(1)}, u32[]{:S(2)}, u32[]{:S(2)}) collective-permute-start(bf16[384,768]{1,0:T(8,128)(2,1)S(1)} %get-tuple-element.68.oth.refs_3_), channel_id=1, source_target_pairs={{0,32},{1,33},{2,34},{3,35},{4,36},{5,37},{6,38},{7,39},{8,40},{9,... | collective-permute-start | bytes 1769480 | tf_op jit(solution)/shard_map/swap/ppermute | solution.py:79
  10.8 24.0 %collective-permute-start.6 = (bf16[384,768]{1,0:T(8,128)(2,1)S(1)}, bf16[384,768]{1,0:T(8,128)(2,1)}, u32[]{:S(2)}, u32[]{:S(2)}) collective-permute-start(bf16[384,768]{1,0:T(8,128)(2,1)S(1)} %get-tuple-element.69.outer.out.refs_0_), channel_id=1, source_target_pairs={{0,448},{1,449},{2,450},{3,451},{4,452},{5,453},{6,454},{7,455},{8... | collective-permute-start | bytes 1769480 | tf_op jit(solution)/shard_map/own_outer1/ppermute | solution.py:79
  12.7 29.9 %collective-permute-start.7 = (bf16[384,768]{1,0:T(8,128)(2,1)S(1)}, bf16[384,768]{1,0:T(8,128)(2,1)S(1)}, u32[]{:S(2)}, u32[]{:S(2)}) collective-permute-start(bf16[384,768]{1,0:T(8,128)(2,1)S(1)} %get-tuple-element.68.oth.refs_3_), channel_id=1, source_target_pairs={{0,96},{1,97},{2,98},{3,99},{4,100},{5,101},{6,102},{7,103},{8,104... | collective-permute-start | bytes 1769480 | tf_op jit(solution)/shard_map/own_inner1/ppermute | solution.py:79
  22.7 13.2 %collective-permute-start.1 = (bf16[192,768]{1,0:T(8,128)(2,1)S(1)}, bf16[192,768]{1,0:T(8,128)(2,1)S(1)}, u32[]{:S(2)}, u32[]{:S(2)}) collective-permute-start(bf16[192,768]{1,0:T(8,128)(2,1)S(1)} %get-tuple-element.25), channel_id=1, source_target_pairs={{0,3},{4,7},{8,11},{12,15},{16,19},{20,23},{24,27},{28,31},{35,32}... | collective-permute-start | bytes 884744 | tf_op jit(solution)/shard_map/spread0/ppermute | solution.py:79
  24.0 11.9 %collective-permute-start.2 = (bf16[192,768]{1,0:T(8,128)(2,1)S(1)}, bf16[192,768]{1,0:T(8,128)(2,1)S(1)}, u32[]{:S(2)}, u32[]{:S(2)}) collective-permute-start(bf16[192,768]{1,0:T(8,128)(2,1)S(1)} %get-tuple-element.26), channel_id=1, source_target_pairs={{0,1},{4,5},{8,9},{12,13},{16,17},{20,21},{24,25},{28,29},{35,34},... | collective-permute-start | bytes 884744 | tf_op jit(solution)/shard_map/spread1/ppermute | solution.py:79
  24.7 11.2 %collective-permute-start.3 = (bf16[192,768]{1,0:T(8,128)(2,1)S(1)}, bf16[192,768]{1,0:T(8,128)(2,1)S(1)}, u32[]{:S(2)}, u32[]{:S(2)}) collective-permute-start(bf16[192,768]{1,0:T(8,128)(2,1)S(1)} %get-tuple-element.27), channel_id=1, source_target_pairs={{0,2},{4,6},{8,10},{12,14},{16,18},{20,22},{24,26},{28,30},{35,33}... | collective-permute-start | bytes 884744 | tf_op jit(solution)/shard_map/spread2/ppermute | solution.py:79
  42.6 19.1 %collective-permute-start.9 = (bf16[768,768]{1,0:T(8,128)(2,1)S(1)}, bf16[768,768]{1,0:T(8,128)(2,1)S(1)}, u32[]{:S(2)}, u32[]{:S(2)}) collective-permute-start(bf16[768,768]{1,0:T(8,128)(2,1)S(1)} %constant_dynamic-update-slice_fusion), channel_id=1, source_target_pairs={{0,32},{1,33},{2,34},{3,35},{4,36},{5,37},{6,38},{7,39},{8,40},{9,... | collective-permute-start | bytes 3538952 | tf_op jit(solution)/shard_map/sibling1/ppermute | solution.py:79
  44.6 39.6 %collective-permute-start.4 = (bf16[768,768]{1,0:T(8,128)(2,1)S(1)}, bf16[768,768]{1,0:T(8,128)(2,1)S(1)}, u32[]{:S(2)}, u32[]{:S(2)}) collective-permute-start(bf16[768,768]{1,0:T(8,128)(2,1)S(1)} %pad_maximum_fusion), channel_id=1, source_target_pairs={{1,0},{2,1},{3,2},{5,4},{6,5},{7,6},{9,8},{10,9},{11,10},{13,12},{... | collective-permute-start | bytes 3538952 | tf_op jit(solution)/shard_map/wide_pair0/ppermute | solution.py:79
  49.8 35.5 %collective-permute-start.8 = (bf16[768,768]{1,0:T(8,128)(2,1)S(1)}, bf16[768,768]{1,0:T(8,128)(2,1)S(1)}, u32[]{:S(2)}, u32[]{:S(2)}) collective-permute-start(bf16[768,768]{1,0:T(8,128)(2,1)S(1)} %constant_dynamic-update-slice_fusion), channel_id=1, source_target_pairs={{1,0},{2,1},{3,2},{5,4},{6,5},{7,6},{9,8},{10,9},{11,10},{13,12},{... | collective-permute-start | bytes 3538952 | tf_op jit(solution)/shard_map/wide_pair1/ppermute | solution.py:79
  53.1 31.2 %collective-permute-start.5 = (bf16[192,768]{1,0:T(8,128)(2,1)S(1)}, bf16[192,768]{1,0:T(8,128)(2,1)S(1)}, u32[]{:S(2)}, u32[]{:S(2)}) collective-permute-start(bf16[192,768]{1,0:T(8,128)(2,1)S(1)} %select_select_fusion), channel_id=1, source_target_pairs={{0,476},{1,477},{2,478},{3,479},{4,448},{5,449},{6,450},{7,451},{8... | collective-permute-start | bytes 884744 | tf_op jit(solution)/shard_map/cross/ppermute | solution.py:79
  64.1 1.0 copy-start.6
  65.1 1.0 copy-start.8
  84.3 1.0 copy-start
  85.3 1.0 copy-start.10
  86.3 22.3 %collective-permute-start.14 = (bf16[192,768]{1,0:T(8,128)(2,1)S(1)}, bf16[192,768]{1,0:T(8,128)(2,1)S(1)}, u32[]{:S(2)}, u32[]{:S(2)}) collective-permute-start(bf16[192,768]{1,0:T(8,128)(2,1)S(1)} %collective-permute-done.5.q0), channel_id=1, source_target_pairs={{0,3},{4,7},{8,11},{12,15},{16,19},{20,23},{24,27},{28,31},{35,32}... | collective-permute-start | bytes 884744 | tf_op jit(solution)/shard_map/gather1_3/ppermute | solution.py:79
  87.6 21.0 %collective-permute-start.13 = (bf16[192,768]{1,0:T(8,128)(2,1)S(1)}, bf16[192,768]{1,0:T(8,128)(2,1)S(1)}, u32[]{:S(2)}, u32[]{:S(2)}) collective-permute-start(bf16[192,768]{1,0:T(8,128)(2,1)S(1)} %collective-permute-done.5.q0), channel_id=1, source_target_pairs={{2,3},{6,7},{10,11},{14,15},{18,19},{22,23},{26,27},{30,31},{33,32... | collective-permute-start | bytes 884744 | tf_op jit(solution)/shard_map/gather1_2/ppermute | solution.py:79
  88.9 20.4 %collective-permute-start.12 = (bf16[192,768]{1,0:T(8,128)(2,1)S(1)}, bf16[192,768]{1,0:T(8,128)(2,1)S(1)}, u32[]{:S(2)}, u32[]{:S(2)}) collective-permute-start(bf16[192,768]{1,0:T(8,128)(2,1)S(1)} %collective-permute-done.5.q0), channel_id=1, source_target_pairs={{1,3},{5,7},{9,11},{13,15},{17,19},{21,23},{25,27},{29,31},{34,32}... | collective-permute-start | bytes 884744 | tf_op jit(solution)/shard_map/gather1_1/ppermute | solution.py:79
  90.2 25.2 %collective-permute-start.10 = (bf16[192,768]{1,0:T(8,128)(2,1)S(1)}, bf16[192,768]{1,0:T(8,128)(2,1)}, u32[]{:S(2)}, u32[]{:S(2)}) collective-permute-start(bf16[192,768]{1,0:T(8,128)(2,1)S(1)} %collective-permute-done.5.q0), channel_id=1, source_target_pairs={{0,64},{1,65},{2,66},{3,67},{4,68},{5,69},{6,70},{7,71},{8,72},{9,... | collective-permute-start | bytes 884744 | tf_op jit(solution)/shard_map/cross_back/ppermute | solution.py:79
  92.2 14.5 %collective-permute-start.11 = (bf16[96,768]{1,0:T(8,128)(2,1)S(1)}, bf16[96,768]{1,0:T(8,128)(2,1)S(1)}, u32[]{:S(2)}, u32[]{:S(2)}) collective-permute-start(bf16[96,768]{1,0:T(8,128)(2,1)S(1)} %slice.3), channel_id=1, source_target_pairs={{0,448},{1,449},{2,450},{3,451},{4,452},{5,453},{6,454},{7,455},{8... | collective-permute-start | bytes 442376 | tf_op jit(solution)/shard_map/cross_ahead/ppermute | solution.py:79
  106.7 15.2 %collective-permute-start.15 = (bf16[384,768]{1,0:T(8,128)(2,1)}, bf16[384,768]{1,0:T(8,128)(2,1)}, u32[]{:S(2)}, u32[]{:S(2)}) collective-permute-start(bf16[384,768]{1,0:T(8,128)(2,1)} %collective-permute-done.6.refs_2_), channel_id=1, source_target_pairs={{0,480},{1,481},{2,482},{3,483},{4,484},{5,485},{6,486},{7,487},{8... | collective-permute-start | bytes 1769480 | tf_op jit(solution)/shard_map/own_outer2/ppermute | solution.py:79
  108.6 0.7 copy-start.14
  109.3 0.7 copy-start.16
  110.0 1.3 copy-start.11
  111.3 1.0 copy-start.15
  112.3 1.0 copy-start.17
  113.2 8.6 %copy-start.7 = (f32[384,768]{1,0:T(8,128)S(1)}, f32[384,768]{1,0:T(8,128)}, u32[]{:S(2)}) copy-start(f32[384,768]{1,0:T(8,128)} %copy-done.6) | copy-start | bytes 3538948
  113.2 8.6 %copy-start.9 = (f32[384,768]{1,0:T(8,128)S(1)}, f32[384,768]{1,0:T(8,128)}, u32[]{:S(2)}) copy-start(f32[384,768]{1,0:T(8,128)} %copy-done.8) | copy-start | bytes 3538948
  113.3 31.2 %collective-permute-start.22 = (bf16[768,768]{1,0:T(8,128)(2,1)S(1)}, bf16[768,768]{1,0:T(8,128)(2,1)}, u32[]{:S(2)}, u32[]{:S(2)}) collective-permute-start(bf16[768,768]{1,0:T(8,128)(2,1)S(1)} %merge1.1.refs_0_), channel_id=1, source_target_pairs={{0,32},{1,33},{2,34},{3,35},{4,36},{5,37},{6,38},{7,39},{8,40},{9,... | collective-permute-start | bytes 3538952 | tf_op jit(solution)/shard_map/sibling_hop1/ppermute | solution.py:79
  116.4 12.6 %collective-permute-start.18 = (bf16[288,768]{1,0:T(8,128)(2,1)S(1)}, bf16[288,768]{1,0:T(8,128)(2,1)S(1)}, u32[]{:S(2)}, u32[]{:S(2)}) collective-permute-start(bf16[288,768]{1,0:T(8,128)(2,1)S(1)} %pad_maximum_fusion.1.q0), channel_id=1, source_target_pairs={{0,3},{4,7},{8,11},{12,15},{16,19},{20,23},{24,27},{28,31},{35,32}... | collective-permute-start | bytes 1327112 | tf_op jit(solution)/shard_map/gather0_3/ppermute | solution.py:79
  117.7 11.3 %collective-permute-start.17 = (bf16[288,768]{1,0:T(8,128)(2,1)S(1)}, bf16[288,768]{1,0:T(8,128)(2,1)S(1)}, u32[]{:S(2)}, u32[]{:S(2)}) collective-permute-start(bf16[288,768]{1,0:T(8,128)(2,1)S(1)} %pad_maximum_fusion.1.q0), channel_id=1, source_target_pairs={{2,3},{6,7},{10,11},{14,15},{18,19},{22,23},{26,27},{30,31},{33,32... | collective-permute-start | bytes 1327112 | tf_op jit(solution)/shard_map/gather0_2/ppermute | solution.py:79
  119.0 14.9 %collective-permute-start.16 = (bf16[288,768]{1,0:T(8,128)(2,1)S(1)}, bf16[288,768]{1,0:T(8,128)(2,1)S(1)}, u32[]{:S(2)}, u32[]{:S(2)}) collective-permute-start(bf16[288,768]{1,0:T(8,128)(2,1)S(1)} %pad_maximum_fusion.1.q0), channel_id=1, source_target_pairs={{1,3},{5,7},{9,11},{13,15},{17,19},{21,23},{25,27},{29,31},{34,32}... | collective-permute-start | bytes 1327112 | tf_op jit(solution)/shard_map/gather0_1/ppermute | solution.py:79
  121.8 12.1 %copy-start.1 = (bf16[768,768]{1,0:T(8,128)(2,1)S(1)}, bf16[768,768]{1,0:T(8,128)(2,1)}, u32[]{:S(2)}) copy-start(bf16[768,768]{1,0:T(8,128)(2,1)} %copy-done) | copy-start | bytes 3538948
  125.4 9.7 %copy-start.2 = (f32[384,768]{1,0:T(8,128)}, f32[384,768]{1,0:T(8,128)S(1)}, u32[]{:S(2)}) copy-start(f32[384,768]{1,0:T(8,128)S(1)} %get-tuple-element.39.refs_3_) | copy-start | bytes 3538948
  125.4 9.7 %copy-start.4 = (f32[384,768]{1,0:T(8,128)}, f32[384,768]{1,0:T(8,128)S(1)}, u32[]{:S(2)}) copy-start(f32[384,768]{1,0:T(8,128)S(1)} %get-tuple-element.40.refs_4_) | copy-start | bytes 3538948
  125.4 19.1 %collective-permute-start.21 = (bf16[384,768]{1,0:T(8,128)(2,1)}, bf16[384,768]{1,0:T(8,128)(2,1)}, u32[]{:S(2)}, u32[]{:S(2)}) collective-permute-start(bf16[384,768]{1,0:T(8,128)(2,1)} %collective-permute-done.15.refs_1_), channel_id=1, source_target_pairs={{0,1},{1,2},{2,3},{4,5},{5,6},{6,7},{8,9},{9,10},{10,11},{12,13},{... | collective-permute-start | bytes 1769480 | tf_op jit(solution)/shard_map/wide_outer2/ppermute | solution.py:79
  135.1 0.8 copy-start.12
  135.9 16.8 %collective-permute-start.20 = (bf16[384,768]{1,0:T(8,128)(2,1)}, bf16[384,768]{1,0:T(8,128)(2,1)}, u32[]{:S(2)}, u32[]{:S(2)}) collective-permute-start(bf16[384,768]{1,0:T(8,128)(2,1)} %get-tuple-element.43), channel_id=1, source_target_pairs={{0,32},{1,33},{2,34},{3,35},{4,36},{5,37},{6,38},{7,39},{8,40},{9,... | collective-permute-start | bytes 1769480 | tf_op jit(solution)/shard_map/sibling_hop2/ppermute | solution.py:79
  142.4 10.3 %collective-permute-start.19 = (bf16[384,768]{1,0:T(8,128)(2,1)}, bf16[384,768]{1,0:T(8,128)(2,1)}, u32[]{:S(2)}, u32[]{:S(2)}) collective-permute-start(bf16[384,768]{1,0:T(8,128)(2,1)} %get-tuple-element.42.refs_1_), channel_id=1, source_target_pairs={{0,32},{1,33},{2,34},{3,35},{4,36},{5,37},{6,38},{7,39},{8,40},{9,... | collective-permute-start | bytes 1769480 | tf_op jit(solution)/shard_map/sibling_hop0/ppermute | solution.py:79
  144.5 1.3 copy-start.3
  145.8 1.3 copy-start.5
  147.0 1.1 copy-start.13

commit v4 on v3

--- a/solution.py
+++ b/solution.py
@@ -170,8 +170,8 @@
         jnp.where(mirrored == 2, spread1, jnp.where(mirrored == 1, spread2, cuts[3])),
     )
     crossed = send("cross", held, across)
-    pair0 = send(
-        "wide_pair0", jnp.concatenate([after(inner, held), outer], axis=0), to_next_wide
+    early = send(
+        "wide_early", jnp.concatenate([after(inner, held), outer, outer1, inner1], axis=0), to_next_wide
     )
     batch = row_lse.shape[0]
 
@@ -225,6 +225,8 @@
                 items = []
                 for ref, (_, places) in zip(refs, blocks):
                     for k, row in enumerate(places):
+                        if row is None:
+                            continue
                         items.append((ref[k * rows : (k + 1) * rows, :], row, row in (0, 8)))
                 before = None if start is None else start[...]
                 end[...] = add_terms(before, query[...], query_factor[:, :1], kf, s[0], items)
@@ -237,12 +239,8 @@
             (other, outer, near_factor, far_factor, key_factors, *arrays, *(sums or ())), weight,
         )
 
-    sums = terms("terms_own0", [(outer, [0]), (inner, [1]), (after(outer1, held), [2])], [(other, [8])], None, 100_000_000)
-    own1 = jnp.concatenate([outer1, after(inner1, *sums)], axis=0)
-    sib1 = send("sibling1", own1, to_sibling)
-    pair1 = send("wide_pair1", own1, to_next_wide)
-    sums = terms("terms_own1", [(inner1, [3])], [(sib1, [9, 10])], sums)
-    crossed = after(crossed, pair0, pair1, *sums)
+    sums = terms("terms_own0", [(outer, [0]), (inner, [1]), (after(outer1, held), [2]), (inner1, [3])], [(other, [8])], None, 100_000_000)
+    crossed = after(crossed, *sums)
 
     back = send("cross_back", crossed, to_previous_chip)
     ahead = send("cross_ahead", crossed[quarter:], to_next_chip)
@@ -254,11 +252,10 @@
         return [mine, q1, q2, q3]
 
     got1 = collect("gather1_", crossed)
-    far2 = send("own_outer2", after(outer1, ahead), to_next_chip_sibling)
-    hop_far2 = send("wide_outer2", far2, to_sibling_next_wide)
+    far2 = send("own_outer2", after(outer1, crossed), to_next_chip_sibling)
     got0 = collect("gather0_", after(jnp.concatenate([back, ahead], axis=0), *got1))
 
-    def merge1_kernel(edge, usual, q0, q1, q2, q3, out):
+    def merge1_kernel(edge, early, outer1, inner1, q0, q1, q2, q3, out):
         @pl.when(edge[0] == 1)
         def _():
             for place, source in enumerate((q0, q1, q2, q3)):
@@ -268,12 +265,41 @@
 
         @pl.when(edge[0] == 0)
         def _():
-            out[...] = usual[...]
-
-    hop1 = call("merge1", merge1_kernel, blocks(2), (at_edge,), (pair1, *got1))
-    hop_sib1 = send("sibling_hop1", hop1, to_sibling)
-    sums = terms("terms_hop1", [(hop1, [4, 5])], [(far2, [11])], sums)
-    got0 = [after(got0[0], far2, *sums), *got0[1:]]
+            out[: 2 * rows, :] = early[2 * rows :, :]
+
+        out[2 * rows : 3 * rows, :] = outer1[...]
+        out[3 * rows :, :] = inner1[...]
+
+    carried = call(
+        "merge1", merge1_kernel, blocks(4), (at_edge,), (early, after(outer1, back, ahead), inner1, *got1)
+    )
+    sib = send("sibling1", carried, to_sibling)
+    hop_far2 = send("wide_outer2", after(far2, carried), to_sibling_next_wide)
+    near_sum, far_sum = sums
+
+    def near_kernel(s, oth, nf, kf, keys, near_in, near):
+        near[...] = add_terms(
+            near_in[...], oth[...], nf[:, :1], kf, s[0],
+            [(keys[:rows, :], 4, False), (keys[rows : 2 * rows, :], 5, False)],
+        )
+
+    near_sum = call(
+        "terms_near1", near_kernel, total, (scale,),
+        (other, near_factor, key_factors, carried, near_sum), 100_000_000,
+    )
+
+    def far_kernel(s, out, ff, kf, keys, last, far_in, far):
+        far[...] = add_terms(
+            far_in[...], out[...], ff[:, :1], kf, s[0],
+            [(keys[k * rows : (k + 1) * rows, :], row, False) for k, row in enumerate((12, 13, 9, 10))]
+            + [(last[...], 11, False)],
+        )
+
+    far_sum = call(
+        "terms_far1", far_kernel, total, (scale,),
+        (outer, far_factor, key_factors, after(sib, near_sum), far2, far_sum),
+    )
+    got0 = [after(got0[0], far2, far_sum), *got0[1:]]
 
     def merge0_kernel(edge, usual, q0, q1, q2, q3, inner0, outer0, farthest):
         @pl.when(edge[0] == 1)
@@ -287,17 +313,23 @@
         @pl.when(edge[0] == 0)
         def _():
             inner0[...] = usual[:rows, :]
-            outer0[...] = usual[rows:, :]
-            farthest[...] = usual[rows:, :]
+            outer0[...] = usual[rows : 2 * rows, :]
+            farthest[...] = usual[:rows, :]
 
     hop_inner0, hop_outer0, hop_outer2 = call(
-        "merge0", merge0_kernel, [blocks(1)] * 3, (at_edge,), (pair0, *got0)
+        "merge0", merge0_kernel, [blocks(1)] * 3, (at_edge,), (early, *got0)
     )
     hop_sib0 = send("sibling_hop0", hop_inner0, to_sibling)
     hop_sib2 = send("sibling_hop2", hop_outer2, to_sibling)
-    sums = terms(
-        "terms_hop0", [(hop_outer0, [7]), (hop_inner0, [6])],
-        [(after(hop_sib1, hop_far2), [12, 13])], sums,
+    def third_kernel(s, oth, nf, kf, outer0, inner0, near_in, near):
+        near[...] = add_terms(
+            near_in[...], oth[...], nf[:, :1], kf, s[0],
+            [(outer0[...], 7, False), (inner0[...], 6, False)],
+        )
+
+    near_sum = call(
+        "terms_2", third_kernel, total, (scale,),
+        (other, near_factor, key_factors, hop_outer0, hop_inner0, near_sum),
     )
 
     def last_kernel(c, e, s, out, ff, kf, hs0, hs2, hf2, near_in, far_in, image_grad, caption_grad):
@@ -320,7 +352,7 @@
 
     image_grad, caption_grad = call(
         "terms_last", last_kernel, [total, total], (core_flag, sibling_at_edge, scale),
-        (outer, far_factor, key_factors, hop_sib0, hop_sib2, hop_far2, *sums),
+        (outer, far_factor, key_factors, hop_sib0, hop_sib2, hop_far2, near_sum, far_sum),
     )
     return image_grad, caption_grad
 

time: 159 us -> 145 us (0.912)
  waiting for transfers between devices: 47.7 us -> 20.3 us
  local copies, waits for them, and re-layouts: 14.6 us -> 25.8 us
  other arithmetic: 3.72 us -> 6.89 us
    ppermute x23 -> x21, waiting for transfers between devices: 47.7 us -> 20.3 us  [send(): return lax.ppermute(x, AXES, pairs(target))]
    another operation x17, local copies, waits for them, and re-layouts: 0.11 us -> 10.7 us  [on_device(): jnp.stack([own_outer, part(True, pal, wide), part(True, blk - 2 * sign, w...]
    ppermute x23 -> x21, starting transfers between devices: 68.5 us -> 67.1 us  [send(): return lax.ppermute(x, AXES, pairs(target))]
    unnamed x37 -> x56, local copies, waits for them, and re-layouts: 14.2 us -> 14 us
  transfers between devices with their start and end apart: 23 -> 21, of which waited for: 7 -> 4; matrix products, arithmetic and copies ran while one was open for 2% -> 12% of each run, Pallas kernels for 10% -> 12%
where the time goes in v4:
time: 145 us; the launch traced here: 143 us
  starting transfers between devices  67.1 us (46%)
  local copies, waits for them, and re-layouts  25.8 us (18%)
  Pallas kernels  21.2 us (15%)
  waiting for transfers between devices  20.3 us (14%)
  other arithmetic  6.89 us (5%)
  between operations  2.16 us (1%)
    ppermute x21, starting transfers between devices, send(): return lax.ppermute(x, AXES, pairs(target))  67.1 us
    pallas_call x8, Pallas kernels, call(): pl.pallas_call(kernel, out_shape=out_shape, in_specs=[scalars() for _ in...  21.2 us
    ppermute x21, waiting for transfers between devices, send(): return lax.ppermute(x, AXES, pairs(target))  20.3 us
    unnamed x56, local copies, waits for them, and re-layouts  14 us
    another operation x17, local copies, waits for them, and re-layouts, on_device(): jnp.stack([own_outer, part(True, pal, wide), part(True, blk - 2 * sign, w...  10.7 us
  transfers between devices with their start and end apart: 21, of which 4 were waited for; matrix products, arithmetic and copies ran while one was open for 12% of the time, Pallas kernels for 12%

profile of v4, /device:TPU:1, one launch (start us, length us, event | category | flops | bytes accessed | tf_op | source)
XLA Modules:
  0.0 143.5 jit_solution(3086338044796937666)
XLA Ops:
  0.6 1.3 broadcast_select_fusion
  2.0 8.8 %collective-permute-start = (bf16[384,768]{1,0:T(8,128)(2,1)S(1)}, bf16[384,768]{1,0:T(8,128)(2,1)S(1)}, u32[]{:S(2)}, u32[]{:S(2)}) collective-permute-start(bf16[384,768]{1,0:T(8,128)(2,1)S(1)} %get-tuple-element.58.oth.refs_4_), channel_id=1, source_target_pairs={{0,32},{1,33},{2,34},{3,35},{4,36},{5,37},{6,38},{7,39},{8,40},{9,... | collective-permute-start | bytes 1769480 | tf_op jit(solution)/shard_map/swap/ppermute | solution.py:79
  10.8 7.4 %collective-permute-start.5 = (bf16[384,768]{1,0:T(8,128)(2,1)S(1)}, bf16[384,768]{1,0:T(8,128)(2,1)S(1)}, u32[]{:S(2)}, u32[]{:S(2)}) collective-permute-start(bf16[384,768]{1,0:T(8,128)(2,1)S(1)} %get-tuple-element.58.oth.refs_4_), channel_id=1, source_target_pairs={{0,96},{1,97},{2,98},{3,99},{4,100},{5,101},{6,102},{7,103},{8,104... | collective-permute-start | bytes 1769480 | tf_op jit(solution)/shard_map/own_inner1/ppermute | solution.py:79
  18.2 1.9 %collective-permute-start.4 = (bf16[384,768]{1,0:T(8,128)(2,1)S(1)}, bf16[384,768]{1,0:T(8,128)(2,1)S(1)}, u32[]{:S(2)}, u32[]{:S(2)}) collective-permute-start(bf16[384,768]{1,0:T(8,128)(2,1)S(1)} %get-tuple-element.59.outer.out.refs_0_), channel_id=1, source_target_pairs={{0,448},{1,449},{2,450},{3,451},{4,452},{5,453},{6,454},{7,455},{8... | collective-permute-start | bytes 1769480 | tf_op jit(solution)/shard_map/own_outer1/ppermute | solution.py:79
  21.1 1.0 cut.1
  22.1 1.3 collective-permute-start.1
  23.4 1.4 collective-permute-start.2
  24.8 1.4 collective-permute-start.3
  26.2 1.1 exponential_multiply_fusion.1
  27.3 0.6 stack.53
  27.9 0.6 stack.54
  28.5 0.6 stack.55
  30.8 0.6 stack.59
  31.4 0.6 stack.60
  31.9 0.6 stack.61
  32.5 0.6 stack.62
  33.7 0.6 stack.64
  34.3 0.6 stack.65
  34.8 0.6 stack.66
  35.4 2.6 %stack.67 = f32[16,384]{1,0:T(8,128)} concatenate(f32[1,384]{1,0:T(1,128)S(1)} %stack.51, f32[1,384]{1,0:T(1,128)S(1)} %stack.52, f32[1,384]{1,0:T(1,128)} %stack.53, f32[1,384]{1,0:T(1,128)} %stack.54, f32[1,384]{1,0:T(1,128)} %stack.55, f32[1,384]{1,0:T(1,128)} %stack.56, f32[1,384]{1,0:T(1,128)} %stack.57, f32[1,384]{1,0:T(1,128)} %stack.58, f32[1,384]{1,0:T(1,128)} %stack.59, ...), dimensions={0} | concatenate | bytes 49152 | tf_op jit(solution)/shard_map/stack | solution.py:192
  38.1 0.7 exponential_multiply_fusion.kf
  38.9 1.0 select_select_fusion
  39.9 5.4 %collective-permute-start.7 = (bf16[192,768]{1,0:T(8,128)(2,1)S(1)}, bf16[192,768]{1,0:T(8,128)(2,1)}, u32[]{:S(2)}, u32[]{:S(2)}) collective-permute-start(bf16[192,768]{1,0:T(8,128)(2,1)S(1)} %select_select_fusion), channel_id=1, source_target_pairs={{0,476},{1,477},{2,478},{3,479},{4,448},{5,449},{6,450},{7,451},{8... | collective-permute-start | bytes 884744 | tf_op jit(solution)/shard_map/cross/ppermute | solution.py:79
  45.4 1.6 %pad_maximum_fusion = bf16[1536,768]{1,0:T(8,128)(2,1)} fusion(bf16[384,768]{1,0:T(8,128)(2,1)S(1)} %collective-permute-done.5.refs_3_.inner1, bf16[384,768]{1,0:T(8,128)(2,1)S(1)} %collective-permute-done.4.refs_2_.outer1, bf16[384,768]{1,0:T(8,128)(2,1)S(1)} %get-tuple-element.59.outer.out.refs_0_, bf16[384,768]{1,0:T(8,128)(2,1)S(1)} %collective-permute-done.inner.refs_1_), kind=kLoop, calls=%fused_computation | loop fusion | flops 9437184 | bytes 4718592 | tf_op jit(solution)/shard_map/concatenate | solution.py:174
  46.9 0.8 copy-done.2
  47.8 3.4 %collective-permute-start.6 = (bf16[1536,768]{1,0:T(8,128)(2,1)}, bf16[1536,768]{1,0:T(8,128)(2,1)S(1)}, u32[]{:S(2)}, u32[]{:S(2)}) collective-permute-start(bf16[1536,768]{1,0:T(8,128)(2,1)} %pad_maximum_fusion), channel_id=1, source_target_pairs={{1,0},{2,1},{3,2},{5,4},{6,5},{7,6},{9,8},{10,9},{11,10},{13,12},{... | collective-permute-start | bytes 7077896 | tf_op jit(solution)/shard_map/wide_early/ppermute | solution.py:79
  51.4 1.1 copy-done.3
  52.5 1.1 copy-done.6
  53.5 1.1 copy-done.10
  54.6 3.6 %terms_own0.1 = (f32[384,768]{1,0:T(8,128)S(1)}, f32[384,768]{1,0:T(8,128)S(1)}) custom-call(f32[1]{0:T(128)} %bitcast.4.s, bf16[384,768]{1,0:T(8,128)(2,1)S(1)} %copy-done.6, bf16[384,768]{1,0:T(8,128)(2,1)S(1)} %get-tuple-element.59.outer.out.refs_0_, f32[384,128]{1,0:T(8,128)S(1)} %broadcast_in_dim.5.nf, f32[384,128]{1,0:T(8,128)S(1)} %broadcast_in_dim.4.ff, ...), custom_call_target="tpu_custom_call" | custom-call | flops 99999997952 | bytes 1000 | tf_op jit(solution)/shard_map/terms_own0/pallas_call | solution.py:94
  58.2 1.0 copy-done.16
  59.2 1.0 copy-done.26
  60.2 14.6 %collective-permute-done.7.q0 = bf16[192,768]{1,0:T(8,128)(2,1)} collective-permute-done((bf16[192,768]{1,0:T(8,128)(2,1)S(1)}, bf16[192,768]{1,0:T(8,128)(2,1)}, u32[]{:S(2)}, u32[]{:S(2)}) %collective-permute-start.7) | collective-permute-done | bytes 294944 | tf_op jit(solution)/shard_map/cross/ppermute | solution.py:79
  74.8 0.9 slice.3
  75.7 2.6 %collective-permute-start.9 = (bf16[96,768]{1,0:T(8,128)(2,1)S(1)}, bf16[96,768]{1,0:T(8,128)(2,1)}, u32[]{:S(2)}, u32[]{:S(2)}) collective-permute-start(bf16[96,768]{1,0:T(8,128)(2,1)S(1)} %slice.3), channel_id=1, source_target_pairs={{0,448},{1,449},{2,450},{3,451},{4,452},{5,453},{6,454},{7,455},{8... | collective-permute-start | bytes 442376 | tf_op jit(solution)/shard_map/cross_ahead/ppermute | solution.py:79
  78.3 9.3 %collective-permute-start.8 = (bf16[192,768]{1,0:T(8,128)(2,1)}, bf16[192,768]{1,0:T(8,128)(2,1)}, u32[]{:S(2)}, u32[]{:S(2)}) collective-permute-start(bf16[192,768]{1,0:T(8,128)(2,1)} %collective-permute-done.7.q0), channel_id=1, source_target_pairs={{0,64},{1,65},{2,66},{3,67},{4,68},{5,69},{6,70},{7,71},{8,72},{9,... | collective-permute-start | bytes 884744 | tf_op jit(solution)/shard_map/cross_back/ppermute | solution.py:79
  87.6 1.3 collective-permute-start.10
  88.9 1.3 collective-permute-start.11
  90.2 1.3 collective-permute-start.12
  91.6 1.9 %collective-permute-start.13 = (bf16[384,768]{1,0:T(8,128)(2,1)S(1)}, bf16[384,768]{1,0:T(8,128)(2,1)}, u32[]{:S(2)}, u32[]{:S(2)}) collective-permute-start(bf16[384,768]{1,0:T(8,128)(2,1)S(1)} %collective-permute-done.4.refs_2_.outer1), channel_id=1, source_target_pairs={{0,480},{1,481},{2,482},{3,483},{4,484},{5,485},{6,486},{7,487},{8... | collective-permute-start | bytes 1769480 | tf_op jit(solution)/shard_map/own_outer2/ppermute | solution.py:79
  93.5 1.1 pad_maximum_fusion.1.q0
  94.6 2.5 %collective-permute-done.10.q1 = bf16[192,768]{1,0:T(8,128)(2,1)} collective-permute-done((bf16[192,768]{1,0:T(8,128)(2,1)}, bf16[192,768]{1,0:T(8,128)(2,1)}, u32[]{:S(2)}, u32[]{:S(2)}) %collective-permute-start.10) | collective-permute-done | bytes 294944 | tf_op jit(solution)/shard_map/gather1_1/ppermute | solution.py:79
  97.0 3.1 %collective-permute-done.12.q3 = bf16[192,768]{1,0:T(8,128)(2,1)} collective-permute-done((bf16[192,768]{1,0:T(8,128)(2,1)}, bf16[192,768]{1,0:T(8,128)(2,1)}, u32[]{:S(2)}, u32[]{:S(2)}) %collective-permute-start.12) | collective-permute-done | bytes 294944 | tf_op jit(solution)/shard_map/gather1_3/ppermute | solution.py:79
  100.1 1.3 collective-permute-start.15
  101.4 1.3 collective-permute-start.16
  102.7 1.3 collective-permute-start.17
  104.0 1.1 copy-done.4
  105.1 1.5 %merge1.1.keys = bf16[1536,768]{1,0:T(8,128)(2,1)S(1)} custom-call(s32[1]{0:T(128)} %bitcast.3.edge, bf16[1536,768]{1,0:T(8,128)(2,1)S(1)} %collective-permute-done.6.early.usual, bf16[384,768]{1,0:T(8,128)(2,1)S(1)} %collective-permute-done.4.refs_2_.outer1, bf16[384,768]{1,0:T(8,128)(2,1)S(1)} %copy-done.4, bf16[192,768]{1,0:T(8,128)(2,1)} %collective-permute-done.7.q0, ...), custom_call_target="tpu_custom_call" | custom-call | flops 1000 | bytes 1000 | tf_op jit(solution)/shard_map/merge1/pallas_call | solution.py:94
  106.6 8.2 %collective-permute-start.14 = (bf16[1536,768]{1,0:T(8,128)(2,1)S(1)}, bf16[1536,768]{1,0:T(8,128)(2,1)S(1)}, u32[]{:S(2)}, u32[]{:S(2)}) collective-permute-start(bf16[1536,768]{1,0:T(8,128)(2,1)S(1)} %merge1.1.keys), channel_id=1, source_target_pairs={{0,32},{1,33},{2,34},{3,35},{4,36},{5,37},{6,38},{7,39},{8,40},{9,... | collective-permute-start | bytes 7077896 | tf_op jit(solution)/shard_map/sibling1/ppermute | solution.py:79
  114.9 1.7 %terms_near1.1.near_in = f32[384,768]{1,0:T(8,128)S(1)} custom-call(f32[1]{0:T(128)} %bitcast.5.s, bf16[384,768]{1,0:T(8,128)(2,1)S(1)} %copy-done.7, f32[384,128]{1,0:T(8,128)S(1)} %copy-done.19, f32[16,384]{1,0:T(8,128)S(1)} %copy-done.24, bf16[1536,768]{1,0:T(8,128)(2,1)S(1)} %merge1.1.keys, f32[384,768]{1,0:T(8,128)S(1)} %copy-done.27), custom_call_target="tpu_custom_call" | custom-call | flops 99999997952 | bytes 1000 | tf_op jit(solution)/shard_map/terms_near1/pallas_call | solution.py:94
  116.6 1.0 copy-done.14
  117.6 1.3 collective-permute-start.20
  118.9 5.0 %terms_far1.1.far_in = f32[384,768]{1,0:T(8,128)S(1)} custom-call(f32[1]{0:T(128)} %bitcast.6.s, bf16[384,768]{1,0:T(8,128)(2,1)S(1)} %get-tuple-element.59.outer.out.refs_0_, f32[384,128]{1,0:T(8,128)S(1)} %copy-done.12, f32[16,384]{1,0:T(8,128)S(1)} %copy-done.24, bf16[1536,768]{1,0:T(8,128)(2,1)S(1)} %collective-permute-done.14.keys, ...), custom_call_target="tpu_custom_call" | custom-call | flops 1000 | bytes 1000 | tf_op jit(solution)/shard_map/terms_far1/pallas_call | solution.py:94
  123.9 1.0 copy-done
  125.0 1.2 merge0.1
  126.1 0.8 copy-done.21
  127.0 3.1 %collective-permute-start.18 = (bf16[384,768]{1,0:T(8,128)(2,1)}, bf16[384,768]{1,0:T(8,128)(2,1)S(1)}, u32[]{:S(2)}, u32[]{:S(2)}) collective-permute-start(bf16[384,768]{1,0:T(8,128)(2,1)} %get-tuple-element.34.inner0), channel_id=1, source_target_pairs={{0,32},{1,33},{2,34},{3,35},{4,36},{5,37},{6,38},{7,39},{8,40},{9,... | collective-permute-start | bytes 1769480 | tf_op jit(solution)/shard_map/sibling_hop0/ppermute | solution.py:79
  130.0 2.1 %collective-permute-start.19 = (bf16[384,768]{1,0:T(8,128)(2,1)}, bf16[384,768]{1,0:T(8,128)(2,1)}, u32[]{:S(2)}, u32[]{:S(2)}) collective-permute-start(bf16[384,768]{1,0:T(8,128)(2,1)} %get-tuple-element.35), channel_id=1, source_target_pairs={{0,32},{1,33},{2,34},{3,35},{4,36},{5,37},{6,38},{7,39},{8,40},{9,... | collective-permute-start | bytes 1769480 | tf_op jit(solution)/shard_map/sibling_hop2/ppermute | solution.py:79
  132.2 1.3 copy-done.15
  133.4 0.9 copy-done.20
  134.4 1.1 copy-done.22
  135.4 0.7 copy-done.25
  136.2 2.7 %terms_2.1.near_in = f32[384,768]{1,0:T(8,128)S(1)} custom-call(f32[1]{0:T(128)} %bitcast.7.s, bf16[384,768]{1,0:T(8,128)(2,1)S(1)} %copy-done.8, f32[384,128]{1,0:T(8,128)S(1)} %copy-done.20, f32[16,384]{1,0:T(8,128)S(1)} %copy-done.25, bf16[384,768]{1,0:T(8,128)(2,1)S(1)} %copy-done.22, bf16[384,768]{1,0:T(8,128)(2,1)} %get-tuple-element.34.inner0, ...), custom_call_target="tpu_custom_call" | custom-call | flops 1000 | bytes 1000 | tf_op jit(solution)/shard_map/terms_2/pallas_call | solution.py:94
  138.9 4.5 %terms_last.1 = (f32[384,768]{1,0:T(8,128)}, f32[384,768]{1,0:T(8,128)}) custom-call(s32[1]{0:T(128)} %bitcast.c, s32[1]{0:T(128)} %bitcast.1.e, f32[1]{0:T(128)} %bitcast.8.s, bf16[384,768]{1,0:T(8,128)(2,1)S(1)} %get-tuple-element.59.outer.out.refs_0_, f32[384,128]{1,0:T(8,128)S(1)} %copy-done.13, f32[16,384]{1,0:T(8,128)S(1)} %copy-done.25, ...), custom_call_target="tpu_custom_call" | custom-call | flops 1000 | bytes 1000 | tf_op jit(solution)/shard_map/terms_last/pallas_call | solution.py:94
  (68 shorter events, 2.7 us)
Async XLA Ops:
  2.0 43.4 %copy-start.5 = (bf16[384,768]{1,0:T(8,128)(2,1)}, bf16[384,768]{1,0:T(8,128)(2,1)S(1)}, u32[]{:S(2)}) copy-start(bf16[384,768]{1,0:T(8,128)(2,1)S(1)} %get-tuple-element.58.oth.refs_4_) | copy-start | bytes 1769476
  2.0 19.1 %collective-permute-start = (bf16[384,768]{1,0:T(8,128)(2,1)S(1)}, bf16[384,768]{1,0:T(8,128)(2,1)S(1)}, u32[]{:S(2)}, u32[]{:S(2)}) collective-permute-start(bf16[384,768]{1,0:T(8,128)(2,1)S(1)} %get-tuple-element.58.oth.refs_4_), channel_id=1, source_target_pairs={{0,32},{1,33},{2,34},{3,35},{4,36},{5,37},{6,38},{7,39},{8,40},{9,... | collective-permute-start | bytes 1769480 | tf_op jit(solution)/shard_map/swap/ppermute | solution.py:79
  10.8 34.5 %collective-permute-start.5 = (bf16[384,768]{1,0:T(8,128)(2,1)S(1)}, bf16[384,768]{1,0:T(8,128)(2,1)S(1)}, u32[]{:S(2)}, u32[]{:S(2)}) collective-permute-start(bf16[384,768]{1,0:T(8,128)(2,1)S(1)} %get-tuple-element.58.oth.refs_4_), channel_id=1, source_target_pairs={{0,96},{1,97},{2,98},{3,99},{4,100},{5,101},{6,102},{7,103},{8,104... | collective-permute-start | bytes 1769480 | tf_op jit(solution)/shard_map/own_inner1/ppermute | solution.py:79
  18.2 27.1 %collective-permute-start.4 = (bf16[384,768]{1,0:T(8,128)(2,1)S(1)}, bf16[384,768]{1,0:T(8,128)(2,1)S(1)}, u32[]{:S(2)}, u32[]{:S(2)}) collective-permute-start(bf16[384,768]{1,0:T(8,128)(2,1)S(1)} %get-tuple-element.59.outer.out.refs_0_), channel_id=1, source_target_pairs={{0,448},{1,449},{2,450},{3,451},{4,452},{5,453},{6,454},{7,455},{8... | collective-permute-start | bytes 1769480 | tf_op jit(solution)/shard_map/own_outer1/ppermute | solution.py:79
  21.1 24.3 %copy-start.9 = (bf16[384,768]{1,0:T(8,128)(2,1)}, bf16[384,768]{1,0:T(8,128)(2,1)S(1)}, u32[]{:S(2)}) copy-start(bf16[384,768]{1,0:T(8,128)(2,1)S(1)} %collective-permute-done.inner.refs_1_) | copy-start | bytes 1769476
  22.1 16.7 %collective-permute-start.1 = (bf16[192,768]{1,0:T(8,128)(2,1)}, bf16[192,768]{1,0:T(8,128)(2,1)}, u32[]{:S(2)}, u32[]{:S(2)}) collective-permute-start(bf16[192,768]{1,0:T(8,128)(2,1)} %get-tuple-element.20), channel_id=1, source_target_pairs={{0,3},{4,7},{8,11},{12,15},{16,19},{20,23},{24,27},{28,31},{35,32}... | collective-permute-start | bytes 884744 | tf_op jit(solution)/shard_map/spread0/ppermute | solution.py:79
  23.4 15.4 %collective-permute-start.2 = (bf16[192,768]{1,0:T(8,128)(2,1)}, bf16[192,768]{1,0:T(8,128)(2,1)}, u32[]{:S(2)}, u32[]{:S(2)}) collective-permute-start(bf16[192,768]{1,0:T(8,128)(2,1)} %get-tuple-element.21), channel_id=1, source_target_pairs={{0,1},{4,5},{8,9},{12,13},{16,17},{20,21},{24,25},{28,29},{35,34},... | collective-permute-start | bytes 884744 | tf_op jit(solution)/shard_map/spread1/ppermute | solution.py:79
  24.8 14.1 %collective-permute-start.3 = (bf16[192,768]{1,0:T(8,128)(2,1)S(1)}, bf16[192,768]{1,0:T(8,128)(2,1)}, u32[]{:S(2)}, u32[]{:S(2)}) collective-permute-start(bf16[192,768]{1,0:T(8,128)(2,1)S(1)} %get-tuple-element.22), channel_id=1, source_target_pairs={{0,2},{4,6},{8,10},{12,14},{16,18},{20,22},{24,26},{28,30},{35,33}... | collective-permute-start | bytes 884744 | tf_op jit(solution)/shard_map/spread2/ppermute | solution.py:79
  38.8 12.6 %copy-start.23 = (f32[16,384]{1,0:T(8,128)}, f32[16,384]{1,0:T(8,128)S(1)}, u32[]{:S(2)}) copy-start(f32[16,384]{1,0:T(8,128)S(1)} %exponential_multiply_fusion.kf) | copy-start | bytes 73732
  39.9 34.9 %collective-permute-start.7 = (bf16[192,768]{1,0:T(8,128)(2,1)S(1)}, bf16[192,768]{1,0:T(8,128)(2,1)}, u32[]{:S(2)}, u32[]{:S(2)}) collective-permute-start(bf16[192,768]{1,0:T(8,128)(2,1)S(1)} %select_select_fusion), channel_id=1, source_target_pairs={{0,476},{1,477},{2,478},{3,479},{4,448},{5,449},{6,450},{7,451},{8... | collective-permute-start | bytes 884744 | tf_op jit(solution)/shard_map/cross/ppermute | solution.py:79
  46.9 0.8 copy-start.2
  47.8 56.2 %collective-permute-start.6 = (bf16[1536,768]{1,0:T(8,128)(2,1)}, bf16[1536,768]{1,0:T(8,128)(2,1)S(1)}, u32[]{:S(2)}, u32[]{:S(2)}) collective-permute-start(bf16[1536,768]{1,0:T(8,128)(2,1)} %pad_maximum_fusion), channel_id=1, source_target_pairs={{1,0},{2,1},{3,2},{5,4},{6,5},{7,6},{9,8},{10,9},{11,10},{13,12},{... | collective-permute-start | bytes 7077896 | tf_op jit(solution)/shard_map/wide_early/ppermute | solution.py:79
  51.3 6.9 %copy-start.11 = (f32[384,128]{1,0:T(8,128)}, f32[384,128]{1,0:T(8,128)S(1)}, u32[]{:S(2)}) copy-start(f32[384,128]{1,0:T(8,128)S(1)} %broadcast_in_dim.4.ff) | copy-start | bytes 589828
  51.4 1.1 copy-start.3
  52.5 1.1 copy-start.6
  53.5 1.1 copy-start.10
  54.6 3.6 %copy-start.18 = (f32[384,128]{1,0:T(8,128)}, f32[384,128]{1,0:T(8,128)S(1)}, u32[]{:S(2)}) copy-start(f32[384,128]{1,0:T(8,128)S(1)} %broadcast_in_dim.5.nf) | copy-start | bytes 589828
  58.2 1.0 copy-start.16
  59.2 1.0 copy-start.26
  75.7 14.5 %collective-permute-start.9 = (bf16[96,768]{1,0:T(8,128)(2,1)S(1)}, bf16[96,768]{1,0:T(8,128)(2,1)}, u32[]{:S(2)}, u32[]{:S(2)}) collective-permute-start(bf16[96,768]{1,0:T(8,128)(2,1)S(1)} %slice.3), channel_id=1, source_target_pairs={{0,448},{1,449},{2,450},{3,451},{4,452},{5,453},{6,454},{7,455},{8... | collective-permute-start | bytes 442376 | tf_op jit(solution)/shard_map/cross_ahead/ppermute | solution.py:79
  78.3 13.3 %collective-permute-start.8 = (bf16[192,768]{1,0:T(8,128)(2,1)}, bf16[192,768]{1,0:T(8,128)(2,1)}, u32[]{:S(2)}, u32[]{:S(2)}) collective-permute-start(bf16[192,768]{1,0:T(8,128)(2,1)} %collective-permute-done.7.q0), channel_id=1, source_target_pairs={{0,64},{1,65},{2,66},{3,67},{4,68},{5,69},{6,70},{7,71},{8,72},{9,... | collective-permute-start | bytes 884744 | tf_op jit(solution)/shard_map/cross_back/ppermute | solution.py:79
  87.6 9.4 %collective-permute-start.10 = (bf16[192,768]{1,0:T(8,128)(2,1)}, bf16[192,768]{1,0:T(8,128)(2,1)}, u32[]{:S(2)}, u32[]{:S(2)}) collective-permute-start(bf16[192,768]{1,0:T(8,128)(2,1)} %collective-permute-done.7.q0), channel_id=1, source_target_pairs={{1,3},{5,7},{9,11},{13,15},{17,19},{21,23},{25,27},{29,31},{34,32}... | collective-permute-start | bytes 884744 | tf_op jit(solution)/shard_map/gather1_1/ppermute | solution.py:79
  88.9 8.1 %collective-permute-start.11 = (bf16[192,768]{1,0:T(8,128)(2,1)}, bf16[192,768]{1,0:T(8,128)(2,1)}, u32[]{:S(2)}, u32[]{:S(2)}) collective-permute-start(bf16[192,768]{1,0:T(8,128)(2,1)} %collective-permute-done.7.q0), channel_id=1, source_target_pairs={{2,3},{6,7},{10,11},{14,15},{18,19},{22,23},{26,27},{30,31},{33,32... | collective-permute-start | bytes 884744 | tf_op jit(solution)/shard_map/gather1_2/ppermute | solution.py:79
  90.2 9.9 %collective-permute-start.12 = (bf16[192,768]{1,0:T(8,128)(2,1)}, bf16[192,768]{1,0:T(8,128)(2,1)}, u32[]{:S(2)}, u32[]{:S(2)}) collective-permute-start(bf16[192,768]{1,0:T(8,128)(2,1)} %collective-permute-done.7.q0), channel_id=1, source_target_pairs={{0,3},{4,7},{8,11},{12,15},{16,19},{20,23},{24,27},{28,31},{35,32}... | collective-permute-start | bytes 884744 | tf_op jit(solution)/shard_map/gather1_3/ppermute | solution.py:79
  91.6 26.0 %collective-permute-start.13 = (bf16[384,768]{1,0:T(8,128)(2,1)S(1)}, bf16[384,768]{1,0:T(8,128)(2,1)}, u32[]{:S(2)}, u32[]{:S(2)}) collective-permute-start(bf16[384,768]{1,0:T(8,128)(2,1)S(1)} %collective-permute-done.4.refs_2_.outer1), channel_id=1, source_target_pairs={{0,480},{1,481},{2,482},{3,483},{4,484},{5,485},{6,486},{7,487},{8... | collective-permute-start | bytes 1769480 | tf_op jit(solution)/shard_map/own_outer2/ppermute | solution.py:79
  100.1 24.8 %collective-permute-start.15 = (bf16[288,768]{1,0:T(8,128)(2,1)S(1)}, bf16[288,768]{1,0:T(8,128)(2,1)S(1)}, u32[]{:S(2)}, u32[]{:S(2)}) collective-permute-start(bf16[288,768]{1,0:T(8,128)(2,1)S(1)} %pad_maximum_fusion.1.q0), channel_id=1, source_target_pairs={{1,3},{5,7},{9,11},{13,15},{17,19},{21,23},{25,27},{29,31},{34,32}... | collective-permute-start | bytes 1327112 | tf_op jit(solution)/shard_map/gather0_1/ppermute | solution.py:79
  101.4 23.6 %collective-permute-start.16 = (bf16[288,768]{1,0:T(8,128)(2,1)S(1)}, bf16[288,768]{1,0:T(8,128)(2,1)S(1)}, u32[]{:S(2)}, u32[]{:S(2)}) collective-permute-start(bf16[288,768]{1,0:T(8,128)(2,1)S(1)} %pad_maximum_fusion.1.q0), channel_id=1, source_target_pairs={{2,3},{6,7},{10,11},{14,15},{18,19},{22,23},{26,27},{30,31},{33,32... | collective-permute-start | bytes 1327112 | tf_op jit(solution)/shard_map/gather0_2/ppermute | solution.py:79
  102.7 22.3 %collective-permute-start.17 = (bf16[288,768]{1,0:T(8,128)(2,1)S(1)}, bf16[288,768]{1,0:T(8,128)(2,1)S(1)}, u32[]{:S(2)}, u32[]{:S(2)}) collective-permute-start(bf16[288,768]{1,0:T(8,128)(2,1)S(1)} %pad_maximum_fusion.1.q0), channel_id=1, source_target_pairs={{0,3},{4,7},{8,11},{12,15},{16,19},{20,23},{24,27},{28,31},{35,32}... | collective-permute-start | bytes 1327112 | tf_op jit(solution)/shard_map/gather0_3/ppermute | solution.py:79
  104.0 1.1 copy-start.4
  105.1 9.7 %copy-start.7 = (bf16[384,768]{1,0:T(8,128)(2,1)S(1)}, bf16[384,768]{1,0:T(8,128)(2,1)}, u32[]{:S(2)}) copy-start(bf16[384,768]{1,0:T(8,128)(2,1)} %copy-done.5) | copy-start | bytes 1769476
  105.1 9.7 %copy-start.19 = (f32[384,128]{1,0:T(8,128)S(1)}, f32[384,128]{1,0:T(8,128)}, u32[]{:S(2)}) copy-start(f32[384,128]{1,0:T(8,128)} %copy-done.18) | copy-start | bytes 589828
  105.1 9.7 %copy-start.24 = (f32[16,384]{1,0:T(8,128)S(1)}, f32[16,384]{1,0:T(8,128)}, u32[]{:S(2)}) copy-start(f32[16,384]{1,0:T(8,128)} %copy-done.23) | copy-start | bytes 73732
  105.1 9.7 %copy-start.27 = (f32[384,768]{1,0:T(8,128)S(1)}, f32[384,768]{1,0:T(8,128)}, u32[]{:S(2)}) copy-start(f32[384,768]{1,0:T(8,128)} %copy-done.26) | copy-start | bytes 3538948
  106.6 12.3 %collective-permute-start.14 = (bf16[1536,768]{1,0:T(8,128)(2,1)S(1)}, bf16[1536,768]{1,0:T(8,128)(2,1)S(1)}, u32[]{:S(2)}, u32[]{:S(2)}) collective-permute-start(bf16[1536,768]{1,0:T(8,128)(2,1)S(1)} %merge1.1.keys), channel_id=1, source_target_pairs={{0,32},{1,33},{2,34},{3,35},{4,36},{5,37},{6,38},{7,39},{8,40},{9,... | collective-permute-start | bytes 7077896 | tf_op jit(solution)/shard_map/sibling1/ppermute | solution.py:79
  114.8 4.1 %copy-start.12 = (f32[384,128]{1,0:T(8,128)S(1)}, f32[384,128]{1,0:T(8,128)}, u32[]{:S(2)}) copy-start(f32[384,128]{1,0:T(8,128)} %copy-done.11) | copy-start | bytes 589828
  114.8 4.1 %copy-start.17 = (f32[384,768]{1,0:T(8,128)S(1)}, f32[384,768]{1,0:T(8,128)}, u32[]{:S(2)}) copy-start(f32[384,768]{1,0:T(8,128)} %copy-done.16) | copy-start | bytes 3538948
  116.6 1.0 copy-start.14
  117.6 21.3 %collective-permute-start.20 = (bf16[384,768]{1,0:T(8,128)(2,1)}, bf16[384,768]{1,0:T(8,128)(2,1)}, u32[]{:S(2)}, u32[]{:S(2)}) collective-permute-start(bf16[384,768]{1,0:T(8,128)(2,1)} %collective-permute-done.13.last), channel_id=1, source_target_pairs={{0,1},{1,2},{2,3},{4,5},{5,6},{6,7},{8,9},{9,10},{10,11},{12,13},{... | collective-permute-start | bytes 1769480 | tf_op jit(solution)/shard_map/wide_outer2/ppermute | solution.py:79
  123.9 1.0 copy-start
  124.9 7.2 %copy-start.8 = (bf16[384,768]{1,0:T(8,128)(2,1)S(1)}, bf16[384,768]{1,0:T(8,128)(2,1)}, u32[]{:S(2)}) copy-start(bf16[384,768]{1,0:T(8,128)(2,1)} %copy-done.5) | copy-start | bytes 1769476
  126.1 0.8 copy-start.21
  127.0 12.0 %copy-start.1 = (f32[384,768]{1,0:T(8,128)S(1)}, f32[384,768]{1,0:T(8,128)}, u32[]{:S(2)}) copy-start(f32[384,768]{1,0:T(8,128)} %copy-done) | copy-start | bytes 3538948
  127.0 12.0 %copy-start.13 = (f32[384,128]{1,0:T(8,128)S(1)}, f32[384,128]{1,0:T(8,128)}, u32[]{:S(2)}) copy-start(f32[384,128]{1,0:T(8,128)} %copy-done.11) | copy-start | bytes 589828
  127.0 11.9 %collective-permute-start.18 = (bf16[384,768]{1,0:T(8,128)(2,1)}, bf16[384,768]{1,0:T(8,128)(2,1)S(1)}, u32[]{:S(2)}, u32[]{:S(2)}) collective-permute-start(bf16[384,768]{1,0:T(8,128)(2,1)} %get-tuple-element.34.inner0), channel_id=1, source_target_pairs={{0,32},{1,33},{2,34},{3,35},{4,36},{5,37},{6,38},{7,39},{8,40},{9,... | collective-permute-start | bytes 1769480 | tf_op jit(solution)/shard_map/sibling_hop0/ppermute | solution.py:79
  130.0 8.9 %collective-permute-start.19 = (bf16[384,768]{1,0:T(8,128)(2,1)}, bf16[384,768]{1,0:T(8,128)(2,1)}, u32[]{:S(2)}, u32[]{:S(2)}) collective-permute-start(bf16[384,768]{1,0:T(8,128)(2,1)} %get-tuple-element.35), channel_id=1, source_target_pairs={{0,32},{1,33},{2,34},{3,35},{4,36},{5,37},{6,38},{7,39},{8,40},{9,... | collective-permute-start | bytes 1769480 | tf_op jit(solution)/shard_map/sibling_hop2/ppermute | solution.py:79
  132.1 1.3 copy-start.15
  133.4 0.9 copy-start.20
  134.3 1.1 copy-start.22
  135.4 0.7 copy-start.25

commit v5 on v4

--- a/solution.py
+++ b/solution.py
@@ -181,37 +181,41 @@
         from_cols = lax.dynamic_slice_in_dim(col_lse, start, rows)
         return jnp.where(carries_captions == carried, from_cols, from_rows)
 
-    def factor(values):
-        return 0.5 * jnp.exp(5.0 - values)
-
     pal = blk + 1 - 2 * core
     near_w, far_w = wide - sign, wide + sign
     own_outer = part(True, blk, wide)
     own_other = part(False, blk, wide)
-    key_factors = factor(
-        jnp.stack(
-            [
-                own_outer,
-                part(True, pal, wide),
-                part(True, blk - 2 * sign, wide),
-                part(True, pal - 2 * sign, wide),
-                part(True, blk - 2 * sign, near_w),
-                part(True, pal - 2 * sign, near_w),
-                part(True, pal, near_w),
-                part(True, blk, near_w),
-                own_other,
-                part(False, pal + 2 * sign, wide),
-                part(False, blk + 2 * sign, wide),
-                part(False, pal + 4 * sign, wide),
-                part(False, pal + 2 * sign, far_w),
-                part(False, blk + 2 * sign, far_w),
-                part(False, blk, far_w),
-                part(False, pal + 4 * sign, far_w),
-            ]
-        )
-    )
-    near_factor = jnp.broadcast_to(factor(own_other)[:, None], (rows, 128))
-    far_factor = jnp.broadcast_to(factor(own_outer)[:, None], (rows, 128))
+    normalizers = [
+        own_outer,
+        part(True, pal, wide),
+        part(True, blk - 2 * sign, wide),
+        part(True, pal - 2 * sign, wide),
+        part(True, blk - 2 * sign, near_w),
+        part(True, pal - 2 * sign, near_w),
+        part(True, pal, near_w),
+        part(True, blk, near_w),
+        own_other,
+        part(False, pal + 2 * sign, wide),
+        part(False, blk + 2 * sign, wide),
+        part(False, pal + 4 * sign, wide),
+        part(False, pal + 2 * sign, far_w),
+        part(False, blk + 2 * sign, far_w),
+        part(False, blk, far_w),
+        part(False, pal + 4 * sign, far_w),
+    ]
+
+    def factors_kernel(*refs):
+        sources, (keys, near, far) = refs[:-3], refs[-3:]
+        for k, source in enumerate(sources):
+            keys[k : k + 1, :] = 0.5 * jnp.exp(5.0 - source[...].reshape(1, rows))
+        near[...] = jnp.broadcast_to(keys[8:9, :], (128, rows)).T
+        far[...] = jnp.broadcast_to(keys[0:1, :], (128, rows)).T
+
+    key_factors, near_factor, far_factor = call(
+        "factors", factors_kernel,
+        [jax.ShapeDtypeStruct(shape, jnp.float32) for shape in ((16, rows), (rows, 128), (rows, 128))],
+        (), tuple(lax.optimization_barrier((*normalizers, held))[:-1]),
+    )
     total = jax.ShapeDtypeStruct((rows, width), jnp.float32)
 
     def terms(name, near_blocks, far_blocks, sums, weight=1):
@@ -288,18 +292,7 @@
         (other, near_factor, key_factors, carried, near_sum), 100_000_000,
     )
 
-    def far_kernel(s, out, ff, kf, keys, last, far_in, far):
-        far[...] = add_terms(
-            far_in[...], out[...], ff[:, :1], kf, s[0],
-            [(keys[k * rows : (k + 1) * rows, :], row, False) for k, row in enumerate((12, 13, 9, 10))]
-            + [(last[...], 11, False)],
-        )
-
-    far_sum = call(
-        "terms_far1", far_kernel, total, (scale,),
-        (outer, far_factor, key_factors, after(sib, near_sum), far2, far_sum),
-    )
-    got0 = [after(got0[0], far2, far_sum), *got0[1:]]
+    got0 = [after(got0[0], far2, near_sum), *got0[1:]]
 
     def merge0_kernel(edge, usual, q0, q1, q2, q3, inner0, outer0, farthest):
         @pl.when(edge[0] == 1)
@@ -321,15 +314,28 @@
     )
     hop_sib0 = send("sibling_hop0", hop_inner0, to_sibling)
     hop_sib2 = send("sibling_hop2", hop_outer2, to_sibling)
-    def third_kernel(s, oth, nf, kf, outer0, inner0, near_in, near):
+
+    def near0_kernel(s, oth, nf, kf, outer0, inner0, near_in, near):
         near[...] = add_terms(
             near_in[...], oth[...], nf[:, :1], kf, s[0],
             [(outer0[...], 7, False), (inner0[...], 6, False)],
         )
 
     near_sum = call(
-        "terms_2", third_kernel, total, (scale,),
-        (other, near_factor, key_factors, hop_outer0, hop_inner0, near_sum),
+        "terms_near0", near0_kernel, total, (scale,),
+        (other, near_factor, key_factors, hop_outer0, hop_inner0, near_sum), 100_000_000,
+    )
+
+    def far1_kernel(s, out, ff, kf, keys, farthest, far_in, far):
+        far[...] = add_terms(
+            far_in[...], out[...], ff[:, :1], kf, s[0],
+            [(keys[k * rows : (k + 1) * rows, :], row, False) for k, row in enumerate((12, 13, 9, 10))]
+            + [(farthest[...], 11, False)],
+        )
+
+    far_sum = call(
+        "terms_far1", far1_kernel, total, (scale,),
+        (outer, far_factor, key_factors, after(sib, hop_far2, near_sum), far2, far_sum),
     )
 
     def last_kernel(c, e, s, out, ff, kf, hs0, hs2, hf2, near_in, far_in, image_grad, caption_grad):

time: 145 us -> 131 us (0.903)
  local copies, waits for them, and re-layouts: 25.8 us -> 8.2 us
  starting transfers between devices: 67.1 us -> 76.4 us
  waiting for transfers between devices: 20.3 us -> 15.7 us
    another operation x17 -> x0, local copies, waits for them, and re-layouts: 10.7 us -> none  [on_device(): jnp.stack([own_outer, part(True, pal, wide), part(True, blk - 2 * sign, w...]
    ppermute x21, starting transfers between devices: 67.1 us -> 76.4 us  [send(): return lax.ppermute(x, AXES, pairs(target))]
    unnamed x56 -> x36, local copies, waits for them, and re-layouts: 14 us -> 7.28 us
    ppermute x21, waiting for transfers between devices: 20.3 us -> 15.7 us  [send(): return lax.ppermute(x, AXES, pairs(target))]
    mul x2 -> x0, other arithmetic: 1.89 us -> none  [factor(): return 0.5 * jnp.exp(5.0 - values)]
    pallas_call x8 -> x9, Pallas kernels: 21.2 us -> 21.7 us  [call(): pl.pallas_call(kernel, out_shape=out_shape, in_specs=[scalars() for _ in...]
  transfers between devices with their start and end apart: 21 -> 21, of which waited for: 4 -> 6; matrix products, arithmetic and copies ran while one was open for 12% -> 4% of each run, Pallas kernels for 12% -> 14%
where the time goes in v5:
time: 131 us; the launch traced here: 130 us
  starting transfers between devices  76.4 us (58%)
  Pallas kernels  21.7 us (17%)
  waiting for transfers between devices  15.7 us (12%)
  local copies, waits for them, and re-layouts  8.2 us (6%)
  other arithmetic  6.21 us (5%)
  between operations  1.81 us (1%)
    ppermute x21, starting transfers between devices, send(): return lax.ppermute(x, AXES, pairs(target))  76.4 us
    pallas_call x9, Pallas kernels, call(): pl.pallas_call(kernel, out_shape=out_shape, in_specs=[scalars() for _ in...  21.7 us
    ppermute x21, waiting for transfers between devices, send(): return lax.ppermute(x, AXES, pairs(target))  15.7 us
    unnamed x36, local copies, waits for them, and re-layouts  7.28 us
  transfers between devices with their start and end apart: 21, of which 6 were waited for; matrix products, arithmetic and copies ran while one was open for 4% of the time, Pallas kernels for 14%

profile of v5, /device:TPU:1, one launch (start us, length us, event | category | flops | bytes accessed | tf_op | source)
XLA Modules:
  0.0 130.0 jit_solution(11074679720566674820)
XLA Ops:
  0.6 1.3 %broadcast_select_fusion = (bf16[384,768]{1,0:T(8,128)(2,1)S(1)}, bf16[384,768]{1,0:T(8,128)(2,1)S(1)}) fusion(bf16[384,768]{1,0:T(8,128)(2,1)} %param.5, bf16[384,768]{1,0:T(8,128)(2,1)} %param.6, pred[]{:T(512)S(6)} %eq.62), kind=kLoop, calls=%fused_computation.1 | loop fusion | flops 589824 | bytes 2359297 | tf_op jit(solution)/shard_map/jit(_where)/select_n | solution.py:153
  2.0 8.8 %collective-permute-start = (bf16[384,768]{1,0:T(8,128)(2,1)S(1)}, bf16[384,768]{1,0:T(8,128)(2,1)S(1)}, u32[]{:S(2)}, u32[]{:S(2)}) collective-permute-start(bf16[384,768]{1,0:T(8,128)(2,1)S(1)} %get-tuple-element.92.oth.refs_4_), channel_id=1, source_target_pairs={{0,32},{1,33},{2,34},{3,35},{4,36},{5,37},{6,38},{7,39},{8,40},{9,... | collective-permute-start | bytes 1769480 | tf_op jit(solution)/shard_map/swap/ppermute | solution.py:79
  10.8 1.9 %collective-permute-start.4 = (bf16[384,768]{1,0:T(8,128)(2,1)S(1)}, bf16[384,768]{1,0:T(8,128)(2,1)S(1)}, u32[]{:S(2)}, u32[]{:S(2)}) collective-permute-start(bf16[384,768]{1,0:T(8,128)(2,1)S(1)} %get-tuple-element.93.outer.out.refs_0_), channel_id=1, source_target_pairs={{0,448},{1,449},{2,450},{3,451},{4,452},{5,453},{6,454},{7,455},{8... | collective-permute-start | bytes 1769480 | tf_op jit(solution)/shard_map/own_outer1/ppermute | solution.py:79
  12.7 7.5 %collective-permute-start.5 = (bf16[384,768]{1,0:T(8,128)(2,1)S(1)}, bf16[384,768]{1,0:T(8,128)(2,1)S(1)}, u32[]{:S(2)}, u32[]{:S(2)}) collective-permute-start(bf16[384,768]{1,0:T(8,128)(2,1)S(1)} %get-tuple-element.92.oth.refs_4_), channel_id=1, source_target_pairs={{0,96},{1,97},{2,98},{3,99},{4,100},{5,101},{6,102},{7,103},{8,104... | collective-permute-start | bytes 1769480 | tf_op jit(solution)/shard_map/own_inner1/ppermute | solution.py:79
  20.2 0.0 collective-permute-done.inner.refs_1_
  20.2 0.0 copy-start.3
  20.2 1.0 cut.1
  21.3 1.3 collective-permute-start.1
  22.5 1.4 %collective-permute-start.2 = (bf16[192,768]{1,0:T(8,128)(2,1)}, bf16[192,768]{1,0:T(8,128)(2,1)}, u32[]{:S(2)}, u32[]{:S(2)}) collective-permute-start(bf16[192,768]{1,0:T(8,128)(2,1)} %get-tuple-element.40), channel_id=1, source_target_pairs={{0,1},{4,5},{8,9},{12,13},{16,17},{20,21},{24,25},{28,29},{35,34},... | collective-permute-start | bytes 884744 | tf_op jit(solution)/shard_map/spread1/ppermute | solution.py:79
  23.9 1.4 %collective-permute-start.3 = (bf16[192,768]{1,0:T(8,128)(2,1)S(1)}, bf16[192,768]{1,0:T(8,128)(2,1)}, u32[]{:S(2)}, u32[]{:S(2)}) collective-permute-start(bf16[192,768]{1,0:T(8,128)(2,1)S(1)} %get-tuple-element.41), channel_id=1, source_target_pairs={{0,2},{4,6},{8,10},{12,14},{16,18},{20,22},{24,26},{28,30},{35,33}... | collective-permute-start | bytes 884744 | tf_op jit(solution)/shard_map/spread2/ppermute | solution.py:79
  26.0 1.2 dynamic-slice_select_fusion
  27.2 3.0 %collective-permute-done.1 = bf16[192,768]{1,0:T(8,128)(2,1)} collective-permute-done((bf16[192,768]{1,0:T(8,128)(2,1)}, bf16[192,768]{1,0:T(8,128)(2,1)}, u32[]{:S(2)}, u32[]{:S(2)}) %collective-permute-start.1) | collective-permute-done | bytes 294944 | tf_op jit(solution)/shard_map/spread0/ppermute | solution.py:79
  30.2 0.0 collective-permute-done.2
  30.2 0.0 collective-permute-done.3
  30.2 1.0 select_select_fusion
  31.3 8.4 %collective-permute-start.7 = (bf16[192,768]{1,0:T(8,128)(2,1)S(1)}, bf16[192,768]{1,0:T(8,128)(2,1)}, u32[]{:S(2)}, u32[]{:S(2)}) collective-permute-start(bf16[192,768]{1,0:T(8,128)(2,1)S(1)} %select_select_fusion), channel_id=1, source_target_pairs={{0,476},{1,477},{2,478},{3,479},{4,448},{5,449},{6,450},{7,451},{8... | collective-permute-start | bytes 884744 | tf_op jit(solution)/shard_map/cross/ppermute | solution.py:79
  39.7 0.0 collective-permute-done.4.refs_2_.outer1
  39.7 3.0 %collective-permute-done.5.refs_3_.inner1 = bf16[384,768]{1,0:T(8,128)(2,1)S(1)} collective-permute-done((bf16[384,768]{1,0:T(8,128)(2,1)S(1)}, bf16[384,768]{1,0:T(8,128)(2,1)S(1)}, u32[]{:S(2)}, u32[]{:S(2)}) %collective-permute-start.5) | collective-permute-done | bytes 589856 | tf_op jit(solution)/shard_map/own_inner1/ppermute | solution.py:79
  42.7 1.6 %pad_maximum_fusion = bf16[1536,768]{1,0:T(8,128)(2,1)} fusion(bf16[384,768]{1,0:T(8,128)(2,1)S(1)} %collective-permute-done.5.refs_3_.inner1, bf16[384,768]{1,0:T(8,128)(2,1)S(1)} %collective-permute-done.4.refs_2_.outer1, bf16[384,768]{1,0:T(8,128)(2,1)S(1)} %get-tuple-element.93.outer.out.refs_0_, bf16[384,768]{1,0:T(8,128)(2,1)S(1)} %collective-permute-done.inner.refs_1_), kind=kLoop, calls=%fused_computation | loop fusion | flops 9437184 | bytes 4718592 | tf_op jit(solution)/shard_map/concatenate | solution.py:174
  44.3 0.8 copy-done
  45.1 5.4 %collective-permute-start.6 = (bf16[1536,768]{1,0:T(8,128)(2,1)}, bf16[1536,768]{1,0:T(8,128)(2,1)S(1)}, u32[]{:S(2)}, u32[]{:S(2)}) collective-permute-start(bf16[1536,768]{1,0:T(8,128)(2,1)} %pad_maximum_fusion), channel_id=1, source_target_pairs={{1,0},{2,1},{3,2},{5,4},{6,5},{7,6},{9,8},{10,9},{11,10},{13,12},{... | collective-permute-start | bytes 7077896 | tf_op jit(solution)/shard_map/wide_early/ppermute | solution.py:79
  50.6 0.2 factors.1
  50.8 1.2 copy-done.1
  52.0 1.1 copy-done.4
  53.1 1.1 copy-done.10
  54.1 3.6 %terms_own0.1 = (f32[384,768]{1,0:T(8,128)S(1)}, f32[384,768]{1,0:T(8,128)S(1)}) custom-call(f32[1]{0:T(128)} %bitcast.4.s, bf16[384,768]{1,0:T(8,128)(2,1)S(1)} %copy-done.10, bf16[384,768]{1,0:T(8,128)(2,1)S(1)} %get-tuple-element.93.outer.out.refs_0_, f32[384,128]{1,0:T(8,128)S(1)} %get-tuple-element.62.nf, f32[384,128]{1,0:T(8,128)S(1)} %get-tuple-element.59.ff, ...), custom_call_target="tpu_custom_call" | custom-call | flops 99999997952 | bytes 1000 | tf_op jit(solution)/shard_map/terms_own0/pallas_call | solution.py:94
  57.8 0.0 copy-start.5
  57.8 1.0 copy-done.5
  58.8 1.0 copy-done.16
  59.8 3.7 %collective-permute-done.7.q0 = bf16[192,768]{1,0:T(8,128)(2,1)} collective-permute-done((bf16[192,768]{1,0:T(8,128)(2,1)S(1)}, bf16[192,768]{1,0:T(8,128)(2,1)}, u32[]{:S(2)}, u32[]{:S(2)}) %collective-permute-start.7) | collective-permute-done | bytes 294944 | tf_op jit(solution)/shard_map/cross/ppermute | solution.py:79
  63.5 0.9 slice.3
  64.5 10.4 %collective-permute-start.9 = (bf16[96,768]{1,0:T(8,128)(2,1)S(1)}, bf16[96,768]{1,0:T(8,128)(2,1)}, u32[]{:S(2)}, u32[]{:S(2)}) collective-permute-start(bf16[96,768]{1,0:T(8,128)(2,1)S(1)} %slice.3), channel_id=1, source_target_pairs={{0,448},{1,449},{2,450},{3,451},{4,452},{5,453},{6,454},{7,455},{8... | collective-permute-start | bytes 442376 | tf_op jit(solution)/shard_map/cross_ahead/ppermute | solution.py:79
  74.9 1.9 %collective-permute-start.8 = (bf16[192,768]{1,0:T(8,128)(2,1)}, bf16[192,768]{1,0:T(8,128)(2,1)}, u32[]{:S(2)}, u32[]{:S(2)}) collective-permute-start(bf16[192,768]{1,0:T(8,128)(2,1)} %collective-permute-done.7.q0), channel_id=1, source_target_pairs={{0,64},{1,65},{2,66},{3,67},{4,68},{5,69},{6,70},{7,71},{8,72},{9,... | collective-permute-start | bytes 884744 | tf_op jit(solution)/shard_map/cross_back/ppermute | solution.py:79
  76.8 1.3 collective-permute-start.10
  78.1 1.3 collective-permute-start.11
  79.4 0.0 collective-permute-done.9
  79.4 1.3 collective-permute-start.12
  80.7 3.9 %collective-permute-done.8 = bf16[192,768]{1,0:T(8,128)(2,1)} collective-permute-done((bf16[192,768]{1,0:T(8,128)(2,1)}, bf16[192,768]{1,0:T(8,128)(2,1)}, u32[]{:S(2)}, u32[]{:S(2)}) %collective-permute-start.8) | collective-permute-done | bytes 294944 | tf_op jit(solution)/shard_map/cross_back/ppermute | solution.py:79
  84.7 4.1 %collective-permute-start.13 = (bf16[384,768]{1,0:T(8,128)(2,1)S(1)}, bf16[384,768]{1,0:T(8,128)(2,1)S(1)}, u32[]{:S(2)}, u32[]{:S(2)}) collective-permute-start(bf16[384,768]{1,0:T(8,128)(2,1)S(1)} %collective-permute-done.4.refs_2_.outer1), channel_id=1, source_target_pairs={{0,480},{1,481},{2,482},{3,483},{4,484},{5,485},{6,486},{7,487},{8... | collective-permute-start | bytes 1769480 | tf_op jit(solution)/shard_map/own_outer2/ppermute | solution.py:79
  88.8 1.1 pad_maximum_fusion.1.q0
  89.8 0.0 collective-permute-done.10.q1
  89.8 0.5 collective-permute-done.11.q2
  90.3 0.0 collective-permute-done.12.q3
  90.3 1.3 collective-permute-start.14
  91.6 1.3 collective-permute-start.15
  92.9 1.3 collective-permute-start.16
  94.2 0.0 collective-permute-done.6.early.usual
  94.2 1.1 copy-done.2
  95.3 3.0 %merge1.1.keys = bf16[1536,768]{1,0:T(8,128)(2,1)} custom-call(s32[1]{0:T(128)} %bitcast.3.edge, bf16[1536,768]{1,0:T(8,128)(2,1)S(1)} %collective-permute-done.6.early.usual, bf16[384,768]{1,0:T(8,128)(2,1)S(1)} %collective-permute-done.4.refs_2_.outer1, bf16[384,768]{1,0:T(8,128)(2,1)S(1)} %copy-done.2, bf16[192,768]{1,0:T(8,128)(2,1)} %collective-permute-done.7.q0, ...), custom_call_target="tpu_custom_call" | custom-call | flops 1000 | bytes 1000 | tf_op jit(solution)/shard_map/merge1/pallas_call | solution.py:94
  98.3 8.8 %collective-permute-start.20 = (bf16[1536,768]{1,0:T(8,128)(2,1)}, bf16[1536,768]{1,0:T(8,128)(2,1)}, u32[]{:S(2)}, u32[]{:S(2)}) collective-permute-start(bf16[1536,768]{1,0:T(8,128)(2,1)} %merge1.1.keys), channel_id=1, source_target_pairs={{0,32},{1,33},{2,34},{3,35},{4,36},{5,37},{6,38},{7,39},{8,40},{9,... | collective-permute-start | bytes 7077896 | tf_op jit(solution)/shard_map/sibling1/ppermute | solution.py:79
  107.2 3.3 %terms_near1.1.near_in = f32[384,768]{1,0:T(8,128)S(1)} custom-call(f32[1]{0:T(128)} %bitcast.5.s, bf16[384,768]{1,0:T(8,128)(2,1)S(1)} %copy-done.11, f32[384,128]{1,0:T(8,128)S(1)} %copy-done.15, f32[16,384]{1,0:T(8,128)S(1)} %copy-done.13, bf16[1536,768]{1,0:T(8,128)(2,1)} %merge1.1.keys, f32[384,768]{1,0:T(8,128)S(1)} %copy-done.17), custom_call_target="tpu_custom_call" | custom-call | flops 99999997952 | bytes 1000 | tf_op jit(solution)/shard_map/terms_near1/pallas_call | solution.py:94
  110.5 0.0 collective-permute-done.13.farthest
  110.5 1.3 collective-permute-start.19
  111.8 0.0 collective-permute-done.15.q2
  111.8 0.0 collective-permute-done.16.q3
  111.8 0.1 merge0.1
  112.0 3.9 %collective-permute-start.17 = (bf16[384,768]{1,0:T(8,128)(2,1)S(1)}, bf16[384,768]{1,0:T(8,128)(2,1)S(1)}, u32[]{:S(2)}, u32[]{:S(2)}) collective-permute-start(bf16[384,768]{1,0:T(8,128)(2,1)S(1)} %get-tuple-element.71.inner0), channel_id=1, source_target_pairs={{0,32},{1,33},{2,34},{3,35},{4,36},{5,37},{6,38},{7,39},{8,40},{9,... | collective-permute-start | bytes 1769480 | tf_op jit(solution)/shard_map/sibling_hop0/ppermute | solution.py:79
  115.9 2.1 %collective-permute-start.18 = (bf16[384,768]{1,0:T(8,128)(2,1)S(1)}, bf16[384,768]{1,0:T(8,128)(2,1)S(1)}, u32[]{:S(2)}, u32[]{:S(2)}) collective-permute-start(bf16[384,768]{1,0:T(8,128)(2,1)S(1)} %get-tuple-element.72), channel_id=1, source_target_pairs={{0,32},{1,33},{2,34},{3,35},{4,36},{5,37},{6,38},{7,39},{8,40},{9,... | collective-permute-start | bytes 1769480 | tf_op jit(solution)/shard_map/sibling_hop2/ppermute | solution.py:79
  118.0 0.0 copy-start.6
  118.0 1.7 %terms_near0.1.near_in = f32[384,768]{1,0:T(8,128)S(1)} custom-call(f32[1]{0:T(128)} %bitcast.6.s, bf16[384,768]{1,0:T(8,128)(2,1)S(1)} %copy-done.11, f32[384,128]{1,0:T(8,128)S(1)} %copy-done.15, f32[16,384]{1,0:T(8,128)S(1)} %copy-done.13, bf16[384,768]{1,0:T(8,128)(2,1)S(1)} %get-tuple-element.74.outer0, bf16[384,768]{1,0:T(8,128)(2,1)S(1)} %get-tuple-element.71.inner0, ...), custom_call_target="tpu_custom_call" | custom-call | flops 99999997952 | bytes 1000 | tf_op jit(solution)/shard_map/terms_near0/pallas_call | solution.py:94
  119.7 1.4 %collective-permute-done.19.hf2 = bf16[384,768]{1,0:T(8,128)(2,1)S(1)} collective-permute-done((bf16[384,768]{1,0:T(8,128)(2,1)S(1)}, bf16[384,768]{1,0:T(8,128)(2,1)S(1)}, u32[]{:S(2)}, u32[]{:S(2)}) %collective-permute-start.19) | collective-permute-done | bytes 589856 | tf_op jit(solution)/shard_map/wide_outer2/ppermute | solution.py:79
  121.2 5.6 %terms_far1.1.far_in = f32[384,768]{1,0:T(8,128)S(1)} custom-call(f32[1]{0:T(128)} %bitcast.7.s, bf16[384,768]{1,0:T(8,128)(2,1)S(1)} %get-tuple-element.93.outer.out.refs_0_, f32[384,128]{1,0:T(8,128)S(1)} %copy-done.8, f32[16,384]{1,0:T(8,128)S(1)} %copy-done.13, bf16[1536,768]{1,0:T(8,128)(2,1)} %collective-permute-done.20.keys, ...), custom_call_target="tpu_custom_call" | custom-call | flops 1000 | bytes 1000 | tf_op jit(solution)/shard_map/terms_far1/pallas_call | solution.py:94
  126.7 0.0 collective-permute-done.17.hs0
  126.7 3.3 %terms_last.1 = (f32[384,768]{1,0:T(8,128)}, f32[384,768]{1,0:T(8,128)}) custom-call(s32[1]{0:T(128)} %bitcast.c, s32[1]{0:T(128)} %bitcast.1.e, f32[1]{0:T(128)} %bitcast.8.s, bf16[384,768]{1,0:T(8,128)(2,1)S(1)} %get-tuple-element.93.outer.out.refs_0_, f32[384,128]{1,0:T(8,128)S(1)} %copy-done.8, f32[16,384]{1,0:T(8,128)S(1)} %copy-done.13, ...), custom_call_target="tpu_custom_call" | custom-call | flops 1000 | bytes 1000 | tf_op jit(solution)/shard_map/terms_last/pallas_call | solution.py:94
  (29 shorter events, 0.1 us)
Async XLA Ops:
  2.0 40.7 %copy-start.9 = (bf16[384,768]{1,0:T(8,128)(2,1)}, bf16[384,768]{1,0:T(8,128)(2,1)S(1)}, u32[]{:S(2)}) copy-start(bf16[384,768]{1,0:T(8,128)(2,1)S(1)} %get-tuple-element.92.oth.refs_4_) | copy-start | bytes 1769476
  2.0 18.2 %collective-permute-start = (bf16[384,768]{1,0:T(8,128)(2,1)S(1)}, bf16[384,768]{1,0:T(8,128)(2,1)S(1)}, u32[]{:S(2)}, u32[]{:S(2)}) collective-permute-start(bf16[384,768]{1,0:T(8,128)(2,1)S(1)} %get-tuple-element.92.oth.refs_4_), channel_id=1, source_target_pairs={{0,32},{1,33},{2,34},{3,35},{4,36},{5,37},{6,38},{7,39},{8,40},{9,... | collective-permute-start | bytes 1769480 | tf_op jit(solution)/shard_map/swap/ppermute | solution.py:79
  10.8 28.9 %collective-permute-start.4 = (bf16[384,768]{1,0:T(8,128)(2,1)S(1)}, bf16[384,768]{1,0:T(8,128)(2,1)S(1)}, u32[]{:S(2)}, u32[]{:S(2)}) collective-permute-start(bf16[384,768]{1,0:T(8,128)(2,1)S(1)} %get-tuple-element.93.outer.out.refs_0_), channel_id=1, source_target_pairs={{0,448},{1,449},{2,450},{3,451},{4,452},{5,453},{6,454},{7,455},{8... | collective-permute-start | bytes 1769480 | tf_op jit(solution)/shard_map/own_outer1/ppermute | solution.py:79
  12.7 30.0 %collective-permute-start.5 = (bf16[384,768]{1,0:T(8,128)(2,1)S(1)}, bf16[384,768]{1,0:T(8,128)(2,1)S(1)}, u32[]{:S(2)}, u32[]{:S(2)}) collective-permute-start(bf16[384,768]{1,0:T(8,128)(2,1)S(1)} %get-tuple-element.92.oth.refs_4_), channel_id=1, source_target_pairs={{0,96},{1,97},{2,98},{3,99},{4,100},{5,101},{6,102},{7,103},{8,104... | collective-permute-start | bytes 1769480 | tf_op jit(solution)/shard_map/own_inner1/ppermute | solution.py:79
  20.2 22.5 %copy-start.3 = (bf16[384,768]{1,0:T(8,128)(2,1)}, bf16[384,768]{1,0:T(8,128)(2,1)S(1)}, u32[]{:S(2)}) copy-start(bf16[384,768]{1,0:T(8,128)(2,1)S(1)} %collective-permute-done.inner.refs_1_) | copy-start | bytes 1769476
  21.3 9.0 %collective-permute-start.1 = (bf16[192,768]{1,0:T(8,128)(2,1)}, bf16[192,768]{1,0:T(8,128)(2,1)}, u32[]{:S(2)}, u32[]{:S(2)}) collective-permute-start(bf16[192,768]{1,0:T(8,128)(2,1)} %get-tuple-element.39), channel_id=1, source_target_pairs={{0,3},{4,7},{8,11},{12,15},{16,19},{20,23},{24,27},{28,31},{35,32}... | collective-permute-start | bytes 884744 | tf_op jit(solution)/shard_map/spread0/ppermute | solution.py:79
  22.5 7.7 %collective-permute-start.2 = (bf16[192,768]{1,0:T(8,128)(2,1)}, bf16[192,768]{1,0:T(8,128)(2,1)}, u32[]{:S(2)}, u32[]{:S(2)}) collective-permute-start(bf16[192,768]{1,0:T(8,128)(2,1)} %get-tuple-element.40), channel_id=1, source_target_pairs={{0,1},{4,5},{8,9},{12,13},{16,17},{20,21},{24,25},{28,29},{35,34},... | collective-permute-start | bytes 884744 | tf_op jit(solution)/shard_map/spread1/ppermute | solution.py:79
  23.9 6.3 %collective-permute-start.3 = (bf16[192,768]{1,0:T(8,128)(2,1)S(1)}, bf16[192,768]{1,0:T(8,128)(2,1)}, u32[]{:S(2)}, u32[]{:S(2)}) collective-permute-start(bf16[192,768]{1,0:T(8,128)(2,1)S(1)} %get-tuple-element.41), channel_id=1, source_target_pairs={{0,2},{4,6},{8,10},{12,14},{16,18},{20,22},{24,26},{28,30},{35,33}... | collective-permute-start | bytes 884744 | tf_op jit(solution)/shard_map/spread2/ppermute | solution.py:79
  31.3 32.3 %collective-permute-start.7 = (bf16[192,768]{1,0:T(8,128)(2,1)S(1)}, bf16[192,768]{1,0:T(8,128)(2,1)}, u32[]{:S(2)}, u32[]{:S(2)}) collective-permute-start(bf16[192,768]{1,0:T(8,128)(2,1)S(1)} %select_select_fusion), channel_id=1, source_target_pairs={{0,476},{1,477},{2,478},{3,479},{4,448},{5,449},{6,450},{7,451},{8... | collective-permute-start | bytes 884744 | tf_op jit(solution)/shard_map/cross/ppermute | solution.py:79
  44.3 0.8 copy-start
  45.1 49.1 %collective-permute-start.6 = (bf16[1536,768]{1,0:T(8,128)(2,1)}, bf16[1536,768]{1,0:T(8,128)(2,1)S(1)}, u32[]{:S(2)}, u32[]{:S(2)}) collective-permute-start(bf16[1536,768]{1,0:T(8,128)(2,1)} %pad_maximum_fusion), channel_id=1, source_target_pairs={{1,0},{2,1},{3,2},{5,4},{6,5},{7,6},{9,8},{10,9},{11,10},{13,12},{... | collective-permute-start | bytes 7077896 | tf_op jit(solution)/shard_map/wide_early/ppermute | solution.py:79
  50.8 7.0 %copy-start.7 = (f32[384,128]{1,0:T(8,128)}, f32[384,128]{1,0:T(8,128)S(1)}, u32[]{:S(2)}) copy-start(f32[384,128]{1,0:T(8,128)S(1)} %get-tuple-element.59.ff) | copy-start | bytes 589828
  50.8 7.0 %copy-start.12 = (f32[16,384]{1,0:T(8,128)}, f32[16,384]{1,0:T(8,128)S(1)}, u32[]{:S(2)}) copy-start(f32[16,384]{1,0:T(8,128)S(1)} %get-tuple-element.60.kf) | copy-start | bytes 73732
  50.8 7.0 %copy-start.14 = (f32[384,128]{1,0:T(8,128)}, f32[384,128]{1,0:T(8,128)S(1)}, u32[]{:S(2)}) copy-start(f32[384,128]{1,0:T(8,128)S(1)} %get-tuple-element.62.nf) | copy-start | bytes 589828
  50.8 1.2 copy-start.1
  52.0 1.1 copy-start.4
  53.1 1.1 copy-start.10
  57.8 1.0 copy-start.5
  58.8 1.0 copy-start.16
  64.5 15.0 %collective-permute-start.9 = (bf16[96,768]{1,0:T(8,128)(2,1)S(1)}, bf16[96,768]{1,0:T(8,128)(2,1)}, u32[]{:S(2)}, u32[]{:S(2)}) collective-permute-start(bf16[96,768]{1,0:T(8,128)(2,1)S(1)} %slice.3), channel_id=1, source_target_pairs={{0,448},{1,449},{2,450},{3,451},{4,452},{5,453},{6,454},{7,455},{8... | collective-permute-start | bytes 442376 | tf_op jit(solution)/shard_map/cross_ahead/ppermute | solution.py:79
  74.9 9.8 %collective-permute-start.8 = (bf16[192,768]{1,0:T(8,128)(2,1)}, bf16[192,768]{1,0:T(8,128)(2,1)}, u32[]{:S(2)}, u32[]{:S(2)}) collective-permute-start(bf16[192,768]{1,0:T(8,128)(2,1)} %collective-permute-done.7.q0), channel_id=1, source_target_pairs={{0,64},{1,65},{2,66},{3,67},{4,68},{5,69},{6,70},{7,71},{8,72},{9,... | collective-permute-start | bytes 884744 | tf_op jit(solution)/shard_map/cross_back/ppermute | solution.py:79
  76.8 13.0 %collective-permute-start.10 = (bf16[192,768]{1,0:T(8,128)(2,1)}, bf16[192,768]{1,0:T(8,128)(2,1)}, u32[]{:S(2)}, u32[]{:S(2)}) collective-permute-start(bf16[192,768]{1,0:T(8,128)(2,1)} %collective-permute-done.7.q0), channel_id=1, source_target_pairs={{1,3},{5,7},{9,11},{13,15},{17,19},{21,23},{25,27},{29,31},{34,32}... | collective-permute-start | bytes 884744 | tf_op jit(solution)/shard_map/gather1_1/ppermute | solution.py:79
  78.1 12.2 %collective-permute-start.11 = (bf16[192,768]{1,0:T(8,128)(2,1)}, bf16[192,768]{1,0:T(8,128)(2,1)}, u32[]{:S(2)}, u32[]{:S(2)}) collective-permute-start(bf16[192,768]{1,0:T(8,128)(2,1)} %collective-permute-done.7.q0), channel_id=1, source_target_pairs={{2,3},{6,7},{10,11},{14,15},{18,19},{22,23},{26,27},{30,31},{33,32... | collective-permute-start | bytes 884744 | tf_op jit(solution)/shard_map/gather1_2/ppermute | solution.py:79
  79.4 10.9 %collective-permute-start.12 = (bf16[192,768]{1,0:T(8,128)(2,1)}, bf16[192,768]{1,0:T(8,128)(2,1)}, u32[]{:S(2)}, u32[]{:S(2)}) collective-permute-start(bf16[192,768]{1,0:T(8,128)(2,1)} %collective-permute-done.7.q0), channel_id=1, source_target_pairs={{0,3},{4,7},{8,11},{12,15},{16,19},{20,23},{24,27},{28,31},{35,32}... | collective-permute-start | bytes 884744 | tf_op jit(solution)/shard_map/gather1_3/ppermute | solution.py:79
  84.7 25.8 %collective-permute-start.13 = (bf16[384,768]{1,0:T(8,128)(2,1)S(1)}, bf16[384,768]{1,0:T(8,128)(2,1)S(1)}, u32[]{:S(2)}, u32[]{:S(2)}) collective-permute-start(bf16[384,768]{1,0:T(8,128)(2,1)S(1)} %collective-permute-done.4.refs_2_.outer1), channel_id=1, source_target_pairs={{0,480},{1,481},{2,482},{3,483},{4,484},{5,485},{6,486},{7,487},{8... | collective-permute-start | bytes 1769480 | tf_op jit(solution)/shard_map/own_outer2/ppermute | solution.py:79
  90.3 21.5 %collective-permute-start.14 = (bf16[288,768]{1,0:T(8,128)(2,1)S(1)}, bf16[288,768]{1,0:T(8,128)(2,1)S(1)}, u32[]{:S(2)}, u32[]{:S(2)}) collective-permute-start(bf16[288,768]{1,0:T(8,128)(2,1)S(1)} %pad_maximum_fusion.1.q0), channel_id=1, source_target_pairs={{1,3},{5,7},{9,11},{13,15},{17,19},{21,23},{25,27},{29,31},{34,32}... | collective-permute-start | bytes 1327112 | tf_op jit(solution)/shard_map/gather0_1/ppermute | solution.py:79
  91.6 20.2 %collective-permute-start.15 = (bf16[288,768]{1,0:T(8,128)(2,1)S(1)}, bf16[288,768]{1,0:T(8,128)(2,1)S(1)}, u32[]{:S(2)}, u32[]{:S(2)}) collective-permute-start(bf16[288,768]{1,0:T(8,128)(2,1)S(1)} %pad_maximum_fusion.1.q0), channel_id=1, source_target_pairs={{2,3},{6,7},{10,11},{14,15},{18,19},{22,23},{26,27},{30,31},{33,32... | collective-permute-start | bytes 1327112 | tf_op jit(solution)/shard_map/gather0_2/ppermute | solution.py:79
  92.9 18.9 %collective-permute-start.16 = (bf16[288,768]{1,0:T(8,128)(2,1)S(1)}, bf16[288,768]{1,0:T(8,128)(2,1)S(1)}, u32[]{:S(2)}, u32[]{:S(2)}) collective-permute-start(bf16[288,768]{1,0:T(8,128)(2,1)S(1)} %pad_maximum_fusion.1.q0), channel_id=1, source_target_pairs={{0,3},{4,7},{8,11},{12,15},{16,19},{20,23},{24,27},{28,31},{35,32}... | collective-permute-start | bytes 1327112 | tf_op jit(solution)/shard_map/gather0_3/ppermute | solution.py:79
  94.2 1.1 copy-start.2
  95.3 11.8 %copy-start.11 = (bf16[384,768]{1,0:T(8,128)(2,1)S(1)}, bf16[384,768]{1,0:T(8,128)(2,1)}, u32[]{:S(2)}) copy-start(bf16[384,768]{1,0:T(8,128)(2,1)} %copy-done.9) | copy-start | bytes 1769476
  95.3 11.8 %copy-start.13 = (f32[16,384]{1,0:T(8,128)S(1)}, f32[16,384]{1,0:T(8,128)}, u32[]{:S(2)}) copy-start(f32[16,384]{1,0:T(8,128)} %copy-done.12) | copy-start | bytes 73732
  95.3 11.8 %copy-start.15 = (f32[384,128]{1,0:T(8,128)S(1)}, f32[384,128]{1,0:T(8,128)}, u32[]{:S(2)}) copy-start(f32[384,128]{1,0:T(8,128)} %copy-done.14) | copy-start | bytes 589828
  95.3 11.8 %copy-start.17 = (f32[384,768]{1,0:T(8,128)S(1)}, f32[384,768]{1,0:T(8,128)}, u32[]{:S(2)}) copy-start(f32[384,768]{1,0:T(8,128)} %copy-done.16) | copy-start | bytes 3538948
  98.3 22.9 %collective-permute-start.20 = (bf16[1536,768]{1,0:T(8,128)(2,1)}, bf16[1536,768]{1,0:T(8,128)(2,1)}, u32[]{:S(2)}, u32[]{:S(2)}) collective-permute-start(bf16[1536,768]{1,0:T(8,128)(2,1)} %merge1.1.keys), channel_id=1, source_target_pairs={{0,32},{1,33},{2,34},{3,35},{4,36},{5,37},{6,38},{7,39},{8,40},{9,... | collective-permute-start | bytes 7077896 | tf_op jit(solution)/shard_map/sibling1/ppermute | solution.py:79
  110.5 10.6 %collective-permute-start.19 = (bf16[384,768]{1,0:T(8,128)(2,1)S(1)}, bf16[384,768]{1,0:T(8,128)(2,1)S(1)}, u32[]{:S(2)}, u32[]{:S(2)}) collective-permute-start(bf16[384,768]{1,0:T(8,128)(2,1)S(1)} %collective-permute-done.13.farthest), channel_id=1, source_target_pairs={{0,1},{1,2},{2,3},{4,5},{5,6},{6,7},{8,9},{9,10},{10,11},{12,13},{... | collective-permute-start | bytes 1769480 | tf_op jit(solution)/shard_map/wide_outer2/ppermute | solution.py:79
  112.0 14.7 %collective-permute-start.17 = (bf16[384,768]{1,0:T(8,128)(2,1)S(1)}, bf16[384,768]{1,0:T(8,128)(2,1)S(1)}, u32[]{:S(2)}, u32[]{:S(2)}) collective-permute-start(bf16[384,768]{1,0:T(8,128)(2,1)S(1)} %get-tuple-element.71.inner0), channel_id=1, source_target_pairs={{0,32},{1,33},{2,34},{3,35},{4,36},{5,37},{6,38},{7,39},{8,40},{9,... | collective-permute-start | bytes 1769480 | tf_op jit(solution)/shard_map/sibling_hop0/ppermute | solution.py:79
  115.9 10.9 %collective-permute-start.18 = (bf16[384,768]{1,0:T(8,128)(2,1)S(1)}, bf16[384,768]{1,0:T(8,128)(2,1)S(1)}, u32[]{:S(2)}, u32[]{:S(2)}) collective-permute-start(bf16[384,768]{1,0:T(8,128)(2,1)S(1)} %get-tuple-element.72), channel_id=1, source_target_pairs={{0,32},{1,33},{2,34},{3,35},{4,36},{5,37},{6,38},{7,39},{8,40},{9,... | collective-permute-start | bytes 1769480 | tf_op jit(solution)/shard_map/sibling_hop2/ppermute | solution.py:79
  118.0 3.2 %copy-start.6 = (f32[384,768]{1,0:T(8,128)S(1)}, f32[384,768]{1,0:T(8,128)}, u32[]{:S(2)}) copy-start(f32[384,768]{1,0:T(8,128)} %copy-done.5) | copy-start | bytes 3538948
  118.0 3.1 %copy-start.8 = (f32[384,128]{1,0:T(8,128)S(1)}, f32[384,128]{1,0:T(8,128)}, u32[]{:S(2)}) copy-start(f32[384,128]{1,0:T(8,128)} %copy-done.7) | copy-start | bytes 589828

commit v6 on v5

--- a/solution.py
+++ b/solution.py
@@ -101,6 +101,34 @@
             ),
             compiler_params=pltpu.CompilerParams(vmem_limit_bytes=16 * 1024 * 1024),
         )(*smem, *vmem)
+
+
+def move(name, kernel, out_shape, smem, arrays, copies):
+    many = isinstance(out_shape, (list, tuple))
+    anywhere = pl.BlockSpec(memory_space=pl.ANY)
+    with jax.named_scope(name):
+        return pl.pallas_call(
+            kernel,
+            out_shape=out_shape,
+            in_specs=[scalars() for _ in smem] + [anywhere for _ in arrays],
+            out_specs=[anywhere for _ in out_shape] if many else anywhere,
+            scratch_shapes=[pltpu.SemaphoreType.DMA((copies,))],
+            cost_estimate=pl.CostEstimate(flops=1000, bytes_accessed=1000, transcendentals=0),
+            compiler_params=pltpu.CompilerParams(vmem_limit_bytes=16 * 1024 * 1024),
+        )(*smem, *arrays)
+
+
+def copy_all(sems, pieces):
+    moves = [
+        pltpu.make_async_copy(
+            source.at[pl.ds(low, count)], target.at[pl.ds(at, count)], sems.at[k]
+        )
+        for k, (source, low, target, at, count) in enumerate(pieces)
+    ]
+    for one in moves:
+        one.start()
+    for one in moves:
+        one.wait()
 
 
 def term(query, query_factor, keys, key_factor, scale, own=False):
@@ -244,7 +272,7 @@
         )
 
     sums = terms("terms_own0", [(outer, [0]), (inner, [1]), (after(outer1, held), [2]), (inner1, [3])], [(other, [8])], None, 100_000_000)
-    crossed = after(crossed, *sums)
+    crossed = after(crossed, early, *sums)
 
     back = send("cross_back", crossed, to_previous_chip)
     ahead = send("cross_ahead", crossed[quarter:], to_next_chip)
@@ -257,25 +285,35 @@
 
     got1 = collect("gather1_", crossed)
     far2 = send("own_outer2", after(outer1, crossed), to_next_chip_sibling)
-    got0 = collect("gather0_", after(jnp.concatenate([back, ahead], axis=0), *got1))
-
-    def merge1_kernel(edge, early, outer1, inner1, q0, q1, q2, q3, out):
+
+    def join_kernel(first, second, out):
+        out[: 2 * quarter, :] = first[...]
+        out[2 * quarter :, :] = second[...]
+
+    joined = call(
+        "join", join_kernel, jax.ShapeDtypeStruct((3 * quarter, width), half), (),
+        (back, ahead), 100_000_000,
+    )
+    got0 = collect("gather0_", after(joined, *got1))
+
+    def merge1_kernel(edge, early, outer1, inner1, q0, q1, q2, q3, out, sems):
+        own = [(outer1, 0, out, 2 * rows, rows), (inner1, 0, out, 3 * rows, rows)]
+
         @pl.when(edge[0] == 1)
         def _():
+            pieces = []
             for place, source in enumerate((q0, q1, q2, q3)):
-                low = place * quarter
-                out[low : low + quarter, :] = source[quarter:, :]
-                out[rows + low : rows + low + quarter, :] = source[:quarter, :]
+                pieces.append((source, quarter, out, place * quarter, quarter))
+                pieces.append((source, 0, out, rows + place * quarter, quarter))
+            copy_all(sems, pieces + own)
 
         @pl.when(edge[0] == 0)
         def _():
-            out[: 2 * rows, :] = early[2 * rows :, :]
-
-        out[2 * rows : 3 * rows, :] = outer1[...]
-        out[3 * rows :, :] = inner1[...]
-
-    carried = call(
-        "merge1", merge1_kernel, blocks(4), (at_edge,), (early, after(outer1, back, ahead), inner1, *got1)
+            copy_all(sems, [(early, 2 * rows, out, 0, 2 * rows)] + own)
+
+    carried = move(
+        "merge1", merge1_kernel, blocks(4), (at_edge,),
+        (early, after(outer1, back, ahead), inner1, *got1), 10,
     )
     sib = send("sibling1", carried, to_sibling)
     hop_far2 = send("wide_outer2", after(far2, carried), to_sibling_next_wide)
@@ -294,36 +332,35 @@
 
     got0 = [after(got0[0], far2, near_sum), *got0[1:]]
 
-    def merge0_kernel(edge, usual, q0, q1, q2, q3, inner0, outer0, farthest):
+    def merge0_kernel(edge, usual, q0, q1, q2, q3, out, outer0, sems):
         @pl.when(edge[0] == 1)
         def _():
+            pieces = []
             for place, source in enumerate((q0, q1, q2, q3)):
                 low = place * quarter
-                inner0[low : low + quarter, :] = source[:quarter, :]
-                outer0[low : low + quarter, :] = source[quarter : 2 * quarter, :]
-                farthest[low : low + quarter, :] = source[2 * quarter :, :]
+                pieces.append((source, 0, out, low, quarter))
+                pieces.append((source, quarter, outer0, low, quarter))
+                pieces.append((source, 2 * quarter, out, rows + low, quarter))
+            copy_all(sems, pieces)
 
         @pl.when(edge[0] == 0)
         def _():
-            inner0[...] = usual[:rows, :]
-            outer0[...] = usual[rows : 2 * rows, :]
-            farthest[...] = usual[:rows, :]
-
-    hop_inner0, hop_outer0, hop_outer2 = call(
-        "merge0", merge0_kernel, [blocks(1)] * 3, (at_edge,), (early, *got0)
-    )
-    hop_sib0 = send("sibling_hop0", hop_inner0, to_sibling)
-    hop_sib2 = send("sibling_hop2", hop_outer2, to_sibling)
+            copy_all(sems, [(usual, 0, out, 0, 2 * rows), (usual, rows, outer0, 0, rows)])
+
+    hop0, hop_outer0 = move(
+        "merge0", merge0_kernel, [blocks(2), blocks(1)], (at_edge,), (early, *got0), 12
+    )
+    hop_sib0 = send("sibling_hop0", hop0, to_sibling)
 
     def near0_kernel(s, oth, nf, kf, outer0, inner0, near_in, near):
         near[...] = add_terms(
             near_in[...], oth[...], nf[:, :1], kf, s[0],
-            [(outer0[...], 7, False), (inner0[...], 6, False)],
+            [(outer0[...], 7, False), (inner0[:rows, :], 6, False)],
         )
 
     near_sum = call(
         "terms_near0", near0_kernel, total, (scale,),
-        (other, near_factor, key_factors, hop_outer0, hop_inner0, near_sum), 100_000_000,
+        (other, near_factor, key_factors, hop_outer0, hop0, near_sum), 100_000_000,
     )
 
     def far1_kernel(s, out, ff, kf, keys, farthest, far_in, far):
@@ -335,14 +372,14 @@
 
     far_sum = call(
         "terms_far1", far1_kernel, total, (scale,),
-        (outer, far_factor, key_factors, after(sib, hop_far2, near_sum), far2, far_sum),
-    )
-
-    def last_kernel(c, e, s, out, ff, kf, hs0, hs2, hf2, near_in, far_in, image_grad, caption_grad):
-        farthest = jnp.where(e[0] == 1, hs2[...], hf2[...])
+        (outer, far_factor, key_factors, after(sib, hop_far2, near_sum), far2, far_sum), 100_000_000,
+    )
+
+    def last_kernel(c, e, s, out, ff, kf, hs0, hf2, near_in, far_in, image_grad, caption_grad):
+        farthest = jnp.where(e[0] == 1, hs0[rows:, :], hf2[...])
         far = s[0] * add_terms(
             far_in[...], out[...], ff[:, :1], kf, s[0],
-            [(hs0[...], 14, False), (farthest, 15, False)],
+            [(hs0[:rows, :], 14, False), (farthest, 15, False)],
         )
         near = s[0] * near_in[...]
 
@@ -358,7 +395,7 @@
 
     image_grad, caption_grad = call(
         "terms_last", last_kernel, [total, total], (core_flag, sibling_at_edge, scale),
-        (outer, far_factor, key_factors, hop_sib0, hop_sib2, hop_far2, near_sum, far_sum),
+        (outer, far_factor, key_factors, hop_sib0, hop_far2, near_sum, far_sum),
     )
     return image_grad, caption_grad
 

time: 131 us -> 170 us (1.30)
  the two profiles are of different devices: /device:TPU:1 before, /device:TPU:483 now
where the time goes in v6:
time: 170 us; the launch traced here: 169 us
  starting transfers between devices  55.6 us (33%)
  Pallas kernels  52.1 us (31%)
  waiting for transfers between devices  45.3 us (27%)
  other arithmetic  8 us (5%)
  local copies, waits for them, and re-layouts  5.92 us (3%)
  between operations  1.82 us (1%)
    ppermute x20, starting transfers between devices, send(): return lax.ppermute(x, AXES, pairs(target))  55.6 us
    ppermute x20, waiting for transfers between devices, send(): return lax.ppermute(x, AXES, pairs(target))  45.3 us
    pallas_call x2, Pallas kernels, move(): pl.pallas_call(kernel, out_shape=out_shape, in_specs=[scalars() for _ in...  29.5 us
    pallas_call x8, Pallas kernels, call(): pl.pallas_call(kernel, out_shape=out_shape, in_specs=[scalars() for _ in...  22.5 us
    concatenate x1, other arithmetic, on_device(): jnp.concatenate([after(inner, held), outer, outer1, inner1], axis=0)  4.5 us
    unnamed x30, local copies, waits for them, and re-layouts  4.34 us
  transfers between devices with their start and end apart: 20, of which 6 were waited for; matrix products, arithmetic and copies ran while one was open for 5% of the time, Pallas kernels for 28%

profile of v6, /device:TPU:483, one launch (start us, length us, event | category | flops | bytes accessed | tf_op | source)
XLA Modules:
  0.0 168.8 jit_solution(1569896415037856396)
XLA Ops:
  0.6 1.3 broadcast_select_fusion
  2.0 2.6 %collective-permute-start = (bf16[384,768]{1,0:T(8,128)(2,1)S(1)}, bf16[384,768]{1,0:T(8,128)(2,1)S(1)}, u32[]{:S(2)}, u32[]{:S(2)}) collective-permute-start(bf16[384,768]{1,0:T(8,128)(2,1)S(1)} %get-tuple-element.90.oth.refs_4_), channel_id=1, source_target_pairs={{0,32},{1,33},{2,34},{3,35},{4,36},{5,37},{6,38},{7,39},{8,40},{9,... | collective-permute-start | bytes 1769480 | tf_op jit(solution)/shard_map/swap/ppermute | solution.py:79
  4.6 6.5 %collective-permute-start.4 = (bf16[384,768]{1,0:T(8,128)(2,1)S(1)}, bf16[384,768]{1,0:T(8,128)(2,1)}, u32[]{:S(2)}, u32[]{:S(2)}) collective-permute-start(bf16[384,768]{1,0:T(8,128)(2,1)S(1)} %get-tuple-element.91.outer.out.refs_0_), channel_id=1, source_target_pairs={{0,448},{1,449},{2,450},{3,451},{4,452},{5,453},{6,454},{7,455},{8... | collective-permute-start | bytes 1769480 | tf_op jit(solution)/shard_map/own_outer1/ppermute | solution.py:79
  11.1 1.9 %collective-permute-start.5 = (bf16[384,768]{1,0:T(8,128)(2,1)S(1)}, bf16[384,768]{1,0:T(8,128)(2,1)S(1)}, u32[]{:S(2)}, u32[]{:S(2)}) collective-permute-start(bf16[384,768]{1,0:T(8,128)(2,1)S(1)} %get-tuple-element.90.oth.refs_4_), channel_id=1, source_target_pairs={{0,96},{1,97},{2,98},{3,99},{4,100},{5,101},{6,102},{7,103},{8,104... | collective-permute-start | bytes 1769480 | tf_op jit(solution)/shard_map/own_inner1/ppermute | solution.py:79
  13.0 0.0 collective-permute-done.inner.refs_1_
  13.0 0.0 copy-start
  13.0 0.1 cut.1
  13.1 1.3 collective-permute-start.1
  14.4 1.4 collective-permute-start.2
  15.8 1.4 collective-permute-start.3
  17.9 1.2 dynamic-slice_select_fusion
  19.1 3.1 %collective-permute-done.1 = bf16[192,768]{1,0:T(8,128)(2,1)} collective-permute-done((bf16[192,768]{1,0:T(8,128)(2,1)S(1)}, bf16[192,768]{1,0:T(8,128)(2,1)}, u32[]{:S(2)}, u32[]{:S(2)}) %collective-permute-start.1) | collective-permute-done | bytes 294944 | tf_op jit(solution)/shard_map/spread0/ppermute | solution.py:79
  22.2 0.0 collective-permute-done.2
  22.2 0.0 collective-permute-done.3
  22.2 1.0 select_select_fusion
  23.2 2.4 %collective-permute-start.7 = (bf16[192,768]{1,0:T(8,128)(2,1)S(1)}, bf16[192,768]{1,0:T(8,128)(2,1)}, u32[]{:S(2)}, u32[]{:S(2)}) collective-permute-start(bf16[192,768]{1,0:T(8,128)(2,1)S(1)} %select_select_fusion), channel_id=1, source_target_pairs={{0,476},{1,477},{2,478},{3,479},{4,448},{5,449},{6,450},{7,451},{8... | collective-permute-start | bytes 884744 | tf_op jit(solution)/shard_map/cross/ppermute | solution.py:79
  25.6 0.0 collective-permute-done.4.refs_2_.outer1
  25.6 17.6 %collective-permute-done.5.refs_3_.inner1 = bf16[384,768]{1,0:T(8,128)(2,1)S(1)} collective-permute-done((bf16[384,768]{1,0:T(8,128)(2,1)S(1)}, bf16[384,768]{1,0:T(8,128)(2,1)S(1)}, u32[]{:S(2)}, u32[]{:S(2)}) %collective-permute-start.5) | collective-permute-done | bytes 589856 | tf_op jit(solution)/shard_map/own_inner1/ppermute | solution.py:79
  43.3 4.5 %pad_maximum_fusion = bf16[1536,768]{1,0:T(8,128)(2,1)S(1)} fusion(bf16[384,768]{1,0:T(8,128)(2,1)S(1)} %collective-permute-done.5.refs_3_.inner1, bf16[384,768]{1,0:T(8,128)(2,1)} %collective-permute-done.4.refs_2_.outer1, bf16[384,768]{1,0:T(8,128)(2,1)S(1)} %get-tuple-element.91.outer.out.refs_0_, bf16[384,768]{1,0:T(8,128)(2,1)S(1)} %collective-permute-done.inner.refs_1_), kind=kLoop, calls=%fused_computation | loop fusion | flops 9437184 | bytes 4718592 | tf_op jit(solution)/shard_map/concatenate | solution.py:202
  47.8 11.2 %collective-permute-start.6 = (bf16[1536,768]{1,0:T(8,128)(2,1)S(1)}, bf16[1536,768]{1,0:T(8,128)(2,1)S(1)}, u32[]{:S(2)}, u32[]{:S(2)}) collective-permute-start(bf16[1536,768]{1,0:T(8,128)(2,1)S(1)} %pad_maximum_fusion), channel_id=1, source_target_pairs={{1,0},{2,1},{3,2},{5,4},{6,5},{7,6},{9,8},{10,9},{11,10},{13,12},{... | collective-permute-start | bytes 7077896 | tf_op jit(solution)/shard_map/wide_early/ppermute | solution.py:79
  59.0 0.2 factors.1
  59.2 0.0 copy-start.1
  59.2 1.2 copy-done.1
  60.4 1.1 copy-done.3
  61.5 4.7 %terms_own0.1 = (f32[384,768]{1,0:T(8,128)S(1)}, f32[384,768]{1,0:T(8,128)S(1)}) custom-call(f32[1]{0:T(128)} %bitcast.4.s, bf16[384,768]{1,0:T(8,128)(2,1)S(1)} %copy-done.3, bf16[384,768]{1,0:T(8,128)(2,1)S(1)} %get-tuple-element.91.outer.out.refs_0_, f32[384,128]{1,0:T(8,128)S(1)} %get-tuple-element.61.nf, f32[384,128]{1,0:T(8,128)S(1)} %get-tuple-element.58.ff, ...), custom_call_target="tpu_custom_call" | custom-call | flops 99999997952 | bytes 1000 | tf_op jit(solution)/shard_map/terms_own0/pallas_call | solution.py:94
  66.2 0.0 copy-start.11
  66.2 1.0 copy-done.11
  67.2 1.0 copy-done.13
  68.2 0.0 collective-permute-done.7.q0
  68.2 16.4 %collective-permute-done.6.early.usual = bf16[1536,768]{1,0:T(8,128)(2,1)S(1)} collective-permute-done((bf16[1536,768]{1,0:T(8,128)(2,1)S(1)}, bf16[1536,768]{1,0:T(8,128)(2,1)S(1)}, u32[]{:S(2)}, u32[]{:S(2)}) %collective-permute-start.6) | collective-permute-done | bytes 2359328 | tf_op jit(solution)/shard_map/wide_early/ppermute | solution.py:79
  84.6 1.9 %collective-permute-start.8 = (bf16[192,768]{1,0:T(8,128)(2,1)}, bf16[192,768]{1,0:T(8,128)(2,1)}, u32[]{:S(2)}, u32[]{:S(2)}) collective-permute-start(bf16[192,768]{1,0:T(8,128)(2,1)} %collective-permute-done.7.q0), channel_id=1, source_target_pairs={{0,64},{1,65},{2,66},{3,67},{4,68},{5,69},{6,70},{7,71},{8,72},{9,... | collective-permute-start | bytes 884744 | tf_op jit(solution)/shard_map/cross_back/ppermute | solution.py:79
  86.5 1.6 slice.3
  88.1 10.0 %collective-permute-start.9 = (bf16[96,768]{1,0:T(8,128)(2,1)}, bf16[96,768]{1,0:T(8,128)(2,1)}, u32[]{:S(2)}, u32[]{:S(2)}) collective-permute-start(bf16[96,768]{1,0:T(8,128)(2,1)} %slice.3), channel_id=1, source_target_pairs={{0,448},{1,449},{2,450},{3,451},{4,452},{5,453},{6,454},{7,455},{8... | collective-permute-start | bytes 442376 | tf_op jit(solution)/shard_map/cross_ahead/ppermute | solution.py:79
  98.1 1.3 collective-permute-start.10
  99.4 1.3 collective-permute-start.11
  100.7 1.3 collective-permute-start.12
  102.0 0.0 collective-permute-done.9.second
  102.1 1.9 %collective-permute-start.13 = (bf16[384,768]{1,0:T(8,128)(2,1)}, bf16[384,768]{1,0:T(8,128)(2,1)}, u32[]{:S(2)}, u32[]{:S(2)}) collective-permute-start(bf16[384,768]{1,0:T(8,128)(2,1)} %collective-permute-done.4.refs_2_.outer1), channel_id=1, source_target_pairs={{0,480},{1,481},{2,482},{3,483},{4,484},{5,485},{6,486},{7,487},{8... | collective-permute-start | bytes 1769480 | tf_op jit(solution)/shard_map/own_outer2/ppermute | solution.py:79
  104.0 0.0 collective-permute-done.8.first
  104.0 1.0 join.1.q0
  105.0 2.4 %collective-permute-done.10.q1 = bf16[192,768]{1,0:T(8,128)(2,1)S(1)} collective-permute-done((bf16[192,768]{1,0:T(8,128)(2,1)}, bf16[192,768]{1,0:T(8,128)(2,1)S(1)}, u32[]{:S(2)}, u32[]{:S(2)}) %collective-permute-start.10) | collective-permute-done | bytes 294944 | tf_op jit(solution)/shard_map/gather1_1/ppermute | solution.py:79
  107.4 0.0 collective-permute-done.11.q2
  107.4 3.1 %collective-permute-done.12.q3 = bf16[192,768]{1,0:T(8,128)(2,1)S(1)} collective-permute-done((bf16[192,768]{1,0:T(8,128)(2,1)}, bf16[192,768]{1,0:T(8,128)(2,1)S(1)}, u32[]{:S(2)}, u32[]{:S(2)}) %collective-permute-start.12) | collective-permute-done | bytes 294944 | tf_op jit(solution)/shard_map/gather1_3/ppermute | solution.py:79
  110.4 1.3 collective-permute-start.14
  111.7 1.3 collective-permute-start.15
  113.0 1.3 collective-permute-start.16
  114.4 0.0 copy-start.14
  114.4 28.0 %merge1.1.keys = bf16[1536,768]{1,0:T(8,128)(2,1)} custom-call(s32[1]{0:T(128)} %bitcast.3.edge, bf16[1536,768]{1,0:T(8,128)(2,1)S(1)} %collective-permute-done.6.early.usual, bf16[384,768]{1,0:T(8,128)(2,1)} %collective-permute-done.4.refs_2_.outer1, bf16[384,768]{1,0:T(8,128)(2,1)S(1)} %collective-permute-done.5.refs_3_.inner1, ...), custom_call_target="tpu_custom_call" | custom-call | flops 1000 | bytes 1000 | tf_op jit(solution)/shard_map/merge1/pallas_call | solution.py:110
  142.4 1.9 %collective-permute-start.19 = (bf16[1536,768]{1,0:T(8,128)(2,1)}, bf16[1536,768]{1,0:T(8,128)(2,1)}, u32[]{:S(2)}, u32[]{:S(2)}) collective-permute-start(bf16[1536,768]{1,0:T(8,128)(2,1)} %merge1.1.keys), channel_id=1, source_target_pairs={{0,32},{1,33},{2,34},{3,35},{4,36},{5,37},{6,38},{7,39},{8,40},{9,... | collective-permute-start | bytes 7077896 | tf_op jit(solution)/shard_map/sibling1/ppermute | solution.py:79
  144.3 3.3 %terms_near1.1.near_in = f32[384,768]{1,0:T(8,128)S(1)} custom-call(f32[1]{0:T(128)} %bitcast.5.s, bf16[384,768]{1,0:T(8,128)(2,1)S(1)} %copy-done.4, f32[384,128]{1,0:T(8,128)S(1)} %copy-done.10, f32[16,384]{1,0:T(8,128)S(1)} %copy-done.8, bf16[1536,768]{1,0:T(8,128)(2,1)} %merge1.1.keys, f32[384,768]{1,0:T(8,128)S(1)} %copy-done.14), custom_call_target="tpu_custom_call" | custom-call | flops 99999997952 | bytes 1000 | tf_op jit(solution)/shard_map/terms_near1/pallas_call | solution.py:94
  147.7 0.0 collective-permute-done.13.farthest
  147.7 1.3 collective-permute-start.18
  149.0 0.0 collective-permute-done.14.q1
  149.0 0.0 collective-permute-done.15.q2
  149.0 0.0 collective-permute-done.16.q3
  149.0 1.5 merge0.1
  150.6 2.2 %collective-permute-start.17 = (bf16[768,768]{1,0:T(8,128)(2,1)}, bf16[768,768]{1,0:T(8,128)(2,1)}, u32[]{:S(2)}, u32[]{:S(2)}) collective-permute-start(bf16[768,768]{1,0:T(8,128)(2,1)} %get-tuple-element.70.inner0), channel_id=1, source_target_pairs={{0,32},{1,33},{2,34},{3,35},{4,36},{5,37},{6,38},{7,39},{8,40},{9,... | collective-permute-start | bytes 3538952 | tf_op jit(solution)/shard_map/sibling_hop0/ppermute | solution.py:79
  152.8 0.0 copy-start.12
  152.8 3.1 %terms_near0.1.near_in = f32[384,768]{1,0:T(8,128)S(1)} custom-call(f32[1]{0:T(128)} %bitcast.6.s, bf16[384,768]{1,0:T(8,128)(2,1)S(1)} %copy-done.4, f32[384,128]{1,0:T(8,128)S(1)} %copy-done.10, f32[16,384]{1,0:T(8,128)S(1)} %copy-done.8, bf16[384,768]{1,0:T(8,128)(2,1)S(1)} %get-tuple-element.72.outer0, bf16[768,768]{1,0:T(8,128)(2,1)} %get-tuple-element.70.inner0, ...), custom_call_target="tpu_custom_call" | custom-call | flops 99999997952 | bytes 1000 | tf_op jit(solution)/shard_map/terms_near0/pallas_call | solution.py:94
  155.9 2.6 %collective-permute-done.18.hf2 = bf16[384,768]{1,0:T(8,128)(2,1)S(1)} collective-permute-done((bf16[384,768]{1,0:T(8,128)(2,1)}, bf16[384,768]{1,0:T(8,128)(2,1)S(1)}, u32[]{:S(2)}, u32[]{:S(2)}) %collective-permute-start.18) | collective-permute-done | bytes 589856 | tf_op jit(solution)/shard_map/wide_outer2/ppermute | solution.py:79
  158.5 0.0 collective-permute-done.19.keys
  158.6 5.6 %terms_far1.1.far_in = f32[384,768]{1,0:T(8,128)S(1)} custom-call(f32[1]{0:T(128)} %bitcast.7.s, bf16[384,768]{1,0:T(8,128)(2,1)S(1)} %get-tuple-element.91.outer.out.refs_0_, f32[384,128]{1,0:T(8,128)S(1)} %copy-done.6, f32[16,384]{1,0:T(8,128)S(1)} %copy-done.8, bf16[1536,768]{1,0:T(8,128)(2,1)} %collective-permute-done.19.keys, ...), custom_call_target="tpu_custom_call" | custom-call | flops 99999997952 | bytes 1000 | tf_op jit(solution)/shard_map/terms_far1/pallas_call | solution.py:94
  164.2 0.0 collective-permute-done.17.hs0
  164.2 4.5 %terms_last.1 = (f32[384,768]{1,0:T(8,128)}, f32[384,768]{1,0:T(8,128)}) custom-call(s32[1]{0:T(128)} %bitcast.c, s32[1]{0:T(128)} %bitcast.1.e, f32[1]{0:T(128)} %bitcast.8.s, bf16[384,768]{1,0:T(8,128)(2,1)S(1)} %get-tuple-element.91.outer.out.refs_0_, f32[384,128]{1,0:T(8,128)S(1)} %copy-done.6, f32[16,384]{1,0:T(8,128)S(1)} %copy-done.8, ...), custom_call_target="tpu_custom_call" | custom-call | flops 1000 | bytes 1000 | tf_op jit(solution)/shard_map/terms_last/pallas_call | solution.py:94
  (21 shorter events, 0.0 us)
Async XLA Ops:
  2.0 41.3 %copy-start.2 = (bf16[384,768]{1,0:T(8,128)(2,1)}, bf16[384,768]{1,0:T(8,128)(2,1)S(1)}, u32[]{:S(2)}) copy-start(bf16[384,768]{1,0:T(8,128)(2,1)S(1)} %get-tuple-element.90.oth.refs_4_) | copy-start | bytes 1769476
  2.0 11.0 %collective-permute-start = (bf16[384,768]{1,0:T(8,128)(2,1)S(1)}, bf16[384,768]{1,0:T(8,128)(2,1)S(1)}, u32[]{:S(2)}, u32[]{:S(2)}) collective-permute-start(bf16[384,768]{1,0:T(8,128)(2,1)S(1)} %get-tuple-element.90.oth.refs_4_), channel_id=1, source_target_pairs={{0,32},{1,33},{2,34},{3,35},{4,36},{5,37},{6,38},{7,39},{8,40},{9,... | collective-permute-start | bytes 1769480 | tf_op jit(solution)/shard_map/swap/ppermute | solution.py:79
  4.6 21.0 %collective-permute-start.4 = (bf16[384,768]{1,0:T(8,128)(2,1)S(1)}, bf16[384,768]{1,0:T(8,128)(2,1)}, u32[]{:S(2)}, u32[]{:S(2)}) collective-permute-start(bf16[384,768]{1,0:T(8,128)(2,1)S(1)} %get-tuple-element.91.outer.out.refs_0_), channel_id=1, source_target_pairs={{0,448},{1,449},{2,450},{3,451},{4,452},{5,453},{6,454},{7,455},{8... | collective-permute-start | bytes 1769480 | tf_op jit(solution)/shard_map/own_outer1/ppermute | solution.py:79
  11.1 32.2 %collective-permute-start.5 = (bf16[384,768]{1,0:T(8,128)(2,1)S(1)}, bf16[384,768]{1,0:T(8,128)(2,1)S(1)}, u32[]{:S(2)}, u32[]{:S(2)}) collective-permute-start(bf16[384,768]{1,0:T(8,128)(2,1)S(1)} %get-tuple-element.90.oth.refs_4_), channel_id=1, source_target_pairs={{0,96},{1,97},{2,98},{3,99},{4,100},{5,101},{6,102},{7,103},{8,104... | collective-permute-start | bytes 1769480 | tf_op jit(solution)/shard_map/own_inner1/ppermute | solution.py:79
  13.0 30.2 %copy-start = (bf16[384,768]{1,0:T(8,128)(2,1)}, bf16[384,768]{1,0:T(8,128)(2,1)S(1)}, u32[]{:S(2)}) copy-start(bf16[384,768]{1,0:T(8,128)(2,1)S(1)} %collective-permute-done.inner.refs_1_) | copy-start | bytes 1769476
  13.1 9.1 %collective-permute-start.1 = (bf16[192,768]{1,0:T(8,128)(2,1)S(1)}, bf16[192,768]{1,0:T(8,128)(2,1)}, u32[]{:S(2)}, u32[]{:S(2)}) collective-permute-start(bf16[192,768]{1,0:T(8,128)(2,1)S(1)} %get-tuple-element.38), channel_id=1, source_target_pairs={{0,3},{4,7},{8,11},{12,15},{16,19},{20,23},{24,27},{28,31},{35,32}... | collective-permute-start | bytes 884744 | tf_op jit(solution)/shard_map/spread0/ppermute | solution.py:79
  14.4 7.8 %collective-permute-start.2 = (bf16[192,768]{1,0:T(8,128)(2,1)S(1)}, bf16[192,768]{1,0:T(8,128)(2,1)}, u32[]{:S(2)}, u32[]{:S(2)}) collective-permute-start(bf16[192,768]{1,0:T(8,128)(2,1)S(1)} %get-tuple-element.39), channel_id=1, source_target_pairs={{0,1},{4,5},{8,9},{12,13},{16,17},{20,21},{24,25},{28,29},{35,34},... | collective-permute-start | bytes 884744 | tf_op jit(solution)/shard_map/spread1/ppermute | solution.py:79
  15.8 6.4 %collective-permute-start.3 = (bf16[192,768]{1,0:T(8,128)(2,1)S(1)}, bf16[192,768]{1,0:T(8,128)(2,1)}, u32[]{:S(2)}, u32[]{:S(2)}) collective-permute-start(bf16[192,768]{1,0:T(8,128)(2,1)S(1)} %get-tuple-element.40), channel_id=1, source_target_pairs={{0,2},{4,6},{8,10},{12,14},{16,18},{20,22},{24,26},{28,30},{35,33}... | collective-permute-start | bytes 884744 | tf_op jit(solution)/shard_map/spread2/ppermute | solution.py:79
  23.2 45.0 %collective-permute-start.7 = (bf16[192,768]{1,0:T(8,128)(2,1)S(1)}, bf16[192,768]{1,0:T(8,128)(2,1)}, u32[]{:S(2)}, u32[]{:S(2)}) collective-permute-start(bf16[192,768]{1,0:T(8,128)(2,1)S(1)} %select_select_fusion), channel_id=1, source_target_pairs={{0,476},{1,477},{2,478},{3,479},{4,448},{5,449},{6,450},{7,451},{8... | collective-permute-start | bytes 884744 | tf_op jit(solution)/shard_map/cross/ppermute | solution.py:79
  47.8 36.8 %collective-permute-start.6 = (bf16[1536,768]{1,0:T(8,128)(2,1)S(1)}, bf16[1536,768]{1,0:T(8,128)(2,1)S(1)}, u32[]{:S(2)}, u32[]{:S(2)}) collective-permute-start(bf16[1536,768]{1,0:T(8,128)(2,1)S(1)} %pad_maximum_fusion), channel_id=1, source_target_pairs={{1,0},{2,1},{3,2},{5,4},{6,5},{7,6},{9,8},{10,9},{11,10},{13,12},{... | collective-permute-start | bytes 7077896 | tf_op jit(solution)/shard_map/wide_early/ppermute | solution.py:79
  59.2 7.0 %copy-start.5 = (f32[384,128]{1,0:T(8,128)}, f32[384,128]{1,0:T(8,128)S(1)}, u32[]{:S(2)}) copy-start(f32[384,128]{1,0:T(8,128)S(1)} %get-tuple-element.58.ff) | copy-start | bytes 589828
  59.2 7.0 %copy-start.7 = (f32[16,384]{1,0:T(8,128)}, f32[16,384]{1,0:T(8,128)S(1)}, u32[]{:S(2)}) copy-start(f32[16,384]{1,0:T(8,128)S(1)} %get-tuple-element.59.kf) | copy-start | bytes 73732
  59.2 7.0 %copy-start.9 = (f32[384,128]{1,0:T(8,128)}, f32[384,128]{1,0:T(8,128)S(1)}, u32[]{:S(2)}) copy-start(f32[384,128]{1,0:T(8,128)S(1)} %get-tuple-element.61.nf) | copy-start | bytes 589828
  59.2 1.2 copy-start.1
  60.4 1.1 copy-start.3
  66.2 1.0 copy-start.11
  67.2 1.0 copy-start.13
  84.6 19.3 %collective-permute-start.8 = (bf16[192,768]{1,0:T(8,128)(2,1)}, bf16[192,768]{1,0:T(8,128)(2,1)}, u32[]{:S(2)}, u32[]{:S(2)}) collective-permute-start(bf16[192,768]{1,0:T(8,128)(2,1)} %collective-permute-done.7.q0), channel_id=1, source_target_pairs={{0,64},{1,65},{2,66},{3,67},{4,68},{5,69},{6,70},{7,71},{8,72},{9,... | collective-permute-start | bytes 884744 | tf_op jit(solution)/shard_map/cross_back/ppermute | solution.py:79
  88.1 13.9 %collective-permute-start.9 = (bf16[96,768]{1,0:T(8,128)(2,1)}, bf16[96,768]{1,0:T(8,128)(2,1)}, u32[]{:S(2)}, u32[]{:S(2)}) collective-permute-start(bf16[96,768]{1,0:T(8,128)(2,1)} %slice.3), channel_id=1, source_target_pairs={{0,448},{1,449},{2,450},{3,451},{4,452},{5,453},{6,454},{7,455},{8... | collective-permute-start | bytes 442376 | tf_op jit(solution)/shard_map/cross_ahead/ppermute | solution.py:79
  98.1 9.3 %collective-permute-start.10 = (bf16[192,768]{1,0:T(8,128)(2,1)}, bf16[192,768]{1,0:T(8,128)(2,1)S(1)}, u32[]{:S(2)}, u32[]{:S(2)}) collective-permute-start(bf16[192,768]{1,0:T(8,128)(2,1)} %collective-permute-done.7.q0), channel_id=1, source_target_pairs={{1,3},{5,7},{9,11},{13,15},{17,19},{21,23},{25,27},{29,31},{34,32}... | collective-permute-start | bytes 884744 | tf_op jit(solution)/shard_map/gather1_1/ppermute | solution.py:79
  99.4 8.0 %collective-permute-start.11 = (bf16[192,768]{1,0:T(8,128)(2,1)}, bf16[192,768]{1,0:T(8,128)(2,1)S(1)}, u32[]{:S(2)}, u32[]{:S(2)}) collective-permute-start(bf16[192,768]{1,0:T(8,128)(2,1)} %collective-permute-done.7.q0), channel_id=1, source_target_pairs={{2,3},{6,7},{10,11},{14,15},{18,19},{22,23},{26,27},{30,31},{33,32... | collective-permute-start | bytes 884744 | tf_op jit(solution)/shard_map/gather1_2/ppermute | solution.py:79
  100.7 9.7 %collective-permute-start.12 = (bf16[192,768]{1,0:T(8,128)(2,1)}, bf16[192,768]{1,0:T(8,128)(2,1)S(1)}, u32[]{:S(2)}, u32[]{:S(2)}) collective-permute-start(bf16[192,768]{1,0:T(8,128)(2,1)} %collective-permute-done.7.q0), channel_id=1, source_target_pairs={{0,3},{4,7},{8,11},{12,15},{16,19},{20,23},{24,27},{28,31},{35,32}... | collective-permute-start | bytes 884744 | tf_op jit(solution)/shard_map/gather1_3/ppermute | solution.py:79
  102.1 45.6 %collective-permute-start.13 = (bf16[384,768]{1,0:T(8,128)(2,1)}, bf16[384,768]{1,0:T(8,128)(2,1)}, u32[]{:S(2)}, u32[]{:S(2)}) collective-permute-start(bf16[384,768]{1,0:T(8,128)(2,1)} %collective-permute-done.4.refs_2_.outer1), channel_id=1, source_target_pairs={{0,480},{1,481},{2,482},{3,483},{4,484},{5,485},{6,486},{7,487},{8... | collective-permute-start | bytes 1769480 | tf_op jit(solution)/shard_map/own_outer2/ppermute | solution.py:79
  110.4 38.6 %collective-permute-start.14 = (bf16[288,768]{1,0:T(8,128)(2,1)S(1)}, bf16[288,768]{1,0:T(8,128)(2,1)S(1)}, u32[]{:S(2)}, u32[]{:S(2)}) collective-permute-start(bf16[288,768]{1,0:T(8,128)(2,1)S(1)} %join.1.q0), channel_id=1, source_target_pairs={{1,3},{5,7},{9,11},{13,15},{17,19},{21,23},{25,27},{29,31},{34,32}... | collective-permute-start | bytes 1327112 | tf_op jit(solution)/shard_map/gather0_1/ppermute | solution.py:79
  111.7 37.3 %collective-permute-start.15 = (bf16[288,768]{1,0:T(8,128)(2,1)S(1)}, bf16[288,768]{1,0:T(8,128)(2,1)S(1)}, u32[]{:S(2)}, u32[]{:S(2)}) collective-permute-start(bf16[288,768]{1,0:T(8,128)(2,1)S(1)} %join.1.q0), channel_id=1, source_target_pairs={{2,3},{6,7},{10,11},{14,15},{18,19},{22,23},{26,27},{30,31},{33,32... | collective-permute-start | bytes 1327112 | tf_op jit(solution)/shard_map/gather0_2/ppermute | solution.py:79
  113.0 36.0 %collective-permute-start.16 = (bf16[288,768]{1,0:T(8,128)(2,1)S(1)}, bf16[288,768]{1,0:T(8,128)(2,1)S(1)}, u32[]{:S(2)}, u32[]{:S(2)}) collective-permute-start(bf16[288,768]{1,0:T(8,128)(2,1)S(1)} %join.1.q0), channel_id=1, source_target_pairs={{0,3},{4,7},{8,11},{12,15},{16,19},{20,23},{24,27},{28,31},{35,32}... | collective-permute-start | bytes 1327112 | tf_op jit(solution)/shard_map/gather0_3/ppermute | solution.py:79
  114.3 30.0 %copy-start.4 = (bf16[384,768]{1,0:T(8,128)(2,1)S(1)}, bf16[384,768]{1,0:T(8,128)(2,1)}, u32[]{:S(2)}) copy-start(bf16[384,768]{1,0:T(8,128)(2,1)} %copy-done.2) | copy-start | bytes 1769476
  114.3 30.0 %copy-start.8 = (f32[16,384]{1,0:T(8,128)S(1)}, f32[16,384]{1,0:T(8,128)}, u32[]{:S(2)}) copy-start(f32[16,384]{1,0:T(8,128)} %copy-done.7) | copy-start | bytes 73732
  114.4 30.0 %copy-start.10 = (f32[384,128]{1,0:T(8,128)S(1)}, f32[384,128]{1,0:T(8,128)}, u32[]{:S(2)}) copy-start(f32[384,128]{1,0:T(8,128)} %copy-done.9) | copy-start | bytes 589828
  114.4 30.0 %copy-start.14 = (f32[384,768]{1,0:T(8,128)S(1)}, f32[384,768]{1,0:T(8,128)}, u32[]{:S(2)}) copy-start(f32[384,768]{1,0:T(8,128)} %copy-done.13) | copy-start | bytes 3538948
  142.4 16.2 %collective-permute-start.19 = (bf16[1536,768]{1,0:T(8,128)(2,1)}, bf16[1536,768]{1,0:T(8,128)(2,1)}, u32[]{:S(2)}, u32[]{:S(2)}) collective-permute-start(bf16[1536,768]{1,0:T(8,128)(2,1)} %merge1.1.keys), channel_id=1, source_target_pairs={{0,32},{1,33},{2,34},{3,35},{4,36},{5,37},{6,38},{7,39},{8,40},{9,... | collective-permute-start | bytes 7077896 | tf_op jit(solution)/shard_map/sibling1/ppermute | solution.py:79
  147.7 10.8 %collective-permute-start.18 = (bf16[384,768]{1,0:T(8,128)(2,1)}, bf16[384,768]{1,0:T(8,128)(2,1)S(1)}, u32[]{:S(2)}, u32[]{:S(2)}) collective-permute-start(bf16[384,768]{1,0:T(8,128)(2,1)} %collective-permute-done.13.farthest), channel_id=1, source_target_pairs={{0,1},{1,2},{2,3},{4,5},{5,6},{6,7},{8,9},{9,10},{10,11},{12,13},{... | collective-permute-start | bytes 1769480 | tf_op jit(solution)/shard_map/wide_outer2/ppermute | solution.py:79
  150.6 13.6 %collective-permute-start.17 = (bf16[768,768]{1,0:T(8,128)(2,1)}, bf16[768,768]{1,0:T(8,128)(2,1)}, u32[]{:S(2)}, u32[]{:S(2)}) collective-permute-start(bf16[768,768]{1,0:T(8,128)(2,1)} %get-tuple-element.70.inner0), channel_id=1, source_target_pairs={{0,32},{1,33},{2,34},{3,35},{4,36},{5,37},{6,38},{7,39},{8,40},{9,... | collective-permute-start | bytes 3538952 | tf_op jit(solution)/shard_map/sibling_hop0/ppermute | solution.py:79
  152.8 5.7 %copy-start.6 = (f32[384,128]{1,0:T(8,128)S(1)}, f32[384,128]{1,0:T(8,128)}, u32[]{:S(2)}) copy-start(f32[384,128]{1,0:T(8,128)} %copy-done.5) | copy-start | bytes 589828
  152.8 5.7 %copy-start.12 = (f32[384,768]{1,0:T(8,128)S(1)}, f32[384,768]{1,0:T(8,128)}, u32[]{:S(2)}) copy-start(f32[384,768]{1,0:T(8,128)} %copy-done.11) | copy-start | bytes 3538948

commit v7 on v5

--- a/solution.py
+++ b/solution.py
@@ -171,8 +171,9 @@
     )
     crossed = send("cross", held, across)
     early = send(
-        "wide_early", jnp.concatenate([after(inner, held), outer, outer1, inner1], axis=0), to_next_wide
-    )
+        "wide_early", jnp.concatenate([after(inner, held), outer, outer1], axis=0), to_next_wide
+    )
+
     batch = row_lse.shape[0]
 
     def part(carried, b, w):
@@ -243,11 +244,22 @@
             (other, outer, near_factor, far_factor, key_factors, *arrays, *(sums or ())), weight,
         )
 
-    sums = terms("terms_own0", [(outer, [0]), (inner, [1]), (after(outer1, held), [2]), (inner1, [3])], [(other, [8])], None, 100_000_000)
-    crossed = after(crossed, *sums)
+    sums = terms("terms_own0", [(outer, [0]), (inner, [1]), (after(outer1, held), [2])], [(other, [8])], None, 100_000_000)
+    inner1 = after(inner1, *sums)
+    late = send("wide_late", inner1, to_next_wide)
+
+    def slice_kernel(block, out):
+        out[...] = block[quarter:, :]
+
+    outer_part = call(
+        "slice", slice_kernel, jax.ShapeDtypeStruct((quarter, width), half), (), (crossed,),
+        100_000_000,
+    )
+    late, early, outer_part = lax.optimization_barrier((late, early, outer_part))
+    crossed = after(crossed, outer_part)
 
     back = send("cross_back", crossed, to_previous_chip)
-    ahead = send("cross_ahead", crossed[quarter:], to_next_chip)
+    ahead = send("cross_ahead", outer_part, to_next_chip)
 
     def collect(name, mine):
         q1 = send(name + "1", mine, line_to_line(2, 0))
@@ -257,9 +269,18 @@
 
     got1 = collect("gather1_", crossed)
     far2 = send("own_outer2", after(outer1, crossed), to_next_chip_sibling)
-    got0 = collect("gather0_", after(jnp.concatenate([back, ahead], axis=0), *got1))
-
-    def merge1_kernel(edge, early, outer1, inner1, q0, q1, q2, q3, out):
+
+    def join_kernel(first, second, out):
+        out[: 2 * quarter, :] = first[...]
+        out[2 * quarter :, :] = second[...]
+
+    joined = call(
+        "join", join_kernel, jax.ShapeDtypeStruct((3 * quarter, width), half), (),
+        (back, ahead), 100_000_000,
+    )
+    got0 = collect("gather0_", after(joined, *got1))
+
+    def merge1_kernel(edge, early, late, outer1, inner1, q0, q1, q2, q3, out):
         @pl.when(edge[0] == 1)
         def _():
             for place, source in enumerate((q0, q1, q2, q3)):
@@ -269,13 +290,15 @@
 
         @pl.when(edge[0] == 0)
         def _():
-            out[: 2 * rows, :] = early[2 * rows :, :]
+            out[:rows, :] = early[2 * rows :, :]
+            out[rows : 2 * rows, :] = late[...]
 
         out[2 * rows : 3 * rows, :] = outer1[...]
         out[3 * rows :, :] = inner1[...]
 
     carried = call(
-        "merge1", merge1_kernel, blocks(4), (at_edge,), (early, after(outer1, back, ahead), inner1, *got1)
+        "merge1", merge1_kernel, blocks(4), (at_edge,),
+        (early, late, after(outer1, back, ahead), inner1, *got1),
     )
     sib = send("sibling1", carried, to_sibling)
     hop_far2 = send("wide_outer2", after(far2, carried), to_sibling_next_wide)
@@ -284,7 +307,8 @@
     def near_kernel(s, oth, nf, kf, keys, near_in, near):
         near[...] = add_terms(
             near_in[...], oth[...], nf[:, :1], kf, s[0],
-            [(keys[:rows, :], 4, False), (keys[rows : 2 * rows, :], 5, False)],
+            [(keys[:rows, :], 4, False), (keys[rows : 2 * rows, :], 5, False),
+             (keys[3 * rows :, :], 3, False)],
         )
 
     near_sum = call(
@@ -294,36 +318,34 @@
 
     got0 = [after(got0[0], far2, near_sum), *got0[1:]]
 
-    def merge0_kernel(edge, usual, q0, q1, q2, q3, inner0, outer0, farthest):
+    def merge0_kernel(edge, usual, q0, q1, q2, q3, out, outer0):
         @pl.when(edge[0] == 1)
         def _():
             for place, source in enumerate((q0, q1, q2, q3)):
                 low = place * quarter
-                inner0[low : low + quarter, :] = source[:quarter, :]
+                out[low : low + quarter, :] = source[:quarter, :]
                 outer0[low : low + quarter, :] = source[quarter : 2 * quarter, :]
-                farthest[low : low + quarter, :] = source[2 * quarter :, :]
+                out[rows + low : rows + low + quarter, :] = source[2 * quarter :, :]
 
         @pl.when(edge[0] == 0)
         def _():
-            inner0[...] = usual[:rows, :]
+            out[...] = usual[: 2 * rows, :]
             outer0[...] = usual[rows : 2 * rows, :]
-            farthest[...] = usual[:rows, :]
-
-    hop_inner0, hop_outer0, hop_outer2 = call(
-        "merge0", merge0_kernel, [blocks(1)] * 3, (at_edge,), (early, *got0)
-    )
-    hop_sib0 = send("sibling_hop0", hop_inner0, to_sibling)
-    hop_sib2 = send("sibling_hop2", hop_outer2, to_sibling)
+
+    hop0, hop_outer0 = call(
+        "merge0", merge0_kernel, [blocks(2), blocks(1)], (at_edge,), (early, *got0)
+    )
+    hop_sib0 = send("sibling_hop0", hop0, to_sibling)
 
     def near0_kernel(s, oth, nf, kf, outer0, inner0, near_in, near):
         near[...] = add_terms(
             near_in[...], oth[...], nf[:, :1], kf, s[0],
-            [(outer0[...], 7, False), (inner0[...], 6, False)],
+            [(outer0[...], 7, False), (inner0[:rows, :], 6, False)],
         )
 
     near_sum = call(
         "terms_near0", near0_kernel, total, (scale,),
-        (other, near_factor, key_factors, hop_outer0, hop_inner0, near_sum), 100_000_000,
+        (other, near_factor, key_factors, hop_outer0, hop0, near_sum), 100_000_000,
     )
 
     def far1_kernel(s, out, ff, kf, keys, farthest, far_in, far):
@@ -335,14 +357,14 @@
 
     far_sum = call(
         "terms_far1", far1_kernel, total, (scale,),
-        (outer, far_factor, key_factors, after(sib, hop_far2, near_sum), far2, far_sum),
-    )
-
-    def last_kernel(c, e, s, out, ff, kf, hs0, hs2, hf2, near_in, far_in, image_grad, caption_grad):
-        farthest = jnp.where(e[0] == 1, hs2[...], hf2[...])
+        (outer, far_factor, key_factors, after(sib, hop_far2, near_sum), far2, far_sum), 100_000_000,
+    )
+
+    def last_kernel(c, e, s, out, ff, kf, hs0, hf2, near_in, far_in, image_grad, caption_grad):
+        farthest = jnp.where(e[0] == 1, hs0[rows:, :], hf2[...])
         far = s[0] * add_terms(
             far_in[...], out[...], ff[:, :1], kf, s[0],
-            [(hs0[...], 14, False), (farthest, 15, False)],
+            [(hs0[:rows, :], 14, False), (farthest, 15, False)],
         )
         near = s[0] * near_in[...]
 
@@ -358,7 +380,7 @@
 
     image_grad, caption_grad = call(
         "terms_last", last_kernel, [total, total], (core_flag, sibling_at_edge, scale),
-        (outer, far_factor, key_factors, hop_sib0, hop_sib2, hop_far2, near_sum, far_sum),
+        (outer, far_factor, key_factors, hop_sib0, hop_far2, near_sum, far_sum),
     )
     return image_grad, caption_grad
 

time: 131 us -> 135 us (1.031)
  waiting for transfers between devices: 15.7 us -> 27.2 us
  local copies, waits for them, and re-layouts: 8.2 us -> 0.05 us
  Pallas kernels: 21.7 us -> 27.7 us
  starting transfers between devices: 76.4 us -> 70.6 us
    ppermute x21, waiting for transfers between devices: 15.7 us -> 27.2 us  [send(): return lax.ppermute(x, AXES, pairs(target))]
    unnamed x36 -> x20, local copies, waits for them, and re-layouts: 7.28 us -> 0.05 us
    pallas_call x9 -> x11, Pallas kernels: 21.7 us -> 27.7 us  [call(): pl.pallas_call(kernel, out_shape=out_shape, in_specs=[scalars() for _ in...]
    ppermute x21, starting transfers between devices: 76.4 us -> 70.6 us  [send(): return lax.ppermute(x, AXES, pairs(target))]
  transfers between devices with their start and end apart: 21 -> 21, of which waited for: 6 -> 2; matrix products, arithmetic and copies ran while one was open for 4% -> 3% of each run, Pallas kernels for 14% -> 17%
where the time goes in v7:
time: 135 us; the launch traced here: 134 us
  starting transfers between devices  70.6 us (52%)
  Pallas kernels  27.7 us (21%)
  waiting for transfers between devices  27.2 us (20%)
  other arithmetic  5.93 us (4%)
  between operations  2.1 us (2%)
    ppermute x21, starting transfers between devices, send(): return lax.ppermute(x, AXES, pairs(target))  70.6 us
    pallas_call x11, Pallas kernels, call(): pl.pallas_call(kernel, out_shape=out_shape, in_specs=[scalars() for _ in...  27.7 us
    ppermute x21, waiting for transfers between devices, send(): return lax.ppermute(x, AXES, pairs(target))  27.2 us
  transfers between devices with their start and end apart: 21, of which 2 were waited for; matrix products, arithmetic and copies ran while one was open for 3% of the time, Pallas kernels for 17%

profile of v7, /device:TPU:1, one launch (start us, length us, event | category | flops | bytes accessed | tf_op | source)
XLA Modules:
  0.0 133.6 jit_solution(16020359241703744705)
XLA Ops:
  0.6 1.3 broadcast_select_fusion
  2.0 8.8 %collective-permute-start = (bf16[384,768]{1,0:T(8,128)(2,1)S(1)}, bf16[384,768]{1,0:T(8,128)(2,1)S(1)}, u32[]{:S(2)}, u32[]{:S(2)}) collective-permute-start(bf16[384,768]{1,0:T(8,128)(2,1)S(1)} %get-tuple-element.98.oth.refs_3_), channel_id=1, source_target_pairs={{0,32},{1,33},{2,34},{3,35},{4,36},{5,37},{6,38},{7,39},{8,40},{9,... | collective-permute-start | bytes 1769480 | tf_op jit(solution)/shard_map/swap/ppermute | solution.py:79
  10.8 1.9 %collective-permute-start.5 = (bf16[384,768]{1,0:T(8,128)(2,1)S(1)}, bf16[384,768]{1,0:T(8,128)(2,1)}, u32[]{:S(2)}, u32[]{:S(2)}) collective-permute-start(bf16[384,768]{1,0:T(8,128)(2,1)S(1)} %get-tuple-element.99.outer.out.refs_0_), channel_id=1, source_target_pairs={{0,448},{1,449},{2,450},{3,451},{4,452},{5,453},{6,454},{7,455},{8... | collective-permute-start | bytes 1769480 | tf_op jit(solution)/shard_map/own_outer1/ppermute | solution.py:79
  12.7 0.0 collective-permute-done.inner.refs_1_
  12.7 0.1 cut.1
  12.8 1.3 collective-permute-start.1
  14.1 1.4 %collective-permute-start.2 = (bf16[192,768]{1,0:T(8,128)(2,1)S(1)}, bf16[192,768]{1,0:T(8,128)(2,1)}, u32[]{:S(2)}, u32[]{:S(2)}) collective-permute-start(bf16[192,768]{1,0:T(8,128)(2,1)S(1)} %get-tuple-element.43), channel_id=1, source_target_pairs={{0,1},{4,5},{8,9},{12,13},{16,17},{20,21},{24,25},{28,29},{35,34},... | collective-permute-start | bytes 884744 | tf_op jit(solution)/shard_map/spread1/ppermute | solution.py:79
  15.5 1.4 %collective-permute-start.3 = (bf16[192,768]{1,0:T(8,128)(2,1)S(1)}, bf16[192,768]{1,0:T(8,128)(2,1)}, u32[]{:S(2)}, u32[]{:S(2)}) collective-permute-start(bf16[192,768]{1,0:T(8,128)(2,1)S(1)} %get-tuple-element.44), channel_id=1, source_target_pairs={{0,2},{4,6},{8,10},{12,14},{16,18},{20,22},{24,26},{28,30},{35,33}... | collective-permute-start | bytes 884744 | tf_op jit(solution)/shard_map/spread2/ppermute | solution.py:79
  16.8 13.1 %collective-permute-start.4 = (bf16[384,768]{1,0:T(8,128)(2,1)S(1)}, bf16[384,768]{1,0:T(8,128)(2,1)S(1)}, u32[]{:S(2)}, u32[]{:S(2)}) collective-permute-start(bf16[384,768]{1,0:T(8,128)(2,1)S(1)} %get-tuple-element.98.oth.refs_3_), channel_id=1, source_target_pairs={{0,96},{1,97},{2,98},{3,99},{4,100},{5,101},{6,102},{7,103},{8,104... | collective-permute-start | bytes 1769480 | tf_op jit(solution)/shard_map/own_inner1/ppermute | solution.py:79
  30.9 1.2 dynamic-slice_select_fusion
  32.0 0.0 collective-permute-done.1
  32.1 0.0 collective-permute-done.2
  32.1 0.0 collective-permute-done.3
  32.1 1.0 select_select_fusion
  33.1 8.4 %collective-permute-start.8 = (bf16[192,768]{1,0:T(8,128)(2,1)S(1)}, bf16[192,768]{1,0:T(8,128)(2,1)S(1)}, u32[]{:S(2)}, u32[]{:S(2)}) collective-permute-start(bf16[192,768]{1,0:T(8,128)(2,1)S(1)} %select_select_fusion), channel_id=1, source_target_pairs={{0,476},{1,477},{2,478},{3,479},{4,448},{5,449},{6,450},{7,451},{8... | collective-permute-start | bytes 884744 | tf_op jit(solution)/shard_map/cross/ppermute | solution.py:79
  41.5 0.0 collective-permute-done.5.refs_2_.outer1
  41.5 2.4 %pad_maximum_fusion = bf16[1152,768]{1,0:T(8,128)(2,1)} fusion(bf16[384,768]{1,0:T(8,128)(2,1)} %collective-permute-done.5.refs_2_.outer1, bf16[384,768]{1,0:T(8,128)(2,1)S(1)} %get-tuple-element.99.outer.out.refs_0_, bf16[384,768]{1,0:T(8,128)(2,1)S(1)} %collective-permute-done.inner.refs_1_), kind=kLoop, calls=%fused_computation | loop fusion | flops 5308416 | bytes 3538944 | tf_op jit(solution)/shard_map/concatenate | solution.py:174
  44.0 2.5 %collective-permute-start.7 = (bf16[1152,768]{1,0:T(8,128)(2,1)}, bf16[1152,768]{1,0:T(8,128)(2,1)}, u32[]{:S(2)}, u32[]{:S(2)}) collective-permute-start(bf16[1152,768]{1,0:T(8,128)(2,1)} %pad_maximum_fusion), channel_id=1, source_target_pairs={{1,0},{2,1},{3,2},{5,4},{6,5},{7,6},{9,8},{10,9},{11,10},{13,12},{... | collective-permute-start | bytes 5308424 | tf_op jit(solution)/shard_map/wide_early/ppermute | solution.py:79
  46.5 0.2 factors.1
  46.7 4.2 %terms_own0.1 = (f32[384,768]{1,0:T(8,128)S(1)}, f32[384,768]{1,0:T(8,128)S(1)}) custom-call(f32[1]{0:T(128)} %bitcast.4.s, bf16[384,768]{1,0:T(8,128)(2,1)S(1)} %get-tuple-element.98.oth.refs_3_, bf16[384,768]{1,0:T(8,128)(2,1)S(1)} %get-tuple-element.99.outer.out.refs_0_, f32[384,128]{1,0:T(8,128)S(1)} %get-tuple-element.64.nf, ...), custom_call_target="tpu_custom_call" | custom-call | flops 99999997952 | bytes 1000 | tf_op jit(solution)/shard_map/terms_own0/pallas_call | solution.py:94
  51.0 0.0 copy-done
  51.0 0.0 copy-done.2
  51.0 0.0 copy-done.4
  51.0 0.0 copy-start.6
  51.0 0.0 copy-start.8
  51.0 0.0 collective-permute-done.4.inner1
  51.0 1.3 collective-permute-start.6
  52.4 0.0 collective-permute-done.8.block.q0
  52.4 18.8 %collective-permute-done.6.late = bf16[384,768]{1,0:T(8,128)(2,1)S(1)} collective-permute-done((bf16[384,768]{1,0:T(8,128)(2,1)S(1)}, bf16[384,768]{1,0:T(8,128)(2,1)S(1)}, u32[]{:S(2)}, u32[]{:S(2)}) %collective-permute-start.6) | collective-permute-done | bytes 589856 | tf_op jit(solution)/shard_map/wide_late/ppermute | solution.py:79
  71.2 0.0 collective-permute-done.7.early.usual
  71.2 2.6 %collective-permute-start.9 = (bf16[192,768]{1,0:T(8,128)(2,1)S(1)}, bf16[192,768]{1,0:T(8,128)(2,1)S(1)}, u32[]{:S(2)}, u32[]{:S(2)}) collective-permute-start(bf16[192,768]{1,0:T(8,128)(2,1)S(1)} %collective-permute-done.8.block.q0), channel_id=1, source_target_pairs={{0,64},{1,65},{2,66},{3,67},{4,68},{5,69},{6,70},{7,71},{8,72},{9,... | collective-permute-start | bytes 884744 | tf_op jit(solution)/shard_map/cross_back/ppermute | solution.py:79
  73.8 2.7 %collective-permute-start.10 = (bf16[96,768]{1,0:T(8,128)(2,1)S(1)}, bf16[96,768]{1,0:T(8,128)(2,1)S(1)}, u32[]{:S(2)}, u32[]{:S(2)}) collective-permute-start(bf16[96,768]{1,0:T(8,128)(2,1)S(1)} %slice.1), channel_id=1, source_target_pairs={{0,448},{1,449},{2,450},{3,451},{4,452},{5,453},{6,454},{7,455},{8... | collective-permute-start | bytes 442376 | tf_op jit(solution)/shard_map/cross_ahead/ppermute | solution.py:79
  76.5 1.3 collective-permute-start.11
  77.8 1.3 collective-permute-start.12
  79.1 1.3 collective-permute-start.13
  80.4 8.3 %collective-permute-done.10.second = bf16[96,768]{1,0:T(8,128)(2,1)S(1)} collective-permute-done((bf16[96,768]{1,0:T(8,128)(2,1)S(1)}, bf16[96,768]{1,0:T(8,128)(2,1)S(1)}, u32[]{:S(2)}, u32[]{:S(2)}) %collective-permute-start.10) | collective-permute-done | bytes 147488 | tf_op jit(solution)/shard_map/cross_ahead/ppermute | solution.py:79
  88.7 3.7 %collective-permute-start.14 = (bf16[384,768]{1,0:T(8,128)(2,1)}, bf16[384,768]{1,0:T(8,128)(2,1)}, u32[]{:S(2)}, u32[]{:S(2)}) collective-permute-start(bf16[384,768]{1,0:T(8,128)(2,1)} %collective-permute-done.5.refs_2_.outer1), channel_id=1, source_target_pairs={{0,480},{1,481},{2,482},{3,483},{4,484},{5,485},{6,486},{7,487},{8... | collective-permute-start | bytes 1769480 | tf_op jit(solution)/shard_map/own_outer2/ppermute | solution.py:79
  92.5 0.0 collective-permute-done.9.first
  92.5 0.0 collective-permute-done.11.q1
  92.5 0.0 collective-permute-done.12.q2
  92.5 0.0 collective-permute-done.13.q3
  92.5 1.3 collective-permute-start.15
  93.8 1.3 collective-permute-start.16
  95.1 1.3 collective-permute-start.17
  96.4 0.0 copy-start.3
  96.5 0.0 copy-start.5
  96.5 0.0 copy-start.9
  96.5 3.3 %merge1.1.keys = bf16[1536,768]{1,0:T(8,128)(2,1)} custom-call(s32[1]{0:T(128)} %bitcast.3.edge, bf16[1152,768]{1,0:T(8,128)(2,1)} %collective-permute-done.7.early.usual, bf16[384,768]{1,0:T(8,128)(2,1)S(1)} %collective-permute-done.6.late, bf16[384,768]{1,0:T(8,128)(2,1)} %collective-permute-done.5.refs_2_.outer1, ...), custom_call_target="tpu_custom_call" | custom-call | flops 1000 | bytes 1000 | tf_op jit(solution)/shard_map/merge1/pallas_call | solution.py:94
  99.8 8.6 %collective-permute-start.20 = (bf16[1536,768]{1,0:T(8,128)(2,1)}, bf16[1536,768]{1,0:T(8,128)(2,1)}, u32[]{:S(2)}, u32[]{:S(2)}) collective-permute-start(bf16[1536,768]{1,0:T(8,128)(2,1)} %merge1.1.keys), channel_id=1, source_target_pairs={{0,32},{1,33},{2,34},{3,35},{4,36},{5,37},{6,38},{7,39},{8,40},{9,... | collective-permute-start | bytes 7077896 | tf_op jit(solution)/shard_map/sibling1/ppermute | solution.py:79
  108.4 4.0 %terms_near1.1.near_in = f32[384,768]{1,0:T(8,128)S(1)} custom-call(f32[1]{0:T(128)} %bitcast.5.s, bf16[384,768]{1,0:T(8,128)(2,1)S(1)} %get-tuple-element.98.oth.refs_3_, f32[384,128]{1,0:T(8,128)S(1)} %copy-done.5, f32[16,384]{1,0:T(8,128)S(1)} %copy-done.3, bf16[1536,768]{1,0:T(8,128)(2,1)} %merge1.1.keys, f32[384,768]{1,0:T(8,128)S(1)} %copy-done.9), custom_call_target="tpu_custom_call" | custom-call | flops 99999997952 | bytes 1000 | tf_op jit(solution)/shard_map/terms_near1/pallas_call | solution.py:94
  112.5 0.0 collective-permute-done.14.farthest
  112.5 1.3 collective-permute-start.19
  113.8 0.0 collective-permute-done.15.q1
  113.8 0.0 collective-permute-done.16.q2
  113.8 0.0 collective-permute-done.17.q3
  113.8 2.6 %merge0.1 = (bf16[768,768]{1,0:T(8,128)(2,1)}, bf16[384,768]{1,0:T(8,128)(2,1)S(1)}) custom-call(s32[1]{0:T(128)} %bitcast.3.edge, bf16[1152,768]{1,0:T(8,128)(2,1)} %collective-permute-done.7.early.usual, bf16[288,768]{1,0:T(8,128)(2,1)S(1)} %join.1.q0, bf16[288,768]{1,0:T(8,128)(2,1)S(1)} %collective-permute-done.15.q1, ...), custom_call_target="tpu_custom_call" | custom-call | flops 1000 | bytes 1000 | tf_op jit(solution)/shard_map/merge0/pallas_call | solution.py:94
  116.4 3.8 %collective-permute-start.18 = (bf16[768,768]{1,0:T(8,128)(2,1)}, bf16[768,768]{1,0:T(8,128)(2,1)}, u32[]{:S(2)}, u32[]{:S(2)}) collective-permute-start(bf16[768,768]{1,0:T(8,128)(2,1)} %get-tuple-element.78.inner0), channel_id=1, source_target_pairs={{0,32},{1,33},{2,34},{3,35},{4,36},{5,37},{6,38},{7,39},{8,40},{9,... | collective-permute-start | bytes 3538952 | tf_op jit(solution)/shard_map/sibling_hop0/ppermute | solution.py:79
  120.3 0.0 copy-start.7
  120.3 3.1 %terms_near0.1.near_in = f32[384,768]{1,0:T(8,128)S(1)} custom-call(f32[1]{0:T(128)} %bitcast.6.s, bf16[384,768]{1,0:T(8,128)(2,1)S(1)} %get-tuple-element.98.oth.refs_3_, f32[384,128]{1,0:T(8,128)S(1)} %copy-done.5, f32[16,384]{1,0:T(8,128)S(1)} %copy-done.3, bf16[384,768]{1,0:T(8,128)(2,1)S(1)} %get-tuple-element.80.outer0, ...), custom_call_target="tpu_custom_call" | custom-call | flops 99999997952 | bytes 1000 | tf_op jit(solution)/shard_map/terms_near0/pallas_call | solution.py:94
  123.3 0.0 collective-permute-done.19.hf2
  123.3 0.0 collective-permute-done.20.keys
  123.4 5.6 %terms_far1.1.far_in = f32[384,768]{1,0:T(8,128)S(1)} custom-call(f32[1]{0:T(128)} %bitcast.7.s, bf16[384,768]{1,0:T(8,128)(2,1)S(1)} %get-tuple-element.99.outer.out.refs_0_, f32[384,128]{1,0:T(8,128)S(1)} %copy-done.1, f32[16,384]{1,0:T(8,128)S(1)} %copy-done.3, bf16[1536,768]{1,0:T(8,128)(2,1)} %collective-permute-done.20.keys, ...), custom_call_target="tpu_custom_call" | custom-call | flops 99999997952 | bytes 1000 | tf_op jit(solution)/shard_map/terms_far1/pallas_call | solution.py:94
  129.0 0.0 collective-permute-done.18.hs0
  129.0 4.6 %terms_last.1 = (f32[384,768]{1,0:T(8,128)}, f32[384,768]{1,0:T(8,128)}) custom-call(s32[1]{0:T(128)} %bitcast.c, s32[1]{0:T(128)} %bitcast.1.e, f32[1]{0:T(128)} %bitcast.8.s, bf16[384,768]{1,0:T(8,128)(2,1)S(1)} %get-tuple-element.99.outer.out.refs_0_, f32[384,128]{1,0:T(8,128)S(1)} %copy-done.1, f32[16,384]{1,0:T(8,128)S(1)} %copy-done.3, ...), custom_call_target="tpu_custom_call" | custom-call | flops 1000 | bytes 1000 | tf_op jit(solution)/shard_map/terms_last/pallas_call | solution.py:94
  (13 shorter events, 0.1 us)
Async XLA Ops:
  2.0 10.7 %collective-permute-start = (bf16[384,768]{1,0:T(8,128)(2,1)S(1)}, bf16[384,768]{1,0:T(8,128)(2,1)S(1)}, u32[]{:S(2)}, u32[]{:S(2)}) collective-permute-start(bf16[384,768]{1,0:T(8,128)(2,1)S(1)} %get-tuple-element.98.oth.refs_3_), channel_id=1, source_target_pairs={{0,32},{1,33},{2,34},{3,35},{4,36},{5,37},{6,38},{7,39},{8,40},{9,... | collective-permute-start | bytes 1769480 | tf_op jit(solution)/shard_map/swap/ppermute | solution.py:79
  10.8 30.8 %collective-permute-start.5 = (bf16[384,768]{1,0:T(8,128)(2,1)S(1)}, bf16[384,768]{1,0:T(8,128)(2,1)}, u32[]{:S(2)}, u32[]{:S(2)}) collective-permute-start(bf16[384,768]{1,0:T(8,128)(2,1)S(1)} %get-tuple-element.99.outer.out.refs_0_), channel_id=1, source_target_pairs={{0,448},{1,449},{2,450},{3,451},{4,452},{5,453},{6,454},{7,455},{8... | collective-permute-start | bytes 1769480 | tf_op jit(solution)/shard_map/own_outer1/ppermute | solution.py:79
  12.8 19.3 %collective-permute-start.1 = (bf16[192,768]{1,0:T(8,128)(2,1)S(1)}, bf16[192,768]{1,0:T(8,128)(2,1)}, u32[]{:S(2)}, u32[]{:S(2)}) collective-permute-start(bf16[192,768]{1,0:T(8,128)(2,1)S(1)} %get-tuple-element.42), channel_id=1, source_target_pairs={{0,3},{4,7},{8,11},{12,15},{16,19},{20,23},{24,27},{28,31},{35,32}... | collective-permute-start | bytes 884744 | tf_op jit(solution)/shard_map/spread0/ppermute | solution.py:79
  14.1 18.0 %collective-permute-start.2 = (bf16[192,768]{1,0:T(8,128)(2,1)S(1)}, bf16[192,768]{1,0:T(8,128)(2,1)}, u32[]{:S(2)}, u32[]{:S(2)}) collective-permute-start(bf16[192,768]{1,0:T(8,128)(2,1)S(1)} %get-tuple-element.43), channel_id=1, source_target_pairs={{0,1},{4,5},{8,9},{12,13},{16,17},{20,21},{24,25},{28,29},{35,34},... | collective-permute-start | bytes 884744 | tf_op jit(solution)/shard_map/spread1/ppermute | solution.py:79
  15.5 16.6 %collective-permute-start.3 = (bf16[192,768]{1,0:T(8,128)(2,1)S(1)}, bf16[192,768]{1,0:T(8,128)(2,1)}, u32[]{:S(2)}, u32[]{:S(2)}) collective-permute-start(bf16[192,768]{1,0:T(8,128)(2,1)S(1)} %get-tuple-element.44), channel_id=1, source_target_pairs={{0,2},{4,6},{8,10},{12,14},{16,18},{20,22},{24,26},{28,30},{35,33}... | collective-permute-start | bytes 884744 | tf_op jit(solution)/shard_map/spread2/ppermute | solution.py:79
  16.8 34.2 %collective-permute-start.4 = (bf16[384,768]{1,0:T(8,128)(2,1)S(1)}, bf16[384,768]{1,0:T(8,128)(2,1)S(1)}, u32[]{:S(2)}, u32[]{:S(2)}) collective-permute-start(bf16[384,768]{1,0:T(8,128)(2,1)S(1)} %get-tuple-element.98.oth.refs_3_), channel_id=1, source_target_pairs={{0,96},{1,97},{2,98},{3,99},{4,100},{5,101},{6,102},{7,103},{8,104... | collective-permute-start | bytes 1769480 | tf_op jit(solution)/shard_map/own_inner1/ppermute | solution.py:79
  33.1 19.3 %collective-permute-start.8 = (bf16[192,768]{1,0:T(8,128)(2,1)S(1)}, bf16[192,768]{1,0:T(8,128)(2,1)S(1)}, u32[]{:S(2)}, u32[]{:S(2)}) collective-permute-start(bf16[192,768]{1,0:T(8,128)(2,1)S(1)} %select_select_fusion), channel_id=1, source_target_pairs={{0,476},{1,477},{2,478},{3,479},{4,448},{5,449},{6,450},{7,451},{8... | collective-permute-start | bytes 884744 | tf_op jit(solution)/shard_map/cross/ppermute | solution.py:79
  44.0 27.3 %collective-permute-start.7 = (bf16[1152,768]{1,0:T(8,128)(2,1)}, bf16[1152,768]{1,0:T(8,128)(2,1)}, u32[]{:S(2)}, u32[]{:S(2)}) collective-permute-start(bf16[1152,768]{1,0:T(8,128)(2,1)} %pad_maximum_fusion), channel_id=1, source_target_pairs={{1,0},{2,1},{3,2},{5,4},{6,5},{7,6},{9,8},{10,9},{11,10},{13,12},{... | collective-permute-start | bytes 5308424 | tf_op jit(solution)/shard_map/wide_early/ppermute | solution.py:79
  46.7 4.3 %copy-start = (f32[384,128]{1,0:T(8,128)}, f32[384,128]{1,0:T(8,128)S(1)}, u32[]{:S(2)}) copy-start(f32[384,128]{1,0:T(8,128)S(1)} %get-tuple-element.62.ff) | copy-start | bytes 589828
  46.7 4.3 %copy-start.2 = (f32[16,384]{1,0:T(8,128)}, f32[16,384]{1,0:T(8,128)S(1)}, u32[]{:S(2)}) copy-start(f32[16,384]{1,0:T(8,128)S(1)} %get-tuple-element.63.kf) | copy-start | bytes 73732
  46.7 4.3 %copy-start.4 = (f32[384,128]{1,0:T(8,128)}, f32[384,128]{1,0:T(8,128)S(1)}, u32[]{:S(2)}) copy-start(f32[384,128]{1,0:T(8,128)S(1)} %get-tuple-element.64.nf) | copy-start | bytes 589828
  51.0 1.4 %copy-start.6 = (f32[384,768]{1,0:T(8,128)}, f32[384,768]{1,0:T(8,128)S(1)}, u32[]{:S(2)}) copy-start(f32[384,768]{1,0:T(8,128)S(1)} %get-tuple-element.67.far_in) | copy-start | bytes 3538948
  51.0 1.4 %copy-start.8 = (f32[384,768]{1,0:T(8,128)}, f32[384,768]{1,0:T(8,128)S(1)}, u32[]{:S(2)}) copy-start(f32[384,768]{1,0:T(8,128)S(1)} %get-tuple-element.66.near_in) | copy-start | bytes 3538948
  51.0 20.2 %collective-permute-start.6 = (bf16[384,768]{1,0:T(8,128)(2,1)S(1)}, bf16[384,768]{1,0:T(8,128)(2,1)S(1)}, u32[]{:S(2)}, u32[]{:S(2)}) collective-permute-start(bf16[384,768]{1,0:T(8,128)(2,1)S(1)} %collective-permute-done.4.inner1), channel_id=1, source_target_pairs={{1,0},{2,1},{3,2},{5,4},{6,5},{7,6},{9,8},{10,9},{11,10},{13,12},{... | collective-permute-start | bytes 1769480 | tf_op jit(solution)/shard_map/wide_late/ppermute | solution.py:79
  71.2 21.2 %collective-permute-start.9 = (bf16[192,768]{1,0:T(8,128)(2,1)S(1)}, bf16[192,768]{1,0:T(8,128)(2,1)S(1)}, u32[]{:S(2)}, u32[]{:S(2)}) collective-permute-start(bf16[192,768]{1,0:T(8,128)(2,1)S(1)} %collective-permute-done.8.block.q0), channel_id=1, source_target_pairs={{0,64},{1,65},{2,66},{3,67},{4,68},{5,69},{6,70},{7,71},{8,72},{9,... | collective-permute-start | bytes 884744 | tf_op jit(solution)/shard_map/cross_back/ppermute | solution.py:79
  73.8 14.9 %collective-permute-start.10 = (bf16[96,768]{1,0:T(8,128)(2,1)S(1)}, bf16[96,768]{1,0:T(8,128)(2,1)S(1)}, u32[]{:S(2)}, u32[]{:S(2)}) collective-permute-start(bf16[96,768]{1,0:T(8,128)(2,1)S(1)} %slice.1), channel_id=1, source_target_pairs={{0,448},{1,449},{2,450},{3,451},{4,452},{5,453},{6,454},{7,455},{8... | collective-permute-start | bytes 442376 | tf_op jit(solution)/shard_map/cross_ahead/ppermute | solution.py:79
  76.5 16.0 %collective-permute-start.11 = (bf16[192,768]{1,0:T(8,128)(2,1)S(1)}, bf16[192,768]{1,0:T(8,128)(2,1)S(1)}, u32[]{:S(2)}, u32[]{:S(2)}) collective-permute-start(bf16[192,768]{1,0:T(8,128)(2,1)S(1)} %collective-permute-done.8.block.q0), channel_id=1, source_target_pairs={{1,3},{5,7},{9,11},{13,15},{17,19},{21,23},{25,27},{29,31},{34,32}... | collective-permute-start | bytes 884744 | tf_op jit(solution)/shard_map/gather1_1/ppermute | solution.py:79
  77.8 14.7 %collective-permute-start.12 = (bf16[192,768]{1,0:T(8,128)(2,1)S(1)}, bf16[192,768]{1,0:T(8,128)(2,1)S(1)}, u32[]{:S(2)}, u32[]{:S(2)}) collective-permute-start(bf16[192,768]{1,0:T(8,128)(2,1)S(1)} %collective-permute-done.8.block.q0), channel_id=1, source_target_pairs={{2,3},{6,7},{10,11},{14,15},{18,19},{22,23},{26,27},{30,31},{33,32... | collective-permute-start | bytes 884744 | tf_op jit(solution)/shard_map/gather1_2/ppermute | solution.py:79
  79.1 13.4 %collective-permute-start.13 = (bf16[192,768]{1,0:T(8,128)(2,1)S(1)}, bf16[192,768]{1,0:T(8,128)(2,1)S(1)}, u32[]{:S(2)}, u32[]{:S(2)}) collective-permute-start(bf16[192,768]{1,0:T(8,128)(2,1)S(1)} %collective-permute-done.8.block.q0), channel_id=1, source_target_pairs={{0,3},{4,7},{8,11},{12,15},{16,19},{20,23},{24,27},{28,31},{35,32}... | collective-permute-start | bytes 884744 | tf_op jit(solution)/shard_map/gather1_3/ppermute | solution.py:79
  88.7 23.7 %collective-permute-start.14 = (bf16[384,768]{1,0:T(8,128)(2,1)}, bf16[384,768]{1,0:T(8,128)(2,1)}, u32[]{:S(2)}, u32[]{:S(2)}) collective-permute-start(bf16[384,768]{1,0:T(8,128)(2,1)} %collective-permute-done.5.refs_2_.outer1), channel_id=1, source_target_pairs={{0,480},{1,481},{2,482},{3,483},{4,484},{5,485},{6,486},{7,487},{8... | collective-permute-start | bytes 1769480 | tf_op jit(solution)/shard_map/own_outer2/ppermute | solution.py:79
  92.5 21.2 %collective-permute-start.15 = (bf16[288,768]{1,0:T(8,128)(2,1)S(1)}, bf16[288,768]{1,0:T(8,128)(2,1)S(1)}, u32[]{:S(2)}, u32[]{:S(2)}) collective-permute-start(bf16[288,768]{1,0:T(8,128)(2,1)S(1)} %join.1.q0), channel_id=1, source_target_pairs={{1,3},{5,7},{9,11},{13,15},{17,19},{21,23},{25,27},{29,31},{34,32}... | collective-permute-start | bytes 1327112 | tf_op jit(solution)/shard_map/gather0_1/ppermute | solution.py:79
  93.8 20.0 %collective-permute-start.16 = (bf16[288,768]{1,0:T(8,128)(2,1)S(1)}, bf16[288,768]{1,0:T(8,128)(2,1)S(1)}, u32[]{:S(2)}, u32[]{:S(2)}) collective-permute-start(bf16[288,768]{1,0:T(8,128)(2,1)S(1)} %join.1.q0), channel_id=1, source_target_pairs={{2,3},{6,7},{10,11},{14,15},{18,19},{22,23},{26,27},{30,31},{33,32... | collective-permute-start | bytes 1327112 | tf_op jit(solution)/shard_map/gather0_2/ppermute | solution.py:79
  95.1 18.7 %collective-permute-start.17 = (bf16[288,768]{1,0:T(8,128)(2,1)S(1)}, bf16[288,768]{1,0:T(8,128)(2,1)S(1)}, u32[]{:S(2)}, u32[]{:S(2)}) collective-permute-start(bf16[288,768]{1,0:T(8,128)(2,1)S(1)} %join.1.q0), channel_id=1, source_target_pairs={{0,3},{4,7},{8,11},{12,15},{16,19},{20,23},{24,27},{28,31},{35,32}... | collective-permute-start | bytes 1327112 | tf_op jit(solution)/shard_map/gather0_3/ppermute | solution.py:79
  96.4 12.0 %copy-start.3 = (f32[16,384]{1,0:T(8,128)S(1)}, f32[16,384]{1,0:T(8,128)}, u32[]{:S(2)}) copy-start(f32[16,384]{1,0:T(8,128)} %copy-done.2) | copy-start | bytes 73732
  96.5 12.0 %copy-start.5 = (f32[384,128]{1,0:T(8,128)S(1)}, f32[384,128]{1,0:T(8,128)}, u32[]{:S(2)}) copy-start(f32[384,128]{1,0:T(8,128)} %copy-done.4) | copy-start | bytes 589828
  96.5 12.0 %copy-start.9 = (f32[384,768]{1,0:T(8,128)S(1)}, f32[384,768]{1,0:T(8,128)}, u32[]{:S(2)}) copy-start(f32[384,768]{1,0:T(8,128)} %copy-done.8) | copy-start | bytes 3538948
  99.8 23.6 %collective-permute-start.20 = (bf16[1536,768]{1,0:T(8,128)(2,1)}, bf16[1536,768]{1,0:T(8,128)(2,1)}, u32[]{:S(2)}, u32[]{:S(2)}) collective-permute-start(bf16[1536,768]{1,0:T(8,128)(2,1)} %merge1.1.keys), channel_id=1, source_target_pairs={{0,32},{1,33},{2,34},{3,35},{4,36},{5,37},{6,38},{7,39},{8,40},{9,... | collective-permute-start | bytes 7077896 | tf_op jit(solution)/shard_map/sibling1/ppermute | solution.py:79
  112.5 10.8 %collective-permute-start.19 = (bf16[384,768]{1,0:T(8,128)(2,1)}, bf16[384,768]{1,0:T(8,128)(2,1)S(1)}, u32[]{:S(2)}, u32[]{:S(2)}) collective-permute-start(bf16[384,768]{1,0:T(8,128)(2,1)} %collective-permute-done.14.farthest), channel_id=1, source_target_pairs={{0,1},{1,2},{2,3},{4,5},{5,6},{6,7},{8,9},{9,10},{10,11},{12,13},{... | collective-permute-start | bytes 1769480 | tf_op jit(solution)/shard_map/wide_outer2/ppermute | solution.py:79
  116.4 12.6 %collective-permute-start.18 = (bf16[768,768]{1,0:T(8,128)(2,1)}, bf16[768,768]{1,0:T(8,128)(2,1)}, u32[]{:S(2)}, u32[]{:S(2)}) collective-permute-start(bf16[768,768]{1,0:T(8,128)(2,1)} %get-tuple-element.78.inner0), channel_id=1, source_target_pairs={{0,32},{1,33},{2,34},{3,35},{4,36},{5,37},{6,38},{7,39},{8,40},{9,... | collective-permute-start | bytes 3538952 | tf_op jit(solution)/shard_map/sibling_hop0/ppermute | solution.py:79
  120.2 3.1 %copy-start.1 = (f32[384,128]{1,0:T(8,128)S(1)}, f32[384,128]{1,0:T(8,128)}, u32[]{:S(2)}) copy-start(f32[384,128]{1,0:T(8,128)} %copy-done) | copy-start | bytes 589828
  120.3 3.1 %copy-start.7 = (f32[384,768]{1,0:T(8,128)S(1)}, f32[384,768]{1,0:T(8,128)}, u32[]{:S(2)}) copy-start(f32[384,768]{1,0:T(8,128)} %copy-done.6) | copy-start | bytes 3538948

commit v8 on v6

--- a/solution.py
+++ b/solution.py
@@ -6,6 +6,7 @@
 from jax.sharding import PartitionSpec as P
 
 AXES = ("blk", "wide")
+LOG2E = 1.4426950408889634
 
 
 def coordinates(blk, wide):
@@ -103,15 +104,14 @@
         )(*smem, *vmem)
 
 
-def move(name, kernel, out_shape, smem, arrays, copies):
+def assemble(name, kernel, out_shape, smem, arrays, copies):
     many = isinstance(out_shape, (list, tuple))
-    anywhere = pl.BlockSpec(memory_space=pl.ANY)
     with jax.named_scope(name):
         return pl.pallas_call(
             kernel,
             out_shape=out_shape,
-            in_specs=[scalars() for _ in smem] + [anywhere for _ in arrays],
-            out_specs=[anywhere for _ in out_shape] if many else anywhere,
+            in_specs=[scalars() for _ in smem] + [pl.BlockSpec(memory_space=pl.ANY) for _ in arrays],
+            out_specs=[whole() for _ in out_shape] if many else whole(),
             scratch_shapes=[pltpu.SemaphoreType.DMA((copies,))],
             cost_estimate=pl.CostEstimate(flops=1000, bytes_accessed=1000, transcendentals=0),
             compiler_params=pltpu.CompilerParams(vmem_limit_bytes=16 * 1024 * 1024),
@@ -135,7 +135,7 @@
     logits = lax.dot_general(
         query, keys, (((1,), (1,)), ((), ())), preferred_element_type=jnp.float32
     )
-    weights = jnp.exp(logits * scale - 5.0) * (query_factor + key_factor)
+    weights = jnp.exp2(logits * (scale * LOG2E) - 5.0 * LOG2E) * (query_factor + key_factor)
     if own:
         rows = lax.broadcasted_iota(jnp.int32, weights.shape, 0)
         cols = lax.broadcasted_iota(jnp.int32, weights.shape, 1)
@@ -199,8 +199,9 @@
     )
     crossed = send("cross", held, across)
     early = send(
-        "wide_early", jnp.concatenate([after(inner, held), outer, outer1, inner1], axis=0), to_next_wide
-    )
+        "wide_early", jnp.concatenate([after(inner, held), outer, outer1], axis=0), to_next_wide
+    )
+
     batch = row_lse.shape[0]
 
     def part(carried, b, w):
@@ -271,11 +272,21 @@
             (other, outer, near_factor, far_factor, key_factors, *arrays, *(sums or ())), weight,
         )
 
-    sums = terms("terms_own0", [(outer, [0]), (inner, [1]), (after(outer1, held), [2]), (inner1, [3])], [(other, [8])], None, 100_000_000)
-    crossed = after(crossed, early, *sums)
-
-    back = send("cross_back", crossed, to_previous_chip)
-    ahead = send("cross_ahead", crossed[quarter:], to_next_chip)
+    sums = terms("terms_own0", [(outer, [0]), (inner, [1]), (after(outer1, held), [2])], [(other, [8])], None, 100_000_000)
+    inner1 = after(inner1, *sums)
+    late = send("wide_late", inner1, to_next_wide)
+
+    def slice_kernel(block, out):
+        out[...] = block[quarter:, :]
+
+    outer_part = call(
+        "slice", slice_kernel, jax.ShapeDtypeStruct((quarter, width), half), (), (crossed,),
+        100_000_000,
+    )
+    back = send("cross_back", after(crossed, outer_part), to_previous_chip)
+    ahead = send("cross_ahead", outer_part, to_next_chip)
+    late, early, _ = lax.optimization_barrier((late, early, outer_part))
+    crossed = after(crossed, late, early)
 
     def collect(name, mine):
         q1 = send(name + "1", mine, line_to_line(2, 0))
@@ -296,7 +307,7 @@
     )
     got0 = collect("gather0_", after(joined, *got1))
 
-    def merge1_kernel(edge, early, outer1, inner1, q0, q1, q2, q3, out, sems):
+    def merge1_kernel(edge, early, late, outer1, inner1, q0, q1, q2, q3, out, sems):
         own = [(outer1, 0, out, 2 * rows, rows), (inner1, 0, out, 3 * rows, rows)]
 
         @pl.when(edge[0] == 1)
@@ -309,11 +320,11 @@
 
         @pl.when(edge[0] == 0)
         def _():
-            copy_all(sems, [(early, 2 * rows, out, 0, 2 * rows)] + own)
-
-    carried = move(
+            copy_all(sems, [(early, 2 * rows, out, 0, rows), (late, 0, out, rows, rows)] + own)
+
+    carried = assemble(
         "merge1", merge1_kernel, blocks(4), (at_edge,),
-        (early, after(outer1, back, ahead), inner1, *got1), 10,
+        (early, late, after(outer1, back, ahead), inner1, *got1), 10,
     )
     sib = send("sibling1", carried, to_sibling)
     hop_far2 = send("wide_outer2", after(far2, carried), to_sibling_next_wide)
@@ -322,7 +333,8 @@
     def near_kernel(s, oth, nf, kf, keys, near_in, near):
         near[...] = add_terms(
             near_in[...], oth[...], nf[:, :1], kf, s[0],
-            [(keys[:rows, :], 4, False), (keys[rows : 2 * rows, :], 5, False)],
+            [(keys[:rows, :], 4, False), (keys[rows : 2 * rows, :], 5, False),
+             (keys[3 * rows :, :], 3, False)],
         )
 
     near_sum = call(
@@ -347,21 +359,43 @@
         def _():
             copy_all(sems, [(usual, 0, out, 0, 2 * rows), (usual, rows, outer0, 0, rows)])
 
-    hop0, hop_outer0 = move(
+    hop0, hop_outer0 = assemble(
         "merge0", merge0_kernel, [blocks(2), blocks(1)], (at_edge,), (early, *got0), 12
     )
     hop_sib0 = send("sibling_hop0", hop0, to_sibling)
 
-    def near0_kernel(s, oth, nf, kf, outer0, inner0, near_in, near):
-        near[...] = add_terms(
+    anywhere = pl.BlockSpec(memory_space=pl.ANY)
+
+    def near0_kernel(c, s, oth, nf, kf, outer0, inner0, near_in, image_grad, caption_grad, held_sum, sem):
+        held_sum[...] = s[0] * add_terms(
             near_in[...], oth[...], nf[:, :1], kf, s[0],
             [(outer0[...], 7, False), (inner0[:rows, :], 6, False)],
         )
 
-    near_sum = call(
-        "terms_near0", near0_kernel, total, (scale,),
-        (other, near_factor, key_factors, hop_outer0, hop0, near_sum), 100_000_000,
-    )
+        @pl.when(c[0] == 1)
+        def _():
+            one = pltpu.make_async_copy(held_sum, image_grad, sem)
+            one.start()
+            one.wait()
+
+        @pl.when(c[0] == 0)
+        def _():
+            one = pltpu.make_async_copy(held_sum, caption_grad, sem)
+            one.start()
+            one.wait()
+
+    with jax.named_scope("terms_near0"):
+        half_done = pl.pallas_call(
+            near0_kernel,
+            out_shape=[total, total],
+            in_specs=[scalars()] * 2 + [whole()] * 6,
+            out_specs=[anywhere] * 2,
+            scratch_shapes=[pltpu.VMEM((rows, width), jnp.float32), pltpu.SemaphoreType.DMA],
+            cost_estimate=pl.CostEstimate(
+                flops=100_000_000_000, bytes_accessed=1000, transcendentals=0
+            ),
+            compiler_params=pltpu.CompilerParams(vmem_limit_bytes=16 * 1024 * 1024),
+        )(core_flag, scale, other, near_factor, key_factors, hop_outer0, hop0, near_sum)
 
     def far1_kernel(s, out, ff, kf, keys, farthest, far_in, far):
         far[...] = add_terms(
@@ -372,31 +406,44 @@
 
     far_sum = call(
         "terms_far1", far1_kernel, total, (scale,),
-        (outer, far_factor, key_factors, after(sib, hop_far2, near_sum), far2, far_sum), 100_000_000,
-    )
-
-    def last_kernel(c, e, s, out, ff, kf, hs0, hf2, near_in, far_in, image_grad, caption_grad):
+        (outer, far_factor, key_factors, after(sib, hop_far2, *half_done), far2, far_sum), 100_000_000,
+    )
+
+    def last_kernel(
+        c, e, s, out, ff, kf, hs0, hf2, far_in, _i, _c, image_grad, caption_grad, held_sum, sem
+    ):
         farthest = jnp.where(e[0] == 1, hs0[rows:, :], hf2[...])
-        far = s[0] * add_terms(
+        held_sum[...] = s[0] * add_terms(
             far_in[...], out[...], ff[:, :1], kf, s[0],
             [(hs0[:rows, :], 14, False), (farthest, 15, False)],
         )
-        near = s[0] * near_in[...]
 
         @pl.when(c[0] == 1)
         def _():
-            image_grad[...] = near
-            caption_grad[...] = far
+            one = pltpu.make_async_copy(held_sum, caption_grad, sem)
+            one.start()
+            one.wait()
 
         @pl.when(c[0] == 0)
         def _():
-            image_grad[...] = far
-            caption_grad[...] = near
-
-    image_grad, caption_grad = call(
-        "terms_last", last_kernel, [total, total], (core_flag, sibling_at_edge, scale),
-        (outer, far_factor, key_factors, hop_sib0, hop_far2, near_sum, far_sum),
-    )
+            one = pltpu.make_async_copy(held_sum, image_grad, sem)
+            one.start()
+            one.wait()
+
+    with jax.named_scope("terms_last"):
+        image_grad, caption_grad = pl.pallas_call(
+            last_kernel,
+            out_shape=[total, total],
+            in_specs=[scalars()] * 3 + [whole()] * 6 + [anywhere] * 2,
+            out_specs=[anywhere] * 2,
+            scratch_shapes=[pltpu.VMEM((rows, width), jnp.float32), pltpu.SemaphoreType.DMA],
+            input_output_aliases={9: 0, 10: 1},
+            cost_estimate=pl.CostEstimate(flops=1000, bytes_accessed=1000, transcendentals=0),
+            compiler_params=pltpu.CompilerParams(vmem_limit_bytes=16 * 1024 * 1024),
+        )(
+            core_flag, sibling_at_edge, scale,
+            outer, far_factor, key_factors, hop_sib0, hop_far2, far_sum, *half_done,
+        )
     return image_grad, caption_grad
 
 

time: 170 us -> 129 us (0.76)
  the two profiles are of different devices: /device:TPU:483 before, /device:TPU:1 now
where the time goes in v8:
time: 129 us; the launch traced here: 128 us
  starting transfers between devices  70.6 us (55%)
  Pallas kernels  30.2 us (23%)
  waiting for transfers between devices  19.8 us (15%)
  other arithmetic  4.88 us (4%)
  between operations  2.23 us (2%)
    ppermute x21, starting transfers between devices, send(): return lax.ppermute(x, AXES, pairs(target))  70.6 us
    ppermute x21, waiting for transfers between devices, send(): return lax.ppermute(x, AXES, pairs(target))  19.8 us
    pallas_call x7, Pallas kernels, call(): pl.pallas_call(kernel, out_shape=out_shape, in_specs=[scalars() for _ in...  15.3 us
    pallas_call x2, Pallas kernels, assemble(): pl.pallas_call(kernel, out_shape=out_shape, in_specs=[scalars() for _ in...  6.82 us
    pallas_call x1, Pallas kernels, on_device(): pl.pallas_call(near0_kernel, out_shape=[total, total], in_specs=[scalars(...  4.08 us
    pallas_call x1, Pallas kernels, on_device(): pl.pallas_call(last_kernel, out_shape=[total, total], in_specs=[scalars()...  3.99 us
  transfers between devices with their start and end apart: 21, of which 3 were waited for; matrix products, arithmetic and copies ran while one was open for 3% of the time, Pallas kernels for 21%

profile of v8, /device:TPU:1, one launch (start us, length us, event | category | flops | bytes accessed | tf_op | source)
XLA Modules:
  0.0 127.7 jit_solution(6289873335264186498)
XLA Ops:
  0.6 1.3 %broadcast_select_fusion = (bf16[384,768]{1,0:T(8,128)(2,1)S(1)}, bf16[384,768]{1,0:T(8,128)(2,1)S(1)}) fusion(bf16[384,768]{1,0:T(8,128)(2,1)} %param.5, bf16[384,768]{1,0:T(8,128)(2,1)} %param.6, pred[]{:T(512)S(6)} %eq.62), kind=kLoop, calls=%fused_computation.1 | loop fusion | flops 589824 | bytes 2359297 | tf_op jit(solution)/shard_map/jit(_where)/select_n | solution.py:181
  2.0 8.8 %collective-permute-start = (bf16[384,768]{1,0:T(8,128)(2,1)S(1)}, bf16[384,768]{1,0:T(8,128)(2,1)S(1)}, u32[]{:S(2)}, u32[]{:S(2)}) collective-permute-start(bf16[384,768]{1,0:T(8,128)(2,1)S(1)} %get-tuple-element.102.oth.refs_3_), channel_id=1, source_target_pairs={{0,32},{1,33},{2,34},{3,35},{4,36},{5,37},{6,38},{7,39},{8,40},{9,... | collective-permute-start | bytes 1769480 | tf_op jit(solution)/shard_map/swap/ppermute | solution.py:80
  10.8 1.9 %collective-permute-start.5 = (bf16[384,768]{1,0:T(8,128)(2,1)S(1)}, bf16[384,768]{1,0:T(8,128)(2,1)S(1)}, u32[]{:S(2)}, u32[]{:S(2)}) collective-permute-start(bf16[384,768]{1,0:T(8,128)(2,1)S(1)} %get-tuple-element.103.outer.out.refs_0_), channel_id=1, source_target_pairs={{0,448},{1,449},{2,450},{3,451},{4,452},{5,453},{6,454},{7,455},{8... | collective-permute-start | bytes 1769480 | tf_op jit(solution)/shard_map/own_outer1/ppermute | solution.py:80
  12.7 0.0 collective-permute-done.inner.refs_1_
  12.7 0.9 cut.1
  13.6 1.3 %collective-permute-start.1 = (bf16[192,768]{1,0:T(8,128)(2,1)}, bf16[192,768]{1,0:T(8,128)(2,1)}, u32[]{:S(2)}, u32[]{:S(2)}) collective-permute-start(bf16[192,768]{1,0:T(8,128)(2,1)} %get-tuple-element.44), channel_id=1, source_target_pairs={{0,3},{4,7},{8,11},{12,15},{16,19},{20,23},{24,27},{28,31},{35,32}... | collective-permute-start | bytes 884744 | tf_op jit(solution)/shard_map/spread0/ppermute | solution.py:80
  14.9 1.4 %collective-permute-start.2 = (bf16[192,768]{1,0:T(8,128)(2,1)}, bf16[192,768]{1,0:T(8,128)(2,1)}, u32[]{:S(2)}, u32[]{:S(2)}) collective-permute-start(bf16[192,768]{1,0:T(8,128)(2,1)} %get-tuple-element.45), channel_id=1, source_target_pairs={{0,1},{4,5},{8,9},{12,13},{16,17},{20,21},{24,25},{28,29},{35,34},... | collective-permute-start | bytes 884744 | tf_op jit(solution)/shard_map/spread1/ppermute | solution.py:80
  16.3 1.4 %collective-permute-start.3 = (bf16[192,768]{1,0:T(8,128)(2,1)S(1)}, bf16[192,768]{1,0:T(8,128)(2,1)}, u32[]{:S(2)}, u32[]{:S(2)}) collective-permute-start(bf16[192,768]{1,0:T(8,128)(2,1)S(1)} %get-tuple-element.46), channel_id=1, source_target_pairs={{0,2},{4,6},{8,10},{12,14},{16,18},{20,22},{24,26},{28,30},{35,33}... | collective-permute-start | bytes 884744 | tf_op jit(solution)/shard_map/spread2/ppermute | solution.py:80
  17.6 13.1 %collective-permute-start.4 = (bf16[384,768]{1,0:T(8,128)(2,1)S(1)}, bf16[384,768]{1,0:T(8,128)(2,1)S(1)}, u32[]{:S(2)}, u32[]{:S(2)}) collective-permute-start(bf16[384,768]{1,0:T(8,128)(2,1)S(1)} %get-tuple-element.102.oth.refs_3_), channel_id=1, source_target_pairs={{0,96},{1,97},{2,98},{3,99},{4,100},{5,101},{6,102},{7,103},{8,104... | collective-permute-start | bytes 1769480 | tf_op jit(solution)/shard_map/own_inner1/ppermute | solution.py:80
  31.6 1.2 dynamic-slice_select_fusion
  32.8 0.0 collective-permute-done.1
  32.8 0.0 collective-permute-done.2
  32.8 0.0 collective-permute-done.3
  32.9 1.0 select_select_fusion
  33.9 8.4 %collective-permute-start.8 = (bf16[192,768]{1,0:T(8,128)(2,1)S(1)}, bf16[192,768]{1,0:T(8,128)(2,1)S(1)}, u32[]{:S(2)}, u32[]{:S(2)}) collective-permute-start(bf16[192,768]{1,0:T(8,128)(2,1)S(1)} %select_select_fusion), channel_id=1, source_target_pairs={{0,476},{1,477},{2,478},{3,479},{4,448},{5,449},{6,450},{7,451},{8... | collective-permute-start | bytes 884744 | tf_op jit(solution)/shard_map/cross/ppermute | solution.py:80
  42.3 0.0 collective-permute-done.5.refs_2_.outer1
  42.3 1.4 %pad_maximum_fusion = bf16[1152,768]{1,0:T(8,128)(2,1)} fusion(bf16[384,768]{1,0:T(8,128)(2,1)S(1)} %collective-permute-done.5.refs_2_.outer1, bf16[384,768]{1,0:T(8,128)(2,1)S(1)} %get-tuple-element.103.outer.out.refs_0_, bf16[384,768]{1,0:T(8,128)(2,1)S(1)} %collective-permute-done.inner.refs_1_), kind=kLoop, calls=%fused_computation | loop fusion | flops 5308416 | bytes 3538944 | tf_op jit(solution)/shard_map/concatenate | solution.py:202
  43.7 2.5 %collective-permute-start.7 = (bf16[1152,768]{1,0:T(8,128)(2,1)}, bf16[1152,768]{1,0:T(8,128)(2,1)}, u32[]{:S(2)}, u32[]{:S(2)}) collective-permute-start(bf16[1152,768]{1,0:T(8,128)(2,1)} %pad_maximum_fusion), channel_id=1, source_target_pairs={{1,0},{2,1},{3,2},{5,4},{6,5},{7,6},{9,8},{10,9},{11,10},{13,12},{... | collective-permute-start | bytes 5308424 | tf_op jit(solution)/shard_map/wide_early/ppermute | solution.py:80
  46.2 0.2 factors.1
  46.4 0.0 copy-start
  46.4 0.0 copy-start.2
  46.4 0.0 copy-start.4
  46.4 3.0 %terms_own0.1 = (f32[384,768]{1,0:T(8,128)S(1)}, f32[384,768]{1,0:T(8,128)S(1)}) custom-call(f32[1]{0:T(128)} %bitcast.4.s, bf16[384,768]{1,0:T(8,128)(2,1)S(1)} %get-tuple-element.102.oth.refs_3_, bf16[384,768]{1,0:T(8,128)(2,1)S(1)} %get-tuple-element.103.outer.out.refs_0_, f32[384,128]{1,0:T(8,128)S(1)} %get-tuple-element.66.nf, ...), custom_call_target="tpu_custom_call" | custom-call | flops 99999997952 | bytes 1000 | tf_op jit(solution)/shard_map/terms_own0/pallas_call | solution.py:95
  49.5 0.0 copy-done
  49.5 0.0 copy-start.8
  49.5 0.0 collective-permute-done.4.inner1
  49.5 1.3 %collective-permute-start.6 = (bf16[384,768]{1,0:T(8,128)(2,1)S(1)}, bf16[384,768]{1,0:T(8,128)(2,1)S(1)}, u32[]{:S(2)}, u32[]{:S(2)}) collective-permute-start(bf16[384,768]{1,0:T(8,128)(2,1)S(1)} %collective-permute-done.4.inner1), channel_id=1, source_target_pairs={{1,0},{2,1},{3,2},{5,4},{6,5},{7,6},{9,8},{10,9},{11,10},{13,12},{... | collective-permute-start | bytes 1769480 | tf_op jit(solution)/shard_map/wide_late/ppermute | solution.py:80
  50.9 13.2 %collective-permute-done.8.block.q0 = bf16[192,768]{1,0:T(8,128)(2,1)S(1)} collective-permute-done((bf16[192,768]{1,0:T(8,128)(2,1)S(1)}, bf16[192,768]{1,0:T(8,128)(2,1)S(1)}, u32[]{:S(2)}, u32[]{:S(2)}) %collective-permute-start.8) | collective-permute-done | bytes 294944 | tf_op jit(solution)/shard_map/cross/ppermute | solution.py:80
  64.1 0.7 slice.1
  64.8 1.9 %collective-permute-start.9 = (bf16[192,768]{1,0:T(8,128)(2,1)S(1)}, bf16[192,768]{1,0:T(8,128)(2,1)S(1)}, u32[]{:S(2)}, u32[]{:S(2)}) collective-permute-start(bf16[192,768]{1,0:T(8,128)(2,1)S(1)} %collective-permute-done.8.block.q0), channel_id=1, source_target_pairs={{0,64},{1,65},{2,66},{3,67},{4,68},{5,69},{6,70},{7,71},{8,72},{9,... | collective-permute-start | bytes 884744 | tf_op jit(solution)/shard_map/cross_back/ppermute | solution.py:80
  66.7 3.4 %collective-permute-start.10 = (bf16[96,768]{1,0:T(8,128)(2,1)}, bf16[96,768]{1,0:T(8,128)(2,1)}, u32[]{:S(2)}, u32[]{:S(2)}) collective-permute-start(bf16[96,768]{1,0:T(8,128)(2,1)} %slice.1), channel_id=1, source_target_pairs={{0,448},{1,449},{2,450},{3,451},{4,452},{5,453},{6,454},{7,455},{8... | collective-permute-start | bytes 442376 | tf_op jit(solution)/shard_map/cross_ahead/ppermute | solution.py:80
  70.1 0.9 collective-permute-done.6.late
  70.9 0.0 collective-permute-done.7.early.usual
  71.0 1.3 %collective-permute-start.11 = (bf16[192,768]{1,0:T(8,128)(2,1)S(1)}, bf16[192,768]{1,0:T(8,128)(2,1)S(1)}, u32[]{:S(2)}, u32[]{:S(2)}) collective-permute-start(bf16[192,768]{1,0:T(8,128)(2,1)S(1)} %collective-permute-done.8.block.q0), channel_id=1, source_target_pairs={{1,3},{5,7},{9,11},{13,15},{17,19},{21,23},{25,27},{29,31},{34,32}... | collective-permute-start | bytes 884744 | tf_op jit(solution)/shard_map/gather1_1/ppermute | solution.py:80
  72.2 1.3 %collective-permute-start.12 = (bf16[192,768]{1,0:T(8,128)(2,1)S(1)}, bf16[192,768]{1,0:T(8,128)(2,1)S(1)}, u32[]{:S(2)}, u32[]{:S(2)}) collective-permute-start(bf16[192,768]{1,0:T(8,128)(2,1)S(1)} %collective-permute-done.8.block.q0), channel_id=1, source_target_pairs={{2,3},{6,7},{10,11},{14,15},{18,19},{22,23},{26,27},{30,31},{33,32... | collective-permute-start | bytes 884744 | tf_op jit(solution)/shard_map/gather1_2/ppermute | solution.py:80
  73.5 1.3 %collective-permute-start.13 = (bf16[192,768]{1,0:T(8,128)(2,1)S(1)}, bf16[192,768]{1,0:T(8,128)(2,1)S(1)}, u32[]{:S(2)}, u32[]{:S(2)}) collective-permute-start(bf16[192,768]{1,0:T(8,128)(2,1)S(1)} %collective-permute-done.8.block.q0), channel_id=1, source_target_pairs={{0,3},{4,7},{8,11},{12,15},{16,19},{20,23},{24,27},{28,31},{35,32}... | collective-permute-start | bytes 884744 | tf_op jit(solution)/shard_map/gather1_3/ppermute | solution.py:80
  74.8 5.7 %collective-permute-done.10.second = bf16[96,768]{1,0:T(8,128)(2,1)} collective-permute-done((bf16[96,768]{1,0:T(8,128)(2,1)}, bf16[96,768]{1,0:T(8,128)(2,1)}, u32[]{:S(2)}, u32[]{:S(2)}) %collective-permute-start.10) | collective-permute-done | bytes 147488 | tf_op jit(solution)/shard_map/cross_ahead/ppermute | solution.py:80
  80.5 0.0 collective-permute-done.9.first
  80.5 0.9 join.1.q0
  81.5 6.0 %collective-permute-start.14 = (bf16[384,768]{1,0:T(8,128)(2,1)S(1)}, bf16[384,768]{1,0:T(8,128)(2,1)S(1)}, u32[]{:S(2)}, u32[]{:S(2)}) collective-permute-start(bf16[384,768]{1,0:T(8,128)(2,1)S(1)} %collective-permute-done.5.refs_2_.outer1), channel_id=1, source_target_pairs={{0,480},{1,481},{2,482},{3,483},{4,484},{5,485},{6,486},{7,487},{8... | collective-permute-start | bytes 1769480 | tf_op jit(solution)/shard_map/own_outer2/ppermute | solution.py:80
  87.5 0.0 collective-permute-done.11.q1
  87.5 0.0 collective-permute-done.12.q2
  87.5 0.0 collective-permute-done.13.q3
  87.5 1.3 %collective-permute-start.15 = (bf16[288,768]{1,0:T(8,128)(2,1)S(1)}, bf16[288,768]{1,0:T(8,128)(2,1)S(1)}, u32[]{:S(2)}, u32[]{:S(2)}) collective-permute-start(bf16[288,768]{1,0:T(8,128)(2,1)S(1)} %join.1.q0), channel_id=1, source_target_pairs={{1,3},{5,7},{9,11},{13,15},{17,19},{21,23},{25,27},{29,31},{34,32}... | collective-permute-start | bytes 1327112 | tf_op jit(solution)/shard_map/gather0_1/ppermute | solution.py:80
  88.8 1.3 %collective-permute-start.16 = (bf16[288,768]{1,0:T(8,128)(2,1)S(1)}, bf16[288,768]{1,0:T(8,128)(2,1)S(1)}, u32[]{:S(2)}, u32[]{:S(2)}) collective-permute-start(bf16[288,768]{1,0:T(8,128)(2,1)S(1)} %join.1.q0), channel_id=1, source_target_pairs={{2,3},{6,7},{10,11},{14,15},{18,19},{22,23},{26,27},{30,31},{33,32... | collective-permute-start | bytes 1327112 | tf_op jit(solution)/shard_map/gather0_2/ppermute | solution.py:80
  90.1 1.3 %collective-permute-start.17 = (bf16[288,768]{1,0:T(8,128)(2,1)S(1)}, bf16[288,768]{1,0:T(8,128)(2,1)S(1)}, u32[]{:S(2)}, u32[]{:S(2)}) collective-permute-start(bf16[288,768]{1,0:T(8,128)(2,1)S(1)} %join.1.q0), channel_id=1, source_target_pairs={{0,3},{4,7},{8,11},{12,15},{16,19},{20,23},{24,27},{28,31},{35,32}... | collective-permute-start | bytes 1327112 | tf_op jit(solution)/shard_map/gather0_3/ppermute | solution.py:80
  91.4 0.0 copy-start.5
  91.4 0.0 copy-start.9
  91.4 3.3 %merge1.1.keys = bf16[1536,768]{1,0:T(8,128)(2,1)} custom-call(s32[1]{0:T(128)} %bitcast.3.edge, bf16[1152,768]{1,0:T(8,128)(2,1)} %collective-permute-done.7.early.usual, bf16[384,768]{1,0:T(8,128)(2,1)S(1)} %collective-permute-done.6.late, bf16[384,768]{1,0:T(8,128)(2,1)S(1)} %collective-permute-done.5.refs_2_.outer1, ...), custom_call_target="tpu_custom_call" | custom-call | flops 1000 | bytes 1000 | tf_op jit(solution)/shard_map/merge1/pallas_call | solution.py:110
  94.7 6.2 %collective-permute-start.20 = (bf16[1536,768]{1,0:T(8,128)(2,1)}, bf16[1536,768]{1,0:T(8,128)(2,1)}, u32[]{:S(2)}, u32[]{:S(2)}) collective-permute-start(bf16[1536,768]{1,0:T(8,128)(2,1)} %merge1.1.keys), channel_id=1, source_target_pairs={{0,32},{1,33},{2,34},{3,35},{4,36},{5,37},{6,38},{7,39},{8,40},{9,... | collective-permute-start | bytes 7077896 | tf_op jit(solution)/shard_map/sibling1/ppermute | solution.py:80
  101.0 4.0 %terms_near1.1.near_in = f32[384,768]{1,0:T(8,128)S(1)} custom-call(f32[1]{0:T(128)} %bitcast.5.s, bf16[384,768]{1,0:T(8,128)(2,1)S(1)} %get-tuple-element.102.oth.refs_3_, f32[384,128]{1,0:T(8,128)S(1)} %copy-done.5, f32[16,384]{1,0:T(8,128)S(1)} %copy-done.3, bf16[1536,768]{1,0:T(8,128)(2,1)} %merge1.1.keys, f32[384,768]{1,0:T(8,128)S(1)} %copy-done.9), custom_call_target="tpu_custom_call" | custom-call | flops 99999997952 | bytes 1000 | tf_op jit(solution)/shard_map/terms_near1/pallas_call | solution.py:95
  105.0 0.0 collective-permute-done.14.farthest
  105.1 1.3 %collective-permute-start.19 = (bf16[384,768]{1,0:T(8,128)(2,1)S(1)}, bf16[384,768]{1,0:T(8,128)(2,1)S(1)}, u32[]{:S(2)}, u32[]{:S(2)}) collective-permute-start(bf16[384,768]{1,0:T(8,128)(2,1)S(1)} %collective-permute-done.14.farthest), channel_id=1, source_target_pairs={{0,1},{1,2},{2,3},{4,5},{5,6},{6,7},{8,9},{9,10},{10,11},{12,13},{... | collective-permute-start | bytes 1769480 | tf_op jit(solution)/shard_map/wide_outer2/ppermute | solution.py:80
  106.4 0.0 collective-permute-done.15.q1
  106.4 0.0 collective-permute-done.16.q2
  106.4 0.0 collective-permute-done.17.q3
  106.4 3.5 %merge0.1 = (bf16[768,768]{1,0:T(8,128)(2,1)}, bf16[384,768]{1,0:T(8,128)(2,1)S(1)}) custom-call(s32[1]{0:T(128)} %bitcast.3.edge, bf16[1152,768]{1,0:T(8,128)(2,1)} %collective-permute-done.7.early.usual, bf16[288,768]{1,0:T(8,128)(2,1)S(1)} %join.1.q0, bf16[288,768]{1,0:T(8,128)(2,1)S(1)} %collective-permute-done.15.q1, ...), custom_call_target="tpu_custom_call" | custom-call | flops 1000 | bytes 1000 | tf_op jit(solution)/shard_map/merge0/pallas_call | solution.py:110
  109.9 3.9 %collective-permute-start.18 = (bf16[768,768]{1,0:T(8,128)(2,1)}, bf16[768,768]{1,0:T(8,128)(2,1)}, u32[]{:S(2)}, u32[]{:S(2)}) collective-permute-start(bf16[768,768]{1,0:T(8,128)(2,1)} %get-tuple-element.80.inner0), channel_id=1, source_target_pairs={{0,32},{1,33},{2,34},{3,35},{4,36},{5,37},{6,38},{7,39},{8,40},{9,... | collective-permute-start | bytes 3538952 | tf_op jit(solution)/shard_map/sibling_hop0/ppermute | solution.py:80
  113.9 4.1 %terms_near0.1 = (f32[384,768]{1,0:T(8,128)}, f32[384,768]{1,0:T(8,128)}) custom-call(s32[1]{0:T(128)} %bitcast.c, f32[1]{0:T(128)} %bitcast.6.s, bf16[384,768]{1,0:T(8,128)(2,1)S(1)} %get-tuple-element.102.oth.refs_3_, f32[384,128]{1,0:T(8,128)S(1)} %copy-done.5, f32[16,384]{1,0:T(8,128)S(1)} %copy-done.3, bf16[384,768]{1,0:T(8,128)(2,1)S(1)} %get-tuple-element.82.outer0, ...), custom_call_target="tpu_custom_call" | custom-call | flops 99999997952 | bytes 1000 | tf_op jit(solution)/shard_map/terms_near0/pallas_call | solution.py:388
  118.0 0.0 collective-permute-done.19.hf2
  118.0 0.0 collective-permute-done.20.keys
  118.0 5.6 %terms_far1.1.far_in = f32[384,768]{1,0:T(8,128)S(1)} custom-call(f32[1]{0:T(128)} %bitcast.7.s, bf16[384,768]{1,0:T(8,128)(2,1)S(1)} %get-tuple-element.103.outer.out.refs_0_, f32[384,128]{1,0:T(8,128)S(1)} %copy-done.1, f32[16,384]{1,0:T(8,128)S(1)} %copy-done.3, bf16[1536,768]{1,0:T(8,128)(2,1)} %collective-permute-done.20.keys, ...), custom_call_target="tpu_custom_call" | custom-call | flops 99999997952 | bytes 1000 | tf_op jit(solution)/shard_map/terms_far1/pallas_call | solution.py:95
  123.6 0.0 collective-permute-done.18.hs0
  123.6 4.0 %terms_last.1 = (f32[384,768]{1,0:T(8,128)}, f32[384,768]{1,0:T(8,128)}) custom-call(s32[1]{0:T(128)} %bitcast.c, s32[1]{0:T(128)} %bitcast.1.e, f32[1]{0:T(128)} %bitcast.8.s, bf16[384,768]{1,0:T(8,128)(2,1)S(1)} %get-tuple-element.103.outer.out.refs_0_, f32[384,128]{1,0:T(8,128)S(1)} %copy-done.1, ...), custom_call_target="tpu_custom_call", output_to_operand_aliasing={{0}: (9, {}), {1}: (10, {})} | custom-call | flops 1000 | bytes 1000 | tf_op jit(solution)/shard_map/terms_last/pallas_call | solution.py:434
  (13 shorter events, 0.0 us)
Async XLA Ops:
  2.0 10.7 %collective-permute-start = (bf16[384,768]{1,0:T(8,128)(2,1)S(1)}, bf16[384,768]{1,0:T(8,128)(2,1)S(1)}, u32[]{:S(2)}, u32[]{:S(2)}) collective-permute-start(bf16[384,768]{1,0:T(8,128)(2,1)S(1)} %get-tuple-element.102.oth.refs_3_), channel_id=1, source_target_pairs={{0,32},{1,33},{2,34},{3,35},{4,36},{5,37},{6,38},{7,39},{8,40},{9,... | collective-permute-start | bytes 1769480 | tf_op jit(solution)/shard_map/swap/ppermute | solution.py:80
  10.8 31.5 %collective-permute-start.5 = (bf16[384,768]{1,0:T(8,128)(2,1)S(1)}, bf16[384,768]{1,0:T(8,128)(2,1)S(1)}, u32[]{:S(2)}, u32[]{:S(2)}) collective-permute-start(bf16[384,768]{1,0:T(8,128)(2,1)S(1)} %get-tuple-element.103.outer.out.refs_0_), channel_id=1, source_target_pairs={{0,448},{1,449},{2,450},{3,451},{4,452},{5,453},{6,454},{7,455},{8... | collective-permute-start | bytes 1769480 | tf_op jit(solution)/shard_map/own_outer1/ppermute | solution.py:80
  13.6 19.2 %collective-permute-start.1 = (bf16[192,768]{1,0:T(8,128)(2,1)}, bf16[192,768]{1,0:T(8,128)(2,1)}, u32[]{:S(2)}, u32[]{:S(2)}) collective-permute-start(bf16[192,768]{1,0:T(8,128)(2,1)} %get-tuple-element.44), channel_id=1, source_target_pairs={{0,3},{4,7},{8,11},{12,15},{16,19},{20,23},{24,27},{28,31},{35,32}... | collective-permute-start | bytes 884744 | tf_op jit(solution)/shard_map/spread0/ppermute | solution.py:80
  14.9 17.9 %collective-permute-start.2 = (bf16[192,768]{1,0:T(8,128)(2,1)}, bf16[192,768]{1,0:T(8,128)(2,1)}, u32[]{:S(2)}, u32[]{:S(2)}) collective-permute-start(bf16[192,768]{1,0:T(8,128)(2,1)} %get-tuple-element.45), channel_id=1, source_target_pairs={{0,1},{4,5},{8,9},{12,13},{16,17},{20,21},{24,25},{28,29},{35,34},... | collective-permute-start | bytes 884744 | tf_op jit(solution)/shard_map/spread1/ppermute | solution.py:80
  16.3 16.6 %collective-permute-start.3 = (bf16[192,768]{1,0:T(8,128)(2,1)S(1)}, bf16[192,768]{1,0:T(8,128)(2,1)}, u32[]{:S(2)}, u32[]{:S(2)}) collective-permute-start(bf16[192,768]{1,0:T(8,128)(2,1)S(1)} %get-tuple-element.46), channel_id=1, source_target_pairs={{0,2},{4,6},{8,10},{12,14},{16,18},{20,22},{24,26},{28,30},{35,33}... | collective-permute-start | bytes 884744 | tf_op jit(solution)/shard_map/spread2/ppermute | solution.py:80
  17.6 31.9 %collective-permute-start.4 = (bf16[384,768]{1,0:T(8,128)(2,1)S(1)}, bf16[384,768]{1,0:T(8,128)(2,1)S(1)}, u32[]{:S(2)}, u32[]{:S(2)}) collective-permute-start(bf16[384,768]{1,0:T(8,128)(2,1)S(1)} %get-tuple-element.102.oth.refs_3_), channel_id=1, source_target_pairs={{0,96},{1,97},{2,98},{3,99},{4,100},{5,101},{6,102},{7,103},{8,104... | collective-permute-start | bytes 1769480 | tf_op jit(solution)/shard_map/own_inner1/ppermute | solution.py:80
  33.9 30.2 %collective-permute-start.8 = (bf16[192,768]{1,0:T(8,128)(2,1)S(1)}, bf16[192,768]{1,0:T(8,128)(2,1)S(1)}, u32[]{:S(2)}, u32[]{:S(2)}) collective-permute-start(bf16[192,768]{1,0:T(8,128)(2,1)S(1)} %select_select_fusion), channel_id=1, source_target_pairs={{0,476},{1,477},{2,478},{3,479},{4,448},{5,449},{6,450},{7,451},{8... | collective-permute-start | bytes 884744 | tf_op jit(solution)/shard_map/cross/ppermute | solution.py:80
  43.7 27.3 %collective-permute-start.7 = (bf16[1152,768]{1,0:T(8,128)(2,1)}, bf16[1152,768]{1,0:T(8,128)(2,1)}, u32[]{:S(2)}, u32[]{:S(2)}) collective-permute-start(bf16[1152,768]{1,0:T(8,128)(2,1)} %pad_maximum_fusion), channel_id=1, source_target_pairs={{1,0},{2,1},{3,2},{5,4},{6,5},{7,6},{9,8},{10,9},{11,10},{13,12},{... | collective-permute-start | bytes 5308424 | tf_op jit(solution)/shard_map/wide_early/ppermute | solution.py:80
  46.4 3.1 %copy-start = (f32[384,128]{1,0:T(8,128)}, f32[384,128]{1,0:T(8,128)S(1)}, u32[]{:S(2)}) copy-start(f32[384,128]{1,0:T(8,128)S(1)} %get-tuple-element.64.ff) | copy-start | bytes 589828
  46.4 3.1 %copy-start.2 = (f32[16,384]{1,0:T(8,128)}, f32[16,384]{1,0:T(8,128)S(1)}, u32[]{:S(2)}) copy-start(f32[16,384]{1,0:T(8,128)S(1)} %get-tuple-element.65.kf) | copy-start | bytes 73732
  46.4 3.1 %copy-start.4 = (f32[384,128]{1,0:T(8,128)}, f32[384,128]{1,0:T(8,128)S(1)}, u32[]{:S(2)}) copy-start(f32[384,128]{1,0:T(8,128)S(1)} %get-tuple-element.66.nf) | copy-start | bytes 589828
  49.5 15.3 %copy-start.6 = (f32[384,768]{1,0:T(8,128)}, f32[384,768]{1,0:T(8,128)S(1)}, u32[]{:S(2)}) copy-start(f32[384,768]{1,0:T(8,128)S(1)} %get-tuple-element.69.far_in) | copy-start | bytes 3538948
  49.5 15.3 %copy-start.8 = (f32[384,768]{1,0:T(8,128)}, f32[384,768]{1,0:T(8,128)S(1)}, u32[]{:S(2)}) copy-start(f32[384,768]{1,0:T(8,128)S(1)} %get-tuple-element.68.near_in) | copy-start | bytes 3538948
  49.5 21.4 %collective-permute-start.6 = (bf16[384,768]{1,0:T(8,128)(2,1)S(1)}, bf16[384,768]{1,0:T(8,128)(2,1)S(1)}, u32[]{:S(2)}, u32[]{:S(2)}) collective-permute-start(bf16[384,768]{1,0:T(8,128)(2,1)S(1)} %collective-permute-done.4.inner1), channel_id=1, source_target_pairs={{1,0},{2,1},{3,2},{5,4},{6,5},{7,6},{9,8},{10,9},{11,10},{13,12},{... | collective-permute-start | bytes 1769480 | tf_op jit(solution)/shard_map/wide_late/ppermute | solution.py:80
  64.8 15.7 %collective-permute-start.9 = (bf16[192,768]{1,0:T(8,128)(2,1)S(1)}, bf16[192,768]{1,0:T(8,128)(2,1)S(1)}, u32[]{:S(2)}, u32[]{:S(2)}) collective-permute-start(bf16[192,768]{1,0:T(8,128)(2,1)S(1)} %collective-permute-done.8.block.q0), channel_id=1, source_target_pairs={{0,64},{1,65},{2,66},{3,67},{4,68},{5,69},{6,70},{7,71},{8,72},{9,... | collective-permute-start | bytes 884744 | tf_op jit(solution)/shard_map/cross_back/ppermute | solution.py:80
  66.7 13.8 %collective-permute-start.10 = (bf16[96,768]{1,0:T(8,128)(2,1)}, bf16[96,768]{1,0:T(8,128)(2,1)}, u32[]{:S(2)}, u32[]{:S(2)}) collective-permute-start(bf16[96,768]{1,0:T(8,128)(2,1)} %slice.1), channel_id=1, source_target_pairs={{0,448},{1,449},{2,450},{3,451},{4,452},{5,453},{6,454},{7,455},{8... | collective-permute-start | bytes 442376 | tf_op jit(solution)/shard_map/cross_ahead/ppermute | solution.py:80
  71.0 16.5 %collective-permute-start.11 = (bf16[192,768]{1,0:T(8,128)(2,1)S(1)}, bf16[192,768]{1,0:T(8,128)(2,1)S(1)}, u32[]{:S(2)}, u32[]{:S(2)}) collective-permute-start(bf16[192,768]{1,0:T(8,128)(2,1)S(1)} %collective-permute-done.8.block.q0), channel_id=1, source_target_pairs={{1,3},{5,7},{9,11},{13,15},{17,19},{21,23},{25,27},{29,31},{34,32}... | collective-permute-start | bytes 884744 | tf_op jit(solution)/shard_map/gather1_1/ppermute | solution.py:80
  72.2 15.2 %collective-permute-start.12 = (bf16[192,768]{1,0:T(8,128)(2,1)S(1)}, bf16[192,768]{1,0:T(8,128)(2,1)S(1)}, u32[]{:S(2)}, u32[]{:S(2)}) collective-permute-start(bf16[192,768]{1,0:T(8,128)(2,1)S(1)} %collective-permute-done.8.block.q0), channel_id=1, source_target_pairs={{2,3},{6,7},{10,11},{14,15},{18,19},{22,23},{26,27},{30,31},{33,32... | collective-permute-start | bytes 884744 | tf_op jit(solution)/shard_map/gather1_2/ppermute | solution.py:80
  73.5 14.0 %collective-permute-start.13 = (bf16[192,768]{1,0:T(8,128)(2,1)S(1)}, bf16[192,768]{1,0:T(8,128)(2,1)S(1)}, u32[]{:S(2)}, u32[]{:S(2)}) collective-permute-start(bf16[192,768]{1,0:T(8,128)(2,1)S(1)} %collective-permute-done.8.block.q0), channel_id=1, source_target_pairs={{0,3},{4,7},{8,11},{12,15},{16,19},{20,23},{24,27},{28,31},{35,32}... | collective-permute-start | bytes 884744 | tf_op jit(solution)/shard_map/gather1_3/ppermute | solution.py:80
  81.5 23.6 %collective-permute-start.14 = (bf16[384,768]{1,0:T(8,128)(2,1)S(1)}, bf16[384,768]{1,0:T(8,128)(2,1)S(1)}, u32[]{:S(2)}, u32[]{:S(2)}) collective-permute-start(bf16[384,768]{1,0:T(8,128)(2,1)S(1)} %collective-permute-done.5.refs_2_.outer1), channel_id=1, source_target_pairs={{0,480},{1,481},{2,482},{3,483},{4,484},{5,485},{6,486},{7,487},{8... | collective-permute-start | bytes 1769480 | tf_op jit(solution)/shard_map/own_outer2/ppermute | solution.py:80
  87.5 18.9 %collective-permute-start.15 = (bf16[288,768]{1,0:T(8,128)(2,1)S(1)}, bf16[288,768]{1,0:T(8,128)(2,1)S(1)}, u32[]{:S(2)}, u32[]{:S(2)}) collective-permute-start(bf16[288,768]{1,0:T(8,128)(2,1)S(1)} %join.1.q0), channel_id=1, source_target_pairs={{1,3},{5,7},{9,11},{13,15},{17,19},{21,23},{25,27},{29,31},{34,32}... | collective-permute-start | bytes 1327112 | tf_op jit(solution)/shard_map/gather0_1/ppermute | solution.py:80
  88.8 17.6 %collective-permute-start.16 = (bf16[288,768]{1,0:T(8,128)(2,1)S(1)}, bf16[288,768]{1,0:T(8,128)(2,1)S(1)}, u32[]{:S(2)}, u32[]{:S(2)}) collective-permute-start(bf16[288,768]{1,0:T(8,128)(2,1)S(1)} %join.1.q0), channel_id=1, source_target_pairs={{2,3},{6,7},{10,11},{14,15},{18,19},{22,23},{26,27},{30,31},{33,32... | collective-permute-start | bytes 1327112 | tf_op jit(solution)/shard_map/gather0_2/ppermute | solution.py:80
  90.1 16.3 %collective-permute-start.17 = (bf16[288,768]{1,0:T(8,128)(2,1)S(1)}, bf16[288,768]{1,0:T(8,128)(2,1)S(1)}, u32[]{:S(2)}, u32[]{:S(2)}) collective-permute-start(bf16[288,768]{1,0:T(8,128)(2,1)S(1)} %join.1.q0), channel_id=1, source_target_pairs={{0,3},{4,7},{8,11},{12,15},{16,19},{20,23},{24,27},{28,31},{35,32}... | collective-permute-start | bytes 1327112 | tf_op jit(solution)/shard_map/gather0_3/ppermute | solution.py:80
  91.4 9.6 %copy-start.3 = (f32[16,384]{1,0:T(8,128)S(1)}, f32[16,384]{1,0:T(8,128)}, u32[]{:S(2)}) copy-start(f32[16,384]{1,0:T(8,128)} %copy-done.2) | copy-start | bytes 73732
  91.4 9.6 %copy-start.5 = (f32[384,128]{1,0:T(8,128)S(1)}, f32[384,128]{1,0:T(8,128)}, u32[]{:S(2)}) copy-start(f32[384,128]{1,0:T(8,128)} %copy-done.4) | copy-start | bytes 589828
  91.4 9.6 %copy-start.9 = (f32[384,768]{1,0:T(8,128)S(1)}, f32[384,768]{1,0:T(8,128)}, u32[]{:S(2)}) copy-start(f32[384,768]{1,0:T(8,128)} %copy-done.8) | copy-start | bytes 3538948
  94.7 23.2 %collective-permute-start.20 = (bf16[1536,768]{1,0:T(8,128)(2,1)}, bf16[1536,768]{1,0:T(8,128)(2,1)}, u32[]{:S(2)}, u32[]{:S(2)}) collective-permute-start(bf16[1536,768]{1,0:T(8,128)(2,1)} %merge1.1.keys), channel_id=1, source_target_pairs={{0,32},{1,33},{2,34},{3,35},{4,36},{5,37},{6,38},{7,39},{8,40},{9,... | collective-permute-start | bytes 7077896 | tf_op jit(solution)/shard_map/sibling1/ppermute | solution.py:80
  105.1 12.9 %collective-permute-start.19 = (bf16[384,768]{1,0:T(8,128)(2,1)S(1)}, bf16[384,768]{1,0:T(8,128)(2,1)S(1)}, u32[]{:S(2)}, u32[]{:S(2)}) collective-permute-start(bf16[384,768]{1,0:T(8,128)(2,1)S(1)} %collective-permute-done.14.farthest), channel_id=1, source_target_pairs={{0,1},{1,2},{2,3},{4,5},{5,6},{6,7},{8,9},{9,10},{10,11},{12,13},{... | collective-permute-start | bytes 1769480 | tf_op jit(solution)/shard_map/wide_outer2/ppermute | solution.py:80
  109.9 13.7 %collective-permute-start.18 = (bf16[768,768]{1,0:T(8,128)(2,1)}, bf16[768,768]{1,0:T(8,128)(2,1)}, u32[]{:S(2)}, u32[]{:S(2)}) collective-permute-start(bf16[768,768]{1,0:T(8,128)(2,1)} %get-tuple-element.80.inner0), channel_id=1, source_target_pairs={{0,32},{1,33},{2,34},{3,35},{4,36},{5,37},{6,38},{7,39},{8,40},{9,... | collective-permute-start | bytes 3538952 | tf_op jit(solution)/shard_map/sibling_hop0/ppermute | solution.py:80
  113.9 4.1 %copy-start.1 = (f32[384,128]{1,0:T(8,128)S(1)}, f32[384,128]{1,0:T(8,128)}, u32[]{:S(2)}) copy-start(f32[384,128]{1,0:T(8,128)} %copy-done) | copy-start | bytes 589828
  113.9 4.1 %copy-start.7 = (f32[384,768]{1,0:T(8,128)S(1)}, f32[384,768]{1,0:T(8,128)}, u32[]{:S(2)}) copy-start(f32[384,768]{1,0:T(8,128)} %copy-done.6) | copy-start | bytes 3538948

commit v9 on v8

--- a/solution.py
+++ b/solution.py
@@ -144,8 +144,10 @@
 
 
 def add_terms(total, query, query_factor, key_factors, scale, items):
-    for keys, row, own in items:
-        part = term(query, query_factor, keys, key_factors[row : row + 1, :], scale, own)
+    rows = query.shape[0]
+    for keys, place, own in items:
+        chosen = key_factors[:, place * rows : place * rows + keys.shape[0]]
+        part = term(query, query_factor, keys, chosen, scale, own)
         total = part if total is None else total + part
     return total
 
@@ -236,13 +238,13 @@
     def factors_kernel(*refs):
         sources, (keys, near, far) = refs[:-3], refs[-3:]
         for k, source in enumerate(sources):
-            keys[k : k + 1, :] = 0.5 * jnp.exp(5.0 - source[...].reshape(1, rows))
-        near[...] = jnp.broadcast_to(keys[8:9, :], (128, rows)).T
-        far[...] = jnp.broadcast_to(keys[0:1, :], (128, rows)).T
+            keys[:, k * rows : (k + 1) * rows] = 0.5 * jnp.exp(5.0 - source[...].reshape(1, rows))
+        near[...] = jnp.broadcast_to(keys[:, 8 * rows : 9 * rows], (128, rows)).T
+        far[...] = jnp.broadcast_to(keys[:, :rows], (128, rows)).T
 
     key_factors, near_factor, far_factor = call(
         "factors", factors_kernel,
-        [jax.ShapeDtypeStruct(shape, jnp.float32) for shape in ((16, rows), (rows, 128), (rows, 128))],
+        [jax.ShapeDtypeStruct(shape, jnp.float32) for shape in ((1, 16 * rows), (rows, 128), (rows, 128))],
         (), tuple(lax.optimization_barrier((*normalizers, held))[:-1]),
     )
     total = jax.ShapeDtypeStruct((rows, width), jnp.float32)
@@ -280,13 +282,13 @@
         out[...] = block[quarter:, :]
 
     outer_part = call(
-        "slice", slice_kernel, jax.ShapeDtypeStruct((quarter, width), half), (), (crossed,),
+        "slice", slice_kernel, jax.ShapeDtypeStruct((quarter, width), half), (), (after(crossed, *sums),),
         100_000_000,
     )
     back = send("cross_back", after(crossed, outer_part), to_previous_chip)
     ahead = send("cross_ahead", outer_part, to_next_chip)
-    late, early, _ = lax.optimization_barrier((late, early, outer_part))
-    crossed = after(crossed, late, early)
+    early, _ = lax.optimization_barrier((early, outer_part))
+    crossed = after(crossed, early)
 
     def collect(name, mine):
         q1 = send(name + "1", mine, line_to_line(2, 0))
@@ -333,8 +335,7 @@
     def near_kernel(s, oth, nf, kf, keys, near_in, near):
         near[...] = add_terms(
             near_in[...], oth[...], nf[:, :1], kf, s[0],
-            [(keys[:rows, :], 4, False), (keys[rows : 2 * rows, :], 5, False),
-             (keys[3 * rows :, :], 3, False)],
+            [(keys[: 2 * rows, :], 4, False), (keys[3 * rows :, :], 3, False)],
         )
 
     near_sum = call(
@@ -369,7 +370,7 @@
     def near0_kernel(c, s, oth, nf, kf, outer0, inner0, near_in, image_grad, caption_grad, held_sum, sem):
         held_sum[...] = s[0] * add_terms(
             near_in[...], oth[...], nf[:, :1], kf, s[0],
-            [(outer0[...], 7, False), (inner0[:rows, :], 6, False)],
+            [(jnp.concatenate([inner0[:rows, :], outer0[...]], axis=0), 6, False)],
         )
 
         @pl.when(c[0] == 1)
@@ -400,8 +401,8 @@
     def far1_kernel(s, out, ff, kf, keys, farthest, far_in, far):
         far[...] = add_terms(
             far_in[...], out[...], ff[:, :1], kf, s[0],
-            [(keys[k * rows : (k + 1) * rows, :], row, False) for k, row in enumerate((12, 13, 9, 10))]
-            + [(farthest[...], 11, False)],
+            [(keys[: 2 * rows, :], 12, False), (keys[2 * rows :, :], 9, False),
+             (farthest[...], 11, False)],
         )
 
     far_sum = call(
@@ -415,7 +416,7 @@
         farthest = jnp.where(e[0] == 1, hs0[rows:, :], hf2[...])
         held_sum[...] = s[0] * add_terms(
             far_in[...], out[...], ff[:, :1], kf, s[0],
-            [(hs0[:rows, :], 14, False), (farthest, 15, False)],
+            [(jnp.concatenate([hs0[:rows, :], farthest], axis=0), 14, False)],
         )
 
         @pl.when(c[0] == 1)

time: 129 us -> 133 us (1.031)
  starting transfers between devices: 70.6 us -> 87.6 us
  waiting for transfers between devices: 19.8 us -> 8.21 us
  Pallas kernels: 30.2 us -> 28.3 us
    ppermute x21, starting transfers between devices: 70.6 us -> 87.6 us  [send(): return lax.ppermute(x, AXES, pairs(target))]
    ppermute x21, waiting for transfers between devices: 19.8 us -> 8.21 us  [send(): return lax.ppermute(x, AXES, pairs(target))]
    pallas_call x7, Pallas kernels: 15.3 us -> 13.3 us  [call(): pl.pallas_call(kernel, out_shape=out_shape, in_specs=[scalars() for _ in...]
  transfers between devices with their start and end apart: 21 -> 21, of which waited for: 3 -> 3; matrix products, arithmetic and copies ran while one was open for 3% -> 2% of each run, Pallas kernels for 21% -> 19%
where the time goes in v9:
time: 133 us; the launch traced here: 132 us
  starting transfers between devices  87.6 us (66%)
  Pallas kernels  28.3 us (21%)
  waiting for transfers between devices  8.21 us (6%)
  other arithmetic  4.79 us (4%)
  between operations  2.07 us (2%)
    ppermute x21, starting transfers between devices, send(): return lax.ppermute(x, AXES, pairs(target))  87.6 us
    pallas_call x7, Pallas kernels, call(): pl.pallas_call(kernel, out_shape=out_shape, in_specs=[scalars() for _ in...  13.3 us
    ppermute x21, waiting for transfers between devices, send(): return lax.ppermute(x, AXES, pairs(target))  8.21 us
    pallas_call x2, Pallas kernels, assemble(): pl.pallas_call(kernel, out_shape=out_shape, in_specs=[scalars() for _ in...  7.65 us
    pallas_call x1, Pallas kernels, on_device(): pl.pallas_call(near0_kernel, out_shape=[total, total], in_specs=[scalars(...  3.78 us
    pallas_call x1, Pallas kernels, on_device(): pl.pallas_call(last_kernel, out_shape=[total, total], in_specs=[scalars()...  3.56 us
  transfers between devices with their start and end apart: 21, of which 3 were waited for; matrix products, arithmetic and copies ran while one was open for 2% of the time, Pallas kernels for 19%

profile of v9, /device:TPU:1, one launch (start us, length us, event | category | flops | bytes accessed | tf_op | source)
XLA Modules:
  0.0 131.9 jit_solution(3269085270001019011)
XLA Ops:
  0.6 2.2 %broadcast_select_fusion = (bf16[384,768]{1,0:T(8,128)(2,1)}, bf16[384,768]{1,0:T(8,128)(2,1)S(1)}) fusion(bf16[384,768]{1,0:T(8,128)(2,1)} %param.5, bf16[384,768]{1,0:T(8,128)(2,1)} %param.6, pred[]{:T(512)S(6)} %eq.62), kind=kLoop, calls=%fused_computation.1 | loop fusion | flops 589824 | bytes 2359297 | tf_op jit(solution)/shard_map/jit(_where)/select_n | solution.py:183
  2.8 8.8 %collective-permute-start = (bf16[384,768]{1,0:T(8,128)(2,1)}, bf16[384,768]{1,0:T(8,128)(2,1)S(1)}, u32[]{:S(2)}, u32[]{:S(2)}) collective-permute-start(bf16[384,768]{1,0:T(8,128)(2,1)} %get-tuple-element.102.oth.refs_3_), channel_id=1, source_target_pairs={{0,32},{1,33},{2,34},{3,35},{4,36},{5,37},{6,38},{7,39},{8,40},{9,... | collective-permute-start | bytes 1769480 | tf_op jit(solution)/shard_map/swap/ppermute | solution.py:80
  11.6 1.9 %collective-permute-start.4 = (bf16[384,768]{1,0:T(8,128)(2,1)S(1)}, bf16[384,768]{1,0:T(8,128)(2,1)S(1)}, u32[]{:S(2)}, u32[]{:S(2)}) collective-permute-start(bf16[384,768]{1,0:T(8,128)(2,1)S(1)} %get-tuple-element.103.outer.out.refs_0_), channel_id=1, source_target_pairs={{0,448},{1,449},{2,450},{3,451},{4,452},{5,453},{6,454},{7,455},{8... | collective-permute-start | bytes 1769480 | tf_op jit(solution)/shard_map/own_outer1/ppermute | solution.py:80
  13.6 0.0 collective-permute-done.inner.refs_1_
  13.6 0.1 cut.1
  13.7 1.3 collective-permute-start.1
  15.0 0.7 collective-permute-start.2
  15.6 1.4 %collective-permute-start.3 = (bf16[192,768]{1,0:T(8,128)(2,1)S(1)}, bf16[192,768]{1,0:T(8,128)(2,1)}, u32[]{:S(2)}, u32[]{:S(2)}) collective-permute-start(bf16[192,768]{1,0:T(8,128)(2,1)S(1)} %get-tuple-element.46), channel_id=1, source_target_pairs={{0,2},{4,6},{8,10},{12,14},{16,18},{20,22},{24,26},{28,30},{35,33}... | collective-permute-start | bytes 884744 | tf_op jit(solution)/shard_map/spread2/ppermute | solution.py:80
  17.0 12.5 %collective-permute-start.13 = (bf16[384,768]{1,0:T(8,128)(2,1)}, bf16[384,768]{1,0:T(8,128)(2,1)}, u32[]{:S(2)}, u32[]{:S(2)}) collective-permute-start(bf16[384,768]{1,0:T(8,128)(2,1)} %get-tuple-element.102.oth.refs_3_), channel_id=1, source_target_pairs={{0,96},{1,97},{2,98},{3,99},{4,100},{5,101},{6,102},{7,103},{8,104... | collective-permute-start | bytes 1769480 | tf_op jit(solution)/shard_map/own_inner1/ppermute | solution.py:80
  30.5 1.2 dynamic-slice_select_fusion
  31.6 0.0 collective-permute-done.1
  31.7 0.0 collective-permute-done.2
  31.7 0.0 collective-permute-done.3
  31.7 0.1 select_select_fusion
  31.8 8.3 %collective-permute-start.6 = (bf16[192,768]{1,0:T(8,128)(2,1)S(1)}, bf16[192,768]{1,0:T(8,128)(2,1)S(1)}, u32[]{:S(2)}, u32[]{:S(2)}) collective-permute-start(bf16[192,768]{1,0:T(8,128)(2,1)S(1)} %select_select_fusion), channel_id=1, source_target_pairs={{0,476},{1,477},{2,478},{3,479},{4,448},{5,449},{6,450},{7,451},{8... | collective-permute-start | bytes 884744 | tf_op jit(solution)/shard_map/cross/ppermute | solution.py:80
  40.0 0.0 collective-permute-done.4.refs_2_.outer1
  40.1 1.4 %pad_maximum_fusion = bf16[1152,768]{1,0:T(8,128)(2,1)} fusion(bf16[384,768]{1,0:T(8,128)(2,1)S(1)} %collective-permute-done.4.refs_2_.outer1, bf16[384,768]{1,0:T(8,128)(2,1)S(1)} %get-tuple-element.103.outer.out.refs_0_, bf16[384,768]{1,0:T(8,128)(2,1)S(1)} %collective-permute-done.inner.refs_1_), kind=kLoop, calls=%fused_computation | loop fusion | flops 5308416 | bytes 3538944 | tf_op jit(solution)/shard_map/concatenate | solution.py:204
  41.4 2.5 %collective-permute-start.5 = (bf16[1152,768]{1,0:T(8,128)(2,1)}, bf16[1152,768]{1,0:T(8,128)(2,1)}, u32[]{:S(2)}, u32[]{:S(2)}) collective-permute-start(bf16[1152,768]{1,0:T(8,128)(2,1)} %pad_maximum_fusion), channel_id=1, source_target_pairs={{1,0},{2,1},{3,2},{5,4},{6,5},{7,6},{9,8},{10,9},{11,10},{13,12},{... | collective-permute-start | bytes 5308424 | tf_op jit(solution)/shard_map/wide_early/ppermute | solution.py:80
  43.9 0.2 factors.1
  44.1 0.0 copy-start
  44.1 0.0 copy-start.2
  44.2 0.0 copy-start.4
  44.2 4.4 %terms_own0.1 = (f32[384,768]{1,0:T(8,128)S(1)}, f32[384,768]{1,0:T(8,128)S(1)}) custom-call(f32[1]{0:T(128)} %bitcast.4.s, bf16[384,768]{1,0:T(8,128)(2,1)} %get-tuple-element.102.oth.refs_3_, bf16[384,768]{1,0:T(8,128)(2,1)S(1)} %get-tuple-element.103.outer.out.refs_0_, f32[384,128]{1,0:T(8,128)S(1)} %get-tuple-element.67.nf, ...), custom_call_target="tpu_custom_call" | custom-call | flops 99999997952 | bytes 1000 | tf_op jit(solution)/shard_map/terms_own0/pallas_call | solution.py:95
  48.6 0.0 copy-done
  48.6 0.0 copy-start.6
  48.6 0.0 collective-permute-done.6.block.q0
  48.7 1.0 copy-done.6
  49.6 15.3 %collective-permute-start.7 = (bf16[192,768]{1,0:T(8,128)(2,1)S(1)}, bf16[192,768]{1,0:T(8,128)(2,1)S(1)}, u32[]{:S(2)}, u32[]{:S(2)}) collective-permute-start(bf16[192,768]{1,0:T(8,128)(2,1)S(1)} %collective-permute-done.6.block.q0), channel_id=1, source_target_pairs={{0,64},{1,65},{2,66},{3,67},{4,68},{5,69},{6,70},{7,71},{8,72},{9,... | collective-permute-start | bytes 884744 | tf_op jit(solution)/shard_map/cross_back/ppermute | solution.py:80
  65.0 3.3 %collective-permute-start.8 = (bf16[96,768]{1,0:T(8,128)(2,1)S(1)}, bf16[96,768]{1,0:T(8,128)(2,1)S(1)}, u32[]{:S(2)}, u32[]{:S(2)}) collective-permute-start(bf16[96,768]{1,0:T(8,128)(2,1)S(1)} %slice.1), channel_id=1, source_target_pairs={{0,448},{1,449},{2,450},{3,451},{4,452},{5,453},{6,454},{7,455},{8... | collective-permute-start | bytes 442376 | tf_op jit(solution)/shard_map/cross_ahead/ppermute | solution.py:80
  68.3 0.0 collective-permute-done.13.inner1
  68.3 11.3 %collective-permute-start.14 = (bf16[384,768]{1,0:T(8,128)(2,1)}, bf16[384,768]{1,0:T(8,128)(2,1)S(1)}, u32[]{:S(2)}, u32[]{:S(2)}) collective-permute-start(bf16[384,768]{1,0:T(8,128)(2,1)} %collective-permute-done.13.inner1), channel_id=1, source_target_pairs={{1,0},{2,1},{3,2},{5,4},{6,5},{7,6},{9,8},{10,9},{11,10},{13,12},{... | collective-permute-start | bytes 1769480 | tf_op jit(solution)/shard_map/wide_late/ppermute | solution.py:80
  79.6 0.0 collective-permute-done.5.early.usual
  79.7 1.3 collective-permute-start.10
  81.0 1.3 collective-permute-start.11
  82.3 0.0 collective-permute-done.8.second
  82.3 1.3 collective-permute-start.9
  83.6 0.0 collective-permute-done.7.first
  83.6 4.0 %collective-permute-start.12 = (bf16[384,768]{1,0:T(8,128)(2,1)S(1)}, bf16[384,768]{1,0:T(8,128)(2,1)S(1)}, u32[]{:S(2)}, u32[]{:S(2)}) collective-permute-start(bf16[384,768]{1,0:T(8,128)(2,1)S(1)} %collective-permute-done.4.refs_2_.outer1), channel_id=1, source_target_pairs={{0,480},{1,481},{2,482},{3,483},{4,484},{5,485},{6,486},{7,487},{8... | collective-permute-start | bytes 1769480 | tf_op jit(solution)/shard_map/own_outer2/ppermute | solution.py:80
  87.6 2.9 %collective-permute-done.10.q2 = bf16[192,768]{1,0:T(8,128)(2,1)S(1)} collective-permute-done((bf16[192,768]{1,0:T(8,128)(2,1)S(1)}, bf16[192,768]{1,0:T(8,128)(2,1)S(1)}, u32[]{:S(2)}, u32[]{:S(2)}) %collective-permute-start.10) | collective-permute-done | bytes 294944 | tf_op jit(solution)/shard_map/gather1_2/ppermute | solution.py:80
  90.5 0.0 collective-permute-done.11.q3
  90.5 5.1 %collective-permute-done.9.q1 = bf16[192,768]{1,0:T(8,128)(2,1)S(1)} collective-permute-done((bf16[192,768]{1,0:T(8,128)(2,1)S(1)}, bf16[192,768]{1,0:T(8,128)(2,1)S(1)}, u32[]{:S(2)}, u32[]{:S(2)}) %collective-permute-start.9) | collective-permute-done | bytes 294944 | tf_op jit(solution)/shard_map/gather1_1/ppermute | solution.py:80
  95.6 1.3 collective-permute-start.15
  96.9 1.3 collective-permute-start.16
  98.2 1.3 collective-permute-start.17
  99.5 0.0 collective-permute-done.14.late
  99.5 0.0 copy-start.5
  99.6 0.0 copy-start.7
  99.6 4.2 %merge1.1.keys = bf16[1536,768]{1,0:T(8,128)(2,1)} custom-call(s32[1]{0:T(128)} %bitcast.3.edge, bf16[1152,768]{1,0:T(8,128)(2,1)} %collective-permute-done.5.early.usual, bf16[384,768]{1,0:T(8,128)(2,1)S(1)} %collective-permute-done.14.late, bf16[384,768]{1,0:T(8,128)(2,1)S(1)} %collective-permute-done.4.refs_2_.outer1, ...), custom_call_target="tpu_custom_call" | custom-call | flops 1000 | bytes 1000 | tf_op jit(solution)/shard_map/merge1/pallas_call | solution.py:110
  103.8 5.3 %collective-permute-start.20 = (bf16[1536,768]{1,0:T(8,128)(2,1)}, bf16[1536,768]{1,0:T(8,128)(2,1)}, u32[]{:S(2)}, u32[]{:S(2)}) collective-permute-start(bf16[1536,768]{1,0:T(8,128)(2,1)} %merge1.1.keys), channel_id=1, source_target_pairs={{0,32},{1,33},{2,34},{3,35},{4,36},{5,37},{6,38},{7,39},{8,40},{9,... | collective-permute-start | bytes 7077896 | tf_op jit(solution)/shard_map/sibling1/ppermute | solution.py:80
  109.1 3.9 %terms_near1.1.near_in = f32[384,768]{1,0:T(8,128)S(1)} custom-call(f32[1]{0:T(128)} %bitcast.5.s, bf16[384,768]{1,0:T(8,128)(2,1)} %get-tuple-element.102.oth.refs_3_, f32[384,128]{1,0:T(8,128)S(1)} %copy-done.5, f32[1,6144]{1,0:T(1,128)S(1)} %copy-done.3, bf16[1536,768]{1,0:T(8,128)(2,1)} %merge1.1.keys, f32[384,768]{1,0:T(8,128)S(1)} %copy-done.7), custom_call_target="tpu_custom_call" | custom-call | flops 99999997952 | bytes 1000 | tf_op jit(solution)/shard_map/terms_near1/pallas_call | solution.py:95
  113.0 0.0 collective-permute-done.12.farthest
  113.1 1.3 collective-permute-start.19
  114.4 0.0 collective-permute-done.15.q1
  114.4 0.0 collective-permute-done.16.q2
  114.4 0.0 collective-permute-done.17.q3
  114.4 3.4 %merge0.1 = (bf16[768,768]{1,0:T(8,128)(2,1)}, bf16[384,768]{1,0:T(8,128)(2,1)S(1)}) custom-call(s32[1]{0:T(128)} %bitcast.3.edge, bf16[1152,768]{1,0:T(8,128)(2,1)} %collective-permute-done.5.early.usual, bf16[288,768]{1,0:T(8,128)(2,1)S(1)} %join.1.q0, bf16[288,768]{1,0:T(8,128)(2,1)S(1)} %collective-permute-done.15.q1, ...), custom_call_target="tpu_custom_call" | custom-call | flops 1000 | bytes 1000 | tf_op jit(solution)/shard_map/merge0/pallas_call | solution.py:110
  117.8 1.9 %collective-permute-start.18 = (bf16[768,768]{1,0:T(8,128)(2,1)}, bf16[768,768]{1,0:T(8,128)(2,1)}, u32[]{:S(2)}, u32[]{:S(2)}) collective-permute-start(bf16[768,768]{1,0:T(8,128)(2,1)} %get-tuple-element.80.inner0), channel_id=1, source_target_pairs={{0,32},{1,33},{2,34},{3,35},{4,36},{5,37},{6,38},{7,39},{8,40},{9,... | collective-permute-start | bytes 3538952 | tf_op jit(solution)/shard_map/sibling_hop0/ppermute | solution.py:80
  119.8 0.0 copy-start.1
  119.8 3.8 %terms_near0.1 = (f32[384,768]{1,0:T(8,128)}, f32[384,768]{1,0:T(8,128)}) custom-call(s32[1]{0:T(128)} %bitcast.c, f32[1]{0:T(128)} %bitcast.6.s, bf16[384,768]{1,0:T(8,128)(2,1)} %get-tuple-element.102.oth.refs_3_, f32[384,128]{1,0:T(8,128)S(1)} %copy-done.5, f32[1,6144]{1,0:T(1,128)S(1)} %copy-done.3, bf16[384,768]{1,0:T(8,128)(2,1)S(1)} %get-tuple-element.82.outer0, ...), custom_call_target="tpu_custom_call" | custom-call | flops 99999997952 | bytes 1000 | tf_op jit(solution)/shard_map/terms_near0/pallas_call | solution.py:389
  123.5 0.1 collective-permute-done.19.hf2
  123.7 0.0 collective-permute-done.20.keys
  123.7 4.7 %terms_far1.1.far_in = f32[384,768]{1,0:T(8,128)S(1)} custom-call(f32[1]{0:T(128)} %bitcast.7.s, bf16[384,768]{1,0:T(8,128)(2,1)S(1)} %get-tuple-element.103.outer.out.refs_0_, f32[384,128]{1,0:T(8,128)S(1)} %copy-done.1, f32[1,6144]{1,0:T(1,128)S(1)} %copy-done.3, bf16[1536,768]{1,0:T(8,128)(2,1)} %collective-permute-done.20.keys, ...), custom_call_target="tpu_custom_call" | custom-call | flops 99999997952 | bytes 1000 | tf_op jit(solution)/shard_map/terms_far1/pallas_call | solution.py:95
  128.4 0.0 collective-permute-done.18.hs0
  128.4 3.6 %terms_last.1 = (f32[384,768]{1,0:T(8,128)}, f32[384,768]{1,0:T(8,128)}) custom-call(s32[1]{0:T(128)} %bitcast.c, s32[1]{0:T(128)} %bitcast.1.e, f32[1]{0:T(128)} %bitcast.8.s, bf16[384,768]{1,0:T(8,128)(2,1)S(1)} %get-tuple-element.103.outer.out.refs_0_, f32[384,128]{1,0:T(8,128)S(1)} %copy-done.1, ...), custom_call_target="tpu_custom_call", output_to_operand_aliasing={{0}: (9, {}), {1}: (10, {})} | custom-call | flops 1000 | bytes 1000 | tf_op jit(solution)/shard_map/terms_last/pallas_call | solution.py:435
  (9 shorter events, 0.1 us)
Async XLA Ops:
  2.8 10.7 %collective-permute-start = (bf16[384,768]{1,0:T(8,128)(2,1)}, bf16[384,768]{1,0:T(8,128)(2,1)S(1)}, u32[]{:S(2)}, u32[]{:S(2)}) collective-permute-start(bf16[384,768]{1,0:T(8,128)(2,1)} %get-tuple-element.102.oth.refs_3_), channel_id=1, source_target_pairs={{0,32},{1,33},{2,34},{3,35},{4,36},{5,37},{6,38},{7,39},{8,40},{9,... | collective-permute-start | bytes 1769480 | tf_op jit(solution)/shard_map/swap/ppermute | solution.py:80
  11.6 28.4 %collective-permute-start.4 = (bf16[384,768]{1,0:T(8,128)(2,1)S(1)}, bf16[384,768]{1,0:T(8,128)(2,1)S(1)}, u32[]{:S(2)}, u32[]{:S(2)}) collective-permute-start(bf16[384,768]{1,0:T(8,128)(2,1)S(1)} %get-tuple-element.103.outer.out.refs_0_), channel_id=1, source_target_pairs={{0,448},{1,449},{2,450},{3,451},{4,452},{5,453},{6,454},{7,455},{8... | collective-permute-start | bytes 1769480 | tf_op jit(solution)/shard_map/own_outer1/ppermute | solution.py:80
  13.7 18.0 %collective-permute-start.1 = (bf16[192,768]{1,0:T(8,128)(2,1)S(1)}, bf16[192,768]{1,0:T(8,128)(2,1)S(1)}, u32[]{:S(2)}, u32[]{:S(2)}) collective-permute-start(bf16[192,768]{1,0:T(8,128)(2,1)S(1)} %get-tuple-element.44), channel_id=1, source_target_pairs={{0,3},{4,7},{8,11},{12,15},{16,19},{20,23},{24,27},{28,31},{35,32}... | collective-permute-start | bytes 884744 | tf_op jit(solution)/shard_map/spread0/ppermute | solution.py:80
  15.0 16.7 %collective-permute-start.2 = (bf16[192,768]{1,0:T(8,128)(2,1)S(1)}, bf16[192,768]{1,0:T(8,128)(2,1)S(1)}, u32[]{:S(2)}, u32[]{:S(2)}) collective-permute-start(bf16[192,768]{1,0:T(8,128)(2,1)S(1)} %get-tuple-element.45), channel_id=1, source_target_pairs={{0,1},{4,5},{8,9},{12,13},{16,17},{20,21},{24,25},{28,29},{35,34},... | collective-permute-start | bytes 884744 | tf_op jit(solution)/shard_map/spread1/ppermute | solution.py:80
  15.6 16.0 %collective-permute-start.3 = (bf16[192,768]{1,0:T(8,128)(2,1)S(1)}, bf16[192,768]{1,0:T(8,128)(2,1)}, u32[]{:S(2)}, u32[]{:S(2)}) collective-permute-start(bf16[192,768]{1,0:T(8,128)(2,1)S(1)} %get-tuple-element.46), channel_id=1, source_target_pairs={{0,2},{4,6},{8,10},{12,14},{16,18},{20,22},{24,26},{28,30},{35,33}... | collective-permute-start | bytes 884744 | tf_op jit(solution)/shard_map/spread2/ppermute | solution.py:80
  17.0 51.3 %collective-permute-start.13 = (bf16[384,768]{1,0:T(8,128)(2,1)}, bf16[384,768]{1,0:T(8,128)(2,1)}, u32[]{:S(2)}, u32[]{:S(2)}) collective-permute-start(bf16[384,768]{1,0:T(8,128)(2,1)} %get-tuple-element.102.oth.refs_3_), channel_id=1, source_target_pairs={{0,96},{1,97},{2,98},{3,99},{4,100},{5,101},{6,102},{7,103},{8,104... | collective-permute-start | bytes 1769480 | tf_op jit(solution)/shard_map/own_inner1/ppermute | solution.py:80
  31.8 16.9 %collective-permute-start.6 = (bf16[192,768]{1,0:T(8,128)(2,1)S(1)}, bf16[192,768]{1,0:T(8,128)(2,1)S(1)}, u32[]{:S(2)}, u32[]{:S(2)}) collective-permute-start(bf16[192,768]{1,0:T(8,128)(2,1)S(1)} %select_select_fusion), channel_id=1, source_target_pairs={{0,476},{1,477},{2,478},{3,479},{4,448},{5,449},{6,450},{7,451},{8... | collective-permute-start | bytes 884744 | tf_op jit(solution)/shard_map/cross/ppermute | solution.py:80
  41.4 38.2 %collective-permute-start.5 = (bf16[1152,768]{1,0:T(8,128)(2,1)}, bf16[1152,768]{1,0:T(8,128)(2,1)}, u32[]{:S(2)}, u32[]{:S(2)}) collective-permute-start(bf16[1152,768]{1,0:T(8,128)(2,1)} %pad_maximum_fusion), channel_id=1, source_target_pairs={{1,0},{2,1},{3,2},{5,4},{6,5},{7,6},{9,8},{10,9},{11,10},{13,12},{... | collective-permute-start | bytes 5308424 | tf_op jit(solution)/shard_map/wide_early/ppermute | solution.py:80
  44.1 4.4 %copy-start = (f32[384,128]{1,0:T(8,128)}, f32[384,128]{1,0:T(8,128)S(1)}, u32[]{:S(2)}) copy-start(f32[384,128]{1,0:T(8,128)S(1)} %get-tuple-element.64.ff) | copy-start | bytes 589828
  44.1 4.4 %copy-start.2 = (f32[1,6144]{1,0:T(1,128)}, f32[1,6144]{1,0:T(1,128)S(1)}, u32[]{:S(2)}) copy-start(f32[1,6144]{1,0:T(1,128)S(1)} %get-tuple-element.65.kf) | copy-start | bytes 73732
  44.2 4.4 %copy-start.4 = (f32[384,128]{1,0:T(8,128)}, f32[384,128]{1,0:T(8,128)S(1)}, u32[]{:S(2)}) copy-start(f32[384,128]{1,0:T(8,128)S(1)} %get-tuple-element.67.nf) | copy-start | bytes 589828
  48.6 1.0 copy-start.6
  49.6 33.9 %collective-permute-start.7 = (bf16[192,768]{1,0:T(8,128)(2,1)S(1)}, bf16[192,768]{1,0:T(8,128)(2,1)S(1)}, u32[]{:S(2)}, u32[]{:S(2)}) collective-permute-start(bf16[192,768]{1,0:T(8,128)(2,1)S(1)} %collective-permute-done.6.block.q0), channel_id=1, source_target_pairs={{0,64},{1,65},{2,66},{3,67},{4,68},{5,69},{6,70},{7,71},{8,72},{9,... | collective-permute-start | bytes 884744 | tf_op jit(solution)/shard_map/cross_back/ppermute | solution.py:80
  65.0 17.3 %collective-permute-start.8 = (bf16[96,768]{1,0:T(8,128)(2,1)S(1)}, bf16[96,768]{1,0:T(8,128)(2,1)S(1)}, u32[]{:S(2)}, u32[]{:S(2)}) collective-permute-start(bf16[96,768]{1,0:T(8,128)(2,1)S(1)} %slice.1), channel_id=1, source_target_pairs={{0,448},{1,449},{2,450},{3,451},{4,452},{5,453},{6,454},{7,455},{8... | collective-permute-start | bytes 442376 | tf_op jit(solution)/shard_map/cross_ahead/ppermute | solution.py:80
  68.3 31.2 %collective-permute-start.14 = (bf16[384,768]{1,0:T(8,128)(2,1)}, bf16[384,768]{1,0:T(8,128)(2,1)S(1)}, u32[]{:S(2)}, u32[]{:S(2)}) collective-permute-start(bf16[384,768]{1,0:T(8,128)(2,1)} %collective-permute-done.13.inner1), channel_id=1, source_target_pairs={{1,0},{2,1},{3,2},{5,4},{6,5},{7,6},{9,8},{10,9},{11,10},{13,12},{... | collective-permute-start | bytes 1769480 | tf_op jit(solution)/shard_map/wide_late/ppermute | solution.py:80
  79.7 10.9 %collective-permute-start.10 = (bf16[192,768]{1,0:T(8,128)(2,1)S(1)}, bf16[192,768]{1,0:T(8,128)(2,1)S(1)}, u32[]{:S(2)}, u32[]{:S(2)}) collective-permute-start(bf16[192,768]{1,0:T(8,128)(2,1)S(1)} %collective-permute-done.6.block.q0), channel_id=1, source_target_pairs={{2,3},{6,7},{10,11},{14,15},{18,19},{22,23},{26,27},{30,31},{33,32... | collective-permute-start | bytes 884744 | tf_op jit(solution)/shard_map/gather1_2/ppermute | solution.py:80
  81.0 9.6 %collective-permute-start.11 = (bf16[192,768]{1,0:T(8,128)(2,1)S(1)}, bf16[192,768]{1,0:T(8,128)(2,1)S(1)}, u32[]{:S(2)}, u32[]{:S(2)}) collective-permute-start(bf16[192,768]{1,0:T(8,128)(2,1)S(1)} %collective-permute-done.6.block.q0), channel_id=1, source_target_pairs={{0,3},{4,7},{8,11},{12,15},{16,19},{20,23},{24,27},{28,31},{35,32}... | collective-permute-start | bytes 884744 | tf_op jit(solution)/shard_map/gather1_3/ppermute | solution.py:80
  82.3 13.4 %collective-permute-start.9 = (bf16[192,768]{1,0:T(8,128)(2,1)S(1)}, bf16[192,768]{1,0:T(8,128)(2,1)S(1)}, u32[]{:S(2)}, u32[]{:S(2)}) collective-permute-start(bf16[192,768]{1,0:T(8,128)(2,1)S(1)} %collective-permute-done.6.block.q0), channel_id=1, source_target_pairs={{1,3},{5,7},{9,11},{13,15},{17,19},{21,23},{25,27},{29,31},{34,32}... | collective-permute-start | bytes 884744 | tf_op jit(solution)/shard_map/gather1_1/ppermute | solution.py:80
  83.6 29.4 %collective-permute-start.12 = (bf16[384,768]{1,0:T(8,128)(2,1)S(1)}, bf16[384,768]{1,0:T(8,128)(2,1)S(1)}, u32[]{:S(2)}, u32[]{:S(2)}) collective-permute-start(bf16[384,768]{1,0:T(8,128)(2,1)S(1)} %collective-permute-done.4.refs_2_.outer1), channel_id=1, source_target_pairs={{0,480},{1,481},{2,482},{3,483},{4,484},{5,485},{6,486},{7,487},{8... | collective-permute-start | bytes 1769480 | tf_op jit(solution)/shard_map/own_outer2/ppermute | solution.py:80
  95.6 18.7 %collective-permute-start.15 = (bf16[288,768]{1,0:T(8,128)(2,1)S(1)}, bf16[288,768]{1,0:T(8,128)(2,1)S(1)}, u32[]{:S(2)}, u32[]{:S(2)}) collective-permute-start(bf16[288,768]{1,0:T(8,128)(2,1)S(1)} %join.1.q0), channel_id=1, source_target_pairs={{1,3},{5,7},{9,11},{13,15},{17,19},{21,23},{25,27},{29,31},{34,32}... | collective-permute-start | bytes 1327112 | tf_op jit(solution)/shard_map/gather0_1/ppermute | solution.py:80
  96.9 17.4 %collective-permute-start.16 = (bf16[288,768]{1,0:T(8,128)(2,1)S(1)}, bf16[288,768]{1,0:T(8,128)(2,1)S(1)}, u32[]{:S(2)}, u32[]{:S(2)}) collective-permute-start(bf16[288,768]{1,0:T(8,128)(2,1)S(1)} %join.1.q0), channel_id=1, source_target_pairs={{2,3},{6,7},{10,11},{14,15},{18,19},{22,23},{26,27},{30,31},{33,32... | collective-permute-start | bytes 1327112 | tf_op jit(solution)/shard_map/gather0_2/ppermute | solution.py:80
  98.2 16.2 %collective-permute-start.17 = (bf16[288,768]{1,0:T(8,128)(2,1)S(1)}, bf16[288,768]{1,0:T(8,128)(2,1)S(1)}, u32[]{:S(2)}, u32[]{:S(2)}) collective-permute-start(bf16[288,768]{1,0:T(8,128)(2,1)S(1)} %join.1.q0), channel_id=1, source_target_pairs={{0,3},{4,7},{8,11},{12,15},{16,19},{20,23},{24,27},{28,31},{35,32}... | collective-permute-start | bytes 1327112 | tf_op jit(solution)/shard_map/gather0_3/ppermute | solution.py:80
  99.5 9.5 %copy-start.3 = (f32[1,6144]{1,0:T(1,128)S(1)}, f32[1,6144]{1,0:T(1,128)}, u32[]{:S(2)}) copy-start(f32[1,6144]{1,0:T(1,128)} %copy-done.2) | copy-start | bytes 73732
  99.5 9.5 %copy-start.5 = (f32[384,128]{1,0:T(8,128)S(1)}, f32[384,128]{1,0:T(8,128)}, u32[]{:S(2)}) copy-start(f32[384,128]{1,0:T(8,128)} %copy-done.4) | copy-start | bytes 589828
  99.6 9.5 %copy-start.7 = (f32[384,768]{1,0:T(8,128)S(1)}, f32[384,768]{1,0:T(8,128)}, u32[]{:S(2)}) copy-start(f32[384,768]{1,0:T(8,128)} %copy-done.6) | copy-start | bytes 3538948
  103.8 19.9 %collective-permute-start.20 = (bf16[1536,768]{1,0:T(8,128)(2,1)}, bf16[1536,768]{1,0:T(8,128)(2,1)}, u32[]{:S(2)}, u32[]{:S(2)}) collective-permute-start(bf16[1536,768]{1,0:T(8,128)(2,1)} %merge1.1.keys), channel_id=1, source_target_pairs={{0,32},{1,33},{2,34},{3,35},{4,36},{5,37},{6,38},{7,39},{8,40},{9,... | collective-permute-start | bytes 7077896 | tf_op jit(solution)/shard_map/sibling1/ppermute | solution.py:80
  113.1 10.6 %collective-permute-start.19 = (bf16[384,768]{1,0:T(8,128)(2,1)S(1)}, bf16[384,768]{1,0:T(8,128)(2,1)S(1)}, u32[]{:S(2)}, u32[]{:S(2)}) collective-permute-start(bf16[384,768]{1,0:T(8,128)(2,1)S(1)} %collective-permute-done.12.farthest), channel_id=1, source_target_pairs={{0,1},{1,2},{2,3},{4,5},{5,6},{6,7},{8,9},{9,10},{10,11},{12,13},{... | collective-permute-start | bytes 1769480 | tf_op jit(solution)/shard_map/wide_outer2/ppermute | solution.py:80
  117.8 10.5 %collective-permute-start.18 = (bf16[768,768]{1,0:T(8,128)(2,1)}, bf16[768,768]{1,0:T(8,128)(2,1)}, u32[]{:S(2)}, u32[]{:S(2)}) collective-permute-start(bf16[768,768]{1,0:T(8,128)(2,1)} %get-tuple-element.80.inner0), channel_id=1, source_target_pairs={{0,32},{1,33},{2,34},{3,35},{4,36},{5,37},{6,38},{7,39},{8,40},{9,... | collective-permute-start | bytes 3538952 | tf_op jit(solution)/shard_map/sibling_hop0/ppermute | solution.py:80
  119.8 3.9 %copy-start.1 = (f32[384,128]{1,0:T(8,128)S(1)}, f32[384,128]{1,0:T(8,128)}, u32[]{:S(2)}) copy-start(f32[384,128]{1,0:T(8,128)} %copy-done) | copy-start | bytes 589828

commit v10 on v9

--- a/solution.py
+++ b/solution.py
@@ -62,8 +62,12 @@
     return (x, h, m + 1, z, c) if m < 3 else None
 
 
-def to_sibling_next_wide(x, h, m, z, c, s):
-    return (x, h, m - 1, z, c) if m > 0 else None
+def farthest_route(x, h, m, z, c, s):
+    return (x, h, m - 1, z, c) if m > 0 else (x, h, m, z + s, 1 - c)
+
+
+def edge_to_previous_chip(x, h, m, z, c, s):
+    return (x, h, m, z - s, c) if m == 0 else None
 
 
 def across(x, h, m, z, c, s):
@@ -172,7 +176,6 @@
     mirrored = jnp.where(core == 1, y, 3 - y)
     carries_captions = core == 1
     at_edge = jnp.where(mirrored == 0, 1, 0).astype(jnp.int32).reshape(1)
-    sibling_at_edge = jnp.where(mirrored == 3, 1, 0).astype(jnp.int32).reshape(1)
     core_flag = core.astype(jnp.int32).reshape(1)
     scale = logit_scale.reshape(1)
 
@@ -275,102 +278,99 @@
         )
 
     sums = terms("terms_own0", [(outer, [0]), (inner, [1]), (after(outer1, held), [2])], [(other, [8])], None, 100_000_000)
-    inner1 = after(inner1, *sums)
+    def copy_kernel(block, out):
+        out[...] = block[...]
+
+    crossed = call(
+        "crossed", copy_kernel, strip, (), (after(crossed, *sums),), 100_000_000
+    )
+    early, _ = lax.optimization_barrier((early, crossed))
+    crossed = after(crossed, early)
+    got = [
+        crossed,
+        send("gather1", crossed, line_to_line(2, 0)),
+        send("gather2", crossed, line_to_line(1, 0)),
+        send("gather3", crossed, line_to_line(3, 0)),
+    ]
+    inner1 = after(inner1, crossed)
     late = send("wide_late", inner1, to_next_wide)
-
-    def slice_kernel(block, out):
-        out[...] = block[quarter:, :]
-
-    outer_part = call(
-        "slice", slice_kernel, jax.ShapeDtypeStruct((quarter, width), half), (), (after(crossed, *sums),),
-        100_000_000,
-    )
-    back = send("cross_back", after(crossed, outer_part), to_previous_chip)
-    ahead = send("cross_ahead", outer_part, to_next_chip)
-    early, _ = lax.optimization_barrier((early, outer_part))
-    crossed = after(crossed, early)
-
-    def collect(name, mine):
-        q1 = send(name + "1", mine, line_to_line(2, 0))
-        q2 = send(name + "2", mine, line_to_line(1, 0))
-        q3 = send(name + "3", mine, line_to_line(3, 0))
-        return [mine, q1, q2, q3]
-
-    got1 = collect("gather1_", crossed)
     far2 = send("own_outer2", after(outer1, crossed), to_next_chip_sibling)
-
-    def join_kernel(first, second, out):
-        out[: 2 * quarter, :] = first[...]
-        out[2 * quarter :, :] = second[...]
-
-    joined = call(
-        "join", join_kernel, jax.ShapeDtypeStruct((3 * quarter, width), half), (),
-        (back, ahead), 100_000_000,
-    )
-    got0 = collect("gather0_", after(joined, *got1))
-
-    def merge1_kernel(edge, early, late, outer1, inner1, q0, q1, q2, q3, out, sems):
-        own = [(outer1, 0, out, 2 * rows, rows), (inner1, 0, out, 3 * rows, rows)]
-
+    near_sum, far_sum = sums
+
+    def own1_kernel(s, oth, nf, kf, keys, near_in, near):
+        near[...] = add_terms(
+            near_in[...], oth[...], nf[:, :1], kf, s[0], [(keys[...], 3, False)]
+        )
+
+    near_sum = call(
+        "terms_own1", own1_kernel, total, (scale,),
+        (other, near_factor, key_factors, after(inner1, *got), near_sum), 100_000_000,
+    )
+
+    def merge_kernel(edge, early, late, q0, q1, q2, q3, out, sems):
         @pl.when(edge[0] == 1)
         def _():
             pieces = []
             for place, source in enumerate((q0, q1, q2, q3)):
                 pieces.append((source, quarter, out, place * quarter, quarter))
                 pieces.append((source, 0, out, rows + place * quarter, quarter))
-            copy_all(sems, pieces + own)
+            copy_all(sems, pieces)
 
         @pl.when(edge[0] == 0)
         def _():
-            copy_all(sems, [(early, 2 * rows, out, 0, rows), (late, 0, out, rows, rows)] + own)
-
-    carried = assemble(
-        "merge1", merge1_kernel, blocks(4), (at_edge,),
-        (early, late, after(outer1, back, ahead), inner1, *got1), 10,
-    )
-    sib = send("sibling1", carried, to_sibling)
-    hop_far2 = send("wide_outer2", after(far2, carried), to_sibling_next_wide)
-    near_sum, far_sum = sums
-
-    def near_kernel(s, oth, nf, kf, keys, near_in, near):
+            copy_all(sems, [(early, 2 * rows, out, 0, rows), (late, 0, out, rows, rows)])
+
+    hop1 = assemble(
+        "merge", merge_kernel, blocks(2), (at_edge,), (early, after(late, near_sum), *got), 8
+    )
+    back = send("edge_back", hop1, edge_to_previous_chip)
+    sib1 = send("sibling_own1", jnp.concatenate([outer1, inner1], axis=0), to_sibling)
+    is_edge = mirrored == 0
+    hop_far2 = send("farthest", jnp.where(is_edge, hop1[:rows], far2), farthest_route)
+
+    def near1_kernel(s, oth, nf, kf, keys, near_in, near):
         near[...] = add_terms(
-            near_in[...], oth[...], nf[:, :1], kf, s[0],
-            [(keys[: 2 * rows, :], 4, False), (keys[3 * rows :, :], 3, False)],
+            near_in[...], oth[...], nf[:, :1], kf, s[0], [(keys[...], 4, False)]
         )
 
     near_sum = call(
-        "terms_near1", near_kernel, total, (scale,),
-        (other, near_factor, key_factors, carried, near_sum), 100_000_000,
-    )
-
-    got0 = [after(got0[0], far2, near_sum), *got0[1:]]
-
-    def merge0_kernel(edge, usual, q0, q1, q2, q3, out, outer0, sems):
-        @pl.when(edge[0] == 1)
-        def _():
-            pieces = []
-            for place, source in enumerate((q0, q1, q2, q3)):
-                low = place * quarter
-                pieces.append((source, 0, out, low, quarter))
-                pieces.append((source, quarter, outer0, low, quarter))
-                pieces.append((source, 2 * quarter, out, rows + low, quarter))
-            copy_all(sems, pieces)
-
-        @pl.when(edge[0] == 0)
-        def _():
-            copy_all(sems, [(usual, 0, out, 0, 2 * rows), (usual, rows, outer0, 0, rows)])
-
-    hop0, hop_outer0 = assemble(
-        "merge0", merge0_kernel, [blocks(2), blocks(1)], (at_edge,), (early, *got0), 12
-    )
-    hop_sib0 = send("sibling_hop0", hop0, to_sibling)
-
+        "terms_near1", near1_kernel, total, (scale,),
+        (other, near_factor, key_factors, after(hop1, far2), near_sum),
+    )
+    hop_sib1 = send("sibling_hop1", hop1, to_sibling)
+
+    def far1_kernel(s, out, ff, kf, own, farthest, far_in, far):
+        far[...] = add_terms(
+            far_in[...], out[...], ff[:, :1], kf, s[0],
+            [(own[...], 9, False), (farthest[...], 11, False)],
+        )
+
+    far_sum = call(
+        "terms_far1", far1_kernel, total, (scale,),
+        (outer, far_factor, key_factors, after(sib1, near_sum), far2, far_sum), 50_000_000,
+    )
+
+    def far2_kernel(s, out, ff, kf, hop, far_in, far):
+        far[...] = add_terms(
+            far_in[...], out[...], ff[:, :1], kf, s[0], [(hop[...], 12, False)]
+        )
+
+    far_sum = call(
+        "terms_far2", far2_kernel, total, (scale,),
+        (outer, far_factor, key_factors, hop_sib1, far_sum),
+    )
+    back = after(back, far_sum)
+    hop_inner0 = jnp.where(is_edge, back[rows:], early[:rows])
+    hop_sib0 = send("sibling_hop0", hop_inner0, to_sibling)
     anywhere = pl.BlockSpec(memory_space=pl.ANY)
 
-    def near0_kernel(c, s, oth, nf, kf, outer0, inner0, near_in, image_grad, caption_grad, held_sum, sem):
+    def near0_kernel(
+        c, e, s, oth, nf, kf, inner0, back, early, near_in, image_grad, caption_grad, held_sum, sem
+    ):
+        outer0 = jnp.where(e[0] == 1, back[:rows, :], early[rows : 2 * rows, :])
         held_sum[...] = s[0] * add_terms(
             near_in[...], oth[...], nf[:, :1], kf, s[0],
-            [(jnp.concatenate([inner0[:rows, :], outer0[...]], axis=0), 6, False)],
+            [(jnp.concatenate([inner0[...], outer0], axis=0), 6, False)],
         )
 
         @pl.when(c[0] == 1)
@@ -389,34 +389,24 @@
         half_done = pl.pallas_call(
             near0_kernel,
             out_shape=[total, total],
-            in_specs=[scalars()] * 2 + [whole()] * 6,
+            in_specs=[scalars()] * 3 + [whole()] * 7,
             out_specs=[anywhere] * 2,
             scratch_shapes=[pltpu.VMEM((rows, width), jnp.float32), pltpu.SemaphoreType.DMA],
             cost_estimate=pl.CostEstimate(
                 flops=100_000_000_000, bytes_accessed=1000, transcendentals=0
             ),
             compiler_params=pltpu.CompilerParams(vmem_limit_bytes=16 * 1024 * 1024),
-        )(core_flag, scale, other, near_factor, key_factors, hop_outer0, hop0, near_sum)
-
-    def far1_kernel(s, out, ff, kf, keys, farthest, far_in, far):
-        far[...] = add_terms(
-            far_in[...], out[...], ff[:, :1], kf, s[0],
-            [(keys[: 2 * rows, :], 12, False), (keys[2 * rows :, :], 9, False),
-             (farthest[...], 11, False)],
-        )
-
-    far_sum = call(
-        "terms_far1", far1_kernel, total, (scale,),
-        (outer, far_factor, key_factors, after(sib, hop_far2, *half_done), far2, far_sum), 100_000_000,
-    )
+        )(
+            core_flag, at_edge, scale,
+            other, near_factor, key_factors, hop_inner0, back, early, near_sum,
+        )
 
     def last_kernel(
-        c, e, s, out, ff, kf, hs0, hf2, far_in, _i, _c, image_grad, caption_grad, held_sum, sem
+        c, s, out, ff, kf, hs0, hf2, far_in, _i, _c, image_grad, caption_grad, held_sum, sem
     ):
-        farthest = jnp.where(e[0] == 1, hs0[rows:, :], hf2[...])
         held_sum[...] = s[0] * add_terms(
             far_in[...], out[...], ff[:, :1], kf, s[0],
-            [(jnp.concatenate([hs0[:rows, :], farthest], axis=0), 14, False)],
+            [(jnp.concatenate([hs0[...], hf2[...]], axis=0), 14, False)],
         )
 
         @pl.when(c[0] == 1)
@@ -435,14 +425,14 @@
         image_grad, caption_grad = pl.pallas_call(
             last_kernel,
             out_shape=[total, total],
-            in_specs=[scalars()] * 3 + [whole()] * 6 + [anywhere] * 2,
+            in_specs=[scalars()] * 2 + [whole()] * 6 + [anywhere] * 2,
             out_specs=[anywhere] * 2,
             scratch_shapes=[pltpu.VMEM((rows, width), jnp.float32), pltpu.SemaphoreType.DMA],
-            input_output_aliases={9: 0, 10: 1},
+            input_output_aliases={8: 0, 9: 1},
             cost_estimate=pl.CostEstimate(flops=1000, bytes_accessed=1000, transcendentals=0),
             compiler_params=pltpu.CompilerParams(vmem_limit_bytes=16 * 1024 * 1024),
         )(
-            core_flag, sibling_at_edge, scale,
+            core_flag, scale,
             outer, far_factor, key_factors, hop_sib0, hop_far2, far_sum, *half_done,
         )
     return image_grad, caption_grad

time: 133 us -> 125 us (0.940)
  the two profiles are of different devices: /device:TPU:1 before, /device:TPU:89 now
where the time goes in v10:
time: 125 us; the launch traced here: 124 us
  starting transfers between devices  57.5 us (46%)
  waiting for transfers between devices  35.8 us (29%)
  Pallas kernels  21.1 us (17%)
  other arithmetic  7.84 us (6%)
  between operations  2.01 us (2%)
    ppermute x18, starting transfers between devices, send(): return lax.ppermute(x, AXES, pairs(target))  57.5 us
    ppermute x18, waiting for transfers between devices, send(): return lax.ppermute(x, AXES, pairs(target))  35.8 us
    pallas_call x8, Pallas kernels, call(): pl.pallas_call(kernel, out_shape=out_shape, in_specs=[scalars() for _ in...  12.6 us
    pallas_call x1, Pallas kernels, on_device(): pl.pallas_call(near0_kernel, out_shape=[total, total], in_specs=[scalars(...  3.98 us
    pallas_call x1, Pallas kernels, on_device(): pl.pallas_call(last_kernel, out_shape=[total, total], in_specs=[scalars()...  3.35 us
  transfers between devices with their start and end apart: 18, of which 4 were waited for; matrix products, arithmetic and copies ran while one was open for 5% of the time, Pallas kernels for 14%

profile of v10, /device:TPU:89, one launch (start us, length us, event | category | flops | bytes accessed | tf_op | source)
XLA Modules:
  0.0 124.2 jit_solution(671978491283854030)
XLA Ops:
  0.6 2.1 %broadcast_select_fusion = (bf16[384,768]{1,0:T(8,128)(2,1)}, bf16[384,768]{1,0:T(8,128)(2,1)S(1)}) fusion(bf16[384,768]{1,0:T(8,128)(2,1)} %param.5, bf16[384,768]{1,0:T(8,128)(2,1)} %param.6, pred[]{:T(512)S(6)} %eq.60), kind=kLoop, calls=%fused_computation.4 | loop fusion | flops 589824 | bytes 2359297 | tf_op jit(solution)/shard_map/jit(_where)/select_n | solution.py:186
  2.8 2.6 %collective-permute-start = (bf16[384,768]{1,0:T(8,128)(2,1)}, bf16[384,768]{1,0:T(8,128)(2,1)S(1)}, u32[]{:S(2)}, u32[]{:S(2)}) collective-permute-start(bf16[384,768]{1,0:T(8,128)(2,1)} %get-tuple-element.96.oth.refs_3_), channel_id=1, source_target_pairs={{0,32},{1,33},{2,34},{3,35},{4,36},{5,37},{6,38},{7,39},{8,40},{9,... | collective-permute-start | bytes 1769480 | tf_op jit(solution)/shard_map/swap/ppermute | solution.py:84
  5.4 3.5 %collective-permute-start.4 = (bf16[384,768]{1,0:T(8,128)(2,1)S(1)}, bf16[384,768]{1,0:T(8,128)(2,1)S(1)}, u32[]{:S(2)}, u32[]{:S(2)}) collective-permute-start(bf16[384,768]{1,0:T(8,128)(2,1)S(1)} %get-tuple-element.97.outer.out.refs_0_), channel_id=1, source_target_pairs={{0,448},{1,449},{2,450},{3,451},{4,452},{5,453},{6,454},{7,455},{8... | collective-permute-start | bytes 1769480 | tf_op jit(solution)/shard_map/own_outer1/ppermute | solution.py:84
  8.9 0.0 collective-permute-done.inner.refs_1_
  8.9 0.1 cut.1
  9.0 1.9 %collective-permute-start.1 = (bf16[192,768]{1,0:T(8,128)(2,1)S(1)}, bf16[192,768]{1,0:T(8,128)(2,1)S(1)}, u32[]{:S(2)}, u32[]{:S(2)}) collective-permute-start(bf16[192,768]{1,0:T(8,128)(2,1)S(1)} %get-tuple-element.41), channel_id=1, source_target_pairs={{0,3},{4,7},{8,11},{12,15},{16,19},{20,23},{24,27},{28,31},{35,32}... | collective-permute-start | bytes 884744 | tf_op jit(solution)/shard_map/spread0/ppermute | solution.py:84
  10.9 2.0 %collective-permute-start.2 = (bf16[192,768]{1,0:T(8,128)(2,1)S(1)}, bf16[192,768]{1,0:T(8,128)(2,1)}, u32[]{:S(2)}, u32[]{:S(2)}) collective-permute-start(bf16[192,768]{1,0:T(8,128)(2,1)S(1)} %get-tuple-element.42), channel_id=1, source_target_pairs={{0,1},{4,5},{8,9},{12,13},{16,17},{20,21},{24,25},{28,29},{35,34},... | collective-permute-start | bytes 884744 | tf_op jit(solution)/shard_map/spread1/ppermute | solution.py:84
  12.9 2.0 %collective-permute-start.3 = (bf16[192,768]{1,0:T(8,128)(2,1)S(1)}, bf16[192,768]{1,0:T(8,128)(2,1)}, u32[]{:S(2)}, u32[]{:S(2)}) collective-permute-start(bf16[192,768]{1,0:T(8,128)(2,1)S(1)} %get-tuple-element.43), channel_id=1, source_target_pairs={{0,2},{4,6},{8,10},{12,14},{16,18},{20,22},{24,26},{28,30},{35,33}... | collective-permute-start | bytes 884744 | tf_op jit(solution)/shard_map/spread2/ppermute | solution.py:84
  14.9 1.9 %collective-permute-start.7 = (bf16[384,768]{1,0:T(8,128)(2,1)}, bf16[384,768]{1,0:T(8,128)(2,1)}, u32[]{:S(2)}, u32[]{:S(2)}) collective-permute-start(bf16[384,768]{1,0:T(8,128)(2,1)} %get-tuple-element.96.oth.refs_3_), channel_id=1, source_target_pairs={{0,96},{1,97},{2,98},{3,99},{4,100},{5,101},{6,102},{7,103},{8,104... | collective-permute-start | bytes 1769480 | tf_op jit(solution)/shard_map/own_inner1/ppermute | solution.py:84
  17.7 1.1 dynamic-slice_select_fusion
  18.9 0.0 collective-permute-done.1
  18.9 0.0 collective-permute-done.2
  18.9 0.1 collective-permute-done.3
  19.0 0.1 select_select_fusion
  19.0 12.3 %collective-permute-start.6 = (bf16[192,768]{1,0:T(8,128)(2,1)S(1)}, bf16[192,768]{1,0:T(8,128)(2,1)S(1)}, u32[]{:S(2)}, u32[]{:S(2)}) collective-permute-start(bf16[192,768]{1,0:T(8,128)(2,1)S(1)} %select_select_fusion), channel_id=1, source_target_pairs={{0,476},{1,477},{2,478},{3,479},{4,448},{5,449},{6,450},{7,451},{8... | collective-permute-start | bytes 884744 | tf_op jit(solution)/shard_map/cross/ppermute | solution.py:84
  31.4 0.0 collective-permute-done.4.refs_2_
  31.4 1.3 %pad_maximum_fusion = bf16[1152,768]{1,0:T(8,128)(2,1)} fusion(bf16[384,768]{1,0:T(8,128)(2,1)S(1)} %collective-permute-done.4.refs_2_, bf16[384,768]{1,0:T(8,128)(2,1)S(1)} %get-tuple-element.97.outer.out.refs_0_, bf16[384,768]{1,0:T(8,128)(2,1)S(1)} %collective-permute-done.inner.refs_1_), kind=kLoop, calls=%fused_computation | loop fusion | flops 5308416 | bytes 3538944 | tf_op jit(solution)/shard_map/concatenate | solution.py:207
  32.7 1.3 %collective-permute-start.5 = (bf16[1152,768]{1,0:T(8,128)(2,1)}, bf16[1152,768]{1,0:T(8,128)(2,1)}, u32[]{:S(2)}, u32[]{:S(2)}) collective-permute-start(bf16[1152,768]{1,0:T(8,128)(2,1)} %pad_maximum_fusion), channel_id=1, source_target_pairs={{1,0},{2,1},{3,2},{5,4},{6,5},{7,6},{9,8},{10,9},{11,10},{13,12},{... | collective-permute-start | bytes 5308424 | tf_op jit(solution)/shard_map/wide_early/ppermute | solution.py:84
  34.0 0.2 factors.1
  34.2 0.0 copy-start
  34.2 4.3 %terms_own0.1 = (f32[384,768]{1,0:T(8,128)S(1)}, f32[384,768]{1,0:T(8,128)S(1)}) custom-call(f32[1]{0:T(128)} %bitcast.3.s, bf16[384,768]{1,0:T(8,128)(2,1)} %get-tuple-element.96.oth.refs_3_, bf16[384,768]{1,0:T(8,128)(2,1)S(1)} %get-tuple-element.97.outer.out.refs_0_, f32[384,128]{1,0:T(8,128)S(1)} %get-tuple-element.64.nf, ...), custom_call_target="tpu_custom_call" | custom-call | flops 99999997952 | bytes 1000 | tf_op jit(solution)/shard_map/terms_own0/pallas_call | solution.py:99
  38.5 0.0 copy-done
  38.5 0.0 copy-start.2
  38.5 0.0 copy-start.4
  38.5 30.1 %collective-permute-done.6.block = bf16[192,768]{1,0:T(8,128)(2,1)S(1)} collective-permute-done((bf16[192,768]{1,0:T(8,128)(2,1)S(1)}, bf16[192,768]{1,0:T(8,128)(2,1)S(1)}, u32[]{:S(2)}, u32[]{:S(2)}) %collective-permute-start.6) | collective-permute-done | bytes 294944 | tf_op jit(solution)/shard_map/cross/ppermute | solution.py:84
  68.6 0.0 copy-done.2
  68.7 0.0 copy-done.4
  68.7 0.0 collective-permute-done.5.early
  68.7 3.2 %collective-permute-start.11 = (bf16[192,768]{1,0:T(8,128)(2,1)S(1)}, bf16[192,768]{1,0:T(8,128)(2,1)S(1)}, u32[]{:S(2)}, u32[]{:S(2)}) collective-permute-start(bf16[192,768]{1,0:T(8,128)(2,1)S(1)} %crossed.1.q0), channel_id=1, source_target_pairs={{0,3},{4,7},{8,11},{12,15},{16,19},{20,23},{24,27},{28,31},{35,32}... | collective-permute-start | bytes 884744 | tf_op jit(solution)/shard_map/gather3/ppermute | solution.py:84
  71.9 0.7 collective-permute-start.10
  72.6 0.7 collective-permute-start.9
  73.3 0.0 copy-start.5
  73.3 0.0 collective-permute-done.7.keys
  73.3 1.4 %collective-permute-start.8 = (bf16[384,768]{1,0:T(8,128)(2,1)}, bf16[384,768]{1,0:T(8,128)(2,1)S(1)}, u32[]{:S(2)}, u32[]{:S(2)}) collective-permute-start(bf16[384,768]{1,0:T(8,128)(2,1)} %collective-permute-done.7.keys), channel_id=1, source_target_pairs={{1,0},{2,1},{3,2},{5,4},{6,5},{7,6},{9,8},{10,9},{11,10},{13,12},{... | collective-permute-start | bytes 1769480 | tf_op jit(solution)/shard_map/wide_late/ppermute | solution.py:84
  74.8 1.9 %collective-permute-start.15 = (bf16[384,768]{1,0:T(8,128)(2,1)S(1)}, bf16[384,768]{1,0:T(8,128)(2,1)S(1)}, u32[]{:S(2)}, u32[]{:S(2)}) collective-permute-start(bf16[384,768]{1,0:T(8,128)(2,1)S(1)} %collective-permute-done.4.refs_2_), channel_id=1, source_target_pairs={{0,480},{1,481},{2,482},{3,483},{4,484},{5,485},{6,486},{7,487},{8... | collective-permute-start | bytes 1769480 | tf_op jit(solution)/shard_map/own_outer2/ppermute | solution.py:84
  76.7 1.1 pad_maximum_fusion.1
  77.8 0.0 collective-permute-done.11.q3
  77.8 1.9 %collective-permute-start.14 = (bf16[768,768]{1,0:T(8,128)(2,1)S(1)}, bf16[768,768]{1,0:T(8,128)(2,1)S(1)}, u32[]{:S(2)}, u32[]{:S(2)}) collective-permute-start(bf16[768,768]{1,0:T(8,128)(2,1)S(1)} %pad_maximum_fusion.1), channel_id=1, source_target_pairs={{0,32},{1,33},{2,34},{3,35},{4,36},{5,37},{6,38},{7,39},{8,40},{9,... | collective-permute-start | bytes 3538952 | tf_op jit(solution)/shard_map/sibling_own1/ppermute | solution.py:84
  79.8 0.0 collective-permute-done.10.q2
  79.8 0.0 collective-permute-done.9.q1
  79.8 0.0 copy-done.5
  79.8 2.2 %terms_own1.1.near_in = f32[384,768]{1,0:T(8,128)S(1)} custom-call(f32[1]{0:T(128)} %bitcast.4.s, bf16[384,768]{1,0:T(8,128)(2,1)} %get-tuple-element.96.oth.refs_3_, f32[384,128]{1,0:T(8,128)S(1)} %get-tuple-element.64.nf, f32[1,6144]{1,0:T(1,128)S(1)} %get-tuple-element.62.kf, bf16[384,768]{1,0:T(8,128)(2,1)} %collective-permute-done.7.keys, ...), custom_call_target="tpu_custom_call" | custom-call | flops 99999997952 | bytes 1000 | tf_op jit(solution)/shard_map/terms_own1/pallas_call | solution.py:99
  82.0 3.8 %collective-permute-done.8.late = bf16[384,768]{1,0:T(8,128)(2,1)S(1)} collective-permute-done((bf16[384,768]{1,0:T(8,128)(2,1)}, bf16[384,768]{1,0:T(8,128)(2,1)S(1)}, u32[]{:S(2)}, u32[]{:S(2)}) %collective-permute-start.8) | collective-permute-done | bytes 589856 | tf_op jit(solution)/shard_map/wide_late/ppermute | solution.py:84
  85.8 1.1 merge.1.keys
  87.0 1.9 %collective-permute-start.13 = (bf16[768,768]{1,0:T(8,128)(2,1)S(1)}, bf16[768,768]{1,0:T(8,128)(2,1)S(1)}, u32[]{:S(2)}, u32[]{:S(2)}) collective-permute-start(bf16[768,768]{1,0:T(8,128)(2,1)S(1)} %merge.1.keys), channel_id=1, source_target_pairs={{0,32},{1,33},{2,34},{3,35},{4,36},{5,37},{6,38},{7,39},{8,40},{9,... | collective-permute-start | bytes 3538952 | tf_op jit(solution)/shard_map/sibling_hop1/ppermute | solution.py:84
  88.9 0.7 collective-permute-start.12
  89.6 1.8 %collective-permute-done.15.farthest = bf16[384,768]{1,0:T(8,128)(2,1)S(1)} collective-permute-done((bf16[384,768]{1,0:T(8,128)(2,1)S(1)}, bf16[384,768]{1,0:T(8,128)(2,1)S(1)}, u32[]{:S(2)}, u32[]{:S(2)}) %collective-permute-start.15) | collective-permute-done | bytes 589856 | tf_op jit(solution)/shard_map/own_outer2/ppermute | solution.py:84
  91.4 0.9 slice_select_fusion
  92.3 4.0 %collective-permute-start.17 = (bf16[384,768]{1,0:T(8,128)(2,1)}, bf16[384,768]{1,0:T(8,128)(2,1)}, u32[]{:S(2)}, u32[]{:S(2)}) collective-permute-start(bf16[384,768]{1,0:T(8,128)(2,1)} %slice_select_fusion), channel_id=1, source_target_pairs={{0,1},{1,2},{2,3},{3,483},{4,5},{5,6},{6,7},{7,487},{8,9},{9,10},{... | collective-permute-start | bytes 1769480 | tf_op jit(solution)/shard_map/farthest/ppermute | solution.py:84
  96.3 0.0 copy-start.3
  96.3 2.4 %terms_near1.1.near_in = f32[384,768]{1,0:T(8,128)S(1)} custom-call(f32[1]{0:T(128)} %bitcast.5.s, bf16[384,768]{1,0:T(8,128)(2,1)} %get-tuple-element.96.oth.refs_3_, f32[384,128]{1,0:T(8,128)S(1)} %get-tuple-element.64.nf, f32[1,6144]{1,0:T(1,128)S(1)} %get-tuple-element.62.kf, bf16[768,768]{1,0:T(8,128)(2,1)S(1)} %merge.1.keys, ...), custom_call_target="tpu_custom_call" | custom-call | flops 1000 | bytes 1000 | tf_op jit(solution)/shard_map/terms_near1/pallas_call | solution.py:99
  98.8 0.0 collective-permute-done.14.own
  98.8 0.0 copy-done.1
  98.8 0.0 copy-done.3
  98.8 2.1 %terms_far1.1.far_in = f32[384,768]{1,0:T(8,128)S(1)} custom-call(f32[1]{0:T(128)} %bitcast.6.s, bf16[384,768]{1,0:T(8,128)(2,1)S(1)} %get-tuple-element.97.outer.out.refs_0_, f32[384,128]{1,0:T(8,128)S(1)} %copy-done.1, f32[1,6144]{1,0:T(1,128)S(1)} %get-tuple-element.62.kf, bf16[768,768]{1,0:T(8,128)(2,1)S(1)} %collective-permute-done.14.own, ...), custom_call_target="tpu_custom_call" | custom-call | flops 49999998976 | bytes 1000 | tf_op jit(solution)/shard_map/terms_far1/pallas_call | solution.py:99
  100.9 0.0 collective-permute-done.13.hop
  100.9 1.3 %terms_far2.1.far_in = f32[384,768]{1,0:T(8,128)S(1)} custom-call(f32[1]{0:T(128)} %bitcast.7.s, bf16[384,768]{1,0:T(8,128)(2,1)S(1)} %get-tuple-element.97.outer.out.refs_0_, f32[384,128]{1,0:T(8,128)S(1)} %copy-done.1, f32[1,6144]{1,0:T(1,128)S(1)} %get-tuple-element.62.kf, bf16[768,768]{1,0:T(8,128)(2,1)S(1)} %collective-permute-done.13.hop, ...), custom_call_target="tpu_custom_call" | custom-call | flops 1000 | bytes 1000 | tf_op jit(solution)/shard_map/terms_far2/pallas_call | solution.py:99
  102.2 0.0 collective-permute-done.12.back
  102.2 1.1 slice_select_fusion.1.inner0
  103.3 13.5 %collective-permute-start.16 = (bf16[384,768]{1,0:T(8,128)(2,1)S(1)}, bf16[384,768]{1,0:T(8,128)(2,1)S(1)}, u32[]{:S(2)}, u32[]{:S(2)}) collective-permute-start(bf16[384,768]{1,0:T(8,128)(2,1)S(1)} %slice_select_fusion.1.inner0), channel_id=1, source_target_pairs={{0,32},{1,33},{2,34},{3,35},{4,36},{5,37},{6,38},{7,39},{8,40},{9,... | collective-permute-start | bytes 1769480 | tf_op jit(solution)/shard_map/sibling_hop0/ppermute | solution.py:84
  116.9 4.0 %terms_near0.1 = (f32[384,768]{1,0:T(8,128)}, f32[384,768]{1,0:T(8,128)}) custom-call(s32[1]{0:T(128)} %bitcast.c, s32[1]{0:T(128)} %bitcast.2.edge.e, f32[1]{0:T(128)} %bitcast.8.s, bf16[384,768]{1,0:T(8,128)(2,1)} %get-tuple-element.96.oth.refs_3_, f32[384,128]{1,0:T(8,128)S(1)} %get-tuple-element.64.nf, f32[1,6144]{1,0:T(1,128)S(1)} %get-tuple-element.62.kf, ...), custom_call_target="tpu_custom_call" | custom-call | flops 99999997952 | bytes 1000 | tf_op jit(solution)/shard_map/terms_near0/pallas_call | solution.py:389
  120.9 0.0 collective-permute-done.17.hf2
  120.9 0.0 collective-permute-done.16.hs0
  120.9 3.4 %terms_last.1 = (f32[384,768]{1,0:T(8,128)}, f32[384,768]{1,0:T(8,128)}) custom-call(s32[1]{0:T(128)} %bitcast.c, f32[1]{0:T(128)} %bitcast.9.s, bf16[384,768]{1,0:T(8,128)(2,1)S(1)} %get-tuple-element.97.outer.out.refs_0_, f32[384,128]{1,0:T(8,128)S(1)} %copy-done.1, ...), custom_call_target="tpu_custom_call", output_to_operand_aliasing={{0}: (8, {}), {1}: (9, {})} | custom-call | flops 1000 | bytes 1000 | tf_op jit(solution)/shard_map/terms_last/pallas_call | solution.py:425
  (2 shorter events, 0.0 us)
Async XLA Ops:
  2.8 6.1 %collective-permute-start = (bf16[384,768]{1,0:T(8,128)(2,1)}, bf16[384,768]{1,0:T(8,128)(2,1)S(1)}, u32[]{:S(2)}, u32[]{:S(2)}) collective-permute-start(bf16[384,768]{1,0:T(8,128)(2,1)} %get-tuple-element.96.oth.refs_3_), channel_id=1, source_target_pairs={{0,32},{1,33},{2,34},{3,35},{4,36},{5,37},{6,38},{7,39},{8,40},{9,... | collective-permute-start | bytes 1769480 | tf_op jit(solution)/shard_map/swap/ppermute | solution.py:84
  5.4 26.0 %collective-permute-start.4 = (bf16[384,768]{1,0:T(8,128)(2,1)S(1)}, bf16[384,768]{1,0:T(8,128)(2,1)S(1)}, u32[]{:S(2)}, u32[]{:S(2)}) collective-permute-start(bf16[384,768]{1,0:T(8,128)(2,1)S(1)} %get-tuple-element.97.outer.out.refs_0_), channel_id=1, source_target_pairs={{0,448},{1,449},{2,450},{3,451},{4,452},{5,453},{6,454},{7,455},{8... | collective-permute-start | bytes 1769480 | tf_op jit(solution)/shard_map/own_outer1/ppermute | solution.py:84
  9.0 9.9 %collective-permute-start.1 = (bf16[192,768]{1,0:T(8,128)(2,1)S(1)}, bf16[192,768]{1,0:T(8,128)(2,1)S(1)}, u32[]{:S(2)}, u32[]{:S(2)}) collective-permute-start(bf16[192,768]{1,0:T(8,128)(2,1)S(1)} %get-tuple-element.41), channel_id=1, source_target_pairs={{0,3},{4,7},{8,11},{12,15},{16,19},{20,23},{24,27},{28,31},{35,32}... | collective-permute-start | bytes 884744 | tf_op jit(solution)/shard_map/spread0/ppermute | solution.py:84
  10.9 8.0 %collective-permute-start.2 = (bf16[192,768]{1,0:T(8,128)(2,1)S(1)}, bf16[192,768]{1,0:T(8,128)(2,1)}, u32[]{:S(2)}, u32[]{:S(2)}) collective-permute-start(bf16[192,768]{1,0:T(8,128)(2,1)S(1)} %get-tuple-element.42), channel_id=1, source_target_pairs={{0,1},{4,5},{8,9},{12,13},{16,17},{20,21},{24,25},{28,29},{35,34},... | collective-permute-start | bytes 884744 | tf_op jit(solution)/shard_map/spread1/ppermute | solution.py:84
  12.9 6.1 %collective-permute-start.3 = (bf16[192,768]{1,0:T(8,128)(2,1)S(1)}, bf16[192,768]{1,0:T(8,128)(2,1)}, u32[]{:S(2)}, u32[]{:S(2)}) collective-permute-start(bf16[192,768]{1,0:T(8,128)(2,1)S(1)} %get-tuple-element.43), channel_id=1, source_target_pairs={{0,2},{4,6},{8,10},{12,14},{16,18},{20,22},{24,26},{28,30},{35,33}... | collective-permute-start | bytes 884744 | tf_op jit(solution)/shard_map/spread2/ppermute | solution.py:84
  14.9 58.4 %collective-permute-start.7 = (bf16[384,768]{1,0:T(8,128)(2,1)}, bf16[384,768]{1,0:T(8,128)(2,1)}, u32[]{:S(2)}, u32[]{:S(2)}) collective-permute-start(bf16[384,768]{1,0:T(8,128)(2,1)} %get-tuple-element.96.oth.refs_3_), channel_id=1, source_target_pairs={{0,96},{1,97},{2,98},{3,99},{4,100},{5,101},{6,102},{7,103},{8,104... | collective-permute-start | bytes 1769480 | tf_op jit(solution)/shard_map/own_inner1/ppermute | solution.py:84
  19.0 49.6 %collective-permute-start.6 = (bf16[192,768]{1,0:T(8,128)(2,1)S(1)}, bf16[192,768]{1,0:T(8,128)(2,1)S(1)}, u32[]{:S(2)}, u32[]{:S(2)}) collective-permute-start(bf16[192,768]{1,0:T(8,128)(2,1)S(1)} %select_select_fusion), channel_id=1, source_target_pairs={{0,476},{1,477},{2,478},{3,479},{4,448},{5,449},{6,450},{7,451},{8... | collective-permute-start | bytes 884744 | tf_op jit(solution)/shard_map/cross/ppermute | solution.py:84
  32.7 36.0 %collective-permute-start.5 = (bf16[1152,768]{1,0:T(8,128)(2,1)}, bf16[1152,768]{1,0:T(8,128)(2,1)}, u32[]{:S(2)}, u32[]{:S(2)}) collective-permute-start(bf16[1152,768]{1,0:T(8,128)(2,1)} %pad_maximum_fusion), channel_id=1, source_target_pairs={{1,0},{2,1},{3,2},{5,4},{6,5},{7,6},{9,8},{10,9},{11,10},{13,12},{... | collective-permute-start | bytes 5308424 | tf_op jit(solution)/shard_map/wide_early/ppermute | solution.py:84
  34.2 4.4 %copy-start = (f32[384,128]{1,0:T(8,128)}, f32[384,128]{1,0:T(8,128)S(1)}, u32[]{:S(2)}) copy-start(f32[384,128]{1,0:T(8,128)S(1)} %get-tuple-element.61.ff) | copy-start | bytes 589828
  38.5 30.1 %copy-start.2 = (f32[384,768]{1,0:T(8,128)}, f32[384,768]{1,0:T(8,128)S(1)}, u32[]{:S(2)}) copy-start(f32[384,768]{1,0:T(8,128)S(1)} %get-tuple-element.67.far_in) | copy-start | bytes 3538948
  38.5 30.1 %copy-start.4 = (f32[384,768]{1,0:T(8,128)}, f32[384,768]{1,0:T(8,128)S(1)}, u32[]{:S(2)}) copy-start(f32[384,768]{1,0:T(8,128)S(1)} %get-tuple-element.66.near_in) | copy-start | bytes 3538948
  68.7 9.2 %collective-permute-start.11 = (bf16[192,768]{1,0:T(8,128)(2,1)S(1)}, bf16[192,768]{1,0:T(8,128)(2,1)S(1)}, u32[]{:S(2)}, u32[]{:S(2)}) collective-permute-start(bf16[192,768]{1,0:T(8,128)(2,1)S(1)} %crossed.1.q0), channel_id=1, source_target_pairs={{0,3},{4,7},{8,11},{12,15},{16,19},{20,23},{24,27},{28,31},{35,32}... | collective-permute-start | bytes 884744 | tf_op jit(solution)/shard_map/gather3/ppermute | solution.py:84
  71.9 7.9 %collective-permute-start.10 = (bf16[192,768]{1,0:T(8,128)(2,1)S(1)}, bf16[192,768]{1,0:T(8,128)(2,1)S(1)}, u32[]{:S(2)}, u32[]{:S(2)}) collective-permute-start(bf16[192,768]{1,0:T(8,128)(2,1)S(1)} %crossed.1.q0), channel_id=1, source_target_pairs={{2,3},{6,7},{10,11},{14,15},{18,19},{22,23},{26,27},{30,31},{33,32... | collective-permute-start | bytes 884744 | tf_op jit(solution)/shard_map/gather2/ppermute | solution.py:84
  72.6 7.2 %collective-permute-start.9 = (bf16[192,768]{1,0:T(8,128)(2,1)S(1)}, bf16[192,768]{1,0:T(8,128)(2,1)S(1)}, u32[]{:S(2)}, u32[]{:S(2)}) collective-permute-start(bf16[192,768]{1,0:T(8,128)(2,1)S(1)} %crossed.1.q0), channel_id=1, source_target_pairs={{1,3},{5,7},{9,11},{13,15},{17,19},{21,23},{25,27},{29,31},{34,32}... | collective-permute-start | bytes 884744 | tf_op jit(solution)/shard_map/gather1/ppermute | solution.py:84
  73.3 6.5 %copy-start.5 = (f32[384,768]{1,0:T(8,128)S(1)}, f32[384,768]{1,0:T(8,128)}, u32[]{:S(2)}) copy-start(f32[384,768]{1,0:T(8,128)} %copy-done.4) | copy-start | bytes 3538948
  73.3 12.5 %collective-permute-start.8 = (bf16[384,768]{1,0:T(8,128)(2,1)}, bf16[384,768]{1,0:T(8,128)(2,1)S(1)}, u32[]{:S(2)}, u32[]{:S(2)}) collective-permute-start(bf16[384,768]{1,0:T(8,128)(2,1)} %collective-permute-done.7.keys), channel_id=1, source_target_pairs={{1,0},{2,1},{3,2},{5,4},{6,5},{7,6},{9,8},{10,9},{11,10},{13,12},{... | collective-permute-start | bytes 1769480 | tf_op jit(solution)/shard_map/wide_late/ppermute | solution.py:84
  74.8 16.6 %collective-permute-start.15 = (bf16[384,768]{1,0:T(8,128)(2,1)S(1)}, bf16[384,768]{1,0:T(8,128)(2,1)S(1)}, u32[]{:S(2)}, u32[]{:S(2)}) collective-permute-start(bf16[384,768]{1,0:T(8,128)(2,1)S(1)} %collective-permute-done.4.refs_2_), channel_id=1, source_target_pairs={{0,480},{1,481},{2,482},{3,483},{4,484},{5,485},{6,486},{7,487},{8... | collective-permute-start | bytes 1769480 | tf_op jit(solution)/shard_map/own_outer2/ppermute | solution.py:84
  77.8 20.9 %collective-permute-start.14 = (bf16[768,768]{1,0:T(8,128)(2,1)S(1)}, bf16[768,768]{1,0:T(8,128)(2,1)S(1)}, u32[]{:S(2)}, u32[]{:S(2)}) collective-permute-start(bf16[768,768]{1,0:T(8,128)(2,1)S(1)} %pad_maximum_fusion.1), channel_id=1, source_target_pairs={{0,32},{1,33},{2,34},{3,35},{4,36},{5,37},{6,38},{7,39},{8,40},{9,... | collective-permute-start | bytes 3538952 | tf_op jit(solution)/shard_map/sibling_own1/ppermute | solution.py:84
  87.0 13.9 %collective-permute-start.13 = (bf16[768,768]{1,0:T(8,128)(2,1)S(1)}, bf16[768,768]{1,0:T(8,128)(2,1)S(1)}, u32[]{:S(2)}, u32[]{:S(2)}) collective-permute-start(bf16[768,768]{1,0:T(8,128)(2,1)S(1)} %merge.1.keys), channel_id=1, source_target_pairs={{0,32},{1,33},{2,34},{3,35},{4,36},{5,37},{6,38},{7,39},{8,40},{9,... | collective-permute-start | bytes 3538952 | tf_op jit(solution)/shard_map/sibling_hop1/ppermute | solution.py:84
  88.9 13.3 %collective-permute-start.12 = (bf16[768,768]{1,0:T(8,128)(2,1)S(1)}, bf16[768,768]{1,0:T(8,128)(2,1)S(1)}, u32[]{:S(2)}, u32[]{:S(2)}) collective-permute-start(bf16[768,768]{1,0:T(8,128)(2,1)S(1)} %merge.1.keys), channel_id=1, source_target_pairs={{3,67},{7,71},{11,75},{15,79},{19,83},{23,87},{27,91},{31,95},{32,... | collective-permute-start | bytes 3538952 | tf_op jit(solution)/shard_map/edge_back/ppermute | solution.py:84
  92.3 28.6 %collective-permute-start.17 = (bf16[384,768]{1,0:T(8,128)(2,1)}, bf16[384,768]{1,0:T(8,128)(2,1)}, u32[]{:S(2)}, u32[]{:S(2)}) collective-permute-start(bf16[384,768]{1,0:T(8,128)(2,1)} %slice_select_fusion), channel_id=1, source_target_pairs={{0,1},{1,2},{2,3},{3,483},{4,5},{5,6},{6,7},{7,487},{8,9},{9,10},{... | collective-permute-start | bytes 1769480 | tf_op jit(solution)/shard_map/farthest/ppermute | solution.py:84
  96.3 2.5 %copy-start.1 = (f32[384,128]{1,0:T(8,128)S(1)}, f32[384,128]{1,0:T(8,128)}, u32[]{:S(2)}) copy-start(f32[384,128]{1,0:T(8,128)} %copy-done) | copy-start | bytes 589828
  96.3 2.5 %copy-start.3 = (f32[384,768]{1,0:T(8,128)S(1)}, f32[384,768]{1,0:T(8,128)}, u32[]{:S(2)}) copy-start(f32[384,768]{1,0:T(8,128)} %copy-done.2) | copy-start | bytes 3538948
  103.3 17.5 %collective-permute-start.16 = (bf16[384,768]{1,0:T(8,128)(2,1)S(1)}, bf16[384,768]{1,0:T(8,128)(2,1)S(1)}, u32[]{:S(2)}, u32[]{:S(2)}) collective-permute-start(bf16[384,768]{1,0:T(8,128)(2,1)S(1)} %slice_select_fusion.1.inner0), channel_id=1, source_target_pairs={{0,32},{1,33},{2,34},{3,35},{4,36},{5,37},{6,38},{7,39},{8,40},{9,... | collective-permute-start | bytes 1769480 | tf_op jit(solution)/shard_map/sibling_hop0/ppermute | solution.py:84

commit v11 on v10

--- a/solution.py
+++ b/solution.py
@@ -292,6 +292,16 @@
         send("gather2", crossed, line_to_line(1, 0)),
         send("gather3", crossed, line_to_line(3, 0)),
     ]
+
+    def gather_kernel(q0, q1, q2, q3, out, sems):
+        pieces = []
+        for place, source in enumerate((q0, q1, q2, q3)):
+            pieces.append((source, quarter, out, place * quarter, quarter))
+            pieces.append((source, 0, out, rows + place * quarter, quarter))
+        copy_all(sems, pieces)
+
+    whole_blocks = assemble("whole_blocks", gather_kernel, blocks(2), (), tuple(got), 8)
+    back = send("edge_back", whole_blocks, edge_to_previous_chip)
     inner1 = after(inner1, crossed)
     late = send("wide_late", inner1, to_next_wide)
     far2 = send("own_outer2", after(outer1, crossed), to_next_chip_sibling)
@@ -304,29 +314,27 @@
 
     near_sum = call(
         "terms_own1", own1_kernel, total, (scale,),
-        (other, near_factor, key_factors, after(inner1, *got), near_sum), 100_000_000,
-    )
-
-    def merge_kernel(edge, early, late, q0, q1, q2, q3, out, sems):
+        (other, near_factor, key_factors, after(inner1, whole_blocks), near_sum), 100_000_000,
+    )
+
+    def merge_kernel(edge, early, late, gathered, out, sems):
         @pl.when(edge[0] == 1)
         def _():
-            pieces = []
-            for place, source in enumerate((q0, q1, q2, q3)):
-                pieces.append((source, quarter, out, place * quarter, quarter))
-                pieces.append((source, 0, out, rows + place * quarter, quarter))
-            copy_all(sems, pieces)
+            copy_all(sems, [(gathered, 0, out, 0, 2 * rows)])
 
         @pl.when(edge[0] == 0)
         def _():
             copy_all(sems, [(early, 2 * rows, out, 0, rows), (late, 0, out, rows, rows)])
 
     hop1 = assemble(
-        "merge", merge_kernel, blocks(2), (at_edge,), (early, after(late, near_sum), *got), 8
-    )
-    back = send("edge_back", hop1, edge_to_previous_chip)
-    sib1 = send("sibling_own1", jnp.concatenate([outer1, inner1], axis=0), to_sibling)
+        "merge", merge_kernel, blocks(2), (at_edge,),
+        (early, after(late, near_sum), whole_blocks), 2,
+    )
+    hop_sib1 = send("sibling_hop1", hop1, to_sibling)
+    sib1 = send(
+        "sibling_own1", jnp.concatenate([outer1, inner1], axis=0), to_sibling
+    )
     is_edge = mirrored == 0
-    hop_far2 = send("farthest", jnp.where(is_edge, hop1[:rows], far2), farthest_route)
 
     def near1_kernel(s, oth, nf, kf, keys, near_in, near):
         near[...] = add_terms(
@@ -348,6 +356,10 @@
     far_sum = call(
         "terms_far1", far1_kernel, total, (scale,),
         (outer, far_factor, key_factors, after(sib1, near_sum), far2, far_sum), 50_000_000,
+    )
+
+    hop_far2 = send(
+        "farthest", jnp.where(is_edge, hop1[:rows], after(far2, far_sum)), farthest_route
     )
 
     def far2_kernel(s, out, ff, kf, hop, far_in, far):

time: 125 us -> 126 us (level)
  the two profiles are of different devices: /device:TPU:89 before, /device:TPU:97 now
where the time goes in v11:
time: 126 us; the launch traced here: 125 us
  starting transfers between devices  55.8 us (44%)
  waiting for transfers between devices  37 us (29%)
  Pallas kernels  23.1 us (18%)
  other arithmetic  7.2 us (6%)
  between operations  2.01 us (2%)
    ppermute x18, starting transfers between devices, send(): return lax.ppermute(x, AXES, pairs(target))  55.8 us
    ppermute x18, waiting for transfers between devices, send(): return lax.ppermute(x, AXES, pairs(target))  37 us
    pallas_call x8, Pallas kernels, call(): pl.pallas_call(kernel, out_shape=out_shape, in_specs=[scalars() for _ in...  12.6 us
    pallas_call x1, Pallas kernels, on_device(): pl.pallas_call(near0_kernel, out_shape=[total, total], in_specs=[scalars(...  4.31 us
    pallas_call x2, Pallas kernels, assemble(): pl.pallas_call(kernel, out_shape=out_shape, in_specs=[scalars() for _ in...  3.91 us
  transfers between devices with their start and end apart: 18, of which 3 were waited for; matrix products, arithmetic and copies ran while one was open for 4% of the time, Pallas kernels for 17%

profile of v11, /device:TPU:97, one launch (start us, length us, event | category | flops | bytes accessed | tf_op | source)
XLA Modules:
  0.0 125.1 jit_solution(14539599103457529643)
XLA Ops:
  0.6 2.2 %broadcast_select_fusion = (bf16[384,768]{1,0:T(8,128)(2,1)}, bf16[384,768]{1,0:T(8,128)(2,1)S(1)}) fusion(bf16[384,768]{1,0:T(8,128)(2,1)} %param.5, bf16[384,768]{1,0:T(8,128)(2,1)} %param.6, pred[]{:T(512)S(6)} %eq.60), kind=kLoop, calls=%fused_computation.4 | loop fusion | flops 589824 | bytes 2359297 | tf_op jit(solution)/shard_map/jit(_where)/select_n | solution.py:186
  2.8 2.6 %collective-permute-start = (bf16[384,768]{1,0:T(8,128)(2,1)}, bf16[384,768]{1,0:T(8,128)(2,1)S(1)}, u32[]{:S(2)}, u32[]{:S(2)}) collective-permute-start(bf16[384,768]{1,0:T(8,128)(2,1)} %get-tuple-element.98.oth.refs_3_), channel_id=1, source_target_pairs={{0,32},{1,33},{2,34},{3,35},{4,36},{5,37},{6,38},{7,39},{8,40},{9,... | collective-permute-start | bytes 1769480 | tf_op jit(solution)/shard_map/swap/ppermute | solution.py:84
  5.4 4.8 %collective-permute-start.5 = (bf16[384,768]{1,0:T(8,128)(2,1)S(1)}, bf16[384,768]{1,0:T(8,128)(2,1)S(1)}, u32[]{:S(2)}, u32[]{:S(2)}) collective-permute-start(bf16[384,768]{1,0:T(8,128)(2,1)S(1)} %get-tuple-element.99.outer.out.refs_0_), channel_id=1, source_target_pairs={{0,448},{1,449},{2,450},{3,451},{4,452},{5,453},{6,454},{7,455},{8... | collective-permute-start | bytes 1769480 | tf_op jit(solution)/shard_map/own_outer1/ppermute | solution.py:84
  10.1 0.0 collective-permute-done.inner.refs_1_
  10.2 0.1 cut.1
  10.2 1.3 %collective-permute-start.1 = (bf16[192,768]{1,0:T(8,128)(2,1)S(1)}, bf16[192,768]{1,0:T(8,128)(2,1)S(1)}, u32[]{:S(2)}, u32[]{:S(2)}) collective-permute-start(bf16[192,768]{1,0:T(8,128)(2,1)S(1)} %get-tuple-element.42), channel_id=1, source_target_pairs={{0,3},{4,7},{8,11},{12,15},{16,19},{20,23},{24,27},{28,31},{35,32}... | collective-permute-start | bytes 884744 | tf_op jit(solution)/shard_map/spread0/ppermute | solution.py:84
  11.5 1.4 %collective-permute-start.2 = (bf16[192,768]{1,0:T(8,128)(2,1)S(1)}, bf16[192,768]{1,0:T(8,128)(2,1)}, u32[]{:S(2)}, u32[]{:S(2)}) collective-permute-start(bf16[192,768]{1,0:T(8,128)(2,1)S(1)} %get-tuple-element.43), channel_id=1, source_target_pairs={{0,1},{4,5},{8,9},{12,13},{16,17},{20,21},{24,25},{28,29},{35,34},... | collective-permute-start | bytes 884744 | tf_op jit(solution)/shard_map/spread1/ppermute | solution.py:84
  12.9 1.4 %collective-permute-start.3 = (bf16[192,768]{1,0:T(8,128)(2,1)S(1)}, bf16[192,768]{1,0:T(8,128)(2,1)}, u32[]{:S(2)}, u32[]{:S(2)}) collective-permute-start(bf16[192,768]{1,0:T(8,128)(2,1)S(1)} %get-tuple-element.44), channel_id=1, source_target_pairs={{0,2},{4,6},{8,10},{12,14},{16,18},{20,22},{24,26},{28,30},{35,33}... | collective-permute-start | bytes 884744 | tf_op jit(solution)/shard_map/spread2/ppermute | solution.py:84
  14.3 3.9 %collective-permute-start.11 = (bf16[384,768]{1,0:T(8,128)(2,1)}, bf16[384,768]{1,0:T(8,128)(2,1)}, u32[]{:S(2)}, u32[]{:S(2)}) collective-permute-start(bf16[384,768]{1,0:T(8,128)(2,1)} %get-tuple-element.98.oth.refs_3_), channel_id=1, source_target_pairs={{0,96},{1,97},{2,98},{3,99},{4,100},{5,101},{6,102},{7,103},{8,104... | collective-permute-start | bytes 1769480 | tf_op jit(solution)/shard_map/own_inner1/ppermute | solution.py:84
  19.2 1.1 dynamic-slice_select_fusion
  20.3 0.0 collective-permute-done.1
  20.3 0.0 collective-permute-done.2
  20.3 0.0 collective-permute-done.3
  20.4 0.1 select_select_fusion
  20.4 14.0 %collective-permute-start.4 = (bf16[192,768]{1,0:T(8,128)(2,1)S(1)}, bf16[192,768]{1,0:T(8,128)(2,1)S(1)}, u32[]{:S(2)}, u32[]{:S(2)}) collective-permute-start(bf16[192,768]{1,0:T(8,128)(2,1)S(1)} %select_select_fusion), channel_id=1, source_target_pairs={{0,476},{1,477},{2,478},{3,479},{4,448},{5,449},{6,450},{7,451},{8... | collective-permute-start | bytes 884744 | tf_op jit(solution)/shard_map/cross/ppermute | solution.py:84
  34.4 0.0 collective-permute-done.5.refs_2_
  34.4 1.3 %pad_maximum_fusion = bf16[1152,768]{1,0:T(8,128)(2,1)} fusion(bf16[384,768]{1,0:T(8,128)(2,1)S(1)} %collective-permute-done.5.refs_2_, bf16[384,768]{1,0:T(8,128)(2,1)S(1)} %get-tuple-element.99.outer.out.refs_0_, bf16[384,768]{1,0:T(8,128)(2,1)S(1)} %collective-permute-done.inner.refs_1_), kind=kLoop, calls=%fused_computation | loop fusion | flops 5308416 | bytes 3538944 | tf_op jit(solution)/shard_map/concatenate | solution.py:207
  35.7 2.8 %collective-permute-start.6 = (bf16[1152,768]{1,0:T(8,128)(2,1)}, bf16[1152,768]{1,0:T(8,128)(2,1)}, u32[]{:S(2)}, u32[]{:S(2)}) collective-permute-start(bf16[1152,768]{1,0:T(8,128)(2,1)} %pad_maximum_fusion), channel_id=1, source_target_pairs={{1,0},{2,1},{3,2},{5,4},{6,5},{7,6},{9,8},{10,9},{11,10},{13,12},{... | collective-permute-start | bytes 5308424 | tf_op jit(solution)/shard_map/wide_early/ppermute | solution.py:84
  38.5 0.2 factors.1
  38.7 0.0 copy-start
  38.7 4.3 %terms_own0.1 = (f32[384,768]{1,0:T(8,128)S(1)}, f32[384,768]{1,0:T(8,128)S(1)}) custom-call(f32[1]{0:T(128)} %bitcast.3.s, bf16[384,768]{1,0:T(8,128)(2,1)} %get-tuple-element.98.oth.refs_3_, bf16[384,768]{1,0:T(8,128)(2,1)S(1)} %get-tuple-element.99.outer.out.refs_0_, f32[384,128]{1,0:T(8,128)S(1)} %get-tuple-element.64.nf, ...), custom_call_target="tpu_custom_call" | custom-call | flops 99999997952 | bytes 1000 | tf_op jit(solution)/shard_map/terms_own0/pallas_call | solution.py:99
  43.1 0.0 copy-done
  43.1 0.0 copy-start.2
  43.1 0.0 copy-start.4
  43.1 25.5 %collective-permute-done.4.block = bf16[192,768]{1,0:T(8,128)(2,1)S(1)} collective-permute-done((bf16[192,768]{1,0:T(8,128)(2,1)S(1)}, bf16[192,768]{1,0:T(8,128)(2,1)S(1)}, u32[]{:S(2)}, u32[]{:S(2)}) %collective-permute-start.4) | collective-permute-done | bytes 294944 | tf_op jit(solution)/shard_map/cross/ppermute | solution.py:84
  68.6 0.0 copy-done.2
  68.6 0.0 copy-done.4
  68.7 0.0 collective-permute-done.6.early
  68.7 1.3 %collective-permute-start.9 = (bf16[192,768]{1,0:T(8,128)(2,1)S(1)}, bf16[192,768]{1,0:T(8,128)(2,1)S(1)}, u32[]{:S(2)}, u32[]{:S(2)}) collective-permute-start(bf16[192,768]{1,0:T(8,128)(2,1)S(1)} %crossed.1.q0), channel_id=1, source_target_pairs={{0,3},{4,7},{8,11},{12,15},{16,19},{20,23},{24,27},{28,31},{35,32}... | collective-permute-start | bytes 884744 | tf_op jit(solution)/shard_map/gather3/ppermute | solution.py:84
  70.0 1.3 %collective-permute-start.8 = (bf16[192,768]{1,0:T(8,128)(2,1)S(1)}, bf16[192,768]{1,0:T(8,128)(2,1)S(1)}, u32[]{:S(2)}, u32[]{:S(2)}) collective-permute-start(bf16[192,768]{1,0:T(8,128)(2,1)S(1)} %crossed.1.q0), channel_id=1, source_target_pairs={{2,3},{6,7},{10,11},{14,15},{18,19},{22,23},{26,27},{30,31},{33,32... | collective-permute-start | bytes 884744 | tf_op jit(solution)/shard_map/gather2/ppermute | solution.py:84
  71.3 1.3 %collective-permute-start.7 = (bf16[192,768]{1,0:T(8,128)(2,1)S(1)}, bf16[192,768]{1,0:T(8,128)(2,1)S(1)}, u32[]{:S(2)}, u32[]{:S(2)}) collective-permute-start(bf16[192,768]{1,0:T(8,128)(2,1)S(1)} %crossed.1.q0), channel_id=1, source_target_pairs={{1,3},{5,7},{9,11},{13,15},{17,19},{21,23},{25,27},{29,31},{34,32}... | collective-permute-start | bytes 884744 | tf_op jit(solution)/shard_map/gather1/ppermute | solution.py:84
  72.6 0.0 collective-permute-done.11.keys
  72.6 3.4 %collective-permute-start.12 = (bf16[384,768]{1,0:T(8,128)(2,1)}, bf16[384,768]{1,0:T(8,128)(2,1)S(1)}, u32[]{:S(2)}, u32[]{:S(2)}) collective-permute-start(bf16[384,768]{1,0:T(8,128)(2,1)} %collective-permute-done.11.keys), channel_id=1, source_target_pairs={{1,0},{2,1},{3,2},{5,4},{6,5},{7,6},{9,8},{10,9},{11,10},{13,12},{... | collective-permute-start | bytes 1769480 | tf_op jit(solution)/shard_map/wide_late/ppermute | solution.py:84
  76.0 1.9 %collective-permute-start.15 = (bf16[384,768]{1,0:T(8,128)(2,1)S(1)}, bf16[384,768]{1,0:T(8,128)(2,1)S(1)}, u32[]{:S(2)}, u32[]{:S(2)}) collective-permute-start(bf16[384,768]{1,0:T(8,128)(2,1)S(1)} %collective-permute-done.5.refs_2_), channel_id=1, source_target_pairs={{0,480},{1,481},{2,482},{3,483},{4,484},{5,485},{6,486},{7,487},{8... | collective-permute-start | bytes 1769480 | tf_op jit(solution)/shard_map/own_outer2/ppermute | solution.py:84
  77.9 1.1 pad_maximum_fusion.1
  79.1 0.0 copy-start.5
  79.1 1.4 %collective-permute-done.9.q3 = bf16[192,768]{1,0:T(8,128)(2,1)S(1)} collective-permute-done((bf16[192,768]{1,0:T(8,128)(2,1)S(1)}, bf16[192,768]{1,0:T(8,128)(2,1)S(1)}, u32[]{:S(2)}, u32[]{:S(2)}) %collective-permute-start.9) | collective-permute-done | bytes 294944 | tf_op jit(solution)/shard_map/gather3/ppermute | solution.py:84
  80.5 2.3 %collective-permute-start.14 = (bf16[768,768]{1,0:T(8,128)(2,1)S(1)}, bf16[768,768]{1,0:T(8,128)(2,1)S(1)}, u32[]{:S(2)}, u32[]{:S(2)}) collective-permute-start(bf16[768,768]{1,0:T(8,128)(2,1)S(1)} %pad_maximum_fusion.1), channel_id=1, source_target_pairs={{0,32},{1,33},{2,34},{3,35},{4,36},{5,37},{6,38},{7,39},{8,40},{9,... | collective-permute-start | bytes 3538952 | tf_op jit(solution)/shard_map/sibling_own1/ppermute | solution.py:84
  82.8 0.0 collective-permute-done.8.q2
  82.8 0.0 collective-permute-done.7.q1
  82.8 2.6 %whole_blocks.1.gathered = bf16[768,768]{1,0:T(8,128)(2,1)} custom-call(bf16[192,768]{1,0:T(8,128)(2,1)S(1)} %crossed.1.q0, bf16[192,768]{1,0:T(8,128)(2,1)S(1)} %collective-permute-done.7.q1, bf16[192,768]{1,0:T(8,128)(2,1)S(1)} %collective-permute-done.8.q2, bf16[192,768]{1,0:T(8,128)(2,1)S(1)} %collective-permute-done.9.q3), custom_call_target="tpu_custom_call" | custom-call | flops 1000 | bytes 1000 | tf_op jit(solution)/shard_map/whole_blocks/pallas_call | solution.py:114
  85.4 2.8 %collective-permute-start.10 = (bf16[768,768]{1,0:T(8,128)(2,1)}, bf16[768,768]{1,0:T(8,128)(2,1)}, u32[]{:S(2)}, u32[]{:S(2)}) collective-permute-start(bf16[768,768]{1,0:T(8,128)(2,1)} %whole_blocks.1.gathered), channel_id=1, source_target_pairs={{3,67},{7,71},{11,75},{15,79},{19,83},{23,87},{27,91},{31,95},{32,... | collective-permute-start | bytes 3538952 | tf_op jit(solution)/shard_map/edge_back/ppermute | solution.py:84
  88.2 0.0 copy-done.5
  88.2 2.2 %terms_own1.1.near_in = f32[384,768]{1,0:T(8,128)S(1)} custom-call(f32[1]{0:T(128)} %bitcast.4.s, bf16[384,768]{1,0:T(8,128)(2,1)} %get-tuple-element.98.oth.refs_3_, f32[384,128]{1,0:T(8,128)S(1)} %get-tuple-element.64.nf, f32[1,6144]{1,0:T(1,128)S(1)} %get-tuple-element.63.kf, bf16[384,768]{1,0:T(8,128)(2,1)} %collective-permute-done.11.keys, ...), custom_call_target="tpu_custom_call" | custom-call | flops 99999997952 | bytes 1000 | tf_op jit(solution)/shard_map/terms_own1/pallas_call | solution.py:99
  90.4 0.0 collective-permute-done.12.late
  90.4 1.3 %merge.1.keys = bf16[768,768]{1,0:T(8,128)(2,1)S(1)} custom-call(s32[1]{0:T(128)} %bitcast.2.edge.e, bf16[1152,768]{1,0:T(8,128)(2,1)} %collective-permute-done.6.early, bf16[384,768]{1,0:T(8,128)(2,1)S(1)} %collective-permute-done.12.late, bf16[768,768]{1,0:T(8,128)(2,1)} %whole_blocks.1.gathered), custom_call_target="tpu_custom_call" | custom-call | flops 1000 | bytes 1000 | tf_op jit(solution)/shard_map/merge/pallas_call | solution.py:114
  91.7 1.9 %collective-permute-start.13 = (bf16[768,768]{1,0:T(8,128)(2,1)S(1)}, bf16[768,768]{1,0:T(8,128)(2,1)S(1)}, u32[]{:S(2)}, u32[]{:S(2)}) collective-permute-start(bf16[768,768]{1,0:T(8,128)(2,1)S(1)} %merge.1.keys), channel_id=1, source_target_pairs={{0,32},{1,33},{2,34},{3,35},{4,36},{5,37},{6,38},{7,39},{8,40},{9,... | collective-permute-start | bytes 3538952 | tf_op jit(solution)/shard_map/sibling_hop1/ppermute | solution.py:84
  93.6 10.1 %collective-permute-done.15.farthest = bf16[384,768]{1,0:T(8,128)(2,1)S(1)} collective-permute-done((bf16[384,768]{1,0:T(8,128)(2,1)S(1)}, bf16[384,768]{1,0:T(8,128)(2,1)S(1)}, u32[]{:S(2)}, u32[]{:S(2)}) %collective-permute-start.15) | collective-permute-done | bytes 589856 | tf_op jit(solution)/shard_map/own_outer2/ppermute | solution.py:84
  103.7 2.4 %terms_near1.1.near_in = f32[384,768]{1,0:T(8,128)S(1)} custom-call(f32[1]{0:T(128)} %bitcast.5.s, bf16[384,768]{1,0:T(8,128)(2,1)} %get-tuple-element.98.oth.refs_3_, f32[384,128]{1,0:T(8,128)S(1)} %get-tuple-element.64.nf, f32[1,6144]{1,0:T(1,128)S(1)} %get-tuple-element.63.kf, bf16[768,768]{1,0:T(8,128)(2,1)S(1)} %merge.1.keys, ...), custom_call_target="tpu_custom_call" | custom-call | flops 1000 | bytes 1000 | tf_op jit(solution)/shard_map/terms_near1/pallas_call | solution.py:99
  106.2 0.0 collective-permute-done.14.own
  106.2 0.0 copy-done.1
  106.2 0.0 copy-done.3
  106.2 2.1 %terms_far1.1.far_in = f32[384,768]{1,0:T(8,128)S(1)} custom-call(f32[1]{0:T(128)} %bitcast.6.s, bf16[384,768]{1,0:T(8,128)(2,1)S(1)} %get-tuple-element.99.outer.out.refs_0_, f32[384,128]{1,0:T(8,128)S(1)} %copy-done.1, f32[1,6144]{1,0:T(1,128)S(1)} %get-tuple-element.63.kf, bf16[768,768]{1,0:T(8,128)(2,1)S(1)} %collective-permute-done.14.own, ...), custom_call_target="tpu_custom_call" | custom-call | flops 49999998976 | bytes 1000 | tf_op jit(solution)/shard_map/terms_far1/pallas_call | solution.py:99
  108.3 0.1 slice_select_fusion
  108.3 5.6 %collective-permute-start.17 = (bf16[384,768]{1,0:T(8,128)(2,1)S(1)}, bf16[384,768]{1,0:T(8,128)(2,1)S(1)}, u32[]{:S(2)}, u32[]{:S(2)}) collective-permute-start(bf16[384,768]{1,0:T(8,128)(2,1)S(1)} %slice_select_fusion), channel_id=1, source_target_pairs={{0,1},{1,2},{2,3},{3,483},{4,5},{5,6},{6,7},{7,487},{8,9},{9,10},{... | collective-permute-start | bytes 1769480 | tf_op jit(solution)/shard_map/farthest/ppermute | solution.py:84
  113.9 0.0 collective-permute-done.13.hop
  114.0 1.3 %terms_far2.1.far_in = f32[384,768]{1,0:T(8,128)S(1)} custom-call(f32[1]{0:T(128)} %bitcast.7.s, bf16[384,768]{1,0:T(8,128)(2,1)S(1)} %get-tuple-element.99.outer.out.refs_0_, f32[384,128]{1,0:T(8,128)S(1)} %copy-done.1, f32[1,6144]{1,0:T(1,128)S(1)} %get-tuple-element.63.kf, bf16[768,768]{1,0:T(8,128)(2,1)S(1)} %collective-permute-done.13.hop, ...), custom_call_target="tpu_custom_call" | custom-call | flops 1000 | bytes 1000 | tf_op jit(solution)/shard_map/terms_far2/pallas_call | solution.py:99
  115.2 0.0 collective-permute-done.10.back
  115.2 1.3 %slice_select_fusion.1.inner0 = bf16[384,768]{1,0:T(8,128)(2,1)S(1)} fusion(bf16[1152,768]{1,0:T(8,128)(2,1)} %collective-permute-done.6.early, bf16[768,768]{1,0:T(8,128)(2,1)} %collective-permute-done.10.back, pred[]{:T(512)S(6)} %eq.62), kind=kLoop, calls=%fused_computation.3 | loop fusion | flops 294912 | bytes 1769473 | tf_op jit(solution)/shard_map/jit(_where)/select_n | solution.py:375
  116.5 1.9 %collective-permute-start.16 = (bf16[384,768]{1,0:T(8,128)(2,1)S(1)}, bf16[384,768]{1,0:T(8,128)(2,1)S(1)}, u32[]{:S(2)}, u32[]{:S(2)}) collective-permute-start(bf16[384,768]{1,0:T(8,128)(2,1)S(1)} %slice_select_fusion.1.inner0), channel_id=1, source_target_pairs={{0,32},{1,33},{2,34},{3,35},{4,36},{5,37},{6,38},{7,39},{8,40},{9,... | collective-permute-start | bytes 1769480 | tf_op jit(solution)/shard_map/sibling_hop0/ppermute | solution.py:84
  118.5 4.3 %terms_near0.1 = (f32[384,768]{1,0:T(8,128)}, f32[384,768]{1,0:T(8,128)}) custom-call(s32[1]{0:T(128)} %bitcast.c, s32[1]{0:T(128)} %bitcast.2.edge.e, f32[1]{0:T(128)} %bitcast.8.s, bf16[384,768]{1,0:T(8,128)(2,1)} %get-tuple-element.98.oth.refs_3_, f32[384,128]{1,0:T(8,128)S(1)} %get-tuple-element.64.nf, f32[1,6144]{1,0:T(1,128)S(1)} %get-tuple-element.63.kf, ...), custom_call_target="tpu_custom_call" | custom-call | flops 99999997952 | bytes 1000 | tf_op jit(solution)/shard_map/terms_near0/pallas_call | solution.py:401
  122.8 0.0 collective-permute-done.17.hf2
  122.8 0.0 collective-permute-done.16.hs0
  122.8 2.3 %terms_last.1 = (f32[384,768]{1,0:T(8,128)}, f32[384,768]{1,0:T(8,128)}) custom-call(s32[1]{0:T(128)} %bitcast.c, f32[1]{0:T(128)} %bitcast.9.s, bf16[384,768]{1,0:T(8,128)(2,1)S(1)} %get-tuple-element.99.outer.out.refs_0_, f32[384,128]{1,0:T(8,128)S(1)} %copy-done.1, ...), custom_call_target="tpu_custom_call", output_to_operand_aliasing={{0}: (8, {}), {1}: (9, {})} | custom-call | flops 1000 | bytes 1000 | tf_op jit(solution)/shard_map/terms_last/pallas_call | solution.py:437
  (3 shorter events, 0.0 us)
Async XLA Ops:
  2.8 7.3 %collective-permute-start = (bf16[384,768]{1,0:T(8,128)(2,1)}, bf16[384,768]{1,0:T(8,128)(2,1)S(1)}, u32[]{:S(2)}, u32[]{:S(2)}) collective-permute-start(bf16[384,768]{1,0:T(8,128)(2,1)} %get-tuple-element.98.oth.refs_3_), channel_id=1, source_target_pairs={{0,32},{1,33},{2,34},{3,35},{4,36},{5,37},{6,38},{7,39},{8,40},{9,... | collective-permute-start | bytes 1769480 | tf_op jit(solution)/shard_map/swap/ppermute | solution.py:84
  5.4 29.0 %collective-permute-start.5 = (bf16[384,768]{1,0:T(8,128)(2,1)S(1)}, bf16[384,768]{1,0:T(8,128)(2,1)S(1)}, u32[]{:S(2)}, u32[]{:S(2)}) collective-permute-start(bf16[384,768]{1,0:T(8,128)(2,1)S(1)} %get-tuple-element.99.outer.out.refs_0_), channel_id=1, source_target_pairs={{0,448},{1,449},{2,450},{3,451},{4,452},{5,453},{6,454},{7,455},{8... | collective-permute-start | bytes 1769480 | tf_op jit(solution)/shard_map/own_outer1/ppermute | solution.py:84
  10.2 10.1 %collective-permute-start.1 = (bf16[192,768]{1,0:T(8,128)(2,1)S(1)}, bf16[192,768]{1,0:T(8,128)(2,1)S(1)}, u32[]{:S(2)}, u32[]{:S(2)}) collective-permute-start(bf16[192,768]{1,0:T(8,128)(2,1)S(1)} %get-tuple-element.42), channel_id=1, source_target_pairs={{0,3},{4,7},{8,11},{12,15},{16,19},{20,23},{24,27},{28,31},{35,32}... | collective-permute-start | bytes 884744 | tf_op jit(solution)/shard_map/spread0/ppermute | solution.py:84
  11.5 8.8 %collective-permute-start.2 = (bf16[192,768]{1,0:T(8,128)(2,1)S(1)}, bf16[192,768]{1,0:T(8,128)(2,1)}, u32[]{:S(2)}, u32[]{:S(2)}) collective-permute-start(bf16[192,768]{1,0:T(8,128)(2,1)S(1)} %get-tuple-element.43), channel_id=1, source_target_pairs={{0,1},{4,5},{8,9},{12,13},{16,17},{20,21},{24,25},{28,29},{35,34},... | collective-permute-start | bytes 884744 | tf_op jit(solution)/shard_map/spread1/ppermute | solution.py:84
  12.9 7.4 %collective-permute-start.3 = (bf16[192,768]{1,0:T(8,128)(2,1)S(1)}, bf16[192,768]{1,0:T(8,128)(2,1)}, u32[]{:S(2)}, u32[]{:S(2)}) collective-permute-start(bf16[192,768]{1,0:T(8,128)(2,1)S(1)} %get-tuple-element.44), channel_id=1, source_target_pairs={{0,2},{4,6},{8,10},{12,14},{16,18},{20,22},{24,26},{28,30},{35,33}... | collective-permute-start | bytes 884744 | tf_op jit(solution)/shard_map/spread2/ppermute | solution.py:84
  14.3 58.3 %collective-permute-start.11 = (bf16[384,768]{1,0:T(8,128)(2,1)}, bf16[384,768]{1,0:T(8,128)(2,1)}, u32[]{:S(2)}, u32[]{:S(2)}) collective-permute-start(bf16[384,768]{1,0:T(8,128)(2,1)} %get-tuple-element.98.oth.refs_3_), channel_id=1, source_target_pairs={{0,96},{1,97},{2,98},{3,99},{4,100},{5,101},{6,102},{7,103},{8,104... | collective-permute-start | bytes 1769480 | tf_op jit(solution)/shard_map/own_inner1/ppermute | solution.py:84
  20.4 48.2 %collective-permute-start.4 = (bf16[192,768]{1,0:T(8,128)(2,1)S(1)}, bf16[192,768]{1,0:T(8,128)(2,1)S(1)}, u32[]{:S(2)}, u32[]{:S(2)}) collective-permute-start(bf16[192,768]{1,0:T(8,128)(2,1)S(1)} %select_select_fusion), channel_id=1, source_target_pairs={{0,476},{1,477},{2,478},{3,479},{4,448},{5,449},{6,450},{7,451},{8... | collective-permute-start | bytes 884744 | tf_op jit(solution)/shard_map/cross/ppermute | solution.py:84
  35.7 32.9 %collective-permute-start.6 = (bf16[1152,768]{1,0:T(8,128)(2,1)}, bf16[1152,768]{1,0:T(8,128)(2,1)}, u32[]{:S(2)}, u32[]{:S(2)}) collective-permute-start(bf16[1152,768]{1,0:T(8,128)(2,1)} %pad_maximum_fusion), channel_id=1, source_target_pairs={{1,0},{2,1},{3,2},{5,4},{6,5},{7,6},{9,8},{10,9},{11,10},{13,12},{... | collective-permute-start | bytes 5308424 | tf_op jit(solution)/shard_map/wide_early/ppermute | solution.py:84
  38.7 4.4 %copy-start = (f32[384,128]{1,0:T(8,128)}, f32[384,128]{1,0:T(8,128)S(1)}, u32[]{:S(2)}) copy-start(f32[384,128]{1,0:T(8,128)S(1)} %get-tuple-element.62.ff) | copy-start | bytes 589828
  43.1 25.5 %copy-start.2 = (f32[384,768]{1,0:T(8,128)}, f32[384,768]{1,0:T(8,128)S(1)}, u32[]{:S(2)}) copy-start(f32[384,768]{1,0:T(8,128)S(1)} %get-tuple-element.67.far_in) | copy-start | bytes 3538948
  43.1 25.5 %copy-start.4 = (f32[384,768]{1,0:T(8,128)}, f32[384,768]{1,0:T(8,128)S(1)}, u32[]{:S(2)}) copy-start(f32[384,768]{1,0:T(8,128)S(1)} %get-tuple-element.66.near_in) | copy-start | bytes 3538948
  68.7 11.8 %collective-permute-start.9 = (bf16[192,768]{1,0:T(8,128)(2,1)S(1)}, bf16[192,768]{1,0:T(8,128)(2,1)S(1)}, u32[]{:S(2)}, u32[]{:S(2)}) collective-permute-start(bf16[192,768]{1,0:T(8,128)(2,1)S(1)} %crossed.1.q0), channel_id=1, source_target_pairs={{0,3},{4,7},{8,11},{12,15},{16,19},{20,23},{24,27},{28,31},{35,32}... | collective-permute-start | bytes 884744 | tf_op jit(solution)/shard_map/gather3/ppermute | solution.py:84
  70.0 12.8 %collective-permute-start.8 = (bf16[192,768]{1,0:T(8,128)(2,1)S(1)}, bf16[192,768]{1,0:T(8,128)(2,1)S(1)}, u32[]{:S(2)}, u32[]{:S(2)}) collective-permute-start(bf16[192,768]{1,0:T(8,128)(2,1)S(1)} %crossed.1.q0), channel_id=1, source_target_pairs={{2,3},{6,7},{10,11},{14,15},{18,19},{22,23},{26,27},{30,31},{33,32... | collective-permute-start | bytes 884744 | tf_op jit(solution)/shard_map/gather2/ppermute | solution.py:84
  71.3 11.5 %collective-permute-start.7 = (bf16[192,768]{1,0:T(8,128)(2,1)S(1)}, bf16[192,768]{1,0:T(8,128)(2,1)S(1)}, u32[]{:S(2)}, u32[]{:S(2)}) collective-permute-start(bf16[192,768]{1,0:T(8,128)(2,1)S(1)} %crossed.1.q0), channel_id=1, source_target_pairs={{1,3},{5,7},{9,11},{13,15},{17,19},{21,23},{25,27},{29,31},{34,32}... | collective-permute-start | bytes 884744 | tf_op jit(solution)/shard_map/gather1/ppermute | solution.py:84
  72.6 17.8 %collective-permute-start.12 = (bf16[384,768]{1,0:T(8,128)(2,1)}, bf16[384,768]{1,0:T(8,128)(2,1)S(1)}, u32[]{:S(2)}, u32[]{:S(2)}) collective-permute-start(bf16[384,768]{1,0:T(8,128)(2,1)} %collective-permute-done.11.keys), channel_id=1, source_target_pairs={{1,0},{2,1},{3,2},{5,4},{6,5},{7,6},{9,8},{10,9},{11,10},{13,12},{... | collective-permute-start | bytes 1769480 | tf_op jit(solution)/shard_map/wide_late/ppermute | solution.py:84
  76.0 27.7 %collective-permute-start.15 = (bf16[384,768]{1,0:T(8,128)(2,1)S(1)}, bf16[384,768]{1,0:T(8,128)(2,1)S(1)}, u32[]{:S(2)}, u32[]{:S(2)}) collective-permute-start(bf16[384,768]{1,0:T(8,128)(2,1)S(1)} %collective-permute-done.5.refs_2_), channel_id=1, source_target_pairs={{0,480},{1,481},{2,482},{3,483},{4,484},{5,485},{6,486},{7,487},{8... | collective-permute-start | bytes 1769480 | tf_op jit(solution)/shard_map/own_outer2/ppermute | solution.py:84
  79.1 9.1 %copy-start.5 = (f32[384,768]{1,0:T(8,128)S(1)}, f32[384,768]{1,0:T(8,128)}, u32[]{:S(2)}) copy-start(f32[384,768]{1,0:T(8,128)} %copy-done.4) | copy-start | bytes 3538948
  80.5 25.7 %collective-permute-start.14 = (bf16[768,768]{1,0:T(8,128)(2,1)S(1)}, bf16[768,768]{1,0:T(8,128)(2,1)S(1)}, u32[]{:S(2)}, u32[]{:S(2)}) collective-permute-start(bf16[768,768]{1,0:T(8,128)(2,1)S(1)} %pad_maximum_fusion.1), channel_id=1, source_target_pairs={{0,32},{1,33},{2,34},{3,35},{4,36},{5,37},{6,38},{7,39},{8,40},{9,... | collective-permute-start | bytes 3538952 | tf_op jit(solution)/shard_map/sibling_own1/ppermute | solution.py:84
  85.4 29.8 %collective-permute-start.10 = (bf16[768,768]{1,0:T(8,128)(2,1)}, bf16[768,768]{1,0:T(8,128)(2,1)}, u32[]{:S(2)}, u32[]{:S(2)}) collective-permute-start(bf16[768,768]{1,0:T(8,128)(2,1)} %whole_blocks.1.gathered), channel_id=1, source_target_pairs={{3,67},{7,71},{11,75},{15,79},{19,83},{23,87},{27,91},{31,95},{32,... | collective-permute-start | bytes 3538952 | tf_op jit(solution)/shard_map/edge_back/ppermute | solution.py:84
  91.7 22.2 %collective-permute-start.13 = (bf16[768,768]{1,0:T(8,128)(2,1)S(1)}, bf16[768,768]{1,0:T(8,128)(2,1)S(1)}, u32[]{:S(2)}, u32[]{:S(2)}) collective-permute-start(bf16[768,768]{1,0:T(8,128)(2,1)S(1)} %merge.1.keys), channel_id=1, source_target_pairs={{0,32},{1,33},{2,34},{3,35},{4,36},{5,37},{6,38},{7,39},{8,40},{9,... | collective-permute-start | bytes 3538952 | tf_op jit(solution)/shard_map/sibling_hop1/ppermute | solution.py:84
  103.7 2.5 %copy-start.1 = (f32[384,128]{1,0:T(8,128)S(1)}, f32[384,128]{1,0:T(8,128)}, u32[]{:S(2)}) copy-start(f32[384,128]{1,0:T(8,128)} %copy-done) | copy-start | bytes 589828
  103.7 2.5 %copy-start.3 = (f32[384,768]{1,0:T(8,128)S(1)}, f32[384,768]{1,0:T(8,128)}, u32[]{:S(2)}) copy-start(f32[384,768]{1,0:T(8,128)} %copy-done.2) | copy-start | bytes 3538948
  108.3 14.5 %collective-permute-start.17 = (bf16[384,768]{1,0:T(8,128)(2,1)S(1)}, bf16[384,768]{1,0:T(8,128)(2,1)S(1)}, u32[]{:S(2)}, u32[]{:S(2)}) collective-permute-start(bf16[384,768]{1,0:T(8,128)(2,1)S(1)} %slice_select_fusion), channel_id=1, source_target_pairs={{0,1},{1,2},{2,3},{3,483},{4,5},{5,6},{6,7},{7,487},{8,9},{9,10},{... | collective-permute-start | bytes 1769480 | tf_op jit(solution)/shard_map/farthest/ppermute | solution.py:84
  116.5 6.3 %collective-permute-start.16 = (bf16[384,768]{1,0:T(8,128)(2,1)S(1)}, bf16[384,768]{1,0:T(8,128)(2,1)S(1)}, u32[]{:S(2)}, u32[]{:S(2)}) collective-permute-start(bf16[384,768]{1,0:T(8,128)(2,1)S(1)} %slice_select_fusion.1.inner0), channel_id=1, source_target_pairs={{0,32},{1,33},{2,34},{3,35},{4,36},{5,37},{6,38},{7,39},{8,40},{9,... | collective-permute-start | bytes 1769480 | tf_op jit(solution)/shard_map/sibling_hop0/ppermute | solution.py:84

commit v12 on v11

--- a/solution.py
+++ b/solution.py
@@ -314,7 +314,7 @@
 
     near_sum = call(
         "terms_own1", own1_kernel, total, (scale,),
-        (other, near_factor, key_factors, after(inner1, whole_blocks), near_sum), 100_000_000,
+        (other, near_factor, key_factors, after(inner1, whole_blocks, far2), near_sum), 100_000_000,
     )
 
     def merge_kernel(edge, early, late, gathered, out, sems):
@@ -343,7 +343,7 @@
 
     near_sum = call(
         "terms_near1", near1_kernel, total, (scale,),
-        (other, near_factor, key_factors, after(hop1, far2), near_sum),
+        (other, near_factor, key_factors, hop1, near_sum),
     )
     hop_sib1 = send("sibling_hop1", hop1, to_sibling)
 

time: 126 us -> 126 us (level)
  the two profiles are of different devices: /device:TPU:97 before, /device:TPU:25 now
where the time goes in v12:
time: 126 us; the launch traced here: 125 us
  starting transfers between devices  74.8 us (59%)
  Pallas kernels  23 us (18%)
  waiting for transfers between devices  17.6 us (14%)
  other arithmetic  7.21 us (6%)
  between operations  2.07 us (2%)
    ppermute x18, starting transfers between devices, send(): return lax.ppermute(x, AXES, pairs(target))  74.8 us
    ppermute x18, waiting for transfers between devices, send(): return lax.ppermute(x, AXES, pairs(target))  17.6 us
    pallas_call x8, Pallas kernels, call(): pl.pallas_call(kernel, out_shape=out_shape, in_specs=[scalars() for _ in...  12.7 us
    pallas_call x1, Pallas kernels, on_device(): pl.pallas_call(near0_kernel, out_shape=[total, total], in_specs=[scalars(...  4.31 us
    pallas_call x2, Pallas kernels, assemble(): pl.pallas_call(kernel, out_shape=out_shape, in_specs=[scalars() for _ in...  3.71 us
  transfers between devices with their start and end apart: 18, of which 2 were waited for; matrix products, arithmetic and copies ran while one was open for 4% of the time, Pallas kernels for 17%

profile of v12, /device:TPU:25, one launch (start us, length us, event | category | flops | bytes accessed | tf_op | source)
XLA Modules:
  0.0 124.7 jit_solution(1362419488670383393)
XLA Ops:
  0.6 2.2 %broadcast_select_fusion = (bf16[384,768]{1,0:T(8,128)(2,1)}, bf16[384,768]{1,0:T(8,128)(2,1)S(1)}) fusion(bf16[384,768]{1,0:T(8,128)(2,1)} %param.5, bf16[384,768]{1,0:T(8,128)(2,1)} %param.6, pred[]{:T(512)S(6)} %eq.60), kind=kLoop, calls=%fused_computation.4 | loop fusion | flops 589824 | bytes 2359297 | tf_op jit(solution)/shard_map/jit(_where)/select_n | solution.py:186
  2.8 2.6 %collective-permute-start = (bf16[384,768]{1,0:T(8,128)(2,1)}, bf16[384,768]{1,0:T(8,128)(2,1)S(1)}, u32[]{:S(2)}, u32[]{:S(2)}) collective-permute-start(bf16[384,768]{1,0:T(8,128)(2,1)} %get-tuple-element.96.oth.refs_3_), channel_id=1, source_target_pairs={{0,32},{1,33},{2,34},{3,35},{4,36},{5,37},{6,38},{7,39},{8,40},{9,... | collective-permute-start | bytes 1769480 | tf_op jit(solution)/shard_map/swap/ppermute | solution.py:84
  5.4 3.5 %collective-permute-start.5 = (bf16[384,768]{1,0:T(8,128)(2,1)S(1)}, bf16[384,768]{1,0:T(8,128)(2,1)S(1)}, u32[]{:S(2)}, u32[]{:S(2)}) collective-permute-start(bf16[384,768]{1,0:T(8,128)(2,1)S(1)} %get-tuple-element.97.outer.out.refs_0_), channel_id=1, source_target_pairs={{0,448},{1,449},{2,450},{3,451},{4,452},{5,453},{6,454},{7,455},{8... | collective-permute-start | bytes 1769480 | tf_op jit(solution)/shard_map/own_outer1/ppermute | solution.py:84
  8.9 0.0 collective-permute-done.inner.refs_1_
  8.9 0.1 cut.1
  9.0 5.6 %collective-permute-start.1 = (bf16[192,768]{1,0:T(8,128)(2,1)S(1)}, bf16[192,768]{1,0:T(8,128)(2,1)S(1)}, u32[]{:S(2)}, u32[]{:S(2)}) collective-permute-start(bf16[192,768]{1,0:T(8,128)(2,1)S(1)} %get-tuple-element.41), channel_id=1, source_target_pairs={{0,3},{4,7},{8,11},{12,15},{16,19},{20,23},{24,27},{28,31},{35,32}... | collective-permute-start | bytes 884744 | tf_op jit(solution)/shard_map/spread0/ppermute | solution.py:84
  14.6 1.3 %collective-permute-start.2 = (bf16[192,768]{1,0:T(8,128)(2,1)S(1)}, bf16[192,768]{1,0:T(8,128)(2,1)S(1)}, u32[]{:S(2)}, u32[]{:S(2)}) collective-permute-start(bf16[192,768]{1,0:T(8,128)(2,1)S(1)} %get-tuple-element.42), channel_id=1, source_target_pairs={{0,1},{4,5},{8,9},{12,13},{16,17},{20,21},{24,25},{28,29},{35,34},... | collective-permute-start | bytes 884744 | tf_op jit(solution)/shard_map/spread1/ppermute | solution.py:84
  16.0 2.0 %collective-permute-start.3 = (bf16[192,768]{1,0:T(8,128)(2,1)S(1)}, bf16[192,768]{1,0:T(8,128)(2,1)}, u32[]{:S(2)}, u32[]{:S(2)}) collective-permute-start(bf16[192,768]{1,0:T(8,128)(2,1)S(1)} %get-tuple-element.43), channel_id=1, source_target_pairs={{0,2},{4,6},{8,10},{12,14},{16,18},{20,22},{24,26},{28,30},{35,33}... | collective-permute-start | bytes 884744 | tf_op jit(solution)/shard_map/spread2/ppermute | solution.py:84
  18.0 5.8 %collective-permute-start.11 = (bf16[384,768]{1,0:T(8,128)(2,1)}, bf16[384,768]{1,0:T(8,128)(2,1)}, u32[]{:S(2)}, u32[]{:S(2)}) collective-permute-start(bf16[384,768]{1,0:T(8,128)(2,1)} %get-tuple-element.96.oth.refs_3_), channel_id=1, source_target_pairs={{0,96},{1,97},{2,98},{3,99},{4,100},{5,101},{6,102},{7,103},{8,104... | collective-permute-start | bytes 1769480 | tf_op jit(solution)/shard_map/own_inner1/ppermute | solution.py:84
  24.7 1.1 dynamic-slice_select_fusion
  25.9 0.0 collective-permute-done.1
  25.9 0.0 collective-permute-done.2
  25.9 0.0 collective-permute-done.3
  25.9 0.1 select_select_fusion
  26.0 8.3 %collective-permute-start.4 = (bf16[192,768]{1,0:T(8,128)(2,1)S(1)}, bf16[192,768]{1,0:T(8,128)(2,1)S(1)}, u32[]{:S(2)}, u32[]{:S(2)}) collective-permute-start(bf16[192,768]{1,0:T(8,128)(2,1)S(1)} %select_select_fusion), channel_id=1, source_target_pairs={{0,476},{1,477},{2,478},{3,479},{4,448},{5,449},{6,450},{7,451},{8... | collective-permute-start | bytes 884744 | tf_op jit(solution)/shard_map/cross/ppermute | solution.py:84
  34.2 0.0 collective-permute-done.5.refs_2_
  34.2 1.3 %pad_maximum_fusion = bf16[1152,768]{1,0:T(8,128)(2,1)} fusion(bf16[384,768]{1,0:T(8,128)(2,1)S(1)} %collective-permute-done.5.refs_2_, bf16[384,768]{1,0:T(8,128)(2,1)S(1)} %get-tuple-element.97.outer.out.refs_0_, bf16[384,768]{1,0:T(8,128)(2,1)S(1)} %collective-permute-done.inner.refs_1_), kind=kLoop, calls=%fused_computation | loop fusion | flops 5308416 | bytes 3538944 | tf_op jit(solution)/shard_map/concatenate | solution.py:207
  35.6 1.3 %collective-permute-start.6 = (bf16[1152,768]{1,0:T(8,128)(2,1)}, bf16[1152,768]{1,0:T(8,128)(2,1)}, u32[]{:S(2)}, u32[]{:S(2)}) collective-permute-start(bf16[1152,768]{1,0:T(8,128)(2,1)} %pad_maximum_fusion), channel_id=1, source_target_pairs={{1,0},{2,1},{3,2},{5,4},{6,5},{7,6},{9,8},{10,9},{11,10},{13,12},{... | collective-permute-start | bytes 5308424 | tf_op jit(solution)/shard_map/wide_early/ppermute | solution.py:84
  36.8 0.2 factors.1
  37.0 0.0 copy-start
  37.0 0.0 copy-start.2
  37.1 0.0 copy-start.4
  37.1 4.4 %terms_own0.1 = (f32[384,768]{1,0:T(8,128)S(1)}, f32[384,768]{1,0:T(8,128)S(1)}) custom-call(f32[1]{0:T(128)} %bitcast.3.s, bf16[384,768]{1,0:T(8,128)(2,1)} %get-tuple-element.96.oth.refs_3_, bf16[384,768]{1,0:T(8,128)(2,1)S(1)} %get-tuple-element.97.outer.out.refs_0_, f32[384,128]{1,0:T(8,128)S(1)} %get-tuple-element.63.nf, ...), custom_call_target="tpu_custom_call" | custom-call | flops 99999997952 | bytes 1000 | tf_op jit(solution)/shard_map/terms_own0/pallas_call | solution.py:99
  41.5 0.0 copy-done
  41.5 0.0 copy-done.2
  41.5 0.0 copy-done.4
  41.5 0.0 copy-start.6
  41.5 0.0 copy-start.8
  41.5 3.3 %collective-permute-done.4.block = bf16[192,768]{1,0:T(8,128)(2,1)S(1)} collective-permute-done((bf16[192,768]{1,0:T(8,128)(2,1)S(1)}, bf16[192,768]{1,0:T(8,128)(2,1)S(1)}, u32[]{:S(2)}, u32[]{:S(2)}) %collective-permute-start.4) | collective-permute-done | bytes 294944 | tf_op jit(solution)/shard_map/cross/ppermute | solution.py:84
  44.9 14.2 %collective-permute-done.6.early = bf16[1152,768]{1,0:T(8,128)(2,1)} collective-permute-done((bf16[1152,768]{1,0:T(8,128)(2,1)}, bf16[1152,768]{1,0:T(8,128)(2,1)}, u32[]{:S(2)}, u32[]{:S(2)}) %collective-permute-start.6) | collective-permute-done | bytes 1769504 | tf_op jit(solution)/shard_map/wide_early/ppermute | solution.py:84
  59.1 11.9 %collective-permute-start.13 = (bf16[384,768]{1,0:T(8,128)(2,1)S(1)}, bf16[384,768]{1,0:T(8,128)(2,1)S(1)}, u32[]{:S(2)}, u32[]{:S(2)}) collective-permute-start(bf16[384,768]{1,0:T(8,128)(2,1)S(1)} %collective-permute-done.5.refs_2_), channel_id=1, source_target_pairs={{0,480},{1,481},{2,482},{3,483},{4,484},{5,485},{6,486},{7,487},{8... | collective-permute-start | bytes 1769480 | tf_op jit(solution)/shard_map/own_outer2/ppermute | solution.py:84
  71.0 1.7 %collective-permute-start.9 = (bf16[192,768]{1,0:T(8,128)(2,1)S(1)}, bf16[192,768]{1,0:T(8,128)(2,1)S(1)}, u32[]{:S(2)}, u32[]{:S(2)}) collective-permute-start(bf16[192,768]{1,0:T(8,128)(2,1)S(1)} %crossed.1.q0), channel_id=1, source_target_pairs={{0,3},{4,7},{8,11},{12,15},{16,19},{20,23},{24,27},{28,31},{35,32}... | collective-permute-start | bytes 884744 | tf_op jit(solution)/shard_map/gather3/ppermute | solution.py:84
  72.8 0.7 collective-permute-start.8
  73.4 0.7 collective-permute-start.7
  74.1 0.0 collective-permute-done.11.keys
  74.1 1.3 %collective-permute-start.12 = (bf16[384,768]{1,0:T(8,128)(2,1)}, bf16[384,768]{1,0:T(8,128)(2,1)S(1)}, u32[]{:S(2)}, u32[]{:S(2)}) collective-permute-start(bf16[384,768]{1,0:T(8,128)(2,1)} %collective-permute-done.11.keys), channel_id=1, source_target_pairs={{1,0},{2,1},{3,2},{5,4},{6,5},{7,6},{9,8},{10,9},{11,10},{13,12},{... | collective-permute-start | bytes 1769480 | tf_op jit(solution)/shard_map/wide_late/ppermute | solution.py:84
  75.4 1.1 pad_maximum_fusion.1
  76.6 0.0 collective-permute-done.9.q3
  76.6 10.1 %collective-permute-start.15 = (bf16[768,768]{1,0:T(8,128)(2,1)S(1)}, bf16[768,768]{1,0:T(8,128)(2,1)S(1)}, u32[]{:S(2)}, u32[]{:S(2)}) collective-permute-start(bf16[768,768]{1,0:T(8,128)(2,1)S(1)} %pad_maximum_fusion.1), channel_id=1, source_target_pairs={{0,32},{1,33},{2,34},{3,35},{4,36},{5,37},{6,38},{7,39},{8,40},{9,... | collective-permute-start | bytes 3538952 | tf_op jit(solution)/shard_map/sibling_own1/ppermute | solution.py:84
  86.8 0.0 collective-permute-done.8.q2
  86.8 0.0 collective-permute-done.7.q1
  86.8 2.6 %whole_blocks.1.gathered = bf16[768,768]{1,0:T(8,128)(2,1)} custom-call(bf16[192,768]{1,0:T(8,128)(2,1)S(1)} %crossed.1.q0, bf16[192,768]{1,0:T(8,128)(2,1)S(1)} %collective-permute-done.7.q1, bf16[192,768]{1,0:T(8,128)(2,1)S(1)} %collective-permute-done.8.q2, bf16[192,768]{1,0:T(8,128)(2,1)S(1)} %collective-permute-done.9.q3), custom_call_target="tpu_custom_call" | custom-call | flops 1000 | bytes 1000 | tf_op jit(solution)/shard_map/whole_blocks/pallas_call | solution.py:114
  89.4 1.7 %collective-permute-start.10 = (bf16[768,768]{1,0:T(8,128)(2,1)}, bf16[768,768]{1,0:T(8,128)(2,1)}, u32[]{:S(2)}, u32[]{:S(2)}) collective-permute-start(bf16[768,768]{1,0:T(8,128)(2,1)} %whole_blocks.1.gathered), channel_id=1, source_target_pairs={{3,67},{7,71},{11,75},{15,79},{19,83},{23,87},{27,91},{31,95},{32,... | collective-permute-start | bytes 3538952 | tf_op jit(solution)/shard_map/edge_back/ppermute | solution.py:84
  91.1 0.0 collective-permute-done.13.farthest
  91.1 0.0 copy-done.3
  91.1 2.2 %terms_own1.1.near_in = f32[384,768]{1,0:T(8,128)S(1)} custom-call(f32[1]{0:T(128)} %bitcast.4.s, bf16[384,768]{1,0:T(8,128)(2,1)} %get-tuple-element.96.oth.refs_3_, f32[384,128]{1,0:T(8,128)S(1)} %copy-done.5, f32[1,6144]{1,0:T(1,128)S(1)} %copy-done.3, bf16[384,768]{1,0:T(8,128)(2,1)} %collective-permute-done.11.keys, f32[384,768]{1,0:T(8,128)S(1)} %copy-done.9), custom_call_target="tpu_custom_call" | custom-call | flops 99999997952 | bytes 1000 | tf_op jit(solution)/shard_map/terms_own1/pallas_call | solution.py:99
  93.3 0.0 collective-permute-done.12.late
  93.3 1.1 merge.1.keys
  94.4 2.4 %collective-permute-start.14 = (bf16[768,768]{1,0:T(8,128)(2,1)S(1)}, bf16[768,768]{1,0:T(8,128)(2,1)S(1)}, u32[]{:S(2)}, u32[]{:S(2)}) collective-permute-start(bf16[768,768]{1,0:T(8,128)(2,1)S(1)} %merge.1.keys), channel_id=1, source_target_pairs={{0,32},{1,33},{2,34},{3,35},{4,36},{5,37},{6,38},{7,39},{8,40},{9,... | collective-permute-start | bytes 3538952 | tf_op jit(solution)/shard_map/sibling_hop1/ppermute | solution.py:84
  96.8 0.0 copy-start.7
  96.8 2.4 %terms_near1.1.near_in = f32[384,768]{1,0:T(8,128)S(1)} custom-call(f32[1]{0:T(128)} %bitcast.5.s, bf16[384,768]{1,0:T(8,128)(2,1)} %get-tuple-element.96.oth.refs_3_, f32[384,128]{1,0:T(8,128)S(1)} %copy-done.5, f32[1,6144]{1,0:T(1,128)S(1)} %copy-done.3, bf16[768,768]{1,0:T(8,128)(2,1)S(1)} %merge.1.keys, f32[384,768]{1,0:T(8,128)S(1)} %terms_own1.1.near_in), custom_call_target="tpu_custom_call" | custom-call | flops 1000 | bytes 1000 | tf_op jit(solution)/shard_map/terms_near1/pallas_call | solution.py:99
  99.3 0.0 collective-permute-done.15.own
  99.3 2.1 %terms_far1.1.far_in = f32[384,768]{1,0:T(8,128)S(1)} custom-call(f32[1]{0:T(128)} %bitcast.6.s, bf16[384,768]{1,0:T(8,128)(2,1)S(1)} %get-tuple-element.97.outer.out.refs_0_, f32[384,128]{1,0:T(8,128)S(1)} %copy-done.1, f32[1,6144]{1,0:T(1,128)S(1)} %copy-done.3, bf16[768,768]{1,0:T(8,128)(2,1)S(1)} %collective-permute-done.15.own, ...), custom_call_target="tpu_custom_call" | custom-call | flops 49999998976 | bytes 1000 | tf_op jit(solution)/shard_map/terms_far1/pallas_call | solution.py:99
  101.4 0.1 slice_select_fusion
  101.5 1.9 %collective-permute-start.17 = (bf16[384,768]{1,0:T(8,128)(2,1)S(1)}, bf16[384,768]{1,0:T(8,128)(2,1)S(1)}, u32[]{:S(2)}, u32[]{:S(2)}) collective-permute-start(bf16[384,768]{1,0:T(8,128)(2,1)S(1)} %slice_select_fusion), channel_id=1, source_target_pairs={{0,1},{1,2},{2,3},{3,483},{4,5},{5,6},{6,7},{7,487},{8,9},{9,10},{... | collective-permute-start | bytes 1769480 | tf_op jit(solution)/shard_map/farthest/ppermute | solution.py:84
  103.4 0.0 collective-permute-done.14.hop
  103.4 1.3 %terms_far2.1.far_in = f32[384,768]{1,0:T(8,128)S(1)} custom-call(f32[1]{0:T(128)} %bitcast.7.s, bf16[384,768]{1,0:T(8,128)(2,1)S(1)} %get-tuple-element.97.outer.out.refs_0_, f32[384,128]{1,0:T(8,128)S(1)} %copy-done.1, f32[1,6144]{1,0:T(1,128)S(1)} %copy-done.3, bf16[768,768]{1,0:T(8,128)(2,1)S(1)} %collective-permute-done.14.hop, ...), custom_call_target="tpu_custom_call" | custom-call | flops 1000 | bytes 1000 | tf_op jit(solution)/shard_map/terms_far2/pallas_call | solution.py:99
  104.7 0.0 collective-permute-done.10.back
  104.7 1.3 %slice_select_fusion.1.inner0 = bf16[384,768]{1,0:T(8,128)(2,1)S(1)} fusion(bf16[1152,768]{1,0:T(8,128)(2,1)} %collective-permute-done.6.early, bf16[768,768]{1,0:T(8,128)(2,1)} %collective-permute-done.10.back, pred[]{:T(512)S(6)} %eq.62), kind=kLoop, calls=%fused_computation.3 | loop fusion | flops 294912 | bytes 1769473 | tf_op jit(solution)/shard_map/jit(_where)/select_n | solution.py:375
  106.0 12.0 %collective-permute-start.16 = (bf16[384,768]{1,0:T(8,128)(2,1)S(1)}, bf16[384,768]{1,0:T(8,128)(2,1)S(1)}, u32[]{:S(2)}, u32[]{:S(2)}) collective-permute-start(bf16[384,768]{1,0:T(8,128)(2,1)S(1)} %slice_select_fusion.1.inner0), channel_id=1, source_target_pairs={{0,32},{1,33},{2,34},{3,35},{4,36},{5,37},{6,38},{7,39},{8,40},{9,... | collective-permute-start | bytes 1769480 | tf_op jit(solution)/shard_map/sibling_hop0/ppermute | solution.py:84
  118.1 4.3 %terms_near0.1 = (f32[384,768]{1,0:T(8,128)}, f32[384,768]{1,0:T(8,128)}) custom-call(s32[1]{0:T(128)} %bitcast.c, s32[1]{0:T(128)} %bitcast.2.edge.e, f32[1]{0:T(128)} %bitcast.8.s, bf16[384,768]{1,0:T(8,128)(2,1)} %get-tuple-element.96.oth.refs_3_, f32[384,128]{1,0:T(8,128)S(1)} %copy-done.5, f32[1,6144]{1,0:T(1,128)S(1)} %copy-done.3, ...), custom_call_target="tpu_custom_call" | custom-call | flops 99999997952 | bytes 1000 | tf_op jit(solution)/shard_map/terms_near0/pallas_call | solution.py:401
  122.4 0.0 collective-permute-done.17.hf2
  122.4 0.0 collective-permute-done.16.hs0
  122.4 2.3 %terms_last.1 = (f32[384,768]{1,0:T(8,128)}, f32[384,768]{1,0:T(8,128)}) custom-call(s32[1]{0:T(128)} %bitcast.c, f32[1]{0:T(128)} %bitcast.9.s, bf16[384,768]{1,0:T(8,128)(2,1)S(1)} %get-tuple-element.97.outer.out.refs_0_, f32[384,128]{1,0:T(8,128)S(1)} %copy-done.1, f32[1,6144]{1,0:T(1,128)S(1)} %copy-done.3, ...), custom_call_target="tpu_custom_call", output_to_operand_aliasing={{0}: (8, {}), {1}: (9, {})} | custom-call | flops 1000 | bytes 1000 | tf_op jit(solution)/shard_map/terms_last/pallas_call | solution.py:437
  (11 shorter events, 0.0 us)
Async XLA Ops:
  2.8 6.1 %collective-permute-start = (bf16[384,768]{1,0:T(8,128)(2,1)}, bf16[384,768]{1,0:T(8,128)(2,1)S(1)}, u32[]{:S(2)}, u32[]{:S(2)}) collective-permute-start(bf16[384,768]{1,0:T(8,128)(2,1)} %get-tuple-element.96.oth.refs_3_), channel_id=1, source_target_pairs={{0,32},{1,33},{2,34},{3,35},{4,36},{5,37},{6,38},{7,39},{8,40},{9,... | collective-permute-start | bytes 1769480 | tf_op jit(solution)/shard_map/swap/ppermute | solution.py:84
  5.4 28.9 %collective-permute-start.5 = (bf16[384,768]{1,0:T(8,128)(2,1)S(1)}, bf16[384,768]{1,0:T(8,128)(2,1)S(1)}, u32[]{:S(2)}, u32[]{:S(2)}) collective-permute-start(bf16[384,768]{1,0:T(8,128)(2,1)S(1)} %get-tuple-element.97.outer.out.refs_0_), channel_id=1, source_target_pairs={{0,448},{1,449},{2,450},{3,451},{4,452},{5,453},{6,454},{7,455},{8... | collective-permute-start | bytes 1769480 | tf_op jit(solution)/shard_map/own_outer1/ppermute | solution.py:84
  9.0 16.8 %collective-permute-start.1 = (bf16[192,768]{1,0:T(8,128)(2,1)S(1)}, bf16[192,768]{1,0:T(8,128)(2,1)S(1)}, u32[]{:S(2)}, u32[]{:S(2)}) collective-permute-start(bf16[192,768]{1,0:T(8,128)(2,1)S(1)} %get-tuple-element.41), channel_id=1, source_target_pairs={{0,3},{4,7},{8,11},{12,15},{16,19},{20,23},{24,27},{28,31},{35,32}... | collective-permute-start | bytes 884744 | tf_op jit(solution)/shard_map/spread0/ppermute | solution.py:84
  14.6 11.2 %collective-permute-start.2 = (bf16[192,768]{1,0:T(8,128)(2,1)S(1)}, bf16[192,768]{1,0:T(8,128)(2,1)S(1)}, u32[]{:S(2)}, u32[]{:S(2)}) collective-permute-start(bf16[192,768]{1,0:T(8,128)(2,1)S(1)} %get-tuple-element.42), channel_id=1, source_target_pairs={{0,1},{4,5},{8,9},{12,13},{16,17},{20,21},{24,25},{28,29},{35,34},... | collective-permute-start | bytes 884744 | tf_op jit(solution)/shard_map/spread1/ppermute | solution.py:84
  16.0 9.9 %collective-permute-start.3 = (bf16[192,768]{1,0:T(8,128)(2,1)S(1)}, bf16[192,768]{1,0:T(8,128)(2,1)}, u32[]{:S(2)}, u32[]{:S(2)}) collective-permute-start(bf16[192,768]{1,0:T(8,128)(2,1)S(1)} %get-tuple-element.43), channel_id=1, source_target_pairs={{0,2},{4,6},{8,10},{12,14},{16,18},{20,22},{24,26},{28,30},{35,33}... | collective-permute-start | bytes 884744 | tf_op jit(solution)/shard_map/spread2/ppermute | solution.py:84
  18.0 56.2 %collective-permute-start.11 = (bf16[384,768]{1,0:T(8,128)(2,1)}, bf16[384,768]{1,0:T(8,128)(2,1)}, u32[]{:S(2)}, u32[]{:S(2)}) collective-permute-start(bf16[384,768]{1,0:T(8,128)(2,1)} %get-tuple-element.96.oth.refs_3_), channel_id=1, source_target_pairs={{0,96},{1,97},{2,98},{3,99},{4,100},{5,101},{6,102},{7,103},{8,104... | collective-permute-start | bytes 1769480 | tf_op jit(solution)/shard_map/own_inner1/ppermute | solution.py:84
  26.0 18.9 %collective-permute-start.4 = (bf16[192,768]{1,0:T(8,128)(2,1)S(1)}, bf16[192,768]{1,0:T(8,128)(2,1)S(1)}, u32[]{:S(2)}, u32[]{:S(2)}) collective-permute-start(bf16[192,768]{1,0:T(8,128)(2,1)S(1)} %select_select_fusion), channel_id=1, source_target_pairs={{0,476},{1,477},{2,478},{3,479},{4,448},{5,449},{6,450},{7,451},{8... | collective-permute-start | bytes 884744 | tf_op jit(solution)/shard_map/cross/ppermute | solution.py:84
  35.6 23.6 %collective-permute-start.6 = (bf16[1152,768]{1,0:T(8,128)(2,1)}, bf16[1152,768]{1,0:T(8,128)(2,1)}, u32[]{:S(2)}, u32[]{:S(2)}) collective-permute-start(bf16[1152,768]{1,0:T(8,128)(2,1)} %pad_maximum_fusion), channel_id=1, source_target_pairs={{1,0},{2,1},{3,2},{5,4},{6,5},{7,6},{9,8},{10,9},{11,10},{13,12},{... | collective-permute-start | bytes 5308424 | tf_op jit(solution)/shard_map/wide_early/ppermute | solution.py:84
  37.0 4.4 %copy-start = (f32[384,128]{1,0:T(8,128)}, f32[384,128]{1,0:T(8,128)S(1)}, u32[]{:S(2)}) copy-start(f32[384,128]{1,0:T(8,128)S(1)} %get-tuple-element.61.ff) | copy-start | bytes 589828
  37.0 4.4 %copy-start.2 = (f32[1,6144]{1,0:T(1,128)}, f32[1,6144]{1,0:T(1,128)S(1)}, u32[]{:S(2)}) copy-start(f32[1,6144]{1,0:T(1,128)S(1)} %get-tuple-element.62.kf) | copy-start | bytes 73732
  37.1 4.4 %copy-start.4 = (f32[384,128]{1,0:T(8,128)}, f32[384,128]{1,0:T(8,128)S(1)}, u32[]{:S(2)}) copy-start(f32[384,128]{1,0:T(8,128)S(1)} %get-tuple-element.63.nf) | copy-start | bytes 589828
  41.5 3.4 %copy-start.6 = (f32[384,768]{1,0:T(8,128)}, f32[384,768]{1,0:T(8,128)S(1)}, u32[]{:S(2)}) copy-start(f32[384,768]{1,0:T(8,128)S(1)} %get-tuple-element.66.far_in) | copy-start | bytes 3538948
  41.5 3.4 %copy-start.8 = (f32[384,768]{1,0:T(8,128)}, f32[384,768]{1,0:T(8,128)S(1)}, u32[]{:S(2)}) copy-start(f32[384,768]{1,0:T(8,128)S(1)} %get-tuple-element.65.near_in) | copy-start | bytes 3538948
  59.1 32.0 %collective-permute-start.13 = (bf16[384,768]{1,0:T(8,128)(2,1)S(1)}, bf16[384,768]{1,0:T(8,128)(2,1)S(1)}, u32[]{:S(2)}, u32[]{:S(2)}) collective-permute-start(bf16[384,768]{1,0:T(8,128)(2,1)S(1)} %collective-permute-done.5.refs_2_), channel_id=1, source_target_pairs={{0,480},{1,481},{2,482},{3,483},{4,484},{5,485},{6,486},{7,487},{8... | collective-permute-start | bytes 1769480 | tf_op jit(solution)/shard_map/own_outer2/ppermute | solution.py:84
  71.0 5.6 %collective-permute-start.9 = (bf16[192,768]{1,0:T(8,128)(2,1)S(1)}, bf16[192,768]{1,0:T(8,128)(2,1)S(1)}, u32[]{:S(2)}, u32[]{:S(2)}) collective-permute-start(bf16[192,768]{1,0:T(8,128)(2,1)S(1)} %crossed.1.q0), channel_id=1, source_target_pairs={{0,3},{4,7},{8,11},{12,15},{16,19},{20,23},{24,27},{28,31},{35,32}... | collective-permute-start | bytes 884744 | tf_op jit(solution)/shard_map/gather3/ppermute | solution.py:84
  72.8 14.0 %collective-permute-start.8 = (bf16[192,768]{1,0:T(8,128)(2,1)S(1)}, bf16[192,768]{1,0:T(8,128)(2,1)S(1)}, u32[]{:S(2)}, u32[]{:S(2)}) collective-permute-start(bf16[192,768]{1,0:T(8,128)(2,1)S(1)} %crossed.1.q0), channel_id=1, source_target_pairs={{2,3},{6,7},{10,11},{14,15},{18,19},{22,23},{26,27},{30,31},{33,32... | collective-permute-start | bytes 884744 | tf_op jit(solution)/shard_map/gather2/ppermute | solution.py:84
  73.4 13.3 %collective-permute-start.7 = (bf16[192,768]{1,0:T(8,128)(2,1)S(1)}, bf16[192,768]{1,0:T(8,128)(2,1)S(1)}, u32[]{:S(2)}, u32[]{:S(2)}) collective-permute-start(bf16[192,768]{1,0:T(8,128)(2,1)S(1)} %crossed.1.q0), channel_id=1, source_target_pairs={{1,3},{5,7},{9,11},{13,15},{17,19},{21,23},{25,27},{29,31},{34,32}... | collective-permute-start | bytes 884744 | tf_op jit(solution)/shard_map/gather1/ppermute | solution.py:84
  74.1 19.2 %collective-permute-start.12 = (bf16[384,768]{1,0:T(8,128)(2,1)}, bf16[384,768]{1,0:T(8,128)(2,1)S(1)}, u32[]{:S(2)}, u32[]{:S(2)}) collective-permute-start(bf16[384,768]{1,0:T(8,128)(2,1)} %collective-permute-done.11.keys), channel_id=1, source_target_pairs={{1,0},{2,1},{3,2},{5,4},{6,5},{7,6},{9,8},{10,9},{11,10},{13,12},{... | collective-permute-start | bytes 1769480 | tf_op jit(solution)/shard_map/wide_late/ppermute | solution.py:84
  76.6 14.5 %copy-start.3 = (f32[1,6144]{1,0:T(1,128)S(1)}, f32[1,6144]{1,0:T(1,128)}, u32[]{:S(2)}) copy-start(f32[1,6144]{1,0:T(1,128)} %copy-done.2) | copy-start | bytes 73732
  76.6 14.5 %copy-start.5 = (f32[384,128]{1,0:T(8,128)S(1)}, f32[384,128]{1,0:T(8,128)}, u32[]{:S(2)}) copy-start(f32[384,128]{1,0:T(8,128)} %copy-done.4) | copy-start | bytes 589828
  76.6 14.5 %copy-start.9 = (f32[384,768]{1,0:T(8,128)S(1)}, f32[384,768]{1,0:T(8,128)}, u32[]{:S(2)}) copy-start(f32[384,768]{1,0:T(8,128)} %copy-done.8) | copy-start | bytes 3538948
  76.6 22.6 %collective-permute-start.15 = (bf16[768,768]{1,0:T(8,128)(2,1)S(1)}, bf16[768,768]{1,0:T(8,128)(2,1)S(1)}, u32[]{:S(2)}, u32[]{:S(2)}) collective-permute-start(bf16[768,768]{1,0:T(8,128)(2,1)S(1)} %pad_maximum_fusion.1), channel_id=1, source_target_pairs={{0,32},{1,33},{2,34},{3,35},{4,36},{5,37},{6,38},{7,39},{8,40},{9,... | collective-permute-start | bytes 3538952 | tf_op jit(solution)/shard_map/sibling_own1/ppermute | solution.py:84
  89.4 15.3 %collective-permute-start.10 = (bf16[768,768]{1,0:T(8,128)(2,1)}, bf16[768,768]{1,0:T(8,128)(2,1)}, u32[]{:S(2)}, u32[]{:S(2)}) collective-permute-start(bf16[768,768]{1,0:T(8,128)(2,1)} %whole_blocks.1.gathered), channel_id=1, source_target_pairs={{3,67},{7,71},{11,75},{15,79},{19,83},{23,87},{27,91},{31,95},{32,... | collective-permute-start | bytes 3538952 | tf_op jit(solution)/shard_map/edge_back/ppermute | solution.py:84
  94.4 9.0 %collective-permute-start.14 = (bf16[768,768]{1,0:T(8,128)(2,1)S(1)}, bf16[768,768]{1,0:T(8,128)(2,1)S(1)}, u32[]{:S(2)}, u32[]{:S(2)}) collective-permute-start(bf16[768,768]{1,0:T(8,128)(2,1)S(1)} %merge.1.keys), channel_id=1, source_target_pairs={{0,32},{1,33},{2,34},{3,35},{4,36},{5,37},{6,38},{7,39},{8,40},{9,... | collective-permute-start | bytes 3538952 | tf_op jit(solution)/shard_map/sibling_hop1/ppermute | solution.py:84
  96.8 2.5 %copy-start.1 = (f32[384,128]{1,0:T(8,128)S(1)}, f32[384,128]{1,0:T(8,128)}, u32[]{:S(2)}) copy-start(f32[384,128]{1,0:T(8,128)} %copy-done) | copy-start | bytes 589828
  96.8 2.5 %copy-start.7 = (f32[384,768]{1,0:T(8,128)S(1)}, f32[384,768]{1,0:T(8,128)}, u32[]{:S(2)}) copy-start(f32[384,768]{1,0:T(8,128)} %copy-done.6) | copy-start | bytes 3538948
  101.5 20.9 %collective-permute-start.17 = (bf16[384,768]{1,0:T(8,128)(2,1)S(1)}, bf16[384,768]{1,0:T(8,128)(2,1)S(1)}, u32[]{:S(2)}, u32[]{:S(2)}) collective-permute-start(bf16[384,768]{1,0:T(8,128)(2,1)S(1)} %slice_select_fusion), channel_id=1, source_target_pairs={{0,1},{1,2},{2,3},{3,483},{4,5},{5,6},{6,7},{7,487},{8,9},{9,10},{... | collective-permute-start | bytes 1769480 | tf_op jit(solution)/shard_map/farthest/ppermute | solution.py:84
  106.0 16.4 %collective-permute-start.16 = (bf16[384,768]{1,0:T(8,128)(2,1)S(1)}, bf16[384,768]{1,0:T(8,128)(2,1)S(1)}, u32[]{:S(2)}, u32[]{:S(2)}) collective-permute-start(bf16[384,768]{1,0:T(8,128)(2,1)S(1)} %slice_select_fusion.1.inner0), channel_id=1, source_target_pairs={{0,32},{1,33},{2,34},{3,35},{4,36},{5,37},{6,38},{7,39},{8,40},{9,... | collective-permute-start | bytes 1769480 | tf_op jit(solution)/shard_map/sibling_hop0/ppermute | solution.py:84

commit v13 on v12

--- a/solution.py
+++ b/solution.py
@@ -317,61 +317,37 @@
         (other, near_factor, key_factors, after(inner1, whole_blocks, far2), near_sum), 100_000_000,
     )
 
-    def merge_kernel(edge, early, late, gathered, out, sems):
+    def merge_kernel(edge, early, late, gathered, outer1, inner1, out, sems):
+        own = [(outer1, 0, out, 2 * rows, rows), (inner1, 0, out, 3 * rows, rows)]
+
         @pl.when(edge[0] == 1)
         def _():
-            copy_all(sems, [(gathered, 0, out, 0, 2 * rows)])
+            copy_all(sems, own + [(gathered, 0, out, 0, 2 * rows)])
 
         @pl.when(edge[0] == 0)
         def _():
-            copy_all(sems, [(early, 2 * rows, out, 0, rows), (late, 0, out, rows, rows)])
-
-    hop1 = assemble(
-        "merge", merge_kernel, blocks(2), (at_edge,),
-        (early, after(late, near_sum), whole_blocks), 2,
-    )
-    hop_sib1 = send("sibling_hop1", hop1, to_sibling)
-    sib1 = send(
-        "sibling_own1", jnp.concatenate([outer1, inner1], axis=0), to_sibling
-    )
+            copy_all(sems, own + [(early, 2 * rows, out, 0, rows), (late, 0, out, rows, rows)])
+
+    carried = assemble(
+        "merge", merge_kernel, blocks(4), (at_edge,),
+        (early, after(late, near_sum), whole_blocks, outer1, inner1), 4,
+    )
+    sib = send("sibling1", carried, to_sibling)
     is_edge = mirrored == 0
 
     def near1_kernel(s, oth, nf, kf, keys, near_in, near):
         near[...] = add_terms(
-            near_in[...], oth[...], nf[:, :1], kf, s[0], [(keys[...], 4, False)]
+            near_in[...], oth[...], nf[:, :1], kf, s[0], [(keys[: 2 * rows, :], 4, False)]
         )
 
     near_sum = call(
         "terms_near1", near1_kernel, total, (scale,),
-        (other, near_factor, key_factors, hop1, near_sum),
-    )
-    hop_sib1 = send("sibling_hop1", hop1, to_sibling)
-
-    def far1_kernel(s, out, ff, kf, own, farthest, far_in, far):
-        far[...] = add_terms(
-            far_in[...], out[...], ff[:, :1], kf, s[0],
-            [(own[...], 9, False), (farthest[...], 11, False)],
-        )
-
-    far_sum = call(
-        "terms_far1", far1_kernel, total, (scale,),
-        (outer, far_factor, key_factors, after(sib1, near_sum), far2, far_sum), 50_000_000,
-    )
-
+        (other, near_factor, key_factors, carried, near_sum), 50_000_000,
+    )
     hop_far2 = send(
-        "farthest", jnp.where(is_edge, hop1[:rows], after(far2, far_sum)), farthest_route
-    )
-
-    def far2_kernel(s, out, ff, kf, hop, far_in, far):
-        far[...] = add_terms(
-            far_in[...], out[...], ff[:, :1], kf, s[0], [(hop[...], 12, False)]
-        )
-
-    far_sum = call(
-        "terms_far2", far2_kernel, total, (scale,),
-        (outer, far_factor, key_factors, hop_sib1, far_sum),
-    )
-    back = after(back, far_sum)
+        "farthest", jnp.where(is_edge, whole_blocks[:rows], after(far2, near_sum)), farthest_route
+    )
+    back = after(back, near_sum)
     hop_inner0 = jnp.where(is_edge, back[rows:], early[:rows])
     hop_sib0 = send("sibling_hop0", hop_inner0, to_sibling)
     anywhere = pl.BlockSpec(memory_space=pl.ANY)
@@ -413,6 +389,19 @@
             other, near_factor, key_factors, hop_inner0, back, early, near_sum,
         )
 
+    def far1_kernel(s, out, ff, kf, keys, farthest, far_in, far):
+        far[...] = add_terms(
+            far_in[...], out[...], ff[:, :1], kf, s[0],
+            [(keys[: 2 * rows, :], 12, False), (keys[2 * rows :, :], 9, False),
+             (farthest[...], 11, False)],
+        )
+
+    far_sum = call(
+        "terms_far1", far1_kernel, total, (scale,),
+        (outer, far_factor, key_factors, after(sib, *half_done), far2, far_sum),
+        100_000_000,
+    )
+
     def last_kernel(
         c, s, out, ff, kf, hs0, hf2, far_in, _i, _c, image_grad, caption_grad, held_sum, sem
     ):

time: 126 us -> 129 us (1.024)
  starting transfers between devices: 74.8 us -> 64.6 us
  waiting for transfers between devices: 17.6 us -> 24.8 us
  Pallas kernels: 23 us -> 28.4 us
  other arithmetic: 7.21 us -> 8.81 us
    ppermute x18 -> x17, starting transfers between devices: 74.8 us -> 64.6 us  [send(): return lax.ppermute(x, AXES, pairs(target))]
    ppermute x18 -> x17, waiting for transfers between devices: 17.6 us -> 24.8 us  [send(): return lax.ppermute(x, AXES, pairs(target))]
    pallas_call x8 -> x7, Pallas kernels: 12.7 us -> 14.8 us  [call(): pl.pallas_call(kernel, out_shape=out_shape, in_specs=[scalars() for _ in...]
    select_n x1, other arithmetic: 0.08 us -> 1.97 us  [on_device(): jnp.where(is_edge, whole_blocks[:rows], after(far2, near_sum))]
    pallas_call x2, Pallas kernels: 3.71 us -> 5.45 us  [assemble(): pl.pallas_call(kernel, out_shape=out_shape, in_specs=[scalars() for _ in...]
  transfers between devices with their start and end apart: 18 -> 17, of which waited for: 2 -> 5; matrix products, arithmetic and copies ran while one was open for 4% -> 5% of each run, Pallas kernels for 17% -> 19%
where the time goes in v13:
time: 129 us
  starting transfers between devices  64.6 us (50%)
  Pallas kernels  28.4 us (22%)
  waiting for transfers between devices  24.8 us (19%)
  other arithmetic  8.81 us (7%)
  between operations  1.98 us (2%)
    ppermute x17, starting transfers between devices, send(): return lax.ppermute(x, AXES, pairs(target))  64.6 us
    ppermute x17, waiting for transfers between devices, send(): return lax.ppermute(x, AXES, pairs(target))  24.8 us
    pallas_call x7, Pallas kernels, call(): pl.pallas_call(kernel, out_shape=out_shape, in_specs=[scalars() for _ in...  14.8 us
    pallas_call x2, Pallas kernels, assemble(): pl.pallas_call(kernel, out_shape=out_shape, in_specs=[scalars() for _ in...  5.45 us
    pallas_call x1, Pallas kernels, on_device(): pl.pallas_call(near0_kernel, out_shape=[total, total], in_specs=[scalars(...  4.58 us
    pallas_call x1, Pallas kernels, on_device(): pl.pallas_call(last_kernel, out_shape=[total, total], in_specs=[scalars()...  3.54 us
  transfers between devices with their start and end apart: 17, of which 5 were waited for; matrix products, arithmetic and copies ran while one was open for 5% of the time, Pallas kernels for 19%

profile of v13, /device:TPU:25, one launch (start us, length us, event | category | flops | bytes accessed | tf_op | source)
XLA Modules:
  0.0 128.7 jit_solution(4678013708413939351)
XLA Ops:
  0.6 2.1 %broadcast_select_fusion = (bf16[384,768]{1,0:T(8,128)(2,1)}, bf16[384,768]{1,0:T(8,128)(2,1)S(1)}) fusion(bf16[384,768]{1,0:T(8,128)(2,1)} %param.5, bf16[384,768]{1,0:T(8,128)(2,1)} %param.6, pred[]{:T(512)S(6)} %eq.60), kind=kLoop, calls=%fused_computation.3 | loop fusion | flops 589824 | bytes 2359297 | tf_op jit(solution)/shard_map/jit(_where)/select_n | solution.py:186
  2.8 2.6 %collective-permute-start = (bf16[384,768]{1,0:T(8,128)(2,1)}, bf16[384,768]{1,0:T(8,128)(2,1)S(1)}, u32[]{:S(2)}, u32[]{:S(2)}) collective-permute-start(bf16[384,768]{1,0:T(8,128)(2,1)} %get-tuple-element.96.oth.refs_3_), channel_id=1, source_target_pairs={{0,32},{1,33},{2,34},{3,35},{4,36},{5,37},{6,38},{7,39},{8,40},{9,... | collective-permute-start | bytes 1769480 | tf_op jit(solution)/shard_map/swap/ppermute | solution.py:84
  5.4 3.5 %collective-permute-start.5 = (bf16[384,768]{1,0:T(8,128)(2,1)S(1)}, bf16[384,768]{1,0:T(8,128)(2,1)S(1)}, u32[]{:S(2)}, u32[]{:S(2)}) collective-permute-start(bf16[384,768]{1,0:T(8,128)(2,1)S(1)} %get-tuple-element.97.outer.out.refs_0_), channel_id=1, source_target_pairs={{0,448},{1,449},{2,450},{3,451},{4,452},{5,453},{6,454},{7,455},{8... | collective-permute-start | bytes 1769480 | tf_op jit(solution)/shard_map/own_outer1/ppermute | solution.py:84
  8.9 0.0 collective-permute-done.inner.refs_1_
  8.9 0.1 cut.1
  9.0 5.6 %collective-permute-start.1 = (bf16[192,768]{1,0:T(8,128)(2,1)S(1)}, bf16[192,768]{1,0:T(8,128)(2,1)S(1)}, u32[]{:S(2)}, u32[]{:S(2)}) collective-permute-start(bf16[192,768]{1,0:T(8,128)(2,1)S(1)} %get-tuple-element.41), channel_id=1, source_target_pairs={{0,3},{4,7},{8,11},{12,15},{16,19},{20,23},{24,27},{28,31},{35,32}... | collective-permute-start | bytes 884744 | tf_op jit(solution)/shard_map/spread0/ppermute | solution.py:84
  14.6 2.0 %collective-permute-start.2 = (bf16[192,768]{1,0:T(8,128)(2,1)S(1)}, bf16[192,768]{1,0:T(8,128)(2,1)}, u32[]{:S(2)}, u32[]{:S(2)}) collective-permute-start(bf16[192,768]{1,0:T(8,128)(2,1)S(1)} %get-tuple-element.42), channel_id=1, source_target_pairs={{0,1},{4,5},{8,9},{12,13},{16,17},{20,21},{24,25},{28,29},{35,34},... | collective-permute-start | bytes 884744 | tf_op jit(solution)/shard_map/spread1/ppermute | solution.py:84
  16.6 2.0 %collective-permute-start.3 = (bf16[192,768]{1,0:T(8,128)(2,1)S(1)}, bf16[192,768]{1,0:T(8,128)(2,1)}, u32[]{:S(2)}, u32[]{:S(2)}) collective-permute-start(bf16[192,768]{1,0:T(8,128)(2,1)S(1)} %get-tuple-element.43), channel_id=1, source_target_pairs={{0,2},{4,6},{8,10},{12,14},{16,18},{20,22},{24,26},{28,30},{35,33}... | collective-permute-start | bytes 884744 | tf_op jit(solution)/shard_map/spread2/ppermute | solution.py:84
  18.6 5.8 %collective-permute-start.11 = (bf16[384,768]{1,0:T(8,128)(2,1)}, bf16[384,768]{1,0:T(8,128)(2,1)}, u32[]{:S(2)}, u32[]{:S(2)}) collective-permute-start(bf16[384,768]{1,0:T(8,128)(2,1)} %get-tuple-element.96.oth.refs_3_), channel_id=1, source_target_pairs={{0,96},{1,97},{2,98},{3,99},{4,100},{5,101},{6,102},{7,103},{8,104... | collective-permute-start | bytes 1769480 | tf_op jit(solution)/shard_map/own_inner1/ppermute | solution.py:84
  25.4 1.1 dynamic-slice_select_fusion
  26.5 0.0 collective-permute-done.1
  26.5 0.0 collective-permute-done.2
  26.5 0.0 collective-permute-done.3
  26.6 0.1 select_select_fusion
  26.6 8.3 %collective-permute-start.4 = (bf16[192,768]{1,0:T(8,128)(2,1)S(1)}, bf16[192,768]{1,0:T(8,128)(2,1)S(1)}, u32[]{:S(2)}, u32[]{:S(2)}) collective-permute-start(bf16[192,768]{1,0:T(8,128)(2,1)S(1)} %select_select_fusion), channel_id=1, source_target_pairs={{0,476},{1,477},{2,478},{3,479},{4,448},{5,449},{6,450},{7,451},{8... | collective-permute-start | bytes 884744 | tf_op jit(solution)/shard_map/cross/ppermute | solution.py:84
  34.9 0.0 collective-permute-done.5.refs_2_.outer1
  34.9 1.4 %pad_maximum_fusion = bf16[1152,768]{1,0:T(8,128)(2,1)} fusion(bf16[384,768]{1,0:T(8,128)(2,1)S(1)} %collective-permute-done.5.refs_2_.outer1, bf16[384,768]{1,0:T(8,128)(2,1)S(1)} %get-tuple-element.97.outer.out.refs_0_, bf16[384,768]{1,0:T(8,128)(2,1)S(1)} %collective-permute-done.inner.refs_1_), kind=kLoop, calls=%fused_computation | loop fusion | flops 5308416 | bytes 3538944 | tf_op jit(solution)/shard_map/concatenate | solution.py:207
  36.3 1.3 collective-permute-start.6
  37.6 0.2 factors.1
  37.7 0.0 copy-start.2
  37.8 4.3 %terms_own0.1 = (f32[384,768]{1,0:T(8,128)S(1)}, f32[384,768]{1,0:T(8,128)S(1)}) custom-call(f32[1]{0:T(128)} %bitcast.3.s, bf16[384,768]{1,0:T(8,128)(2,1)} %get-tuple-element.96.oth.refs_3_, bf16[384,768]{1,0:T(8,128)(2,1)S(1)} %get-tuple-element.97.outer.out.refs_0_, f32[384,128]{1,0:T(8,128)S(1)} %get-tuple-element.63.nf, ...), custom_call_target="tpu_custom_call" | custom-call | flops 99999997952 | bytes 1000 | tf_op jit(solution)/shard_map/terms_own0/pallas_call | solution.py:99
  42.1 0.0 copy-done.2
  42.1 0.0 copy-start.4
  42.1 0.0 copy-start.6
  42.1 2.7 %collective-permute-done.4.block = bf16[192,768]{1,0:T(8,128)(2,1)S(1)} collective-permute-done((bf16[192,768]{1,0:T(8,128)(2,1)S(1)}, bf16[192,768]{1,0:T(8,128)(2,1)S(1)}, u32[]{:S(2)}, u32[]{:S(2)}) %collective-permute-start.4) | collective-permute-done | bytes 294944 | tf_op jit(solution)/shard_map/cross/ppermute | solution.py:84
  44.8 0.0 copy-done.4
  44.8 0.0 copy-done.6
  44.8 15.0 %collective-permute-done.6.early = bf16[1152,768]{1,0:T(8,128)(2,1)} collective-permute-done((bf16[1152,768]{1,0:T(8,128)(2,1)}, bf16[1152,768]{1,0:T(8,128)(2,1)}, u32[]{:S(2)}, u32[]{:S(2)}) %collective-permute-start.6) | collective-permute-done | bytes 1769504 | tf_op jit(solution)/shard_map/wide_early/ppermute | solution.py:84
  59.8 11.2 %collective-permute-start.13 = (bf16[384,768]{1,0:T(8,128)(2,1)S(1)}, bf16[384,768]{1,0:T(8,128)(2,1)S(1)}, u32[]{:S(2)}, u32[]{:S(2)}) collective-permute-start(bf16[384,768]{1,0:T(8,128)(2,1)S(1)} %collective-permute-done.5.refs_2_.outer1), channel_id=1, source_target_pairs={{0,480},{1,481},{2,482},{3,483},{4,484},{5,485},{6,486},{7,487},{8... | collective-permute-start | bytes 1769480 | tf_op jit(solution)/shard_map/own_outer2/ppermute | solution.py:84
  71.0 1.7 %collective-permute-start.9 = (bf16[192,768]{1,0:T(8,128)(2,1)S(1)}, bf16[192,768]{1,0:T(8,128)(2,1)S(1)}, u32[]{:S(2)}, u32[]{:S(2)}) collective-permute-start(bf16[192,768]{1,0:T(8,128)(2,1)S(1)} %crossed.1.q0), channel_id=1, source_target_pairs={{0,3},{4,7},{8,11},{12,15},{16,19},{20,23},{24,27},{28,31},{35,32}... | collective-permute-start | bytes 884744 | tf_op jit(solution)/shard_map/gather3/ppermute | solution.py:84
  72.8 0.7 collective-permute-start.8
  73.5 0.7 collective-permute-start.7
  74.2 0.0 copy-start.7
  74.2 0.0 collective-permute-done.11.keys.inner1
  74.2 1.4 %collective-permute-start.12 = (bf16[384,768]{1,0:T(8,128)(2,1)}, bf16[384,768]{1,0:T(8,128)(2,1)S(1)}, u32[]{:S(2)}, u32[]{:S(2)}) collective-permute-start(bf16[384,768]{1,0:T(8,128)(2,1)} %collective-permute-done.11.keys.inner1), channel_id=1, source_target_pairs={{1,0},{2,1},{3,2},{5,4},{6,5},{7,6},{9,8},{10,9},{11,10},{13,12},{... | collective-permute-start | bytes 1769480 | tf_op jit(solution)/shard_map/wide_late/ppermute | solution.py:84
  75.6 0.8 collective-permute-done.9.q3
  76.4 0.0 collective-permute-done.8.q2
  76.4 0.0 collective-permute-done.7.q1
  76.4 2.6 %whole_blocks.1.gathered = bf16[768,768]{1,0:T(8,128)(2,1)} custom-call(bf16[192,768]{1,0:T(8,128)(2,1)S(1)} %crossed.1.q0, bf16[192,768]{1,0:T(8,128)(2,1)S(1)} %collective-permute-done.7.q1, bf16[192,768]{1,0:T(8,128)(2,1)S(1)} %collective-permute-done.8.q2, bf16[192,768]{1,0:T(8,128)(2,1)S(1)} %collective-permute-done.9.q3), custom_call_target="tpu_custom_call" | custom-call | flops 1000 | bytes 1000 | tf_op jit(solution)/shard_map/whole_blocks/pallas_call | solution.py:114
  79.0 1.8 %collective-permute-start.10 = (bf16[768,768]{1,0:T(8,128)(2,1)}, bf16[768,768]{1,0:T(8,128)(2,1)}, u32[]{:S(2)}, u32[]{:S(2)}) collective-permute-start(bf16[768,768]{1,0:T(8,128)(2,1)} %whole_blocks.1.gathered), channel_id=1, source_target_pairs={{3,67},{7,71},{11,75},{15,79},{19,83},{23,87},{27,91},{31,95},{32,... | collective-permute-start | bytes 3538952 | tf_op jit(solution)/shard_map/edge_back/ppermute | solution.py:84
  80.8 4.0 %collective-permute-done.13.farthest = bf16[384,768]{1,0:T(8,128)(2,1)S(1)} collective-permute-done((bf16[384,768]{1,0:T(8,128)(2,1)S(1)}, bf16[384,768]{1,0:T(8,128)(2,1)S(1)}, u32[]{:S(2)}, u32[]{:S(2)}) %collective-permute-start.13) | collective-permute-done | bytes 589856 | tf_op jit(solution)/shard_map/own_outer2/ppermute | solution.py:84
  84.8 0.0 copy-done.7
  84.8 2.4 %terms_own1.1.near_in = f32[384,768]{1,0:T(8,128)S(1)} custom-call(f32[1]{0:T(128)} %bitcast.4.s, bf16[384,768]{1,0:T(8,128)(2,1)} %get-tuple-element.96.oth.refs_3_, f32[384,128]{1,0:T(8,128)S(1)} %get-tuple-element.63.nf, f32[1,6144]{1,0:T(1,128)S(1)} %get-tuple-element.62.kf, bf16[384,768]{1,0:T(8,128)(2,1)} %collective-permute-done.11.keys.inner1, ...), custom_call_target="tpu_custom_call" | custom-call | flops 99999997952 | bytes 1000 | tf_op jit(solution)/shard_map/terms_own1/pallas_call | solution.py:99
  87.2 0.0 copy-done
  87.2 2.3 %collective-permute-done.12.late = bf16[384,768]{1,0:T(8,128)(2,1)S(1)} collective-permute-done((bf16[384,768]{1,0:T(8,128)(2,1)}, bf16[384,768]{1,0:T(8,128)(2,1)S(1)}, u32[]{:S(2)}, u32[]{:S(2)}) %collective-permute-start.12) | collective-permute-done | bytes 589856 | tf_op jit(solution)/shard_map/wide_late/ppermute | solution.py:84
  89.5 2.8 %merge.1.keys = bf16[1536,768]{1,0:T(8,128)(2,1)} custom-call(s32[1]{0:T(128)} %bitcast.2.edge.e, bf16[1152,768]{1,0:T(8,128)(2,1)} %collective-permute-done.6.early, bf16[384,768]{1,0:T(8,128)(2,1)S(1)} %collective-permute-done.12.late, bf16[768,768]{1,0:T(8,128)(2,1)} %whole_blocks.1.gathered, bf16[384,768]{1,0:T(8,128)(2,1)S(1)} %collective-permute-done.5.refs_2_.outer1, ...), custom_call_target="tpu_custom_call" | custom-call | flops 1000 | bytes 1000 | tf_op jit(solution)/shard_map/merge/pallas_call | solution.py:114
  92.4 4.2 %collective-permute-start.16 = (bf16[1536,768]{1,0:T(8,128)(2,1)}, bf16[1536,768]{1,0:T(8,128)(2,1)}, u32[]{:S(2)}, u32[]{:S(2)}) collective-permute-start(bf16[1536,768]{1,0:T(8,128)(2,1)} %merge.1.keys), channel_id=1, source_target_pairs={{0,32},{1,33},{2,34},{3,35},{4,36},{5,37},{6,38},{7,39},{8,40},{9,... | collective-permute-start | bytes 7077896 | tf_op jit(solution)/shard_map/sibling1/ppermute | solution.py:84
  96.5 0.0 copy-start.1
  96.6 3.2 %terms_near1.1.near_in = f32[384,768]{1,0:T(8,128)S(1)} custom-call(f32[1]{0:T(128)} %bitcast.5.s, bf16[384,768]{1,0:T(8,128)(2,1)} %get-tuple-element.96.oth.refs_3_, f32[384,128]{1,0:T(8,128)S(1)} %get-tuple-element.63.nf, f32[1,6144]{1,0:T(1,128)S(1)} %get-tuple-element.62.kf, bf16[1536,768]{1,0:T(8,128)(2,1)} %merge.1.keys, f32[384,768]{1,0:T(8,128)S(1)} %terms_own1.1.near_in), custom_call_target="tpu_custom_call" | custom-call | flops 49999998976 | bytes 1000 | tf_op jit(solution)/shard_map/terms_near1/pallas_call | solution.py:99
  99.7 0.0 copy-done.1
  99.7 2.0 %slice_select_fusion = bf16[384,768]{1,0:T(8,128)(2,1)} fusion(bf16[384,768]{1,0:T(8,128)(2,1)S(1)} %copy-done.1, bf16[768,768]{1,0:T(8,128)(2,1)} %whole_blocks.1.gathered, pred[]{:T(512)S(6)} %eq.62), kind=kLoop, calls=%fused_computation.1 | loop fusion | flops 294912 | bytes 1769473 | tf_op jit(solution)/shard_map/jit(_where)/select_n | solution.py:348
  101.7 1.9 %collective-permute-start.15 = (bf16[384,768]{1,0:T(8,128)(2,1)}, bf16[384,768]{1,0:T(8,128)(2,1)}, u32[]{:S(2)}, u32[]{:S(2)}) collective-permute-start(bf16[384,768]{1,0:T(8,128)(2,1)} %slice_select_fusion), channel_id=1, source_target_pairs={{0,1},{1,2},{2,3},{3,483},{4,5},{5,6},{6,7},{7,487},{8,9},{9,10},{... | collective-permute-start | bytes 1769480 | tf_op jit(solution)/shard_map/farthest/ppermute | solution.py:84
  103.6 0.0 collective-permute-done.10.back
  103.6 2.1 %slice_select_fusion.1.inner0 = bf16[384,768]{1,0:T(8,128)(2,1)} fusion(bf16[1152,768]{1,0:T(8,128)(2,1)} %collective-permute-done.6.early, bf16[768,768]{1,0:T(8,128)(2,1)} %collective-permute-done.10.back, pred[]{:T(512)S(6)} %eq.62), kind=kLoop, calls=%fused_computation.2 | loop fusion | flops 294912 | bytes 1769473 | tf_op jit(solution)/shard_map/jit(_where)/select_n | solution.py:351
  105.8 10.0 %collective-permute-start.14 = (bf16[384,768]{1,0:T(8,128)(2,1)}, bf16[384,768]{1,0:T(8,128)(2,1)}, u32[]{:S(2)}, u32[]{:S(2)}) collective-permute-start(bf16[384,768]{1,0:T(8,128)(2,1)} %slice_select_fusion.1.inner0), channel_id=1, source_target_pairs={{0,32},{1,33},{2,34},{3,35},{4,36},{5,37},{6,38},{7,39},{8,40},{9,... | collective-permute-start | bytes 1769480 | tf_op jit(solution)/shard_map/sibling_hop0/ppermute | solution.py:84
  115.8 0.0 copy-start.3
  115.8 0.0 copy-start.5
  115.8 4.6 %terms_near0.1 = (f32[384,768]{1,0:T(8,128)}, f32[384,768]{1,0:T(8,128)}) custom-call(s32[1]{0:T(128)} %bitcast.c, s32[1]{0:T(128)} %bitcast.2.edge.e, f32[1]{0:T(128)} %bitcast.6.s, bf16[384,768]{1,0:T(8,128)(2,1)} %get-tuple-element.96.oth.refs_3_, f32[384,128]{1,0:T(8,128)S(1)} %get-tuple-element.63.nf, f32[1,6144]{1,0:T(1,128)S(1)} %get-tuple-element.62.kf, ...), custom_call_target="tpu_custom_call" | custom-call | flops 99999997952 | bytes 1000 | tf_op jit(solution)/shard_map/terms_near0/pallas_call | solution.py:377
  120.4 0.0 collective-permute-done.16.keys
  120.4 0.0 copy-done.3
  120.4 4.6 %terms_far1.1.far_in = f32[384,768]{1,0:T(8,128)S(1)} custom-call(f32[1]{0:T(128)} %bitcast.7.s, bf16[384,768]{1,0:T(8,128)(2,1)S(1)} %get-tuple-element.97.outer.out.refs_0_, f32[384,128]{1,0:T(8,128)S(1)} %copy-done.3, f32[1,6144]{1,0:T(1,128)S(1)} %get-tuple-element.62.kf, bf16[1536,768]{1,0:T(8,128)(2,1)} %collective-permute-done.16.keys, ...), custom_call_target="tpu_custom_call" | custom-call | flops 99999997952 | bytes 1000 | tf_op jit(solution)/shard_map/terms_far1/pallas_call | solution.py:99
  125.1 0.0 collective-permute-done.15.hf2
  125.1 0.0 collective-permute-done.14.hs0
  125.1 3.5 %terms_last.1 = (f32[384,768]{1,0:T(8,128)}, f32[384,768]{1,0:T(8,128)}) custom-call(s32[1]{0:T(128)} %bitcast.c, f32[1]{0:T(128)} %bitcast.8.s, bf16[384,768]{1,0:T(8,128)(2,1)S(1)} %get-tuple-element.97.outer.out.refs_0_, f32[384,128]{1,0:T(8,128)S(1)} %copy-done.3, ...), custom_call_target="tpu_custom_call", output_to_operand_aliasing={{0}: (8, {}), {1}: (9, {})} | custom-call | flops 1000 | bytes 1000 | tf_op jit(solution)/shard_map/terms_last/pallas_call | solution.py:426
  (3 shorter events, 0.0 us)
Async XLA Ops:
  2.8 6.1 %collective-permute-start = (bf16[384,768]{1,0:T(8,128)(2,1)}, bf16[384,768]{1,0:T(8,128)(2,1)S(1)}, u32[]{:S(2)}, u32[]{:S(2)}) collective-permute-start(bf16[384,768]{1,0:T(8,128)(2,1)} %get-tuple-element.96.oth.refs_3_), channel_id=1, source_target_pairs={{0,32},{1,33},{2,34},{3,35},{4,36},{5,37},{6,38},{7,39},{8,40},{9,... | collective-permute-start | bytes 1769480 | tf_op jit(solution)/shard_map/swap/ppermute | solution.py:84
  5.4 29.5 %collective-permute-start.5 = (bf16[384,768]{1,0:T(8,128)(2,1)S(1)}, bf16[384,768]{1,0:T(8,128)(2,1)S(1)}, u32[]{:S(2)}, u32[]{:S(2)}) collective-permute-start(bf16[384,768]{1,0:T(8,128)(2,1)S(1)} %get-tuple-element.97.outer.out.refs_0_), channel_id=1, source_target_pairs={{0,448},{1,449},{2,450},{3,451},{4,452},{5,453},{6,454},{7,455},{8... | collective-permute-start | bytes 1769480 | tf_op jit(solution)/shard_map/own_outer1/ppermute | solution.py:84
  9.0 17.5 %collective-permute-start.1 = (bf16[192,768]{1,0:T(8,128)(2,1)S(1)}, bf16[192,768]{1,0:T(8,128)(2,1)S(1)}, u32[]{:S(2)}, u32[]{:S(2)}) collective-permute-start(bf16[192,768]{1,0:T(8,128)(2,1)S(1)} %get-tuple-element.41), channel_id=1, source_target_pairs={{0,3},{4,7},{8,11},{12,15},{16,19},{20,23},{24,27},{28,31},{35,32}... | collective-permute-start | bytes 884744 | tf_op jit(solution)/shard_map/spread0/ppermute | solution.py:84
  14.6 11.9 %collective-permute-start.2 = (bf16[192,768]{1,0:T(8,128)(2,1)S(1)}, bf16[192,768]{1,0:T(8,128)(2,1)}, u32[]{:S(2)}, u32[]{:S(2)}) collective-permute-start(bf16[192,768]{1,0:T(8,128)(2,1)S(1)} %get-tuple-element.42), channel_id=1, source_target_pairs={{0,1},{4,5},{8,9},{12,13},{16,17},{20,21},{24,25},{28,29},{35,34},... | collective-permute-start | bytes 884744 | tf_op jit(solution)/shard_map/spread1/ppermute | solution.py:84
  16.6 9.9 %collective-permute-start.3 = (bf16[192,768]{1,0:T(8,128)(2,1)S(1)}, bf16[192,768]{1,0:T(8,128)(2,1)}, u32[]{:S(2)}, u32[]{:S(2)}) collective-permute-start(bf16[192,768]{1,0:T(8,128)(2,1)S(1)} %get-tuple-element.43), channel_id=1, source_target_pairs={{0,2},{4,6},{8,10},{12,14},{16,18},{20,22},{24,26},{28,30},{35,33}... | collective-permute-start | bytes 884744 | tf_op jit(solution)/shard_map/spread2/ppermute | solution.py:84
  18.6 55.5 %collective-permute-start.11 = (bf16[384,768]{1,0:T(8,128)(2,1)}, bf16[384,768]{1,0:T(8,128)(2,1)}, u32[]{:S(2)}, u32[]{:S(2)}) collective-permute-start(bf16[384,768]{1,0:T(8,128)(2,1)} %get-tuple-element.96.oth.refs_3_), channel_id=1, source_target_pairs={{0,96},{1,97},{2,98},{3,99},{4,100},{5,101},{6,102},{7,103},{8,104... | collective-permute-start | bytes 1769480 | tf_op jit(solution)/shard_map/own_inner1/ppermute | solution.py:84
  26.6 18.1 %collective-permute-start.4 = (bf16[192,768]{1,0:T(8,128)(2,1)S(1)}, bf16[192,768]{1,0:T(8,128)(2,1)S(1)}, u32[]{:S(2)}, u32[]{:S(2)}) collective-permute-start(bf16[192,768]{1,0:T(8,128)(2,1)S(1)} %select_select_fusion), channel_id=1, source_target_pairs={{0,476},{1,477},{2,478},{3,479},{4,448},{5,449},{6,450},{7,451},{8... | collective-permute-start | bytes 884744 | tf_op jit(solution)/shard_map/cross/ppermute | solution.py:84
  36.3 23.6 %collective-permute-start.6 = (bf16[1152,768]{1,0:T(8,128)(2,1)}, bf16[1152,768]{1,0:T(8,128)(2,1)}, u32[]{:S(2)}, u32[]{:S(2)}) collective-permute-start(bf16[1152,768]{1,0:T(8,128)(2,1)} %pad_maximum_fusion), channel_id=1, source_target_pairs={{1,0},{2,1},{3,2},{5,4},{6,5},{7,6},{9,8},{10,9},{11,10},{13,12},{... | collective-permute-start | bytes 5308424 | tf_op jit(solution)/shard_map/wide_early/ppermute | solution.py:84
  37.7 4.4 %copy-start.2 = (f32[384,128]{1,0:T(8,128)}, f32[384,128]{1,0:T(8,128)S(1)}, u32[]{:S(2)}) copy-start(f32[384,128]{1,0:T(8,128)S(1)} %get-tuple-element.61.ff) | copy-start | bytes 589828
  42.1 2.7 %copy-start.4 = (f32[384,768]{1,0:T(8,128)}, f32[384,768]{1,0:T(8,128)S(1)}, u32[]{:S(2)}) copy-start(f32[384,768]{1,0:T(8,128)S(1)} %get-tuple-element.66.far_in) | copy-start | bytes 3538948
  42.1 2.7 %copy-start.6 = (f32[384,768]{1,0:T(8,128)}, f32[384,768]{1,0:T(8,128)S(1)}, u32[]{:S(2)}) copy-start(f32[384,768]{1,0:T(8,128)S(1)} %get-tuple-element.65.near_in) | copy-start | bytes 3538948
  59.8 25.0 %collective-permute-start.13 = (bf16[384,768]{1,0:T(8,128)(2,1)S(1)}, bf16[384,768]{1,0:T(8,128)(2,1)S(1)}, u32[]{:S(2)}, u32[]{:S(2)}) collective-permute-start(bf16[384,768]{1,0:T(8,128)(2,1)S(1)} %collective-permute-done.5.refs_2_.outer1), channel_id=1, source_target_pairs={{0,480},{1,481},{2,482},{3,483},{4,484},{5,485},{6,486},{7,487},{8... | collective-permute-start | bytes 1769480 | tf_op jit(solution)/shard_map/own_outer2/ppermute | solution.py:84
  71.0 5.4 %collective-permute-start.9 = (bf16[192,768]{1,0:T(8,128)(2,1)S(1)}, bf16[192,768]{1,0:T(8,128)(2,1)S(1)}, u32[]{:S(2)}, u32[]{:S(2)}) collective-permute-start(bf16[192,768]{1,0:T(8,128)(2,1)S(1)} %crossed.1.q0), channel_id=1, source_target_pairs={{0,3},{4,7},{8,11},{12,15},{16,19},{20,23},{24,27},{28,31},{35,32}... | collective-permute-start | bytes 884744 | tf_op jit(solution)/shard_map/gather3/ppermute | solution.py:84
  72.8 3.6 %collective-permute-start.8 = (bf16[192,768]{1,0:T(8,128)(2,1)S(1)}, bf16[192,768]{1,0:T(8,128)(2,1)S(1)}, u32[]{:S(2)}, u32[]{:S(2)}) collective-permute-start(bf16[192,768]{1,0:T(8,128)(2,1)S(1)} %crossed.1.q0), channel_id=1, source_target_pairs={{2,3},{6,7},{10,11},{14,15},{18,19},{22,23},{26,27},{30,31},{33,32... | collective-permute-start | bytes 884744 | tf_op jit(solution)/shard_map/gather2/ppermute | solution.py:84
  73.5 3.0 %collective-permute-start.7 = (bf16[192,768]{1,0:T(8,128)(2,1)S(1)}, bf16[192,768]{1,0:T(8,128)(2,1)S(1)}, u32[]{:S(2)}, u32[]{:S(2)}) collective-permute-start(bf16[192,768]{1,0:T(8,128)(2,1)S(1)} %crossed.1.q0), channel_id=1, source_target_pairs={{1,3},{5,7},{9,11},{13,15},{17,19},{21,23},{25,27},{29,31},{34,32}... | collective-permute-start | bytes 884744 | tf_op jit(solution)/shard_map/gather1/ppermute | solution.py:84
  74.2 10.7 %copy-start.7 = (f32[384,768]{1,0:T(8,128)S(1)}, f32[384,768]{1,0:T(8,128)}, u32[]{:S(2)}) copy-start(f32[384,768]{1,0:T(8,128)} %copy-done.6) | copy-start | bytes 3538948
  74.2 15.3 %collective-permute-start.12 = (bf16[384,768]{1,0:T(8,128)(2,1)}, bf16[384,768]{1,0:T(8,128)(2,1)S(1)}, u32[]{:S(2)}, u32[]{:S(2)}) collective-permute-start(bf16[384,768]{1,0:T(8,128)(2,1)} %collective-permute-done.11.keys.inner1), channel_id=1, source_target_pairs={{1,0},{2,1},{3,2},{5,4},{6,5},{7,6},{9,8},{10,9},{11,10},{13,12},{... | collective-permute-start | bytes 1769480 | tf_op jit(solution)/shard_map/wide_late/ppermute | solution.py:84
  79.0 24.6 %collective-permute-start.10 = (bf16[768,768]{1,0:T(8,128)(2,1)}, bf16[768,768]{1,0:T(8,128)(2,1)}, u32[]{:S(2)}, u32[]{:S(2)}) collective-permute-start(bf16[768,768]{1,0:T(8,128)(2,1)} %whole_blocks.1.gathered), channel_id=1, source_target_pairs={{3,67},{7,71},{11,75},{15,79},{19,83},{23,87},{27,91},{31,95},{32,... | collective-permute-start | bytes 3538952 | tf_op jit(solution)/shard_map/edge_back/ppermute | solution.py:84
  84.8 2.4 %copy-start = (bf16[384,768]{1,0:T(8,128)(2,1)}, bf16[384,768]{1,0:T(8,128)(2,1)S(1)}, u32[]{:S(2)}) copy-start(bf16[384,768]{1,0:T(8,128)(2,1)S(1)} %collective-permute-done.13.farthest) | copy-start | bytes 1769476
  92.4 28.0 %collective-permute-start.16 = (bf16[1536,768]{1,0:T(8,128)(2,1)}, bf16[1536,768]{1,0:T(8,128)(2,1)}, u32[]{:S(2)}, u32[]{:S(2)}) collective-permute-start(bf16[1536,768]{1,0:T(8,128)(2,1)} %merge.1.keys), channel_id=1, source_target_pairs={{0,32},{1,33},{2,34},{3,35},{4,36},{5,37},{6,38},{7,39},{8,40},{9,... | collective-permute-start | bytes 7077896 | tf_op jit(solution)/shard_map/sibling1/ppermute | solution.py:84
  96.5 3.2 %copy-start.1 = (bf16[384,768]{1,0:T(8,128)(2,1)S(1)}, bf16[384,768]{1,0:T(8,128)(2,1)}, u32[]{:S(2)}) copy-start(bf16[384,768]{1,0:T(8,128)(2,1)} %copy-done) | copy-start | bytes 1769476
  101.7 23.4 %collective-permute-start.15 = (bf16[384,768]{1,0:T(8,128)(2,1)}, bf16[384,768]{1,0:T(8,128)(2,1)}, u32[]{:S(2)}, u32[]{:S(2)}) collective-permute-start(bf16[384,768]{1,0:T(8,128)(2,1)} %slice_select_fusion), channel_id=1, source_target_pairs={{0,1},{1,2},{2,3},{3,483},{4,5},{5,6},{6,7},{7,487},{8,9},{9,10},{... | collective-permute-start | bytes 1769480 | tf_op jit(solution)/shard_map/farthest/ppermute | solution.py:84
  105.8 19.3 %collective-permute-start.14 = (bf16[384,768]{1,0:T(8,128)(2,1)}, bf16[384,768]{1,0:T(8,128)(2,1)}, u32[]{:S(2)}, u32[]{:S(2)}) collective-permute-start(bf16[384,768]{1,0:T(8,128)(2,1)} %slice_select_fusion.1.inner0), channel_id=1, source_target_pairs={{0,32},{1,33},{2,34},{3,35},{4,36},{5,37},{6,38},{7,39},{8,40},{9,... | collective-permute-start | bytes 1769480 | tf_op jit(solution)/shard_map/sibling_hop0/ppermute | solution.py:84
  115.8 4.6 %copy-start.3 = (f32[384,128]{1,0:T(8,128)S(1)}, f32[384,128]{1,0:T(8,128)}, u32[]{:S(2)}) copy-start(f32[384,128]{1,0:T(8,128)} %copy-done.2) | copy-start | bytes 589828
  115.8 4.6 %copy-start.5 = (f32[384,768]{1,0:T(8,128)S(1)}, f32[384,768]{1,0:T(8,128)}, u32[]{:S(2)}) copy-start(f32[384,768]{1,0:T(8,128)} %copy-done.4) | copy-start | bytes 3538948

commit v14 on v13

--- a/solution.py
+++ b/solution.py
@@ -314,7 +314,7 @@
 
     near_sum = call(
         "terms_own1", own1_kernel, total, (scale,),
-        (other, near_factor, key_factors, after(inner1, whole_blocks, far2), near_sum), 100_000_000,
+        (other, near_factor, key_factors, after(inner1, whole_blocks), near_sum), 100_000_000,
     )
 
     def merge_kernel(edge, early, late, gathered, outer1, inner1, out, sems):
@@ -342,7 +342,7 @@
 
     near_sum = call(
         "terms_near1", near1_kernel, total, (scale,),
-        (other, near_factor, key_factors, carried, near_sum), 50_000_000,
+        (other, near_factor, key_factors, after(carried, far2), near_sum), 50_000_000,
     )
     hop_far2 = send(
         "farthest", jnp.where(is_edge, whole_blocks[:rows], after(far2, near_sum)), farthest_route

time: 129 us -> 132 us (1.023)
  the two profiles are of different devices: /device:TPU:25 before, /device:TPU:65 now
where the time goes in v14:
time: 132 us
  starting transfers between devices  54 us (41%)
  waiting for transfers between devices  38.3 us (29%)
  Pallas kernels  28.3 us (21%)
  other arithmetic  8.83 us (7%)
  between operations  1.98 us (2%)
    ppermute x17, starting transfers between devices, send(): return lax.ppermute(x, AXES, pairs(target))  54 us
    ppermute x17, waiting for transfers between devices, send(): return lax.ppermute(x, AXES, pairs(target))  38.3 us
    pallas_call x7, Pallas kernels, call(): pl.pallas_call(kernel, out_shape=out_shape, in_specs=[scalars() for _ in...  14.6 us
    pallas_call x2, Pallas kernels, assemble(): pl.pallas_call(kernel, out_shape=out_shape, in_specs=[scalars() for _ in...  5.66 us
    pallas_call x1, Pallas kernels, on_device(): pl.pallas_call(near0_kernel, out_shape=[total, total], in_specs=[scalars(...  4.59 us
    pallas_call x1, Pallas kernels, on_device(): pl.pallas_call(last_kernel, out_shape=[total, total], in_specs=[scalars()...  3.54 us
  transfers between devices with their start and end apart: 17, of which 4 were waited for; matrix products, arithmetic and copies ran while one was open for 5% of the time, Pallas kernels for 19%

profile of v14, /device:TPU:65, one launch (start us, length us, event | category | flops | bytes accessed | tf_op | source)
XLA Modules:
  0.0 131.5 jit_solution(12077703834233393309)
XLA Ops:
  0.6 2.1 %broadcast_select_fusion = (bf16[384,768]{1,0:T(8,128)(2,1)}, bf16[384,768]{1,0:T(8,128)(2,1)S(1)}) fusion(bf16[384,768]{1,0:T(8,128)(2,1)} %param.5, bf16[384,768]{1,0:T(8,128)(2,1)} %param.6, pred[]{:T(512)S(6)} %eq.60), kind=kLoop, calls=%fused_computation.3 | loop fusion | flops 589824 | bytes 2359297 | tf_op jit(solution)/shard_map/jit(_where)/select_n | solution.py:186
  2.8 2.6 %collective-permute-start = (bf16[384,768]{1,0:T(8,128)(2,1)}, bf16[384,768]{1,0:T(8,128)(2,1)S(1)}, u32[]{:S(2)}, u32[]{:S(2)}) collective-permute-start(bf16[384,768]{1,0:T(8,128)(2,1)} %get-tuple-element.98.oth.refs_3_), channel_id=1, source_target_pairs={{0,32},{1,33},{2,34},{3,35},{4,36},{5,37},{6,38},{7,39},{8,40},{9,... | collective-permute-start | bytes 1769480 | tf_op jit(solution)/shard_map/swap/ppermute | solution.py:84
  5.4 3.5 %collective-permute-start.5 = (bf16[384,768]{1,0:T(8,128)(2,1)S(1)}, bf16[384,768]{1,0:T(8,128)(2,1)S(1)}, u32[]{:S(2)}, u32[]{:S(2)}) collective-permute-start(bf16[384,768]{1,0:T(8,128)(2,1)S(1)} %get-tuple-element.99.outer.out.refs_0_), channel_id=1, source_target_pairs={{0,448},{1,449},{2,450},{3,451},{4,452},{5,453},{6,454},{7,455},{8... | collective-permute-start | bytes 1769480 | tf_op jit(solution)/shard_map/own_outer1/ppermute | solution.py:84
  8.9 0.0 collective-permute-done.inner.refs_1_
  8.9 0.1 cut.1
  9.0 1.3 collective-permute-start.1
  10.3 1.4 %collective-permute-start.2 = (bf16[192,768]{1,0:T(8,128)(2,1)S(1)}, bf16[192,768]{1,0:T(8,128)(2,1)}, u32[]{:S(2)}, u32[]{:S(2)}) collective-permute-start(bf16[192,768]{1,0:T(8,128)(2,1)S(1)} %get-tuple-element.43), channel_id=1, source_target_pairs={{0,1},{4,5},{8,9},{12,13},{16,17},{20,21},{24,25},{28,29},{35,34},... | collective-permute-start | bytes 884744 | tf_op jit(solution)/shard_map/spread1/ppermute | solution.py:84
  11.7 1.4 %collective-permute-start.3 = (bf16[192,768]{1,0:T(8,128)(2,1)S(1)}, bf16[192,768]{1,0:T(8,128)(2,1)}, u32[]{:S(2)}, u32[]{:S(2)}) collective-permute-start(bf16[192,768]{1,0:T(8,128)(2,1)S(1)} %get-tuple-element.44), channel_id=1, source_target_pairs={{0,2},{4,6},{8,10},{12,14},{16,18},{20,22},{24,26},{28,30},{35,33}... | collective-permute-start | bytes 884744 | tf_op jit(solution)/shard_map/spread2/ppermute | solution.py:84
  13.1 6.7 %collective-permute-start.11 = (bf16[384,768]{1,0:T(8,128)(2,1)}, bf16[384,768]{1,0:T(8,128)(2,1)}, u32[]{:S(2)}, u32[]{:S(2)}) collective-permute-start(bf16[384,768]{1,0:T(8,128)(2,1)} %get-tuple-element.98.oth.refs_3_), channel_id=1, source_target_pairs={{0,96},{1,97},{2,98},{3,99},{4,100},{5,101},{6,102},{7,103},{8,104... | collective-permute-start | bytes 1769480 | tf_op jit(solution)/shard_map/own_inner1/ppermute | solution.py:84
  20.8 1.1 dynamic-slice_select_fusion
  21.9 0.0 collective-permute-done.1
  21.9 0.0 collective-permute-done.2
  21.9 0.0 collective-permute-done.3
  22.0 0.1 select_select_fusion
  22.0 13.3 %collective-permute-start.4 = (bf16[192,768]{1,0:T(8,128)(2,1)S(1)}, bf16[192,768]{1,0:T(8,128)(2,1)S(1)}, u32[]{:S(2)}, u32[]{:S(2)}) collective-permute-start(bf16[192,768]{1,0:T(8,128)(2,1)S(1)} %select_select_fusion), channel_id=1, source_target_pairs={{0,476},{1,477},{2,478},{3,479},{4,448},{5,449},{6,450},{7,451},{8... | collective-permute-start | bytes 884744 | tf_op jit(solution)/shard_map/cross/ppermute | solution.py:84
  35.4 0.0 collective-permute-done.5.refs_2_.outer1
  35.4 1.4 %pad_maximum_fusion = bf16[1152,768]{1,0:T(8,128)(2,1)} fusion(bf16[384,768]{1,0:T(8,128)(2,1)S(1)} %collective-permute-done.5.refs_2_.outer1, bf16[384,768]{1,0:T(8,128)(2,1)S(1)} %get-tuple-element.99.outer.out.refs_0_, bf16[384,768]{1,0:T(8,128)(2,1)S(1)} %collective-permute-done.inner.refs_1_), kind=kLoop, calls=%fused_computation | loop fusion | flops 5308416 | bytes 3538944 | tf_op jit(solution)/shard_map/concatenate | solution.py:207
  36.7 4.3 %collective-permute-start.6 = (bf16[1152,768]{1,0:T(8,128)(2,1)}, bf16[1152,768]{1,0:T(8,128)(2,1)}, u32[]{:S(2)}, u32[]{:S(2)}) collective-permute-start(bf16[1152,768]{1,0:T(8,128)(2,1)} %pad_maximum_fusion), channel_id=1, source_target_pairs={{1,0},{2,1},{3,2},{5,4},{6,5},{7,6},{9,8},{10,9},{11,10},{13,12},{... | collective-permute-start | bytes 5308424 | tf_op jit(solution)/shard_map/wide_early/ppermute | solution.py:84
  41.0 0.2 factors.1
  41.2 0.0 copy-start
  41.2 4.3 %terms_own0.1 = (f32[384,768]{1,0:T(8,128)S(1)}, f32[384,768]{1,0:T(8,128)S(1)}) custom-call(f32[1]{0:T(128)} %bitcast.3.s, bf16[384,768]{1,0:T(8,128)(2,1)} %get-tuple-element.98.oth.refs_3_, bf16[384,768]{1,0:T(8,128)(2,1)S(1)} %get-tuple-element.99.outer.out.refs_0_, f32[384,128]{1,0:T(8,128)S(1)} %get-tuple-element.64.nf, ...), custom_call_target="tpu_custom_call" | custom-call | flops 99999997952 | bytes 1000 | tf_op jit(solution)/shard_map/terms_own0/pallas_call | solution.py:99
  45.6 0.0 copy-done
  45.6 0.0 copy-start.2
  45.6 0.0 copy-start.4
  45.6 24.4 %collective-permute-done.4.block = bf16[192,768]{1,0:T(8,128)(2,1)S(1)} collective-permute-done((bf16[192,768]{1,0:T(8,128)(2,1)S(1)}, bf16[192,768]{1,0:T(8,128)(2,1)S(1)}, u32[]{:S(2)}, u32[]{:S(2)}) %collective-permute-start.4) | collective-permute-done | bytes 294944 | tf_op jit(solution)/shard_map/cross/ppermute | solution.py:84
  70.0 0.0 copy-done.2
  70.0 0.0 copy-done.4
  70.0 0.0 collective-permute-done.6.early
  70.1 1.3 collective-permute-start.9
  71.4 1.3 collective-permute-start.8
  72.7 1.3 collective-permute-start.7
  74.0 0.0 copy-start.5
  74.0 0.0 collective-permute-done.11.keys.inner1
  74.0 3.6 %collective-permute-start.12 = (bf16[384,768]{1,0:T(8,128)(2,1)}, bf16[384,768]{1,0:T(8,128)(2,1)S(1)}, u32[]{:S(2)}, u32[]{:S(2)}) collective-permute-start(bf16[384,768]{1,0:T(8,128)(2,1)} %collective-permute-done.11.keys.inner1), channel_id=1, source_target_pairs={{1,0},{2,1},{3,2},{5,4},{6,5},{7,6},{9,8},{10,9},{11,10},{13,12},{... | collective-permute-start | bytes 1769480 | tf_op jit(solution)/shard_map/wide_late/ppermute | solution.py:84
  77.5 1.9 %collective-permute-start.13 = (bf16[384,768]{1,0:T(8,128)(2,1)S(1)}, bf16[384,768]{1,0:T(8,128)(2,1)S(1)}, u32[]{:S(2)}, u32[]{:S(2)}) collective-permute-start(bf16[384,768]{1,0:T(8,128)(2,1)S(1)} %collective-permute-done.5.refs_2_.outer1), channel_id=1, source_target_pairs={{0,480},{1,481},{2,482},{3,483},{4,484},{5,485},{6,486},{7,487},{8... | collective-permute-start | bytes 1769480 | tf_op jit(solution)/shard_map/own_outer2/ppermute | solution.py:84
  79.5 2.4 %collective-permute-done.9.q3 = bf16[192,768]{1,0:T(8,128)(2,1)S(1)} collective-permute-done((bf16[192,768]{1,0:T(8,128)(2,1)S(1)}, bf16[192,768]{1,0:T(8,128)(2,1)S(1)}, u32[]{:S(2)}, u32[]{:S(2)}) %collective-permute-start.9) | collective-permute-done | bytes 294944 | tf_op jit(solution)/shard_map/gather3/ppermute | solution.py:84
  81.9 0.4 collective-permute-done.8.q2
  82.3 0.0 collective-permute-done.7.q1
  82.3 2.6 %whole_blocks.1.gathered = bf16[768,768]{1,0:T(8,128)(2,1)} custom-call(bf16[192,768]{1,0:T(8,128)(2,1)S(1)} %crossed.1.q0, bf16[192,768]{1,0:T(8,128)(2,1)S(1)} %collective-permute-done.7.q1, bf16[192,768]{1,0:T(8,128)(2,1)S(1)} %collective-permute-done.8.q2, bf16[192,768]{1,0:T(8,128)(2,1)S(1)} %collective-permute-done.9.q3), custom_call_target="tpu_custom_call" | custom-call | flops 1000 | bytes 1000 | tf_op jit(solution)/shard_map/whole_blocks/pallas_call | solution.py:114
  84.9 1.9 %collective-permute-start.10 = (bf16[768,768]{1,0:T(8,128)(2,1)}, bf16[768,768]{1,0:T(8,128)(2,1)}, u32[]{:S(2)}, u32[]{:S(2)}) collective-permute-start(bf16[768,768]{1,0:T(8,128)(2,1)} %whole_blocks.1.gathered), channel_id=1, source_target_pairs={{3,67},{7,71},{11,75},{15,79},{19,83},{23,87},{27,91},{31,95},{32,... | collective-permute-start | bytes 3538952 | tf_op jit(solution)/shard_map/edge_back/ppermute | solution.py:84
  86.9 0.0 copy-done.5
  86.9 2.2 %terms_own1.1.near_in = f32[384,768]{1,0:T(8,128)S(1)} custom-call(f32[1]{0:T(128)} %bitcast.4.s, bf16[384,768]{1,0:T(8,128)(2,1)} %get-tuple-element.98.oth.refs_3_, f32[384,128]{1,0:T(8,128)S(1)} %get-tuple-element.64.nf, f32[1,6144]{1,0:T(1,128)S(1)} %get-tuple-element.63.kf, bf16[384,768]{1,0:T(8,128)(2,1)} %collective-permute-done.11.keys.inner1, ...), custom_call_target="tpu_custom_call" | custom-call | flops 99999997952 | bytes 1000 | tf_op jit(solution)/shard_map/terms_own1/pallas_call | solution.py:99
  89.1 0.0 collective-permute-done.12.late
  89.1 3.1 %merge.1.keys = bf16[1536,768]{1,0:T(8,128)(2,1)} custom-call(s32[1]{0:T(128)} %bitcast.2.edge.e, bf16[1152,768]{1,0:T(8,128)(2,1)} %collective-permute-done.6.early, bf16[384,768]{1,0:T(8,128)(2,1)S(1)} %collective-permute-done.12.late, bf16[768,768]{1,0:T(8,128)(2,1)} %whole_blocks.1.gathered, bf16[384,768]{1,0:T(8,128)(2,1)S(1)} %collective-permute-done.5.refs_2_.outer1, ...), custom_call_target="tpu_custom_call" | custom-call | flops 1000 | bytes 1000 | tf_op jit(solution)/shard_map/merge/pallas_call | solution.py:114
  92.2 1.9 %collective-permute-start.16 = (bf16[1536,768]{1,0:T(8,128)(2,1)}, bf16[1536,768]{1,0:T(8,128)(2,1)}, u32[]{:S(2)}, u32[]{:S(2)}) collective-permute-start(bf16[1536,768]{1,0:T(8,128)(2,1)} %merge.1.keys), channel_id=1, source_target_pairs={{0,32},{1,33},{2,34},{3,35},{4,36},{5,37},{6,38},{7,39},{8,40},{9,... | collective-permute-start | bytes 7077896 | tf_op jit(solution)/shard_map/sibling1/ppermute | solution.py:84
  94.1 11.0 %collective-permute-done.13.farthest = bf16[384,768]{1,0:T(8,128)(2,1)S(1)} collective-permute-done((bf16[384,768]{1,0:T(8,128)(2,1)S(1)}, bf16[384,768]{1,0:T(8,128)(2,1)S(1)}, u32[]{:S(2)}, u32[]{:S(2)}) %collective-permute-start.13) | collective-permute-done | bytes 589856 | tf_op jit(solution)/shard_map/own_outer2/ppermute | solution.py:84
  105.1 3.1 %terms_near1.1.near_in = f32[384,768]{1,0:T(8,128)S(1)} custom-call(f32[1]{0:T(128)} %bitcast.5.s, bf16[384,768]{1,0:T(8,128)(2,1)} %get-tuple-element.98.oth.refs_3_, f32[384,128]{1,0:T(8,128)S(1)} %get-tuple-element.64.nf, f32[1,6144]{1,0:T(1,128)S(1)} %get-tuple-element.63.kf, bf16[1536,768]{1,0:T(8,128)(2,1)} %merge.1.keys, f32[384,768]{1,0:T(8,128)S(1)} %terms_own1.1.near_in), custom_call_target="tpu_custom_call" | custom-call | flops 49999998976 | bytes 1000 | tf_op jit(solution)/shard_map/terms_near1/pallas_call | solution.py:99
  108.2 2.0 %slice_select_fusion = bf16[384,768]{1,0:T(8,128)(2,1)} fusion(bf16[384,768]{1,0:T(8,128)(2,1)S(1)} %collective-permute-done.13.farthest, bf16[768,768]{1,0:T(8,128)(2,1)} %whole_blocks.1.gathered, pred[]{:T(512)S(6)} %eq.62), kind=kLoop, calls=%fused_computation.1 | loop fusion | flops 294912 | bytes 1769473 | tf_op jit(solution)/shard_map/jit(_where)/select_n | solution.py:348
  110.2 4.4 %collective-permute-start.15 = (bf16[384,768]{1,0:T(8,128)(2,1)}, bf16[384,768]{1,0:T(8,128)(2,1)}, u32[]{:S(2)}, u32[]{:S(2)}) collective-permute-start(bf16[384,768]{1,0:T(8,128)(2,1)} %slice_select_fusion), channel_id=1, source_target_pairs={{0,1},{1,2},{2,3},{3,483},{4,5},{5,6},{6,7},{7,487},{8,9},{9,10},{... | collective-permute-start | bytes 1769480 | tf_op jit(solution)/shard_map/farthest/ppermute | solution.py:84
  114.6 0.0 collective-permute-done.10.back
  114.6 2.1 %slice_select_fusion.1.inner0 = bf16[384,768]{1,0:T(8,128)(2,1)} fusion(bf16[1152,768]{1,0:T(8,128)(2,1)} %collective-permute-done.6.early, bf16[768,768]{1,0:T(8,128)(2,1)} %collective-permute-done.10.back, pred[]{:T(512)S(6)} %eq.62), kind=kLoop, calls=%fused_computation.2 | loop fusion | flops 294912 | bytes 1769473 | tf_op jit(solution)/shard_map/jit(_where)/select_n | solution.py:351
  116.7 1.9 %collective-permute-start.14 = (bf16[384,768]{1,0:T(8,128)(2,1)}, bf16[384,768]{1,0:T(8,128)(2,1)}, u32[]{:S(2)}, u32[]{:S(2)}) collective-permute-start(bf16[384,768]{1,0:T(8,128)(2,1)} %slice_select_fusion.1.inner0), channel_id=1, source_target_pairs={{0,32},{1,33},{2,34},{3,35},{4,36},{5,37},{6,38},{7,39},{8,40},{9,... | collective-permute-start | bytes 1769480 | tf_op jit(solution)/shard_map/sibling_hop0/ppermute | solution.py:84
  118.7 0.0 copy-start.1
  118.7 0.0 copy-start.3
  118.7 4.6 %terms_near0.1 = (f32[384,768]{1,0:T(8,128)}, f32[384,768]{1,0:T(8,128)}) custom-call(s32[1]{0:T(128)} %bitcast.c, s32[1]{0:T(128)} %bitcast.2.edge.e, f32[1]{0:T(128)} %bitcast.6.s, bf16[384,768]{1,0:T(8,128)(2,1)} %get-tuple-element.98.oth.refs_3_, f32[384,128]{1,0:T(8,128)S(1)} %get-tuple-element.64.nf, f32[1,6144]{1,0:T(1,128)S(1)} %get-tuple-element.63.kf, ...), custom_call_target="tpu_custom_call" | custom-call | flops 99999997952 | bytes 1000 | tf_op jit(solution)/shard_map/terms_near0/pallas_call | solution.py:377
  123.3 0.0 collective-permute-done.16.keys
  123.3 0.0 copy-done.1
  123.3 0.0 copy-done.3
  123.3 4.6 %terms_far1.1.far_in = f32[384,768]{1,0:T(8,128)S(1)} custom-call(f32[1]{0:T(128)} %bitcast.7.s, bf16[384,768]{1,0:T(8,128)(2,1)S(1)} %get-tuple-element.99.outer.out.refs_0_, f32[384,128]{1,0:T(8,128)S(1)} %copy-done.1, f32[1,6144]{1,0:T(1,128)S(1)} %get-tuple-element.63.kf, bf16[1536,768]{1,0:T(8,128)(2,1)} %collective-permute-done.16.keys, ...), custom_call_target="tpu_custom_call" | custom-call | flops 99999997952 | bytes 1000 | tf_op jit(solution)/shard_map/terms_far1/pallas_call | solution.py:99
  128.0 0.0 collective-permute-done.15.hf2
  128.0 0.0 collective-permute-done.14.hs0
  128.0 3.5 %terms_last.1 = (f32[384,768]{1,0:T(8,128)}, f32[384,768]{1,0:T(8,128)}) custom-call(s32[1]{0:T(128)} %bitcast.c, f32[1]{0:T(128)} %bitcast.8.s, bf16[384,768]{1,0:T(8,128)(2,1)S(1)} %get-tuple-element.99.outer.out.refs_0_, f32[384,128]{1,0:T(8,128)S(1)} %copy-done.1, ...), custom_call_target="tpu_custom_call", output_to_operand_aliasing={{0}: (8, {}), {1}: (9, {})} | custom-call | flops 1000 | bytes 1000 | tf_op jit(solution)/shard_map/terms_last/pallas_call | solution.py:426
  (1 shorter events, 0.0 us)
Async XLA Ops:
  2.8 6.1 %collective-permute-start = (bf16[384,768]{1,0:T(8,128)(2,1)}, bf16[384,768]{1,0:T(8,128)(2,1)S(1)}, u32[]{:S(2)}, u32[]{:S(2)}) collective-permute-start(bf16[384,768]{1,0:T(8,128)(2,1)} %get-tuple-element.98.oth.refs_3_), channel_id=1, source_target_pairs={{0,32},{1,33},{2,34},{3,35},{4,36},{5,37},{6,38},{7,39},{8,40},{9,... | collective-permute-start | bytes 1769480 | tf_op jit(solution)/shard_map/swap/ppermute | solution.py:84
  5.4 30.0 %collective-permute-start.5 = (bf16[384,768]{1,0:T(8,128)(2,1)S(1)}, bf16[384,768]{1,0:T(8,128)(2,1)S(1)}, u32[]{:S(2)}, u32[]{:S(2)}) collective-permute-start(bf16[384,768]{1,0:T(8,128)(2,1)S(1)} %get-tuple-element.99.outer.out.refs_0_), channel_id=1, source_target_pairs={{0,448},{1,449},{2,450},{3,451},{4,452},{5,453},{6,454},{7,455},{8... | collective-permute-start | bytes 1769480 | tf_op jit(solution)/shard_map/own_outer1/ppermute | solution.py:84
  9.0 12.9 %collective-permute-start.1 = (bf16[192,768]{1,0:T(8,128)(2,1)S(1)}, bf16[192,768]{1,0:T(8,128)(2,1)S(1)}, u32[]{:S(2)}, u32[]{:S(2)}) collective-permute-start(bf16[192,768]{1,0:T(8,128)(2,1)S(1)} %get-tuple-element.42), channel_id=1, source_target_pairs={{0,3},{4,7},{8,11},{12,15},{16,19},{20,23},{24,27},{28,31},{35,32}... | collective-permute-start | bytes 884744 | tf_op jit(solution)/shard_map/spread0/ppermute | solution.py:84
  10.3 11.6 %collective-permute-start.2 = (bf16[192,768]{1,0:T(8,128)(2,1)S(1)}, bf16[192,768]{1,0:T(8,128)(2,1)}, u32[]{:S(2)}, u32[]{:S(2)}) collective-permute-start(bf16[192,768]{1,0:T(8,128)(2,1)S(1)} %get-tuple-element.43), channel_id=1, source_target_pairs={{0,1},{4,5},{8,9},{12,13},{16,17},{20,21},{24,25},{28,29},{35,34},... | collective-permute-start | bytes 884744 | tf_op jit(solution)/shard_map/spread1/ppermute | solution.py:84
  11.7 10.2 %collective-permute-start.3 = (bf16[192,768]{1,0:T(8,128)(2,1)S(1)}, bf16[192,768]{1,0:T(8,128)(2,1)}, u32[]{:S(2)}, u32[]{:S(2)}) collective-permute-start(bf16[192,768]{1,0:T(8,128)(2,1)S(1)} %get-tuple-element.44), channel_id=1, source_target_pairs={{0,2},{4,6},{8,10},{12,14},{16,18},{20,22},{24,26},{28,30},{35,33}... | collective-permute-start | bytes 884744 | tf_op jit(solution)/shard_map/spread2/ppermute | solution.py:84
  13.1 60.9 %collective-permute-start.11 = (bf16[384,768]{1,0:T(8,128)(2,1)}, bf16[384,768]{1,0:T(8,128)(2,1)}, u32[]{:S(2)}, u32[]{:S(2)}) collective-permute-start(bf16[384,768]{1,0:T(8,128)(2,1)} %get-tuple-element.98.oth.refs_3_), channel_id=1, source_target_pairs={{0,96},{1,97},{2,98},{3,99},{4,100},{5,101},{6,102},{7,103},{8,104... | collective-permute-start | bytes 1769480 | tf_op jit(solution)/shard_map/own_inner1/ppermute | solution.py:84
  22.0 48.0 %collective-permute-start.4 = (bf16[192,768]{1,0:T(8,128)(2,1)S(1)}, bf16[192,768]{1,0:T(8,128)(2,1)S(1)}, u32[]{:S(2)}, u32[]{:S(2)}) collective-permute-start(bf16[192,768]{1,0:T(8,128)(2,1)S(1)} %select_select_fusion), channel_id=1, source_target_pairs={{0,476},{1,477},{2,478},{3,479},{4,448},{5,449},{6,450},{7,451},{8... | collective-permute-start | bytes 884744 | tf_op jit(solution)/shard_map/cross/ppermute | solution.py:84
  36.7 33.3 %collective-permute-start.6 = (bf16[1152,768]{1,0:T(8,128)(2,1)}, bf16[1152,768]{1,0:T(8,128)(2,1)}, u32[]{:S(2)}, u32[]{:S(2)}) collective-permute-start(bf16[1152,768]{1,0:T(8,128)(2,1)} %pad_maximum_fusion), channel_id=1, source_target_pairs={{1,0},{2,1},{3,2},{5,4},{6,5},{7,6},{9,8},{10,9},{11,10},{13,12},{... | collective-permute-start | bytes 5308424 | tf_op jit(solution)/shard_map/wide_early/ppermute | solution.py:84
  41.2 4.4 %copy-start = (f32[384,128]{1,0:T(8,128)}, f32[384,128]{1,0:T(8,128)S(1)}, u32[]{:S(2)}) copy-start(f32[384,128]{1,0:T(8,128)S(1)} %get-tuple-element.62.ff) | copy-start | bytes 589828
  45.6 24.4 %copy-start.2 = (f32[384,768]{1,0:T(8,128)}, f32[384,768]{1,0:T(8,128)S(1)}, u32[]{:S(2)}) copy-start(f32[384,768]{1,0:T(8,128)S(1)} %get-tuple-element.67.far_in) | copy-start | bytes 3538948
  45.6 24.4 %copy-start.4 = (f32[384,768]{1,0:T(8,128)}, f32[384,768]{1,0:T(8,128)S(1)}, u32[]{:S(2)}) copy-start(f32[384,768]{1,0:T(8,128)S(1)} %get-tuple-element.66.near_in) | copy-start | bytes 3538948
  70.1 11.8 %collective-permute-start.9 = (bf16[192,768]{1,0:T(8,128)(2,1)S(1)}, bf16[192,768]{1,0:T(8,128)(2,1)S(1)}, u32[]{:S(2)}, u32[]{:S(2)}) collective-permute-start(bf16[192,768]{1,0:T(8,128)(2,1)S(1)} %crossed.1.q0), channel_id=1, source_target_pairs={{0,3},{4,7},{8,11},{12,15},{16,19},{20,23},{24,27},{28,31},{35,32}... | collective-permute-start | bytes 884744 | tf_op jit(solution)/shard_map/gather3/ppermute | solution.py:84
  71.4 11.0 %collective-permute-start.8 = (bf16[192,768]{1,0:T(8,128)(2,1)S(1)}, bf16[192,768]{1,0:T(8,128)(2,1)S(1)}, u32[]{:S(2)}, u32[]{:S(2)}) collective-permute-start(bf16[192,768]{1,0:T(8,128)(2,1)S(1)} %crossed.1.q0), channel_id=1, source_target_pairs={{2,3},{6,7},{10,11},{14,15},{18,19},{22,23},{26,27},{30,31},{33,32... | collective-permute-start | bytes 884744 | tf_op jit(solution)/shard_map/gather2/ppermute | solution.py:84
  72.7 9.7 %collective-permute-start.7 = (bf16[192,768]{1,0:T(8,128)(2,1)S(1)}, bf16[192,768]{1,0:T(8,128)(2,1)S(1)}, u32[]{:S(2)}, u32[]{:S(2)}) collective-permute-start(bf16[192,768]{1,0:T(8,128)(2,1)S(1)} %crossed.1.q0), channel_id=1, source_target_pairs={{1,3},{5,7},{9,11},{13,15},{17,19},{21,23},{25,27},{29,31},{34,32}... | collective-permute-start | bytes 884744 | tf_op jit(solution)/shard_map/gather1/ppermute | solution.py:84
  74.0 12.9 %copy-start.5 = (f32[384,768]{1,0:T(8,128)S(1)}, f32[384,768]{1,0:T(8,128)}, u32[]{:S(2)}) copy-start(f32[384,768]{1,0:T(8,128)} %copy-done.4) | copy-start | bytes 3538948
  74.0 15.1 %collective-permute-start.12 = (bf16[384,768]{1,0:T(8,128)(2,1)}, bf16[384,768]{1,0:T(8,128)(2,1)S(1)}, u32[]{:S(2)}, u32[]{:S(2)}) collective-permute-start(bf16[384,768]{1,0:T(8,128)(2,1)} %collective-permute-done.11.keys.inner1), channel_id=1, source_target_pairs={{1,0},{2,1},{3,2},{5,4},{6,5},{7,6},{9,8},{10,9},{11,10},{13,12},{... | collective-permute-start | bytes 1769480 | tf_op jit(solution)/shard_map/wide_late/ppermute | solution.py:84
  77.5 27.6 %collective-permute-start.13 = (bf16[384,768]{1,0:T(8,128)(2,1)S(1)}, bf16[384,768]{1,0:T(8,128)(2,1)S(1)}, u32[]{:S(2)}, u32[]{:S(2)}) collective-permute-start(bf16[384,768]{1,0:T(8,128)(2,1)S(1)} %collective-permute-done.5.refs_2_.outer1), channel_id=1, source_target_pairs={{0,480},{1,481},{2,482},{3,483},{4,484},{5,485},{6,486},{7,487},{8... | collective-permute-start | bytes 1769480 | tf_op jit(solution)/shard_map/own_outer2/ppermute | solution.py:84
  84.9 29.7 %collective-permute-start.10 = (bf16[768,768]{1,0:T(8,128)(2,1)}, bf16[768,768]{1,0:T(8,128)(2,1)}, u32[]{:S(2)}, u32[]{:S(2)}) collective-permute-start(bf16[768,768]{1,0:T(8,128)(2,1)} %whole_blocks.1.gathered), channel_id=1, source_target_pairs={{3,67},{7,71},{11,75},{15,79},{19,83},{23,87},{27,91},{31,95},{32,... | collective-permute-start | bytes 3538952 | tf_op jit(solution)/shard_map/edge_back/ppermute | solution.py:84
  92.2 31.1 %collective-permute-start.16 = (bf16[1536,768]{1,0:T(8,128)(2,1)}, bf16[1536,768]{1,0:T(8,128)(2,1)}, u32[]{:S(2)}, u32[]{:S(2)}) collective-permute-start(bf16[1536,768]{1,0:T(8,128)(2,1)} %merge.1.keys), channel_id=1, source_target_pairs={{0,32},{1,33},{2,34},{3,35},{4,36},{5,37},{6,38},{7,39},{8,40},{9,... | collective-permute-start | bytes 7077896 | tf_op jit(solution)/shard_map/sibling1/ppermute | solution.py:84
  110.2 17.7 %collective-permute-start.15 = (bf16[384,768]{1,0:T(8,128)(2,1)}, bf16[384,768]{1,0:T(8,128)(2,1)}, u32[]{:S(2)}, u32[]{:S(2)}) collective-permute-start(bf16[384,768]{1,0:T(8,128)(2,1)} %slice_select_fusion), channel_id=1, source_target_pairs={{0,1},{1,2},{2,3},{3,483},{4,5},{5,6},{6,7},{7,487},{8,9},{9,10},{... | collective-permute-start | bytes 1769480 | tf_op jit(solution)/shard_map/farthest/ppermute | solution.py:84
  116.7 11.2 %collective-permute-start.14 = (bf16[384,768]{1,0:T(8,128)(2,1)}, bf16[384,768]{1,0:T(8,128)(2,1)}, u32[]{:S(2)}, u32[]{:S(2)}) collective-permute-start(bf16[384,768]{1,0:T(8,128)(2,1)} %slice_select_fusion.1.inner0), channel_id=1, source_target_pairs={{0,32},{1,33},{2,34},{3,35},{4,36},{5,37},{6,38},{7,39},{8,40},{9,... | collective-permute-start | bytes 1769480 | tf_op jit(solution)/shard_map/sibling_hop0/ppermute | solution.py:84
  118.7 4.6 %copy-start.1 = (f32[384,128]{1,0:T(8,128)S(1)}, f32[384,128]{1,0:T(8,128)}, u32[]{:S(2)}) copy-start(f32[384,128]{1,0:T(8,128)} %copy-done) | copy-start | bytes 589828
  118.7 4.6 %copy-start.3 = (f32[384,768]{1,0:T(8,128)S(1)}, f32[384,768]{1,0:T(8,128)}, u32[]{:S(2)}) copy-start(f32[384,768]{1,0:T(8,128)} %copy-done.2) | copy-start | bytes 3538948

commit v15 on v12

--- a/solution.py
+++ b/solution.py
@@ -359,7 +359,7 @@
     )
 
     hop_far2 = send(
-        "farthest", jnp.where(is_edge, hop1[:rows], after(far2, far_sum)), farthest_route
+        "farthest", jnp.where(is_edge, whole_blocks[:rows], far2), farthest_route
     )
 
     def far2_kernel(s, out, ff, kf, hop, far_in, far):

time: 126 us -> 127 us (level)
  other arithmetic: 7.21 us -> 9.2 us
  starting transfers between devices: 74.8 us -> 72.9 us
    select_n x1, other arithmetic: 0.08 us -> 2.05 us  [on_device(): jnp.where(is_edge, whole_blocks[:rows], far2)]
    ppermute x18, starting transfers between devices: 74.8 us -> 72.9 us  [send(): return lax.ppermute(x, AXES, pairs(target))]
  transfers between devices with their start and end apart: 18 -> 18, of which waited for: 2 -> 2; matrix products, arithmetic and copies ran while one was open for 4% -> 6% of each run, Pallas kernels for 17% -> 16%
where the time goes in v15:
time: 127 us; the launch traced here: 126 us
  starting transfers between devices  72.9 us (57%)
  Pallas kernels  23.9 us (19%)
  waiting for transfers between devices  17.6 us (14%)
  other arithmetic  9.2 us (7%)
  between operations  2.06 us (2%)
    ppermute x18, starting transfers between devices, send(): return lax.ppermute(x, AXES, pairs(target))  72.9 us
    ppermute x18, waiting for transfers between devices, send(): return lax.ppermute(x, AXES, pairs(target))  17.6 us
    pallas_call x8, Pallas kernels, call(): pl.pallas_call(kernel, out_shape=out_shape, in_specs=[scalars() for _ in...  12.6 us
    pallas_call x1, Pallas kernels, on_device(): pl.pallas_call(near0_kernel, out_shape=[total, total], in_specs=[scalars(...  4.31 us
    pallas_call x2, Pallas kernels, assemble(): pl.pallas_call(kernel, out_shape=out_shape, in_specs=[scalars() for _ in...  3.71 us
    pallas_call x1, Pallas kernels, on_device(): pl.pallas_call(last_kernel, out_shape=[total, total], in_specs=[scalars()...  3.36 us
  transfers between devices with their start and end apart: 18, of which 2 were waited for; matrix products, arithmetic and copies ran while one was open for 6% of the time, Pallas kernels for 16%

profile of v15, /device:TPU:25, one launch (start us, length us, event | category | flops | bytes accessed | tf_op | source)
XLA Modules:
  0.0 125.7 jit_solution(2014263376838730790)
XLA Ops:
  0.6 2.1 %broadcast_select_fusion = (bf16[384,768]{1,0:T(8,128)(2,1)}, bf16[384,768]{1,0:T(8,128)(2,1)S(1)}) fusion(bf16[384,768]{1,0:T(8,128)(2,1)} %param.5, bf16[384,768]{1,0:T(8,128)(2,1)} %param.6, pred[]{:T(512)S(6)} %eq.60), kind=kLoop, calls=%fused_computation.4 | loop fusion | flops 589824 | bytes 2359297 | tf_op jit(solution)/shard_map/jit(_where)/select_n | solution.py:186
  2.8 2.6 %collective-permute-start = (bf16[384,768]{1,0:T(8,128)(2,1)}, bf16[384,768]{1,0:T(8,128)(2,1)S(1)}, u32[]{:S(2)}, u32[]{:S(2)}) collective-permute-start(bf16[384,768]{1,0:T(8,128)(2,1)} %get-tuple-element.94.oth.refs_3_), channel_id=1, source_target_pairs={{0,32},{1,33},{2,34},{3,35},{4,36},{5,37},{6,38},{7,39},{8,40},{9,... | collective-permute-start | bytes 1769480 | tf_op jit(solution)/shard_map/swap/ppermute | solution.py:84
  5.4 3.5 %collective-permute-start.5 = (bf16[384,768]{1,0:T(8,128)(2,1)S(1)}, bf16[384,768]{1,0:T(8,128)(2,1)S(1)}, u32[]{:S(2)}, u32[]{:S(2)}) collective-permute-start(bf16[384,768]{1,0:T(8,128)(2,1)S(1)} %get-tuple-element.95.outer.out.refs_0_), channel_id=1, source_target_pairs={{0,448},{1,449},{2,450},{3,451},{4,452},{5,453},{6,454},{7,455},{8... | collective-permute-start | bytes 1769480 | tf_op jit(solution)/shard_map/own_outer1/ppermute | solution.py:84
  8.9 0.0 collective-permute-done.inner.refs_1_
  8.9 0.1 cut.1
  9.0 5.6 %collective-permute-start.1 = (bf16[192,768]{1,0:T(8,128)(2,1)S(1)}, bf16[192,768]{1,0:T(8,128)(2,1)S(1)}, u32[]{:S(2)}, u32[]{:S(2)}) collective-permute-start(bf16[192,768]{1,0:T(8,128)(2,1)S(1)} %get-tuple-element.40), channel_id=1, source_target_pairs={{0,3},{4,7},{8,11},{12,15},{16,19},{20,23},{24,27},{28,31},{35,32}... | collective-permute-start | bytes 884744 | tf_op jit(solution)/shard_map/spread0/ppermute | solution.py:84
  14.6 1.3 %collective-permute-start.2 = (bf16[192,768]{1,0:T(8,128)(2,1)S(1)}, bf16[192,768]{1,0:T(8,128)(2,1)S(1)}, u32[]{:S(2)}, u32[]{:S(2)}) collective-permute-start(bf16[192,768]{1,0:T(8,128)(2,1)S(1)} %get-tuple-element.41), channel_id=1, source_target_pairs={{0,1},{4,5},{8,9},{12,13},{16,17},{20,21},{24,25},{28,29},{35,34},... | collective-permute-start | bytes 884744 | tf_op jit(solution)/shard_map/spread1/ppermute | solution.py:84
  15.9 2.0 %collective-permute-start.3 = (bf16[192,768]{1,0:T(8,128)(2,1)S(1)}, bf16[192,768]{1,0:T(8,128)(2,1)}, u32[]{:S(2)}, u32[]{:S(2)}) collective-permute-start(bf16[192,768]{1,0:T(8,128)(2,1)S(1)} %get-tuple-element.42), channel_id=1, source_target_pairs={{0,2},{4,6},{8,10},{12,14},{16,18},{20,22},{24,26},{28,30},{35,33}... | collective-permute-start | bytes 884744 | tf_op jit(solution)/shard_map/spread2/ppermute | solution.py:84
  18.0 5.8 %collective-permute-start.11 = (bf16[384,768]{1,0:T(8,128)(2,1)}, bf16[384,768]{1,0:T(8,128)(2,1)}, u32[]{:S(2)}, u32[]{:S(2)}) collective-permute-start(bf16[384,768]{1,0:T(8,128)(2,1)} %get-tuple-element.94.oth.refs_3_), channel_id=1, source_target_pairs={{0,96},{1,97},{2,98},{3,99},{4,100},{5,101},{6,102},{7,103},{8,104... | collective-permute-start | bytes 1769480 | tf_op jit(solution)/shard_map/own_inner1/ppermute | solution.py:84
  24.7 1.2 dynamic-slice_select_fusion
  25.8 0.0 collective-permute-done.1
  25.9 0.0 collective-permute-done.2
  25.9 0.0 collective-permute-done.3
  25.9 0.1 select_select_fusion
  26.0 8.3 %collective-permute-start.4 = (bf16[192,768]{1,0:T(8,128)(2,1)S(1)}, bf16[192,768]{1,0:T(8,128)(2,1)S(1)}, u32[]{:S(2)}, u32[]{:S(2)}) collective-permute-start(bf16[192,768]{1,0:T(8,128)(2,1)S(1)} %select_select_fusion), channel_id=1, source_target_pairs={{0,476},{1,477},{2,478},{3,479},{4,448},{5,449},{6,450},{7,451},{8... | collective-permute-start | bytes 884744 | tf_op jit(solution)/shard_map/cross/ppermute | solution.py:84
  34.2 0.0 collective-permute-done.5.refs_2_
  34.2 1.3 %pad_maximum_fusion = bf16[1152,768]{1,0:T(8,128)(2,1)} fusion(bf16[384,768]{1,0:T(8,128)(2,1)S(1)} %collective-permute-done.5.refs_2_, bf16[384,768]{1,0:T(8,128)(2,1)S(1)} %get-tuple-element.95.outer.out.refs_0_, bf16[384,768]{1,0:T(8,128)(2,1)S(1)} %collective-permute-done.inner.refs_1_), kind=kLoop, calls=%fused_computation | loop fusion | flops 5308416 | bytes 3538944 | tf_op jit(solution)/shard_map/concatenate | solution.py:207
  35.6 1.3 %collective-permute-start.6 = (bf16[1152,768]{1,0:T(8,128)(2,1)}, bf16[1152,768]{1,0:T(8,128)(2,1)}, u32[]{:S(2)}, u32[]{:S(2)}) collective-permute-start(bf16[1152,768]{1,0:T(8,128)(2,1)} %pad_maximum_fusion), channel_id=1, source_target_pairs={{1,0},{2,1},{3,2},{5,4},{6,5},{7,6},{9,8},{10,9},{11,10},{13,12},{... | collective-permute-start | bytes 5308424 | tf_op jit(solution)/shard_map/wide_early/ppermute | solution.py:84
  36.9 0.2 factors.1
  37.0 0.0 copy-start
  37.1 0.0 copy-start.2
  37.1 0.0 copy-start.4
  37.1 4.4 %terms_own0.1 = (f32[384,768]{1,0:T(8,128)S(1)}, f32[384,768]{1,0:T(8,128)S(1)}) custom-call(f32[1]{0:T(128)} %bitcast.3.s, bf16[384,768]{1,0:T(8,128)(2,1)} %get-tuple-element.94.oth.refs_3_, bf16[384,768]{1,0:T(8,128)(2,1)S(1)} %get-tuple-element.95.outer.out.refs_0_, f32[384,128]{1,0:T(8,128)S(1)} %get-tuple-element.62.nf, ...), custom_call_target="tpu_custom_call" | custom-call | flops 99999997952 | bytes 1000 | tf_op jit(solution)/shard_map/terms_own0/pallas_call | solution.py:99
  41.5 0.0 copy-done
  41.5 0.0 copy-start.6
  41.5 3.3 %collective-permute-done.4.block = bf16[192,768]{1,0:T(8,128)(2,1)S(1)} collective-permute-done((bf16[192,768]{1,0:T(8,128)(2,1)S(1)}, bf16[192,768]{1,0:T(8,128)(2,1)S(1)}, u32[]{:S(2)}, u32[]{:S(2)}) %collective-permute-start.4) | collective-permute-done | bytes 294944 | tf_op jit(solution)/shard_map/cross/ppermute | solution.py:84
  44.9 14.3 %collective-permute-done.6.early = bf16[1152,768]{1,0:T(8,128)(2,1)} collective-permute-done((bf16[1152,768]{1,0:T(8,128)(2,1)}, bf16[1152,768]{1,0:T(8,128)(2,1)}, u32[]{:S(2)}, u32[]{:S(2)}) %collective-permute-start.6) | collective-permute-done | bytes 1769504 | tf_op jit(solution)/shard_map/wide_early/ppermute | solution.py:84
  59.1 11.9 %collective-permute-start.13 = (bf16[384,768]{1,0:T(8,128)(2,1)S(1)}, bf16[384,768]{1,0:T(8,128)(2,1)S(1)}, u32[]{:S(2)}, u32[]{:S(2)}) collective-permute-start(bf16[384,768]{1,0:T(8,128)(2,1)S(1)} %collective-permute-done.5.refs_2_), channel_id=1, source_target_pairs={{0,480},{1,481},{2,482},{3,483},{4,484},{5,485},{6,486},{7,487},{8... | collective-permute-start | bytes 1769480 | tf_op jit(solution)/shard_map/own_outer2/ppermute | solution.py:84
  71.0 0.7 collective-permute-start.7
  71.7 0.7 collective-permute-start.8
  72.4 3.0 %collective-permute-start.9 = (bf16[192,768]{1,0:T(8,128)(2,1)S(1)}, bf16[192,768]{1,0:T(8,128)(2,1)S(1)}, u32[]{:S(2)}, u32[]{:S(2)}) collective-permute-start(bf16[192,768]{1,0:T(8,128)(2,1)S(1)} %crossed.1.q0), channel_id=1, source_target_pairs={{0,3},{4,7},{8,11},{12,15},{16,19},{20,23},{24,27},{28,31},{35,32}... | collective-permute-start | bytes 884744 | tf_op jit(solution)/shard_map/gather3/ppermute | solution.py:84
  75.4 0.0 collective-permute-done.11.keys
  75.4 1.3 %collective-permute-start.12 = (bf16[384,768]{1,0:T(8,128)(2,1)}, bf16[384,768]{1,0:T(8,128)(2,1)S(1)}, u32[]{:S(2)}, u32[]{:S(2)}) collective-permute-start(bf16[384,768]{1,0:T(8,128)(2,1)} %collective-permute-done.11.keys), channel_id=1, source_target_pairs={{1,0},{2,1},{3,2},{5,4},{6,5},{7,6},{9,8},{10,9},{11,10},{13,12},{... | collective-permute-start | bytes 1769480 | tf_op jit(solution)/shard_map/wide_late/ppermute | solution.py:84
  76.7 1.1 pad_maximum_fusion.1
  77.8 0.0 copy-start.3
  77.8 0.0 copy-start.5
  77.8 0.0 copy-start.9
  77.9 0.0 collective-permute-done.7.q1
  77.9 7.3 %collective-permute-start.15 = (bf16[768,768]{1,0:T(8,128)(2,1)S(1)}, bf16[768,768]{1,0:T(8,128)(2,1)S(1)}, u32[]{:S(2)}, u32[]{:S(2)}) collective-permute-start(bf16[768,768]{1,0:T(8,128)(2,1)S(1)} %pad_maximum_fusion.1), channel_id=1, source_target_pairs={{0,32},{1,33},{2,34},{3,35},{4,36},{5,37},{6,38},{7,39},{8,40},{9,... | collective-permute-start | bytes 3538952 | tf_op jit(solution)/shard_map/sibling_own1/ppermute | solution.py:84
  85.2 0.0 collective-permute-done.8.q2
  85.2 0.0 collective-permute-done.9.q3
  85.2 2.6 %whole_blocks.1.gathered = bf16[768,768]{1,0:T(8,128)(2,1)} custom-call(bf16[192,768]{1,0:T(8,128)(2,1)S(1)} %crossed.1.q0, bf16[192,768]{1,0:T(8,128)(2,1)S(1)} %collective-permute-done.7.q1, bf16[192,768]{1,0:T(8,128)(2,1)S(1)} %collective-permute-done.8.q2, bf16[192,768]{1,0:T(8,128)(2,1)S(1)} %collective-permute-done.9.q3), custom_call_target="tpu_custom_call" | custom-call | flops 1000 | bytes 1000 | tf_op jit(solution)/shard_map/whole_blocks/pallas_call | solution.py:114
  87.8 1.7 %collective-permute-start.10 = (bf16[768,768]{1,0:T(8,128)(2,1)}, bf16[768,768]{1,0:T(8,128)(2,1)}, u32[]{:S(2)}, u32[]{:S(2)}) collective-permute-start(bf16[768,768]{1,0:T(8,128)(2,1)} %whole_blocks.1.gathered), channel_id=1, source_target_pairs={{3,67},{7,71},{11,75},{15,79},{19,83},{23,87},{27,91},{31,95},{32,... | collective-permute-start | bytes 3538952 | tf_op jit(solution)/shard_map/edge_back/ppermute | solution.py:84
  89.5 0.0 collective-permute-done.13.farthest
  89.5 0.0 copy-done.3
  89.6 2.2 %terms_own1.1.near_in = f32[384,768]{1,0:T(8,128)S(1)} custom-call(f32[1]{0:T(128)} %bitcast.4.s, bf16[384,768]{1,0:T(8,128)(2,1)} %get-tuple-element.94.oth.refs_3_, f32[384,128]{1,0:T(8,128)S(1)} %copy-done.5, f32[1,6144]{1,0:T(1,128)S(1)} %copy-done.3, bf16[384,768]{1,0:T(8,128)(2,1)} %collective-permute-done.11.keys, f32[384,768]{1,0:T(8,128)S(1)} %copy-done.9), custom_call_target="tpu_custom_call" | custom-call | flops 99999997952 | bytes 1000 | tf_op jit(solution)/shard_map/terms_own1/pallas_call | solution.py:99
  91.7 0.0 collective-permute-done.12.late
  91.8 1.1 merge.1.keys
  92.9 3.4 %collective-permute-start.14 = (bf16[768,768]{1,0:T(8,128)(2,1)S(1)}, bf16[768,768]{1,0:T(8,128)(2,1)S(1)}, u32[]{:S(2)}, u32[]{:S(2)}) collective-permute-start(bf16[768,768]{1,0:T(8,128)(2,1)S(1)} %merge.1.keys), channel_id=1, source_target_pairs={{0,32},{1,33},{2,34},{3,35},{4,36},{5,37},{6,38},{7,39},{8,40},{9,... | collective-permute-start | bytes 3538952 | tf_op jit(solution)/shard_map/sibling_hop1/ppermute | solution.py:84
  96.3 2.3 %terms_near1.1.near_in = f32[384,768]{1,0:T(8,128)S(1)} custom-call(f32[1]{0:T(128)} %bitcast.5.s, bf16[384,768]{1,0:T(8,128)(2,1)} %get-tuple-element.94.oth.refs_3_, f32[384,128]{1,0:T(8,128)S(1)} %copy-done.5, f32[1,6144]{1,0:T(1,128)S(1)} %copy-done.3, bf16[768,768]{1,0:T(8,128)(2,1)S(1)} %merge.1.keys, f32[384,768]{1,0:T(8,128)S(1)} %terms_own1.1.near_in), custom_call_target="tpu_custom_call" | custom-call | flops 1000 | bytes 1000 | tf_op jit(solution)/shard_map/terms_near1/pallas_call | solution.py:99
  98.6 0.0 copy-start.7
  98.7 2.1 %slice_select_fusion = bf16[384,768]{1,0:T(8,128)(2,1)} fusion(bf16[384,768]{1,0:T(8,128)(2,1)S(1)} %collective-permute-done.13.farthest, bf16[768,768]{1,0:T(8,128)(2,1)} %whole_blocks.1.gathered, pred[]{:T(512)S(6)} %eq.62), kind=kLoop, calls=%fused_computation.2 | loop fusion | flops 294912 | bytes 1769473 | tf_op jit(solution)/shard_map/jit(_where)/select_n | solution.py:362
  100.7 1.9 %collective-permute-start.17 = (bf16[384,768]{1,0:T(8,128)(2,1)}, bf16[384,768]{1,0:T(8,128)(2,1)}, u32[]{:S(2)}, u32[]{:S(2)}) collective-permute-start(bf16[384,768]{1,0:T(8,128)(2,1)} %slice_select_fusion), channel_id=1, source_target_pairs={{0,1},{1,2},{2,3},{3,483},{4,5},{5,6},{6,7},{7,487},{8,9},{9,10},{... | collective-permute-start | bytes 1769480 | tf_op jit(solution)/shard_map/farthest/ppermute | solution.py:84
  102.6 0.0 collective-permute-done.15.own
  102.7 2.1 %terms_far1.1.far_in = f32[384,768]{1,0:T(8,128)S(1)} custom-call(f32[1]{0:T(128)} %bitcast.6.s, bf16[384,768]{1,0:T(8,128)(2,1)S(1)} %get-tuple-element.95.outer.out.refs_0_, f32[384,128]{1,0:T(8,128)S(1)} %copy-done.1, f32[1,6144]{1,0:T(1,128)S(1)} %copy-done.3, bf16[768,768]{1,0:T(8,128)(2,1)S(1)} %collective-permute-done.15.own, ...), custom_call_target="tpu_custom_call" | custom-call | flops 49999998976 | bytes 1000 | tf_op jit(solution)/shard_map/terms_far1/pallas_call | solution.py:99
  104.8 0.0 collective-permute-done.14.hop
  104.8 1.3 %terms_far2.1.far_in = f32[384,768]{1,0:T(8,128)S(1)} custom-call(f32[1]{0:T(128)} %bitcast.7.s, bf16[384,768]{1,0:T(8,128)(2,1)S(1)} %get-tuple-element.95.outer.out.refs_0_, f32[384,128]{1,0:T(8,128)S(1)} %copy-done.1, f32[1,6144]{1,0:T(1,128)S(1)} %copy-done.3, bf16[768,768]{1,0:T(8,128)(2,1)S(1)} %collective-permute-done.14.hop, ...), custom_call_target="tpu_custom_call" | custom-call | flops 1000 | bytes 1000 | tf_op jit(solution)/shard_map/terms_far2/pallas_call | solution.py:99
  106.0 0.0 collective-permute-done.10.back
  106.0 1.3 %slice_select_fusion.1.inner0 = bf16[384,768]{1,0:T(8,128)(2,1)S(1)} fusion(bf16[1152,768]{1,0:T(8,128)(2,1)} %collective-permute-done.6.early, bf16[768,768]{1,0:T(8,128)(2,1)} %collective-permute-done.10.back, pred[]{:T(512)S(6)} %eq.62), kind=kLoop, calls=%fused_computation.3 | loop fusion | flops 294912 | bytes 1769473 | tf_op jit(solution)/shard_map/jit(_where)/select_n | solution.py:375
  107.4 10.6 %collective-permute-start.16 = (bf16[384,768]{1,0:T(8,128)(2,1)S(1)}, bf16[384,768]{1,0:T(8,128)(2,1)S(1)}, u32[]{:S(2)}, u32[]{:S(2)}) collective-permute-start(bf16[384,768]{1,0:T(8,128)(2,1)S(1)} %slice_select_fusion.1.inner0), channel_id=1, source_target_pairs={{0,32},{1,33},{2,34},{3,35},{4,36},{5,37},{6,38},{7,39},{8,40},{9,... | collective-permute-start | bytes 1769480 | tf_op jit(solution)/shard_map/sibling_hop0/ppermute | solution.py:84
  118.0 4.3 %terms_near0.1 = (f32[384,768]{1,0:T(8,128)}, f32[384,768]{1,0:T(8,128)}) custom-call(s32[1]{0:T(128)} %bitcast.c, s32[1]{0:T(128)} %bitcast.2.edge.e, f32[1]{0:T(128)} %bitcast.8.s, bf16[384,768]{1,0:T(8,128)(2,1)} %get-tuple-element.94.oth.refs_3_, f32[384,128]{1,0:T(8,128)S(1)} %copy-done.5, f32[1,6144]{1,0:T(1,128)S(1)} %copy-done.3, ...), custom_call_target="tpu_custom_call" | custom-call | flops 99999997952 | bytes 1000 | tf_op jit(solution)/shard_map/terms_near0/pallas_call | solution.py:401
  122.3 0.0 collective-permute-done.17.hf2
  122.3 0.0 collective-permute-done.16.hs0
  122.4 3.4 %terms_last.1 = (f32[384,768]{1,0:T(8,128)}, f32[384,768]{1,0:T(8,128)}) custom-call(s32[1]{0:T(128)} %bitcast.c, f32[1]{0:T(128)} %bitcast.9.s, bf16[384,768]{1,0:T(8,128)(2,1)S(1)} %get-tuple-element.95.outer.out.refs_0_, f32[384,128]{1,0:T(8,128)S(1)} %copy-done.1, f32[1,6144]{1,0:T(1,128)S(1)} %copy-done.3, ...), custom_call_target="tpu_custom_call", output_to_operand_aliasing={{0}: (8, {}), {1}: (9, {})} | custom-call | flops 1000 | bytes 1000 | tf_op jit(solution)/shard_map/terms_last/pallas_call | solution.py:437
  (11 shorter events, 0.0 us)
Async XLA Ops:
  2.8 6.1 %collective-permute-start = (bf16[384,768]{1,0:T(8,128)(2,1)}, bf16[384,768]{1,0:T(8,128)(2,1)S(1)}, u32[]{:S(2)}, u32[]{:S(2)}) collective-permute-start(bf16[384,768]{1,0:T(8,128)(2,1)} %get-tuple-element.94.oth.refs_3_), channel_id=1, source_target_pairs={{0,32},{1,33},{2,34},{3,35},{4,36},{5,37},{6,38},{7,39},{8,40},{9,... | collective-permute-start | bytes 1769480 | tf_op jit(solution)/shard_map/swap/ppermute | solution.py:84
  5.4 28.9 %collective-permute-start.5 = (bf16[384,768]{1,0:T(8,128)(2,1)S(1)}, bf16[384,768]{1,0:T(8,128)(2,1)S(1)}, u32[]{:S(2)}, u32[]{:S(2)}) collective-permute-start(bf16[384,768]{1,0:T(8,128)(2,1)S(1)} %get-tuple-element.95.outer.out.refs_0_), channel_id=1, source_target_pairs={{0,448},{1,449},{2,450},{3,451},{4,452},{5,453},{6,454},{7,455},{8... | collective-permute-start | bytes 1769480 | tf_op jit(solution)/shard_map/own_outer1/ppermute | solution.py:84
  9.0 16.8 %collective-permute-start.1 = (bf16[192,768]{1,0:T(8,128)(2,1)S(1)}, bf16[192,768]{1,0:T(8,128)(2,1)S(1)}, u32[]{:S(2)}, u32[]{:S(2)}) collective-permute-start(bf16[192,768]{1,0:T(8,128)(2,1)S(1)} %get-tuple-element.40), channel_id=1, source_target_pairs={{0,3},{4,7},{8,11},{12,15},{16,19},{20,23},{24,27},{28,31},{35,32}... | collective-permute-start | bytes 884744 | tf_op jit(solution)/shard_map/spread0/ppermute | solution.py:84
  14.6 11.2 %collective-permute-start.2 = (bf16[192,768]{1,0:T(8,128)(2,1)S(1)}, bf16[192,768]{1,0:T(8,128)(2,1)S(1)}, u32[]{:S(2)}, u32[]{:S(2)}) collective-permute-start(bf16[192,768]{1,0:T(8,128)(2,1)S(1)} %get-tuple-element.41), channel_id=1, source_target_pairs={{0,1},{4,5},{8,9},{12,13},{16,17},{20,21},{24,25},{28,29},{35,34},... | collective-permute-start | bytes 884744 | tf_op jit(solution)/shard_map/spread1/ppermute | solution.py:84
  15.9 9.9 %collective-permute-start.3 = (bf16[192,768]{1,0:T(8,128)(2,1)S(1)}, bf16[192,768]{1,0:T(8,128)(2,1)}, u32[]{:S(2)}, u32[]{:S(2)}) collective-permute-start(bf16[192,768]{1,0:T(8,128)(2,1)S(1)} %get-tuple-element.42), channel_id=1, source_target_pairs={{0,2},{4,6},{8,10},{12,14},{16,18},{20,22},{24,26},{28,30},{35,33}... | collective-permute-start | bytes 884744 | tf_op jit(solution)/shard_map/spread2/ppermute | solution.py:84
  18.0 57.4 %collective-permute-start.11 = (bf16[384,768]{1,0:T(8,128)(2,1)}, bf16[384,768]{1,0:T(8,128)(2,1)}, u32[]{:S(2)}, u32[]{:S(2)}) collective-permute-start(bf16[384,768]{1,0:T(8,128)(2,1)} %get-tuple-element.94.oth.refs_3_), channel_id=1, source_target_pairs={{0,96},{1,97},{2,98},{3,99},{4,100},{5,101},{6,102},{7,103},{8,104... | collective-permute-start | bytes 1769480 | tf_op jit(solution)/shard_map/own_inner1/ppermute | solution.py:84
  26.0 18.9 %collective-permute-start.4 = (bf16[192,768]{1,0:T(8,128)(2,1)S(1)}, bf16[192,768]{1,0:T(8,128)(2,1)S(1)}, u32[]{:S(2)}, u32[]{:S(2)}) collective-permute-start(bf16[192,768]{1,0:T(8,128)(2,1)S(1)} %select_select_fusion), channel_id=1, source_target_pairs={{0,476},{1,477},{2,478},{3,479},{4,448},{5,449},{6,450},{7,451},{8... | collective-permute-start | bytes 884744 | tf_op jit(solution)/shard_map/cross/ppermute | solution.py:84
  35.6 23.6 %collective-permute-start.6 = (bf16[1152,768]{1,0:T(8,128)(2,1)}, bf16[1152,768]{1,0:T(8,128)(2,1)}, u32[]{:S(2)}, u32[]{:S(2)}) collective-permute-start(bf16[1152,768]{1,0:T(8,128)(2,1)} %pad_maximum_fusion), channel_id=1, source_target_pairs={{1,0},{2,1},{3,2},{5,4},{6,5},{7,6},{9,8},{10,9},{11,10},{13,12},{... | collective-permute-start | bytes 5308424 | tf_op jit(solution)/shard_map/wide_early/ppermute | solution.py:84
  37.0 4.4 %copy-start = (f32[384,128]{1,0:T(8,128)}, f32[384,128]{1,0:T(8,128)S(1)}, u32[]{:S(2)}) copy-start(f32[384,128]{1,0:T(8,128)S(1)} %get-tuple-element.60.ff) | copy-start | bytes 589828
  37.1 4.4 %copy-start.2 = (f32[1,6144]{1,0:T(1,128)}, f32[1,6144]{1,0:T(1,128)S(1)}, u32[]{:S(2)}) copy-start(f32[1,6144]{1,0:T(1,128)S(1)} %get-tuple-element.61.kf) | copy-start | bytes 73732
  37.1 4.4 %copy-start.4 = (f32[384,128]{1,0:T(8,128)}, f32[384,128]{1,0:T(8,128)S(1)}, u32[]{:S(2)}) copy-start(f32[384,128]{1,0:T(8,128)S(1)} %get-tuple-element.62.nf) | copy-start | bytes 589828
  41.5 3.3 %copy-start.6 = (f32[384,768]{1,0:T(8,128)}, f32[384,768]{1,0:T(8,128)S(1)}, u32[]{:S(2)}) copy-start(f32[384,768]{1,0:T(8,128)S(1)} %get-tuple-element.65.far_in) | copy-start | bytes 3538948
  41.5 3.3 %copy-start.8 = (f32[384,768]{1,0:T(8,128)}, f32[384,768]{1,0:T(8,128)S(1)}, u32[]{:S(2)}) copy-start(f32[384,768]{1,0:T(8,128)S(1)} %get-tuple-element.64.near_in) | copy-start | bytes 3538948
  59.1 30.4 %collective-permute-start.13 = (bf16[384,768]{1,0:T(8,128)(2,1)S(1)}, bf16[384,768]{1,0:T(8,128)(2,1)S(1)}, u32[]{:S(2)}, u32[]{:S(2)}) collective-permute-start(bf16[384,768]{1,0:T(8,128)(2,1)S(1)} %collective-permute-done.5.refs_2_), channel_id=1, source_target_pairs={{0,480},{1,481},{2,482},{3,483},{4,484},{5,485},{6,486},{7,487},{8... | collective-permute-start | bytes 1769480 | tf_op jit(solution)/shard_map/own_outer2/ppermute | solution.py:84
  71.0 6.8 %collective-permute-start.7 = (bf16[192,768]{1,0:T(8,128)(2,1)S(1)}, bf16[192,768]{1,0:T(8,128)(2,1)S(1)}, u32[]{:S(2)}, u32[]{:S(2)}) collective-permute-start(bf16[192,768]{1,0:T(8,128)(2,1)S(1)} %crossed.1.q0), channel_id=1, source_target_pairs={{1,3},{5,7},{9,11},{13,15},{17,19},{21,23},{25,27},{29,31},{34,32}... | collective-permute-start | bytes 884744 | tf_op jit(solution)/shard_map/gather1/ppermute | solution.py:84
  71.7 13.5 %collective-permute-start.8 = (bf16[192,768]{1,0:T(8,128)(2,1)S(1)}, bf16[192,768]{1,0:T(8,128)(2,1)S(1)}, u32[]{:S(2)}, u32[]{:S(2)}) collective-permute-start(bf16[192,768]{1,0:T(8,128)(2,1)S(1)} %crossed.1.q0), channel_id=1, source_target_pairs={{2,3},{6,7},{10,11},{14,15},{18,19},{22,23},{26,27},{30,31},{33,32... | collective-permute-start | bytes 884744 | tf_op jit(solution)/shard_map/gather2/ppermute | solution.py:84
  72.4 12.8 %collective-permute-start.9 = (bf16[192,768]{1,0:T(8,128)(2,1)S(1)}, bf16[192,768]{1,0:T(8,128)(2,1)S(1)}, u32[]{:S(2)}, u32[]{:S(2)}) collective-permute-start(bf16[192,768]{1,0:T(8,128)(2,1)S(1)} %crossed.1.q0), channel_id=1, source_target_pairs={{0,3},{4,7},{8,11},{12,15},{16,19},{20,23},{24,27},{28,31},{35,32}... | collective-permute-start | bytes 884744 | tf_op jit(solution)/shard_map/gather3/ppermute | solution.py:84
  75.4 16.4 %collective-permute-start.12 = (bf16[384,768]{1,0:T(8,128)(2,1)}, bf16[384,768]{1,0:T(8,128)(2,1)S(1)}, u32[]{:S(2)}, u32[]{:S(2)}) collective-permute-start(bf16[384,768]{1,0:T(8,128)(2,1)} %collective-permute-done.11.keys), channel_id=1, source_target_pairs={{1,0},{2,1},{3,2},{5,4},{6,5},{7,6},{9,8},{10,9},{11,10},{13,12},{... | collective-permute-start | bytes 1769480 | tf_op jit(solution)/shard_map/wide_late/ppermute | solution.py:84
  77.8 11.7 %copy-start.3 = (f32[1,6144]{1,0:T(1,128)S(1)}, f32[1,6144]{1,0:T(1,128)}, u32[]{:S(2)}) copy-start(f32[1,6144]{1,0:T(1,128)} %copy-done.2) | copy-start | bytes 73732
  77.8 11.7 %copy-start.5 = (f32[384,128]{1,0:T(8,128)S(1)}, f32[384,128]{1,0:T(8,128)}, u32[]{:S(2)}) copy-start(f32[384,128]{1,0:T(8,128)} %copy-done.4) | copy-start | bytes 589828
  77.8 11.7 %copy-start.9 = (f32[384,768]{1,0:T(8,128)S(1)}, f32[384,768]{1,0:T(8,128)}, u32[]{:S(2)}) copy-start(f32[384,768]{1,0:T(8,128)} %copy-done.8) | copy-start | bytes 3538948
  77.9 24.8 %collective-permute-start.15 = (bf16[768,768]{1,0:T(8,128)(2,1)S(1)}, bf16[768,768]{1,0:T(8,128)(2,1)S(1)}, u32[]{:S(2)}, u32[]{:S(2)}) collective-permute-start(bf16[768,768]{1,0:T(8,128)(2,1)S(1)} %pad_maximum_fusion.1), channel_id=1, source_target_pairs={{0,32},{1,33},{2,34},{3,35},{4,36},{5,37},{6,38},{7,39},{8,40},{9,... | collective-permute-start | bytes 3538952 | tf_op jit(solution)/shard_map/sibling_own1/ppermute | solution.py:84
  87.8 18.2 %collective-permute-start.10 = (bf16[768,768]{1,0:T(8,128)(2,1)}, bf16[768,768]{1,0:T(8,128)(2,1)}, u32[]{:S(2)}, u32[]{:S(2)}) collective-permute-start(bf16[768,768]{1,0:T(8,128)(2,1)} %whole_blocks.1.gathered), channel_id=1, source_target_pairs={{3,67},{7,71},{11,75},{15,79},{19,83},{23,87},{27,91},{31,95},{32,... | collective-permute-start | bytes 3538952 | tf_op jit(solution)/shard_map/edge_back/ppermute | solution.py:84
  92.9 11.9 %collective-permute-start.14 = (bf16[768,768]{1,0:T(8,128)(2,1)S(1)}, bf16[768,768]{1,0:T(8,128)(2,1)S(1)}, u32[]{:S(2)}, u32[]{:S(2)}) collective-permute-start(bf16[768,768]{1,0:T(8,128)(2,1)S(1)} %merge.1.keys), channel_id=1, source_target_pairs={{0,32},{1,33},{2,34},{3,35},{4,36},{5,37},{6,38},{7,39},{8,40},{9,... | collective-permute-start | bytes 3538952 | tf_op jit(solution)/shard_map/sibling_hop1/ppermute | solution.py:84
  98.6 4.0 %copy-start.1 = (f32[384,128]{1,0:T(8,128)S(1)}, f32[384,128]{1,0:T(8,128)}, u32[]{:S(2)}) copy-start(f32[384,128]{1,0:T(8,128)} %copy-done) | copy-start | bytes 589828
  98.6 4.0 %copy-start.7 = (f32[384,768]{1,0:T(8,128)S(1)}, f32[384,768]{1,0:T(8,128)}, u32[]{:S(2)}) copy-start(f32[384,768]{1,0:T(8,128)} %copy-done.6) | copy-start | bytes 3538948
  100.7 21.6 %collective-permute-start.17 = (bf16[384,768]{1,0:T(8,128)(2,1)}, bf16[384,768]{1,0:T(8,128)(2,1)}, u32[]{:S(2)}, u32[]{:S(2)}) collective-permute-start(bf16[384,768]{1,0:T(8,128)(2,1)} %slice_select_fusion), channel_id=1, source_target_pairs={{0,1},{1,2},{2,3},{3,483},{4,5},{5,6},{6,7},{7,487},{8,9},{9,10},{... | collective-permute-start | bytes 1769480 | tf_op jit(solution)/shard_map/farthest/ppermute | solution.py:84
  107.4 15.0 %collective-permute-start.16 = (bf16[384,768]{1,0:T(8,128)(2,1)S(1)}, bf16[384,768]{1,0:T(8,128)(2,1)S(1)}, u32[]{:S(2)}, u32[]{:S(2)}) collective-permute-start(bf16[384,768]{1,0:T(8,128)(2,1)S(1)} %slice_select_fusion.1.inner0), channel_id=1, source_target_pairs={{0,32},{1,33},{2,34},{3,35},{4,36},{5,37},{6,38},{7,39},{8,40},{9,... | collective-permute-start | bytes 1769480 | tf_op jit(solution)/shard_map/sibling_hop0/ppermute | solution.py:84
